TPU v7x, 128 devices: a whole 4x4x4 slice. The times are simulated.
128 devices in a mesh: head: 8 (over y, core), exp: 16 (over z, x).
Axes of the slice: x: 4, y: 4, z: 4, core: 2. Of those that a mesh axis runs over, the one named last changes fastest.
Arguments:
- hidden_in: bfloat16 [4, 128, 6144], P(None, 'exp'), may hold values from -6 to 6
- step_qkv: bfloat16 [4, 128, 3, 8192], P(None, 'exp', None, 'head'), may hold values from -6 to 6
- decay_rates: float32 [4, 64], P(None, 'head'), may hold values from 0.005 to 1
- kv_state: float32 [128, 64, 128, 128], P('exp', 'head'), may hold values from -6 to 6
- attn_gain: float32 [8192], P('head'), may hold values from 0.1 to 1.9
- out_proj: bfloat16 [8192, 6144], P('head', 'exp'), may hold values from -0.0625 to 0.0625
- ffn_gain: float32 [6144], replicated, may hold values from 0.1 to 1.9
- routes: int32 [4, 128, 2], P(None, 'exp'), may hold values from 0 to 15, all different within a row; in each aligned block of 8 rows (0 to 7, 8 to 15, ..., all dimensions but the last counted through in order) at most 2 rows name the same one
- route_weights: float32 [4, 128, 2], P(None, 'exp'), may hold values from 0.2 to 1
- w_gate: bfloat16 [16, 6144, 4608], P('exp', None, 'head'), may hold values from -0.078125 to 0.078125
- w_up: bfloat16 [16, 6144, 4608], P('exp', None, 'head'), may hold values from -0.078125 to 0.078125
- w_down: bfloat16 [16, 4608, 6144], P('exp', 'head'), may hold values from -0.09375 to 0.09375
Outputs:
- attended: bfloat16 [4, 128, 6144], P(None, 'exp', 'head')
- expert_out: bfloat16 [4, 128, 6144], P(None, 'exp', 'head')
Inputs may be any that keep to these rules, and one draw needn't show every extreme that they name: `routes`: in each step the two experts of a row differ; in each step the rows of one device name one expert at most 2 times, a bound that some block reaches.
All inputs are finite; a program needn't handle non-finite values.
Results may differ from a plain program's by a relative error of at most 0.013.
Values may be sent and summed in bfloat16 or wider, within the bound.
No kernel may reach another device: no remote copies, remote signals or barrier semaphores. Data moves between devices by JAX's collectives and lax.ppermute only.
A program may use at most 128 MiB of HBM per device.

v0:
```python
import jax
import jax.numpy as jnp
from jax import lax
from jax.sharding import PartitionSpec as P

DECODE_STEPS = 4


def rms_rows(values, gain_vec):
    return values * lax.rsqrt(jnp.mean(values * values, axis=-1, keepdims=True) + 1e-06) * gain_vec


def slot_tables(route_ids, gate_weights, experts, capacity):
    row_count = route_ids.shape[0]
    flat_ids = route_ids.reshape(-1)
    expert_iota = jnp.arange(experts, dtype=jnp.int32)
    hit_table = (flat_ids[:, None] == expert_iota[None, :]).astype(jnp.int32)
    before = jnp.cumsum(hit_table, axis=0) - hit_table
    rank_pos = jnp.sum(before * hit_table, axis=1)
    target = flat_ids * capacity + rank_pos
    slot_iota = jnp.arange(experts * capacity, dtype=jnp.int32)
    slot_match = (target[None, :] == slot_iota[:, None]).astype(jnp.float32)
    placed = slot_match.reshape(experts * capacity, row_count, 2)
    send_table = jnp.sum(placed, axis=2)
    mix_table = jnp.sum(placed * gate_weights[None, :, :], axis=2)
    return (send_table, mix_table)


def shards(
    hidden_in,
    step_qkv,
    decay_rates,
    kv_state,
    attn_gain,
    out_proj,
    ffn_gain,
    routes,
    route_weights,
    w_gate,
    w_up,
    w_down,
):
    block_rows = hidden_in.shape[1]
    width = hidden_in.shape[2]
    head_count = decay_rates.shape[1]
    head_size = kv_state.shape[2]
    experts = w_gate.shape[0] * lax.axis_size("exp")
    capacity = max(2, 4 * block_rows // experts)
    share = width // lax.axis_size("head")
    head_pos = lax.axis_index("head")
    gain_heads = attn_gain.reshape(head_count, head_size)
    state_now = kv_state
    attended_list = []
    expert_list = []
    for step in range(DECODE_STEPS):
        queries = (
            step_qkv[step, :, 0].astype(jnp.float32).reshape(block_rows, head_count, head_size)
        )
        key_vecs = step_qkv[step, :, 1].reshape(block_rows, head_count, head_size)
        value_vecs = step_qkv[step, :, 2].reshape(block_rows, head_count, head_size)
        outer = jnp.einsum(
            "bhk,bhv->bhkv", key_vecs, value_vecs, preferred_element_type=jnp.float32
        )
        state_now = decay_rates[step][None, :, None, None] * state_now + outer
        readout = jnp.einsum("bhk,bhkv->bhv", queries, state_now, precision=lax.Precision.HIGHEST)
        readout = (
            rms_rows(readout, gain_heads)
            .reshape(block_rows, head_count * head_size)
            .astype(jnp.bfloat16)
        )
        partial_value = jnp.dot(
            lax.all_gather(readout, "exp", axis=0, tiled=True),
            out_proj,
            preferred_element_type=jnp.float32,
        )
        summed = lax.psum(partial_value, "head")
        summed_rows = lax.all_to_all(summed, "exp", split_axis=0, concat_axis=1, tiled=True)
        attended_full = (hidden_in[step].astype(jnp.float32) + summed_rows).astype(jnp.bfloat16)
        attended_now = lax.dynamic_slice_in_dim(attended_full, head_pos * share, share, 1)
        normed_full = rms_rows(attended_full.astype(jnp.float32), ffn_gain).astype(jnp.bfloat16)
        normed_part = lax.dynamic_slice_in_dim(normed_full, head_pos * share, share, 1)
        send_table, mix_table = slot_tables(routes[step], route_weights[step], experts, capacity)
        source_rows = lax.all_gather(normed_part, "head", axis=1, tiled=True)
        sent = jnp.dot(
            send_table.astype(jnp.bfloat16), source_rows, preferred_element_type=jnp.float32
        )
        sent = sent.astype(jnp.bfloat16).reshape(experts, capacity, source_rows.shape[1])
        received = lax.all_to_all(sent, "exp", split_axis=0, concat_axis=0, tiled=True)
        sources = received.shape[0]
        items = received.shape[1]
        rows_in = received.reshape(sources * items, width)
        gate_val = jnp.dot(rows_in, w_gate[0], preferred_element_type=jnp.float32)
        up_val = jnp.dot(rows_in, w_up[0], preferred_element_type=jnp.float32)
        hidden_val = (jax.nn.silu(gate_val) * up_val).astype(jnp.bfloat16)
        down_val = jnp.dot(hidden_val, w_down[0], preferred_element_type=jnp.float32)
        reduced = lax.psum(down_val, "head")
        results = reduced.astype(jnp.bfloat16).reshape(sources, items, reduced.shape[1])
        back = lax.all_to_all(results, "exp", split_axis=0, concat_axis=0, tiled=True)
        back_rows = back.reshape(experts * capacity, back.shape[2]).astype(jnp.float32)
        mixed = jnp.dot(
            mix_table.T,
            back_rows,
            precision=lax.Precision.HIGHEST,
            preferred_element_type=jnp.float32,
        )
        mixed = lax.dynamic_slice_in_dim(mixed, head_pos * share, share, 1)
        attended_list.append(attended_now)
        expert_list.append(mixed.astype(jnp.bfloat16))
    return (jnp.stack(attended_list, 0), jnp.stack(expert_list, 0))


def solution(mesh):
    return jax.shard_map(
        shards,
        mesh=mesh,
        in_specs=(
            P(None, "exp", None),
            P(None, "exp", None, "head"),
            P(None, "head"),
            P("exp", "head", None, None),
            P("head"),
            P("head", "exp"),
            P(),
            P(None, "exp", None),
            P(None, "exp", None),
            P("exp", None, "head"),
            P("exp", None, "head"),
            P("exp", "head", None),
        ),
        out_specs=(P(None, "exp", "head"), P(None, "exp", "head")),
        check_vma=False,
    )
```

profile of v0, /device:TPU:0, one launch (start us, length us, event | category | flops | bytes accessed | tf_op | source)
XLA Modules:
  0.0 498.7 jit_solution(4812294804849868683)
XLA Ops:
  26.3 25.2 %all_gather.27 = bf16[128,1024]{1,0:T(8,128)(2,1)S(1)} all-gather(bf16[8,1024]{1,0:T(8,128)(2,1)S(1)} %bitcast.272), channel_id=1, replica_groups=mesh['head'=8,'exp'=16] {'exp'}, dimensions={0}, use_global_device_ids=true | all-gather | bytes 278528 | tf_op jit(solution)/shard_map/all_gather | solution.py:72
  51.4 23.1 %all_gather.26 = bf16[128,1024]{1,0:T(8,128)(2,1)S(1)} all-gather(bf16[8,1024]{1,0:T(8,128)(2,1)S(1)} %bitcast.271), channel_id=1, replica_groups=mesh['head'=8,'exp'=16] {'exp'}, dimensions={0}, use_global_device_ids=true | all-gather | bytes 278528 | tf_op jit(solution)/shard_map/all_gather | solution.py:72
  76.5 21.6 %all_gather.25 = bf16[128,1024]{1,0:T(8,128)(2,1)S(1)} all-gather(bf16[8,1024]{1,0:T(8,128)(2,1)S(1)} %bitcast.270), channel_id=1, replica_groups=mesh['head'=8,'exp'=16] {'exp'}, dimensions={0}, use_global_device_ids=true | all-gather | bytes 278528 | tf_op jit(solution)/shard_map/all_gather | solution.py:72
  99.1 23.0 %all_gather.24 = bf16[128,1024]{1,0:T(8,128)(2,1)S(1)} all-gather(bf16[8,1024]{1,0:T(8,128)(2,1)S(1)} %bitcast.269), channel_id=1, replica_groups=mesh['head'=8,'exp'=16] {'exp'}, dimensions={0}, use_global_device_ids=true | all-gather | bytes 278528 | tf_op jit(solution)/shard_map/all_gather | solution.py:72
  126.7 57.1 %all-reduce.5.cloned.1.call-done = (f32[16,8,384]{2,1,0:T(8,128)}, f32[16,8,384]{2,1,0:T(8,128)}, f32[16,8,384]{2,1,0:T(8,128)}, f32[16,8,384]{2,1,0:T(8,128)}) async-done(((f32[16,8,384]{2,1,0:T(8,128)}, f32[16,8,384]{2,1,0:T(8,128)}, f32[16,8,384]{2,1,0:T(8,128)}, f32[16,8,384]{2,1,0:T(8,128)}), (f32[16,8,384]{2,1,0:T(8,128)}, f32[16,8,384]{2,1,0:T(8,128)}, f32[16,8,384]{2,1,0:T(8,128)}, ...) | async-done | bytes 786448 | tf_op jit(solution)/shard_map/psum | solution.py:76
  183.8 6.9 %all-to-all-start.3 = ((f32[16,8,384]{2,1,0:T(8,128)}), f32[16,8,384]{2,1,0:T(8,128)S(1)}, u32[]{:S(2)}, u32[]{:S(2)}) async-start(f32[16,8,384]{2,1,0:T(8,128)} %get-tuple-element.14), calls=%async_computation.3 | async-start | bytes 393216 | tf_op jit(solution)/shard_map/all_to_all | solution.py:77
  190.9 8.2 %all-to-all-done.3 = f32[16,8,384]{2,1,0:T(8,128)S(1)} async-done(((f32[16,8,384]{2,1,0:T(8,128)}), f32[16,8,384]{2,1,0:T(8,128)S(1)}, u32[]{:S(2)}, u32[]{:S(2)}) %all-to-all-start.3) | async-done | bytes 196640 | tf_op jit(solution)/shard_map/all_to_all | solution.py:77
  202.8 8.1 %all-to-all-done.2 = f32[16,8,384]{2,1,0:T(8,128)S(1)} async-done(((f32[16,8,384]{2,1,0:T(8,128)}), f32[16,8,384]{2,1,0:T(8,128)S(1)}, u32[]{:S(2)}, u32[]{:S(2)}) %all-to-all-start.2) | async-done | bytes 196640 | tf_op jit(solution)/shard_map/all_to_all | solution.py:77
  214.7 8.1 %all-to-all-done.1 = f32[16,8,384]{2,1,0:T(8,128)S(1)} async-done(((f32[16,8,384]{2,1,0:T(8,128)}), f32[16,8,384]{2,1,0:T(8,128)S(1)}, u32[]{:S(2)}, u32[]{:S(2)}) %all-to-all-start.1) | async-done | bytes 196640 | tf_op jit(solution)/shard_map/all_to_all | solution.py:77
  226.5 8.1 %all-to-all-done = f32[16,8,384]{2,1,0:T(8,128)S(1)} async-done(((f32[16,8,384]{2,1,0:T(8,128)}), f32[16,8,384]{2,1,0:T(8,128)S(1)}, u32[]{:S(2)}, u32[]{:S(2)}) %all-to-all-start) | async-done | bytes 196640 | tf_op jit(solution)/shard_map/all_to_all | solution.py:77
  235.0 12.7 %all_gather.29 = bf16[8,6144]{1,0:T(8,128)(2,1)S(1)} all-gather(bf16[8,768]{1,0:T(8,128)(2,1)S(1)} %get-tuple-element.51), channel_id=1, replica_groups=mesh['head'=8,'exp'=16] {'head'}, dimensions={1}, use_global_device_ids=true | all-gather | bytes 110592 | tf_op jit(solution)/shard_map/all_gather | solution.py:83
  247.7 12.9 %all_gather.30 = bf16[8,6144]{1,0:T(8,128)(2,1)S(1)} all-gather(bf16[8,768]{1,0:T(8,128)(2,1)S(1)} %get-tuple-element.52), channel_id=1, replica_groups=mesh['head'=8,'exp'=16] {'head'}, dimensions={1}, use_global_device_ids=true | all-gather | bytes 110592 | tf_op jit(solution)/shard_map/all_gather | solution.py:83
  260.6 12.7 %all_gather.31 = bf16[8,6144]{1,0:T(8,128)(2,1)S(1)} all-gather(bf16[8,768]{1,0:T(8,128)(2,1)S(1)} %get-tuple-element.53), channel_id=1, replica_groups=mesh['head'=8,'exp'=16] {'head'}, dimensions={1}, use_global_device_ids=true | all-gather | bytes 110592 | tf_op jit(solution)/shard_map/all_gather | solution.py:83
  280.9 12.7 %all_gather.28 = bf16[8,6144]{1,0:T(8,128)(2,1)S(1)} all-gather(bf16[8,768]{1,0:T(8,128)(2,1)S(1)} %get-tuple-element.50), channel_id=1, replica_groups=mesh['head'=8,'exp'=16] {'head'}, dimensions={1}, use_global_device_ids=true | all-gather | bytes 110592 | tf_op jit(solution)/shard_map/all_gather | solution.py:83
  294.9 7.2 %all-to-all-start.8 = ((bf16[16,2,6144]{2,1,0:T(2,128)(2,1)}), bf16[16,2,6144]{2,1,0:T(2,128)(2,1)S(1)}, u32[]{:S(2)}, u32[]{:S(2)}) async-start(bf16[16,2,6144]{2,1,0:T(2,128)(2,1)} %reshape.314), calls=%async_computation.8 | async-start | bytes 786432 | tf_op jit(solution)/shard_map/all_to_all | solution.py:88
  307.4 5.3 %all-to-all-done.8 = bf16[16,2,6144]{2,1,0:T(2,128)(2,1)S(1)} async-done(((bf16[16,2,6144]{2,1,0:T(2,128)(2,1)}), bf16[16,2,6144]{2,1,0:T(2,128)(2,1)S(1)}, u32[]{:S(2)}, u32[]{:S(2)}) %all-to-all-start.8) | async-done | bytes 393248 | tf_op jit(solution)/shard_map/all_to_all | solution.py:88
  343.8 8.6 %fusion.6 = f32[32,6144]{1,0:T(8,128)S(1)} fusion(bf16[1,576,6144]{2,1,0:T(8,128)(2,1)} %param.23, bf16[32,6144]{1,0:T(8,128)(2,1)S(1)} %reshape.307, bf16[1,6144,576]{1,2,0:T(8,128)(2,1)} %param.22, f32[32,576]{1,0:T(8,128)S(1)} %fusion.22), kind=kOutput, calls=%fused_computation.6 | convolution fusion | flops 453095424 | bytes 15409152 | tf_op jit(solution)/shard_map/dot_general | solution.py:95
  352.5 9.5 %fusion.4 = f32[32,6144]{1,0:T(8,128)} fusion(bf16[1,576,6144]{2,1,0:T(8,128)(2,1)} %param.23, bf16[32,6144]{1,0:T(8,128)(2,1)S(1)} %reshape.311, bf16[1,6144,576]{1,2,0:T(8,128)(2,1)} %param.22, f32[32,576]{1,0:T(8,128)S(1)} %fusion.20), kind=kOutput, calls=%fused_computation.4 | convolution fusion | flops 453095424 | bytes 15409152 | tf_op jit(solution)/shard_map/dot_general | solution.py:95
  362.0 9.5 %fusion.2 = f32[32,6144]{1,0:T(8,128)} fusion(bf16[1,576,6144]{2,1,0:T(8,128)(2,1)} %param.23, bf16[32,6144]{1,0:T(8,128)(2,1)S(1)} %reshape.315, bf16[1,6144,576]{1,2,0:T(8,128)(2,1)} %param.22, f32[32,576]{1,0:T(8,128)S(1)} %fusion.18), kind=kOutput, calls=%fused_computation.2 | convolution fusion | flops 453095424 | bytes 15409152 | tf_op jit(solution)/shard_map/dot_general | solution.py:95
  371.6 9.8 %fusion = f32[32,6144]{1,0:T(8,128)} fusion(bf16[1,576,6144]{2,1,0:T(8,128)(2,1)} %param.23, bf16[32,6144]{1,0:T(8,128)(2,1)S(1)} %reshape.319, bf16[1,6144,576]{1,2,0:T(8,128)(2,1)} %param.22, f32[32,576]{1,0:T(8,128)S(1)} %fusion.16), kind=kOutput, calls=%fused_computation | convolution fusion | flops 453095424 | bytes 15409152 | tf_op jit(solution)/shard_map/dot_general | solution.py:95
  381.4 54.9 %all-reduce.6 = (bf16[32,6144]{1,0:T(8,128)(2,1)}, bf16[32,6144]{1,0:T(8,128)(2,1)S(1)}, bf16[32,6144]{1,0:T(8,128)(2,1)S(1)}, bf16[32,6144]{1,0:T(8,128)(2,1)S(1)}) all-reduce(f32[32,6144]{1,0:T(8,128)} %fusion, f32[32,6144]{1,0:T(8,128)} %fusion.2, f32[32,6144]{1,0:T(8,128)S(1)} %copy-done.2, ...), channel_id=1, replica_groups=mesh['head'=8,'exp'=16] {'head'}, use_global_device_ids=true, to_apply=%region_31.32 | all-reduce | flops 786432 | bytes 4718592 | tf_op jit(solution)/shard_map/psum | solution.py:96
  443.6 7.9 %all-to-all-done.11 = bf16[16,2,6144]{2,1,0:T(2,128)(2,1)S(1)} async-done(((bf16[16,2,6144]{2,1,0:T(2,128)(2,1)}), bf16[16,2,6144]{2,1,0:T(2,128)(2,1)S(1)}, u32[]{:S(2)}, u32[]{:S(2)}) %all-to-all-start.11) | async-done | bytes 393248 | tf_op jit(solution)/shard_map/all_to_all | solution.py:98
  468.7 8.6 %all-to-all-done.7 = bf16[16,2,6144]{2,1,0:T(2,128)(2,1)S(1)} async-done(((bf16[16,2,6144]{2,1,0:T(2,128)(2,1)}), bf16[16,2,6144]{2,1,0:T(2,128)(2,1)S(1)}, u32[]{:S(2)}, u32[]{:S(2)}) %all-to-all-start.7) | async-done | bytes 393248 | tf_op jit(solution)/shard_map/all_to_all | solution.py:98
  481.4 8.9 %all-to-all-done.5 = bf16[16,2,6144]{2,1,0:T(2,128)(2,1)S(1)} async-done(((bf16[16,2,6144]{2,1,0:T(2,128)(2,1)}), bf16[16,2,6144]{2,1,0:T(2,128)(2,1)S(1)}, u32[]{:S(2)}, u32[]{:S(2)}) %all-to-all-start.5) | async-done | bytes 393248 | tf_op jit(solution)/shard_map/all_to_all | solution.py:98
  (153 shorter events, 112.7 us)
Async XLA Ops:
  7.2 67.3 %copy-start = (bf16[1024,384]{1,0:T(8,128)(2,1)S(1)}, bf16[1024,384]{1,0:T(8,128)(2,1)}, u32[]{:S(2)}) copy-start(bf16[1024,384]{1,0:T(8,128)(2,1)} %param.17) | copy-start | bytes 2359300
  7.2 176.6 %all-reduce.5.cloned.1.call-start = ((), (), s32[]{:S(2)}) async-start(), calls=%async_computation.12 | async-start | bytes 1572864 | tf_op jit(solution)/shard_map/psum | solution.py:76
  7.2 6.5 %copy-start.1 = (f32[8,8,128,128]{3,2,1,0:T(8,128)S(1)}, f32[8,8,128,128]{3,2,1,0:T(8,128)}, u32[]{:S(2)}) copy-start(f32[8,8,128,128]{3,2,1,0:T(8,128)} %param.15) | copy-start | bytes 12582916
  21.0 5.1 %copy-start.9 = (f32[1024]{0:T(1024)S(1)}, f32[1024]{0:T(1024)}, u32[]{:S(2)}) copy-start(f32[1024]{0:T(1024)} %param.16) | copy-start | bytes 12292
  25.8 97.4 %copy-start.8 = (s32[4,8,2]{1,2,0:T(2,128)S(1)}, s32[4,8,2]{1,2,0:T(2,128)}, u32[]{:S(2)}) copy-start(s32[4,8,2]{1,2,0:T(2,128)} %param.19) | copy-start | bytes 772
  25.8 99.9 %copy-start.3 = (bf16[4,8,6144]{2,1,0:T(8,128)(2,1)S(1)}, bf16[4,8,6144]{2,1,0:T(8,128)(2,1)}, u32[]{:S(2)}) copy-start(bf16[4,8,6144]{2,1,0:T(8,128)(2,1)} %param.12) | copy-start | bytes 1179652
  26.2 100.3 %copy-start.10 = (f32[4,8,2]{1,2,0:T(2,128)S(1)}, f32[4,8,2]{1,2,0:T(2,128)}, u32[]{:S(2)}) copy-start(f32[4,8,2]{1,2,0:T(2,128)} %param.20) | copy-start | bytes 772
  183.8 15.3 %all-to-all-start.3 = ((f32[16,8,384]{2,1,0:T(8,128)}), f32[16,8,384]{2,1,0:T(8,128)S(1)}, u32[]{:S(2)}, u32[]{:S(2)}) async-start(f32[16,8,384]{2,1,0:T(8,128)} %get-tuple-element.14), calls=%async_computation.3 | async-start | bytes 393216 | tf_op jit(solution)/shard_map/all_to_all | solution.py:77
  199.1 11.8 %all-to-all-start.2 = ((f32[16,8,384]{2,1,0:T(8,128)}), f32[16,8,384]{2,1,0:T(8,128)S(1)}, u32[]{:S(2)}, u32[]{:S(2)}) async-start(f32[16,8,384]{2,1,0:T(8,128)} %get-tuple-element.15), calls=%async_computation.2 | async-start | bytes 393216 | tf_op jit(solution)/shard_map/all_to_all | solution.py:77
  210.9 11.8 %all-to-all-start.1 = ((f32[16,8,384]{2,1,0:T(8,128)}), f32[16,8,384]{2,1,0:T(8,128)S(1)}, u32[]{:S(2)}, u32[]{:S(2)}) async-start(f32[16,8,384]{2,1,0:T(8,128)} %get-tuple-element.16), calls=%async_computation.1 | async-start | bytes 393216 | tf_op jit(solution)/shard_map/all_to_all | solution.py:77
  222.8 11.8 %all-to-all-start = ((f32[16,8,384]{2,1,0:T(8,128)}), f32[16,8,384]{2,1,0:T(8,128)S(1)}, u32[]{:S(2)}, u32[]{:S(2)}) async-start(f32[16,8,384]{2,1,0:T(8,128)} %get-tuple-element.17), calls=%async_computation | async-start | bytes 393216 | tf_op jit(solution)/shard_map/all_to_all | solution.py:77
  234.9 38.5 %copy-start.4 = (bf16[8,6144]{1,0:T(8,128)(2,1)}, bf16[8,6144]{1,0:T(8,128)(2,1)S(1)}, u32[]{:S(2)}) copy-start(bf16[8,6144]{1,0:T(8,128)(2,1)S(1)} %get-tuple-element.25) | copy-start | bytes 294916
  234.9 38.5 %copy-start.5 = (bf16[8,6144]{1,0:T(8,128)(2,1)}, bf16[8,6144]{1,0:T(8,128)(2,1)S(1)}, u32[]{:S(2)}) copy-start(bf16[8,6144]{1,0:T(8,128)(2,1)S(1)} %get-tuple-element.24) | copy-start | bytes 294916
  234.9 38.5 %copy-start.6 = (bf16[8,6144]{1,0:T(8,128)(2,1)}, bf16[8,6144]{1,0:T(8,128)(2,1)S(1)}, u32[]{:S(2)}) copy-start(bf16[8,6144]{1,0:T(8,128)(2,1)S(1)} %get-tuple-element.23) | copy-start | bytes 294916
  234.9 38.5 %copy-start.7 = (bf16[8,6144]{1,0:T(8,128)(2,1)}, bf16[8,6144]{1,0:T(8,128)(2,1)S(1)}, u32[]{:S(2)}) copy-start(bf16[8,6144]{1,0:T(8,128)(2,1)S(1)} %get-tuple-element.22) | copy-start | bytes 294916
  274.7 20.2 %all-to-all-start.10 = ((bf16[16,2,6144]{2,1,0:T(2,128)(2,1)}), bf16[16,2,6144]{2,1,0:T(2,128)(2,1)S(1)}, u32[]{:S(2)}, u32[]{:S(2)}) async-start(bf16[16,2,6144]{2,1,0:T(2,128)(2,1)} %reshape.318), calls=%async_computation.10 | async-start | bytes 786432 | tf_op jit(solution)/shard_map/all_to_all | solution.py:88
  294.9 17.7 %all-to-all-start.8 = ((bf16[16,2,6144]{2,1,0:T(2,128)(2,1)}), bf16[16,2,6144]{2,1,0:T(2,128)(2,1)S(1)}, u32[]{:S(2)}, u32[]{:S(2)}) async-start(bf16[16,2,6144]{2,1,0:T(2,128)(2,1)} %reshape.314), calls=%async_computation.8 | async-start | bytes 786432 | tf_op jit(solution)/shard_map/all_to_all | solution.py:88
  312.7 13.0 %all-to-all-start.6 = ((bf16[16,2,6144]{2,1,0:T(2,128)(2,1)}), bf16[16,2,6144]{2,1,0:T(2,128)(2,1)S(1)}, u32[]{:S(2)}, u32[]{:S(2)}) async-start(bf16[16,2,6144]{2,1,0:T(2,128)(2,1)} %reshape.310), calls=%async_computation.6 | async-start | bytes 786432 | tf_op jit(solution)/shard_map/all_to_all | solution.py:88
  325.6 12.9 %all-to-all-start.4 = ((bf16[16,2,6144]{2,1,0:T(2,128)(2,1)}), bf16[16,2,6144]{2,1,0:T(2,128)(2,1)S(1)}, u32[]{:S(2)}, u32[]{:S(2)}) async-start(bf16[16,2,6144]{2,1,0:T(2,128)(2,1)} %reshape.306), calls=%async_computation.4 | async-start | bytes 786432 | tf_op jit(solution)/shard_map/all_to_all | solution.py:88
  371.6 9.8 %copy-start.2 = (f32[32,6144]{1,0:T(8,128)S(1)}, f32[32,6144]{1,0:T(8,128)}, u32[]{:S(2)}) copy-start(f32[32,6144]{1,0:T(8,128)} %fusion.4) | copy-start | bytes 2359300
  438.3 13.2 %all-to-all-start.11 = ((bf16[16,2,6144]{2,1,0:T(2,128)(2,1)}), bf16[16,2,6144]{2,1,0:T(2,128)(2,1)S(1)}, u32[]{:S(2)}, u32[]{:S(2)}) async-start(bf16[16,2,6144]{2,1,0:T(2,128)(2,1)} %reshape.320), calls=%async_computation.11 | async-start | bytes 786432 | tf_op jit(solution)/shard_map/all_to_all | solution.py:98
  451.5 12.9 %all-to-all-start.9 = ((bf16[16,2,6144]{2,1,0:T(2,128)(2,1)}), bf16[16,2,6144]{2,1,0:T(2,128)(2,1)S(1)}, u32[]{:S(2)}, u32[]{:S(2)}) async-start(bf16[16,2,6144]{2,1,0:T(2,128)(2,1)} %reshape.316), calls=%async_computation.9 | async-start | bytes 786432 | tf_op jit(solution)/shard_map/all_to_all | solution.py:98
  464.5 12.9 %all-to-all-start.7 = ((bf16[16,2,6144]{2,1,0:T(2,128)(2,1)}), bf16[16,2,6144]{2,1,0:T(2,128)(2,1)S(1)}, u32[]{:S(2)}, u32[]{:S(2)}) async-start(bf16[16,2,6144]{2,1,0:T(2,128)(2,1)} %reshape.312), calls=%async_computation.7 | async-start | bytes 786432 | tf_op jit(solution)/shard_map/all_to_all | solution.py:98
  477.4 12.9 %all-to-all-start.5 = ((bf16[16,2,6144]{2,1,0:T(2,128)(2,1)}), bf16[16,2,6144]{2,1,0:T(2,128)(2,1)S(1)}, u32[]{:S(2)}, u32[]{:S(2)}) async-start(bf16[16,2,6144]{2,1,0:T(2,128)(2,1)} %reshape.308), calls=%async_computation.5 | async-start | bytes 786432 | tf_op jit(solution)/shard_map/all_to_all | solution.py:98
Sparse Core Ops, SparseCore 0:
  123.3 60.5 all-reduce.4
where the time goes:
time: 509 us; the launch traced here: 499 us
  blocking collectives  199 us (39%)
  waiting for transfers between devices  133 us (26%)
  matrix products  78.2 us (15%)
  starting transfers between devices  49.8 us (10%)
  local copies, waits for them, and re-layouts  16.3 us (3%)
  between operations  15 us (3%)
  other arithmetic  7.75 us (2%)
    all_gather x4, blocking collectives, shards(): lax.all_gather(readout, 'exp', axis=0, tiled=True)  92.8 us
    psum x1, waiting for transfers between devices, shards(): summed = lax.psum(partial_value, 'head')  57.1 us
    psum x1, blocking collectives, shards(): reduced = lax.psum(down_val, 'head')  54.9 us
    all_gather x4, blocking collectives, shards(): source_rows = lax.all_gather(normed_part, 'head', axis=1, tiled=True)  51.1 us
    dot_general x4, matrix products, shards(): jnp.dot(hidden_val, w_down[0], preferred_element_type=jnp.float32)  37.6 us
    all_to_all x4, waiting for transfers between devices, shards(): lax.all_to_all(summed, 'exp', split_axis=0, concat_axis=1, tiled=True)  32.6 us
    all_to_all x4, waiting for transfers between devices, shards(): lax.all_to_all(results, 'exp', split_axis=0, concat_axis=0, tiled=True)  29.9 us
    dot_general x4, matrix products, shards(): gate_val = jnp.dot(rows_in, w_gate[0], preferred_element_type=jnp.float32)  20.6 us
  transfers between devices with their start and end apart: 13, of which 12 were waited for; matrix products, arithmetic and copies ran while one was open for 6% of the time, Pallas kernels for 0%

commit v1 on v0

v1 whole, which is shorter than its diff:
```python
import functools

import jax
import jax.numpy as jnp
from jax import lax
from jax.experimental import pallas as pl
from jax.experimental.pallas import tpu as pltpu
from jax.sharding import PartitionSpec as P

STEPS = 4
ROWS = 8
EPS = 1e-06
F32 = jnp.float32
BF16 = jnp.bfloat16
MIB = 1 << 20


def vmem_params(mib):
    return pltpu.CompilerParams(vmem_limit_bytes=mib * MIB)


def over_head(value, bits):
    return lax.ppermute(value, "head", [(i, i ^ bits) for i in range(8)])


def over_exp(value, bits):
    return lax.ppermute(value, "exp", [(i, i ^ bits) for i in range(16)])


def over_all(value, dest):
    pairs = []
    for i in range(128):
        y, c, z, x = i // 32, i // 16 % 2, i // 4 % 4, i % 4
        y, c, z, x = dest(y, c, z, x)
        pairs.append((i, ((y * 2 + c) * 4 + z) * 4 + x))
    return lax.ppermute(value, ("head", "exp"), pairs)


def readout_kernel(qkv_ref, state_ref, first_ref, mix_ref, gain_ref, out_ref, acc_ref):
    row = pl.program_id(0)
    heads = state_ref.shape[1]
    size = state_ref.shape[2]
    q = qkv_ref[0, 0]
    k = qkv_ref[0, 1]
    v = qkv_ref[0, 2]
    row_head = lax.broadcasted_iota(jnp.int32, (heads * STEPS, size), 0) % heads
    q_twice = jnp.concatenate([q, q], axis=1)
    scores = lax.dot_general(q, k, (((1,), (1,)), ((), ())), preferred_element_type=F32)
    carried = jnp.zeros((heads * STEPS, size), F32)
    for pair in range(heads // 2):
        wide = jnp.concatenate([state_ref[0, 2 * pair], state_ref[0, 2 * pair + 1]], axis=1)
        high = wide.astype(BF16)
        low = (wide - high.astype(F32)).astype(BF16)
        both = jnp.dot(
            q_twice, jnp.concatenate([high, low], axis=0), preferred_element_type=F32
        )
        carried = jnp.where(row_head == 2 * pair, both[:, :size], carried)
        carried = jnp.where(row_head == 2 * pair + 1, both[:, size:], carried)
    o = carried * first_ref[...]
    o += jnp.dot(
        scores * mix_ref[...],
        v.astype(F32),
        precision=lax.Precision.HIGHEST,
        preferred_element_type=F32,
    )
    o = o * lax.rsqrt(jnp.mean(o * o, axis=-1, keepdims=True) + EPS) * gain_ref[...]
    for t in range(STEPS):
        acc_ref[t * ROWS + row] = o[t * heads : (t + 1) * heads]

    @pl.when(row == pl.num_programs(0) - 1)
    def _():
        for head in range(heads):
            out_ref[:, head * size : (head + 1) * size] = acc_ref[:, head, :].astype(BF16)


def readouts(step_qkv, decay, state, attn_gain):
    heads, size = state.shape[1], state.shape[2]
    n = heads * STEPS
    qkv = step_qkv.reshape(STEPS, ROWS, 3, heads, size).transpose(1, 2, 0, 3, 4)
    qkv = qkv.reshape(ROWS, 3, n, size)
    one = jnp.ones((heads,), F32)
    zero = jnp.zeros((heads,), F32)
    first = [decay[0]]
    for t in range(1, STEPS):
        first.append(first[-1] * decay[t])
    first = jnp.stack(first, 0).reshape(n, 1)
    rows = []
    for t in range(STEPS):
        row, run = [zero] * STEPS, one
        for s in range(t, -1, -1):
            row[s] = run
            run = run * decay[s]
        rows.append(jnp.stack(row, 0))
    causal = jnp.stack(rows, 0)
    same = jnp.eye(heads, dtype=F32)
    mix = (causal[:, None, :, :] * same[None, :, None, :]).reshape(n, n)
    gain = jnp.broadcast_to(attn_gain.reshape(1, heads, size), (STEPS, heads, size))
    return pl.pallas_call(
        readout_kernel,
        out_shape=jax.ShapeDtypeStruct((STEPS * ROWS, heads * size), BF16),
        grid=(ROWS,),
        in_specs=[
            pl.BlockSpec((1, 3, n, size), lambda i: (i, 0, 0, 0)),
            pl.BlockSpec((1, heads, size, size), lambda i: (i, 0, 0, 0)),
            pl.BlockSpec((n, size), lambda i: (0, 0)),
            pl.BlockSpec((n, n), lambda i: (0, 0)),
            pl.BlockSpec((n, size), lambda i: (0, 0)),
        ],
        out_specs=pl.BlockSpec((STEPS * ROWS, heads * size), lambda i: (0, 0)),
        scratch_shapes=[pltpu.VMEM((STEPS * ROWS, heads, size), F32)],
        compiler_params=vmem_params(16),
        cost_estimate=pl.CostEstimate(
            flops=2 * ROWS * 2 * STEPS * heads * size * size * 2,
            bytes_accessed=state.size * 4,
            transcendentals=0,
        ),
        name="readout",
    )(qkv, state, jnp.broadcast_to(first, (n, size)), mix, gain.reshape(n, size))


def ranks(ids, experts):
    blocks = ids.shape[0]
    flat = ids.reshape(blocks, 2 * ROWS)
    same = flat[:, :, None] == flat[:, None, :]
    index = jnp.arange(2 * ROWS)
    earlier = index[None, :] < index[:, None]
    return jnp.sum((same & earlier[None]).astype(jnp.int32), axis=2).reshape(ids.shape)


def gate_up_kernel(*refs):
    x_refs, (gate_ref, up_ref, out_ref, gate_acc, up_acc) = refs[:8], refs[8:]
    step = pl.program_id(0)
    x = jnp.concatenate([r[...] for r in x_refs], axis=0)
    gate = jnp.dot(x, gate_ref[0], preferred_element_type=F32)
    up = jnp.dot(x, up_ref[0], preferred_element_type=F32)

    @pl.when(step == 0)
    def _():
        gate_acc[...] = gate
        up_acc[...] = up

    @pl.when(step > 0)
    def _():
        gate_acc[...] += gate
        up_acc[...] += up

    @pl.when(step == pl.num_programs(0) - 1)
    def _():
        g = gate_acc[...]
        out_ref[...] = (g / (1.0 + jnp.exp(-g)) * up_acc[...]).astype(BF16)


def gate_up(pieces, w_gate, w_up):
    slots, width = pieces[0].shape
    hidden = w_gate.shape[2]
    chunk = width // 8
    rows = slots * len(pieces)
    return pl.pallas_call(
        gate_up_kernel,
        out_shape=jax.ShapeDtypeStruct((rows, hidden), BF16),
        grid=(width // chunk,),
        in_specs=[pl.BlockSpec((slots, chunk), lambda i: (0, i))] * len(pieces)
        + [pl.BlockSpec((1, chunk, hidden), lambda i: (0, i, 0))] * 2,
        out_specs=pl.BlockSpec((rows, hidden), lambda i: (0, 0)),
        scratch_shapes=[pltpu.VMEM((rows, hidden), F32)] * 2,
        compiler_params=vmem_params(24),
        cost_estimate=pl.CostEstimate(
            flops=4 * rows * width * hidden,
            bytes_accessed=4 * width * hidden,
            transcendentals=rows * hidden,
        ),
        name="gate_up",
    )(*pieces, w_gate, w_up)


def down_kernel(place_ref, x_ref, w_ref, out_ref):
    out_ref[0] = jnp.dot(x_ref[...], w_ref[0], preferred_element_type=F32).astype(BF16)


def down(place, x, w_down, share):
    rows, hidden = x.shape
    parts = place.shape[0]
    return pl.pallas_call(
        down_kernel,
        out_shape=jax.ShapeDtypeStruct((parts, rows, share), BF16),
        grid_spec=pltpu.PrefetchScalarGridSpec(
            num_scalar_prefetch=1,
            grid=(parts,),
            in_specs=[
                pl.BlockSpec((rows, hidden), lambda i, p: (0, 0)),
                pl.BlockSpec((1, hidden, share), lambda i, p: (0, 0, p[i])),
            ],
            out_specs=pl.BlockSpec((1, rows, share), lambda i, p: (i, 0, 0)),
        ),
        compiler_params=vmem_params(16),
        cost_estimate=pl.CostEstimate(
            flops=2 * rows * hidden * share * parts,
            bytes_accessed=2 * hidden * share * parts,
            transcendentals=0,
        ),
        name="down",
    )(place, x, w_down)


def final_sum_kernel(place_ref, own_ref, got1_ref, got2_ref, got3_ref, out_ref):
    y, c = place_ref[0], place_ref[1]
    for ky in range(4):
        sums = []
        for kc in range(2):
            total = own_ref[0, kc, ky].astype(F32)
            for k, ref in ((1, got1_ref), (2, got2_ref), (3, got3_ref)):
                total += ref[kc, ky ^ k].astype(F32)
            sums.append(total)
        low = jnp.where(c == 0, sums[0], sums[1])
        high = jnp.where(c == 0, sums[1], sums[0])
        for x in range(4):
            block = jnp.concatenate([low[4 * x : 4 * x + 4], high[4 * x : 4 * x + 4]], axis=0)
            out_ref[lax.bitwise_xor(y, ky) * 4 + x] = block.astype(BF16)


def final_sum(place, own, got):
    share = own.shape[-1]
    return pl.pallas_call(
        final_sum_kernel,
        out_shape=jax.ShapeDtypeStruct((16, 8, share), BF16),
        in_specs=[pl.BlockSpec(memory_space=pltpu.SMEM)]
        + [pl.BlockSpec(memory_space=pltpu.VMEM)] * 4,
        out_specs=pl.BlockSpec(memory_space=pltpu.VMEM),
        compiler_params=vmem_params(16),
        cost_estimate=pl.CostEstimate(flops=4 * 128 * share, bytes_accessed=1 << 20, transcendentals=0),
        name="final_sum",
    )(place, own, *got)


def shards(
    hidden_in,
    step_qkv,
    decay_rates,
    kv_state,
    attn_gain,
    out_proj,
    ffn_gain,
    routes,
    route_weights,
    w_gate,
    w_up,
    w_down,
):
    width = hidden_in.shape[2]
    experts = 16
    cols = width // 16
    share = width // 8
    head, exp = lax.axis_index("head"), lax.axis_index("exp")
    y, c, z, x = head // 2, head % 2, exp // 4, exp % 4

    pair_rows = lax.dynamic_slice(hidden_in, (2 * c, 0, y * 4 * cols), (2, ROWS, 4 * cols))
    pair_rows = pair_rows.reshape(2 * ROWS, 4 * cols)
    pair_routes = lax.dynamic_slice(routes, (2 * c, 0, 0), (2, ROWS, 2)).reshape(2 * ROWS, 2)
    pair_routes = jnp.pad(pair_routes.astype(BF16), ((0, 0), (0, 126)))
    arrived = []
    for k in range(4):
        block = lax.dynamic_slice(pair_rows, (0, (x ^ k) * cols), (2 * ROWS, cols))
        block = jnp.concatenate([block, pair_routes], axis=1)
        arrived.append(over_all(block, lambda y, c, z, x, k=k: (z, c, y, x ^ k)))
    arrived = jnp.stack(arrived, 0)
    hidden_rows = arrived[:, :, :cols]
    row_routes = arrived[:, :, cols : cols + 2].astype(jnp.int32)

    readout = readouts(step_qkv, decay_rates, kv_state, attn_gain)
    half_a, half_b = readout[: 2 * ROWS], readout[2 * ROWS :]
    by_z = jnp.stack([half_a] + [over_exp(half_a, 4 * k) for k in (1, 2, 3)], 0)
    by_x = jnp.stack([half_b] + [over_exp(half_b, k) for k in (1, 2, 3)], 0)
    all_a = [by_z] + [over_exp(by_z, k) for k in (1, 2, 3)]
    all_b = [by_x] + [over_exp(by_x, 4 * k) for k in (1, 2, 3)]
    depth = readout.shape[1]

    def project(pieces):
        rows = jnp.concatenate([p.reshape(8 * ROWS, depth) for p in pieces], axis=0)
        out = jnp.dot(rows, out_proj, preferred_element_type=F32).astype(BF16)
        return out.reshape(4, 4, 2 * ROWS, cols)

    part_a = project(all_a)
    part_b = project(all_b).transpose(1, 0, 2, 3)
    mine = jnp.where(c == 0, part_a, part_b)
    other = jnp.where(c == 0, part_b, part_a)
    mine = (mine.astype(F32) + over_head(other, 1).astype(F32)).astype(BF16)

    def for_y(k):
        return lax.dynamic_index_in_dim(mine, y ^ k ^ z, 1, keepdims=False)

    summed = for_y(0).astype(F32)
    for k in (1, 2, 3):
        summed += over_head(for_y(k), 2 * k).astype(F32)
    attended = (hidden_rows.astype(F32) + summed).astype(BF16)

    pieces = []
    for k in range(4):
        source = (2 * c + x % 2) ^ k
        block = lax.dynamic_index_in_dim(attended, source ^ x, 0, keepdims=False)
        pieces.append(
            over_all(block, lambda y, c, z, x, k=k: (z, x // 2, y, (2 * c + x % 2) ^ k))
        )
    pieces = jnp.stack(pieces, 0)
    ordered = [lax.dynamic_index_in_dim(pieces, j ^ x, 0, keepdims=False) for j in range(4)]
    attended_out = jnp.concatenate(
        [jnp.concatenate(ordered[:2], axis=1), jnp.concatenate(ordered[2:], axis=1)], axis=0
    ).reshape(STEPS, ROWS, share)

    ids = row_routes.reshape(8, ROWS, 2)
    rank = ranks(ids, experts)
    group = jnp.arange(8)
    base = ((group // 2) ^ x) * 4 + (group % 2) * 2
    target = (ids * 16 + base[:, None, None] + rank).reshape(8 * ROWS, 2)
    slot = jnp.arange(16 * experts)
    select = jnp.sum((slot[:, None, None] == target[None]).astype(F32), axis=2).astype(BF16)
    sent = jnp.dot(select, attended.reshape(8 * ROWS, cols), preferred_element_type=F32)
    sent = sent.astype(BF16).reshape(experts, 16, cols)
    got = lax.all_to_all(sent, "exp", split_axis=0, concat_axis=0, tiled=True)
    got = got.transpose(1, 0, 2).reshape(16, width).astype(F32)
    normed = got * lax.rsqrt(jnp.mean(got * got, axis=-1, keepdims=True) + EPS) * ffn_gain
    normed = normed.astype(BF16)
    by_y = [normed] + [over_head(normed, 2 * k) for k in (1, 2, 3)]
    by_core = [over_head(piece, 1) for piece in by_y]

    hidden = gate_up(by_y + by_core, w_gate, w_up)
    ky = jnp.arange(4)
    theirs = down((y ^ ky) * 2 + (1 - c), hidden, w_down, share)
    theirs = over_head(theirs, 1)
    ours = down((y ^ ky) * 2 + c, hidden, w_down, share)
    theirs = theirs.reshape(4, 2, 4, 16, share)
    ours = ours.reshape(4, 2, 4, 16, share)
    both = (ours.astype(F32) + theirs[:, ::-1].astype(F32)).astype(BF16)
    got = [over_head(both[k], 2 * k) for k in (1, 2, 3)]
    place = jnp.stack([y, c]).astype(jnp.int32)
    results = final_sum(place, both, got)
    back = lax.all_to_all(results, "exp", split_axis=0, concat_axis=0, tiled=True)

    rank = ranks(routes, experts)
    target = routes * 8 + jnp.arange(STEPS)[:, None, None] * 2 + rank
    slot = jnp.arange(8 * experts)
    match = (target.reshape(STEPS * ROWS, 2, 1) == slot).astype(F32)
    mix = jnp.sum(match * route_weights.reshape(STEPS * ROWS, 2, 1), axis=1)
    mixed = jnp.dot(
        mix,
        back.reshape(8 * experts, share).astype(F32),
        precision=lax.Precision.HIGHEST,
        preferred_element_type=F32,
    )
    return attended_out, mixed.astype(BF16).reshape(STEPS, ROWS, share)


def solution(mesh):
    return jax.shard_map(
        shards,
        mesh=mesh,
        in_specs=(
            P(None, "exp", None),
            P(None, "exp", None, "head"),
            P(None, "head"),
            P("exp", "head", None, None),
            P("head"),
            P("head", "exp"),
            P(),
            P(None, "exp", None),
            P(None, "exp", None),
            P("exp", None, "head"),
            P("exp", None, "head"),
            P("exp", "head", None),
        ),
        out_specs=(P(None, "exp", "head"), P(None, "exp", "head")),
        check_vma=False,
    )
```

time: 509 us -> 178 us (0.35); the launches traced: 499 us -> 177 us
  blocking collectives: 199 us -> 13.2 us
  waiting for transfers between devices: 133 us -> 35.7 us
  matrix products: 78.2 us -> 1.93 us
  local copies, waits for them, and re-layouts: 16.3 us -> 39.5 us
  starting transfers between devices: 49.8 us -> 67.9 us
  between operations: 15 us -> 1.12 us
  Pallas kernels: 0 us -> 13.5 us
    all_gather x8 -> x0, blocking collectives: 144 us -> none  [the longest x4 92.8 us: shards(): lax.all_gather(readout, 'exp', axis=0, tiled=True)]
    dot_general x24 -> x4, matrix products: 78.2 us -> 1.93 us  [the longest x2 0.87 us: project(): out = jnp.dot(rows, out_proj, preferred_element_type=F32).astype(BF16)]
    ppermute x0 -> x35, starting transfers between devices: none -> 63.2 us  [the longest x12 30.5 us: over_exp(): return lax.ppermute(value, 'exp', [(i, i ^ bits) for i in range(16)])]
    psum x1 -> x0, waiting for transfers between devices: 57.1 us -> none  [shards(): summed = lax.psum(partial_value, 'head')]
    psum x1 -> x0, blocking collectives: 54.9 us -> none  [shards(): reduced = lax.psum(down_val, 'head')]
    all_to_all x8 -> x0, waiting for transfers between devices: 45.8 us -> none  [the longest x4 32.6 us: shards(): lax.all_to_all(summed, 'exp', split_axis=0, concat_axis=1, tiled=True)]
    all_to_all x8 -> x0, starting transfers between devices: 35.5 us -> none  [the longest x4 18 us: shards(): lax.all_to_all(sent, 'exp', split_axis=0, concat_axis=0, tiled=True)]
    unnamed x26 -> x23, local copies, waits for them, and re-layouts: 0.08 us -> 35.6 us
  transfers between devices with their start and end apart: 13 -> 36, of which waited for: 12 -> 13; matrix products, arithmetic and copies ran while one was open for 6% -> 16% of each run, Pallas kernels for 0% -> 3%
where the time goes in v1:
time: 178 us; the launch traced here: 177 us
  starting transfers between devices  67.9 us (38%)
  local copies, waits for them, and re-layouts  39.5 us (22%)
  waiting for transfers between devices  35.7 us (20%)
  Pallas kernels  13.5 us (8%)
  blocking collectives  13.2 us (7%)
  other arithmetic  4.57 us (3%)
  matrix products  1.93 us (1%)
    unnamed x23, local copies, waits for them, and re-layouts  35.6 us
    ppermute x12, starting transfers between devices, over_exp(): return lax.ppermute(value, 'exp', [(i, i ^ bits) for i in range(16)])  30.5 us
    ppermute x15, waiting for transfers between devices, over_head(): return lax.ppermute(value, 'head', [(i, i ^ bits) for i in range(8)])  22.4 us
    ppermute x15, starting transfers between devices, over_head(): return lax.ppermute(value, 'head', [(i, i ^ bits) for i in range(8)])  21.2 us
    all_to_all x1, blocking collectives, shards(): got = lax.all_to_all(sent, 'exp', split_axis=0, concat_axis=0, tiled=True)  13.2 us
    ppermute x8, starting transfers between devices, over_all(): return lax.ppermute(value, ('head', 'exp'), pairs)  11.5 us
    all_to_all x1, waiting for transfers between devices, shards(): lax.all_to_all(results, 'exp', split_axis=0, concat_axis=0, tiled=True)  7.69 us
    ppermute x12, waiting for transfers between devices, over_exp(): return lax.ppermute(value, 'exp', [(i, i ^ bits) for i in range(16)])  5.63 us
  transfers between devices with their start and end apart: 36, of which 13 were waited for; matrix products, arithmetic and copies ran while one was open for 16% of the time, Pallas kernels for 3%

profile of v1, /device:TPU:0, one launch (start us, length us, event | category | flops | bytes accessed | tf_op | source)
XLA Modules:
  0.0 177.4 jit_solution(12051513087865761487)
XLA Ops:
  13.7 3.0 %readout.1 = bf16[32,1024]{1,0:T(8,128)(2,1)S(1)} custom-call(bf16[8,3,32,128]{3,2,1,0:T(8,128)(2,1)S(1)} %bitcast.111, f32[8,8,128,128]{3,2,1,0:T(8,128)S(1)} %copy-done.5, f32[32,128]{1,0:T(8,128)S(1)} %broadcast_in_dim.9.first_ref, f32[32,32]{1,0:T(8,128)S(1)} %mul.160.mix_ref, f32[32,128]{1,0:T(8,128)S(1)} %broadcast_bitcast_fusion.gain_ref), custom_call_target="tpu_custom_call" | custom-call | flops 33554432 | bytes 4194304 | tf_op jit(solution)/shard_map/readout/pallas_call | solution.py:98
  16.8 7.5 %collective-permute-start.4 = (bf16[16,1024]{1,0:T(8,128)(2,1)S(1)}, bf16[16,1024]{1,0:T(8,128)(2,1)S(1)}, u32[]{:S(2)}, u32[]{:S(2)}) collective-permute-start(bf16[16,1024]{1,0:T(8,128)(2,1)S(1)} %get-tuple-element.18), channel_id=1, source_target_pairs={{0,4},{1,5},{2,6},{3,7},{4,0},{5,1},{6,2},{7,3},{8,12},{9,13},{10,... | collective-permute-start | bytes 98312 | tf_op jit(solution)/shard_map/ppermute | solution.py:27
  24.5 8.5 %collective-permute-start.5 = (bf16[16,1024]{1,0:T(8,128)(2,1)S(1)}, bf16[16,1024]{1,0:T(8,128)(2,1)S(1)}, u32[]{:S(2)}, u32[]{:S(2)}) collective-permute-start(bf16[16,1024]{1,0:T(8,128)(2,1)S(1)} %get-tuple-element.18), channel_id=1, source_target_pairs={{0,8},{1,9},{2,10},{3,11},{4,12},{5,13},{6,14},{7,15},{8,0},{9,1},... | collective-permute-start | bytes 98312 | tf_op jit(solution)/shard_map/ppermute | solution.py:27
  33.5 3.9 %collective-permute-start.11 = (bf16[16,1024]{1,0:T(8,128)(2,1)S(1)}, bf16[16,1024]{1,0:T(8,128)(2,1)S(1)}, u32[]{:S(2)}, u32[]{:S(2)}) collective-permute-start(bf16[16,1024]{1,0:T(8,128)(2,1)S(1)} %get-tuple-element.17), channel_id=1, source_target_pairs={{0,2},{1,3},{2,0},{3,1},{4,6},{5,7},{6,4},{7,5},{8,10},{9,11},{10,... | collective-permute-start | bytes 98312 | tf_op jit(solution)/shard_map/ppermute | solution.py:27
  38.5 3.9 %collective-permute-start.8 = (bf16[4,16,1024]{2,1,0:T(8,128)(2,1)S(1)}, bf16[4,16,1024]{2,1,0:T(8,128)(2,1)S(1)}, u32[]{:S(2)}, u32[]{:S(2)}) collective-permute-start(bf16[4,16,1024]{2,1,0:T(8,128)(2,1)S(1)} %pad_maximum_fusion), channel_id=1, source_target_pairs={{0,2},{1,3},{2,0},{3,1},{4,6},{5,7},{6,4},{7,5},{8,10},{9,11},{10,... | collective-permute-start | bytes 393224 | tf_op jit(solution)/shard_map/ppermute | solution.py:27
  44.7 3.4 %collective-permute-start.14 = (bf16[4,16,1024]{2,1,0:T(8,128)(2,1)S(1)}, bf16[4,16,1024]{2,1,0:T(8,128)(2,1)S(1)}, u32[]{:S(2)}, u32[]{:S(2)}) collective-permute-start(bf16[4,16,1024]{2,1,0:T(8,128)(2,1)S(1)} %pad_maximum_fusion.1), channel_id=1, source_target_pairs={{0,8},{1,9},{2,10},{3,11},{4,12},{5,13},{6,14},{7,15},{8,0},{9,1},... | collective-permute-start | bytes 393224 | tf_op jit(solution)/shard_map/ppermute | solution.py:27
  49.1 3.3 %collective-permute-done.14 = bf16[4,16,1024]{2,1,0:T(8,128)(2,1)S(1)} collective-permute-done((bf16[4,16,1024]{2,1,0:T(8,128)(2,1)S(1)}, bf16[4,16,1024]{2,1,0:T(8,128)(2,1)S(1)}, u32[]{:S(2)}, u32[]{:S(2)}) %collective-permute-start.14) | collective-permute-done | bytes 131104 | tf_op jit(solution)/shard_map/ppermute | solution.py:27
  56.4 2.8 %collective-permute-start.17 = (bf16[4,16,384]{2,1,0:T(8,128)(2,1)S(1)}, bf16[4,16,384]{2,1,0:T(8,128)(2,1)S(1)}, u32[]{:S(2)}, u32[]{:S(2)}) collective-permute-start(bf16[4,16,384]{2,1,0:T(8,128)(2,1)S(1)} %get-tuple-element.12), channel_id=1, source_target_pairs={{0,32},{16,48},{32,0},{48,16},{64,96},{80,112},{96,64},{112,80},{1... | collective-permute-start | bytes 147464 | tf_op jit(solution)/shard_map/ppermute | solution.py:23
  62.0 2.9 %collective-permute-done.18 = bf16[4,16,384]{2,1,0:T(8,128)(2,1)S(1)} collective-permute-done((bf16[4,16,384]{2,1,0:T(8,128)(2,1)S(1)}, bf16[4,16,384]{2,1,0:T(8,128)(2,1)S(1)}, u32[]{:S(2)}, u32[]{:S(2)}) %collective-permute-start.18) | collective-permute-done | bytes 49184 | tf_op jit(solution)/shard_map/ppermute | solution.py:23
  65.3 13.2 %all_to_all.10 = bf16[16,16,384]{2,1,0:T(8,128)(2,1)S(1)} all-to-all(bf16[16,16,384]{2,1,0:T(8,128)(2,1)S(1)} %bitcast.113), channel_id=1, replica_groups=mesh['head'=8,'exp'=16] {'exp'}, dimensions={0} | all-to-all | bytes 393216 | tf_op jit(solution)/shard_map/all_to_all | solution.py:318
  90.2 10.5 %copy.126.refs_8_ = bf16[1,6144,576]{2,1,0:T(8,128)(2,1)} copy(bf16[1,6144,576]{1,2,0:T(8,128)(2,1)} %param.21) | data formatting | bytes 14155776 | tf_op args[9]
  100.7 10.2 %copy.127.refs_9_ = bf16[1,6144,576]{2,1,0:T(8,128)(2,1)} copy(bf16[1,6144,576]{1,2,0:T(8,128)(2,1)} %param.22) | data formatting | bytes 14155776 | tf_op args[10]
  111.0 3.2 %copy-done.1 = bf16[1,6144,576]{2,1,0:T(8,128)(2,1)S(1)} copy-done((bf16[1,6144,576]{2,1,0:T(8,128)(2,1)S(1)}, bf16[1,6144,576]{2,1,0:T(8,128)(2,1)}, u32[]{:S(2)}) %copy-start.1) | copy-done | bytes 7077912
  114.3 3.2 %copy-done.2 = bf16[1,6144,576]{2,1,0:T(8,128)(2,1)S(1)} copy-done((bf16[1,6144,576]{2,1,0:T(8,128)(2,1)S(1)}, bf16[1,6144,576]{2,1,0:T(8,128)(2,1)}, u32[]{:S(2)}) %copy-start.2) | copy-done | bytes 7077912
  117.5 4.8 %gate_up.1.x_ref = bf16[128,576]{1,0:T(8,128)(2,1)S(1)} custom-call(bf16[16,6144]{1,0:T(8,128)(2,1)S(1)} %multiply_convert_fusion.refs_0_, bf16[16,6144]{1,0:T(8,128)(2,1)S(1)} %collective-permute-done.24.refs_1_, bf16[16,6144]{1,0:T(8,128)(2,1)S(1)} %collective-permute-done.25.refs_2_, bf16[16,6144]{1,0:T(8,128)(2,1)S(1)} %collective-permute-done.26.refs_3_, ...), custom_call_target="tpu_custom_call" | custom-call | flops 1811939328 | bytes 14155776 | tf_op jit(solution)/shard_map/gate_up/pallas_call | solution.py:158
  122.3 3.0 %copy-done.3 = bf16[1,576,6144]{2,1,0:T(8,128)(2,1)S(1)} copy-done((bf16[1,576,6144]{2,1,0:T(8,128)(2,1)S(1)}, bf16[1,576,6144]{2,1,0:T(8,128)(2,1)}, u32[]{:S(2)}) %copy-start.3) | copy-done | bytes 7077912
  130.4 4.2 %collective-permute-start.22 = (bf16[16,384]{1,0:T(8,128)(2,1)S(1)}, bf16[16,384]{1,0:T(8,128)(2,1)S(1)}, u32[]{:S(2)}, u32[]{:S(2)}) collective-permute-start(bf16[16,384]{1,0:T(8,128)(2,1)S(1)} %get-tuple-element.25), channel_id=1, source_target_pairs={{0,2},{1,3},{2,18},{3,19},{4,34},{5,35},{6,50},{7,51},{8,66},{9,67... | collective-permute-start | bytes 36872 | tf_op jit(solution)/shard_map/ppermute | solution.py:36
  135.1 3.0 %copy-done.4 = bf16[1,576,6144]{2,1,0:T(8,128)(2,1)S(1)} copy-done((bf16[1,576,6144]{2,1,0:T(8,128)(2,1)S(1)}, bf16[1,576,6144]{2,1,0:T(8,128)(2,1)}, u32[]{:S(2)}) %copy-start.4) | copy-done | bytes 7077912
  140.5 3.3 %collective-permute-start.32 = (bf16[2,4,16,768]{3,2,1,0:T(8,128)(2,1)S(1)}, bf16[2,4,16,768]{3,2,1,0:T(8,128)(2,1)S(1)}, u32[]{:S(2)}, u32[]{:S(2)}) collective-permute-start(bf16[2,4,16,768]{3,2,1,0:T(8,128)(2,1)S(1)} %get-tuple-element.11), channel_id=1, source_target_pairs={{0,32},{16,48},{32,0},{48,16},{64,96},{80,112},{96,64},{112,80},{1... | collective-permute-start | bytes 589832 | tf_op jit(solution)/shard_map/ppermute | solution.py:23
  143.9 6.6 %collective-permute-start.33 = (bf16[2,4,16,768]{3,2,1,0:T(8,128)(2,1)S(1)}, bf16[2,4,16,768]{3,2,1,0:T(8,128)(2,1)S(1)}, u32[]{:S(2)}, u32[]{:S(2)}) collective-permute-start(bf16[2,4,16,768]{3,2,1,0:T(8,128)(2,1)S(1)} %get-tuple-element.10), channel_id=1, source_target_pairs={{0,64},{16,80},{32,96},{48,112},{64,0},{80,16},{96,32},{112,48},{1... | collective-permute-start | bytes 589832 | tf_op jit(solution)/shard_map/ppermute | solution.py:23
  150.6 7.6 %collective-permute-done.33.got2_ref = bf16[2,4,16,768]{3,2,1,0:T(8,128)(2,1)S(1)} collective-permute-done((bf16[2,4,16,768]{3,2,1,0:T(8,128)(2,1)S(1)}, bf16[2,4,16,768]{3,2,1,0:T(8,128)(2,1)S(1)}, u32[]{:S(2)}, u32[]{:S(2)}) %collective-permute-start.33) | collective-permute-done | bytes 196640 | tf_op jit(solution)/shard_map/ppermute | solution.py:23
  158.1 4.0 %collective-permute-done.34.got3_ref = bf16[2,4,16,768]{3,2,1,0:T(8,128)(2,1)S(1)} collective-permute-done((bf16[2,4,16,768]{3,2,1,0:T(8,128)(2,1)S(1)}, bf16[2,4,16,768]{3,2,1,0:T(8,128)(2,1)S(1)}, u32[]{:S(2)}, u32[]{:S(2)}) %collective-permute-start.34) | collective-permute-done | bytes 196640 | tf_op jit(solution)/shard_map/ppermute | solution.py:23
  163.5 4.7 %all-to-all-start.1 = ((bf16[16,8,768]{2,1,0:T(8,128)(2,1)}), bf16[16,8,768]{2,1,0:T(8,128)(2,1)S(1)}, u32[]{:S(2)}, u32[]{:S(2)}) async-start(bf16[16,8,768]{2,1,0:T(8,128)(2,1)} %final_sum.1), calls=%async_computation.1 | async-start | bytes 393216 | tf_op jit(solution)/shard_map/all_to_all | solution.py:336
  168.9 7.7 %all-to-all-done.1 = bf16[16,8,768]{2,1,0:T(8,128)(2,1)S(1)} async-done(((bf16[16,8,768]{2,1,0:T(8,128)(2,1)}), bf16[16,8,768]{2,1,0:T(8,128)(2,1)S(1)}, u32[]{:S(2)}, u32[]{:S(2)}) %all-to-all-start.1) | async-done | bytes 196640 | tf_op jit(solution)/shard_map/all_to_all | solution.py:336
  (143 shorter events, 47.7 us)
Async XLA Ops:
  2.4 22.1 %collective-permute-start = (bf16[16,512]{1,0:T(8,128)(2,1)S(1)}, bf16[16,512]{1,0:T(8,128)(2,1)S(1)}, u32[]{:S(2)}, u32[]{:S(2)}) collective-permute-start(bf16[16,512]{1,0:T(8,128)(2,1)S(1)} %get-tuple-element.31), channel_id=1, source_target_pairs={{0,0},{1,1},{2,2},{3,3},{4,32},{5,33},{6,34},{7,35},{8,64},{9,65},... | collective-permute-start | bytes 49160 | tf_op jit(solution)/shard_map/ppermute | solution.py:36
  3.1 29.9 %collective-permute-start.1 = (bf16[16,512]{1,0:T(8,128)(2,1)S(1)}, bf16[16,512]{1,0:T(8,128)(2,1)S(1)}, u32[]{:S(2)}, u32[]{:S(2)}) collective-permute-start(bf16[16,512]{1,0:T(8,128)(2,1)S(1)} %get-tuple-element.32), channel_id=1, source_target_pairs={{0,1},{1,0},{2,3},{3,2},{4,33},{5,32},{6,35},{7,34},{8,65},{9,64},... | collective-permute-start | bytes 49160 | tf_op jit(solution)/shard_map/ppermute | solution.py:36
  4.7 28.5 %collective-permute-start.2 = (bf16[16,512]{1,0:T(8,128)(2,1)S(1)}, bf16[16,512]{1,0:T(8,128)(2,1)S(1)}, u32[]{:S(2)}, u32[]{:S(2)}) collective-permute-start(bf16[16,512]{1,0:T(8,128)(2,1)S(1)} %get-tuple-element.33), channel_id=1, source_target_pairs={{0,2},{1,3},{2,0},{3,1},{4,34},{5,35},{6,32},{7,33},{8,66},{9,67},... | collective-permute-start | bytes 49160 | tf_op jit(solution)/shard_map/ppermute | solution.py:36
  7.4 26.1 %collective-permute-start.3 = (bf16[16,512]{1,0:T(8,128)(2,1)S(1)}, bf16[16,512]{1,0:T(8,128)(2,1)S(1)}, u32[]{:S(2)}, u32[]{:S(2)}) collective-permute-start(bf16[16,512]{1,0:T(8,128)(2,1)S(1)} %get-tuple-element.34), channel_id=1, source_target_pairs={{0,3},{1,2},{2,1},{3,0},{4,35},{5,34},{6,33},{7,32},{8,67},{9,66},... | collective-permute-start | bytes 49160 | tf_op jit(solution)/shard_map/ppermute | solution.py:36
  16.8 20.7 %collective-permute-start.4 = (bf16[16,1024]{1,0:T(8,128)(2,1)S(1)}, bf16[16,1024]{1,0:T(8,128)(2,1)S(1)}, u32[]{:S(2)}, u32[]{:S(2)}) collective-permute-start(bf16[16,1024]{1,0:T(8,128)(2,1)S(1)} %get-tuple-element.18), channel_id=1, source_target_pairs={{0,4},{1,5},{2,6},{3,7},{4,0},{5,1},{6,2},{7,3},{8,12},{9,13},{10,... | collective-permute-start | bytes 98312 | tf_op jit(solution)/shard_map/ppermute | solution.py:27
  24.5 13.6 %collective-permute-start.5 = (bf16[16,1024]{1,0:T(8,128)(2,1)S(1)}, bf16[16,1024]{1,0:T(8,128)(2,1)S(1)}, u32[]{:S(2)}, u32[]{:S(2)}) collective-permute-start(bf16[16,1024]{1,0:T(8,128)(2,1)S(1)} %get-tuple-element.18), channel_id=1, source_target_pairs={{0,8},{1,9},{2,10},{3,11},{4,12},{5,13},{6,14},{7,15},{8,0},{9,1},... | collective-permute-start | bytes 98312 | tf_op jit(solution)/shard_map/ppermute | solution.py:27
  33.2 9.2 %collective-permute-start.10 = (bf16[16,1024]{1,0:T(8,128)(2,1)S(1)}, bf16[16,1024]{1,0:T(8,128)(2,1)S(1)}, u32[]{:S(2)}, u32[]{:S(2)}) collective-permute-start(bf16[16,1024]{1,0:T(8,128)(2,1)S(1)} %get-tuple-element.17), channel_id=1, source_target_pairs={{0,1},{1,0},{2,3},{3,2},{4,5},{5,4},{6,7},{7,6},{8,9},{9,8},{10,11... | collective-permute-start | bytes 98312 | tf_op jit(solution)/shard_map/ppermute | solution.py:27
  33.5 9.9 %collective-permute-start.11 = (bf16[16,1024]{1,0:T(8,128)(2,1)S(1)}, bf16[16,1024]{1,0:T(8,128)(2,1)S(1)}, u32[]{:S(2)}, u32[]{:S(2)}) collective-permute-start(bf16[16,1024]{1,0:T(8,128)(2,1)S(1)} %get-tuple-element.17), channel_id=1, source_target_pairs={{0,2},{1,3},{2,0},{3,1},{4,6},{5,7},{6,4},{7,5},{8,10},{9,11},{10,... | collective-permute-start | bytes 98312 | tf_op jit(solution)/shard_map/ppermute | solution.py:27
  38.2 9.9 %collective-permute-start.7 = (bf16[4,16,1024]{2,1,0:T(8,128)(2,1)S(1)}, bf16[4,16,1024]{2,1,0:T(8,128)(2,1)S(1)}, u32[]{:S(2)}, u32[]{:S(2)}) collective-permute-start(bf16[4,16,1024]{2,1,0:T(8,128)(2,1)S(1)} %pad_maximum_fusion), channel_id=1, source_target_pairs={{0,1},{1,0},{2,3},{3,2},{4,5},{5,4},{6,7},{7,6},{8,9},{9,8},{10,11... | collective-permute-start | bytes 393224 | tf_op jit(solution)/shard_map/ppermute | solution.py:27
  38.5 10.0 %collective-permute-start.8 = (bf16[4,16,1024]{2,1,0:T(8,128)(2,1)S(1)}, bf16[4,16,1024]{2,1,0:T(8,128)(2,1)S(1)}, u32[]{:S(2)}, u32[]{:S(2)}) collective-permute-start(bf16[4,16,1024]{2,1,0:T(8,128)(2,1)S(1)} %pad_maximum_fusion), channel_id=1, source_target_pairs={{0,2},{1,3},{2,0},{3,1},{4,6},{5,7},{6,4},{7,5},{8,10},{9,11},{10,... | collective-permute-start | bytes 393224 | tf_op jit(solution)/shard_map/ppermute | solution.py:27
  78.9 9.1 %collective-permute-start.25 = (bf16[16,6144]{1,0:T(8,128)(2,1)S(1)}, bf16[16,6144]{1,0:T(8,128)(2,1)S(1)}, u32[]{:S(2)}, u32[]{:S(2)}) collective-permute-start(bf16[16,6144]{1,0:T(8,128)(2,1)S(1)} %multiply_convert_fusion.refs_0_), channel_id=1, source_target_pairs={{0,64},{16,80},{32,96},{48,112},{64,0},{80,16},{96,32},{112,48},{1... | collective-permute-start | bytes 589832 | tf_op jit(solution)/shard_map/ppermute | solution.py:23
  83.6 27.4 %collective-permute-start.27 = (bf16[16,6144]{1,0:T(8,128)(2,1)S(1)}, bf16[16,6144]{1,0:T(8,128)(2,1)S(1)}, u32[]{:S(2)}, u32[]{:S(2)}) collective-permute-start(bf16[16,6144]{1,0:T(8,128)(2,1)S(1)} %multiply_convert_fusion.refs_0_), channel_id=1, source_target_pairs={{0,16},{16,0},{32,48},{48,32},{64,80},{80,64},{96,112},{112,96},{1... | collective-permute-start | bytes 589832 | tf_op jit(solution)/shard_map/ppermute | solution.py:23
  85.4 25.6 %collective-permute-start.28 = (bf16[16,6144]{1,0:T(8,128)(2,1)S(1)}, bf16[16,6144]{1,0:T(8,128)(2,1)S(1)}, u32[]{:S(2)}, u32[]{:S(2)}) collective-permute-start(bf16[16,6144]{1,0:T(8,128)(2,1)S(1)} %collective-permute-done.24.refs_1_), channel_id=1, source_target_pairs={{0,16},{16,0},{32,48},{48,32},{64,80},{80,64},{96,112},{112,96},{1... | collective-permute-start | bytes 589832 | tf_op jit(solution)/shard_map/ppermute | solution.py:23
  88.1 22.9 %collective-permute-start.29 = (bf16[16,6144]{1,0:T(8,128)(2,1)S(1)}, bf16[16,6144]{1,0:T(8,128)(2,1)S(1)}, u32[]{:S(2)}, u32[]{:S(2)}) collective-permute-start(bf16[16,6144]{1,0:T(8,128)(2,1)S(1)} %collective-permute-done.25.refs_2_), channel_id=1, source_target_pairs={{0,16},{16,0},{32,48},{48,32},{64,80},{80,64},{96,112},{112,96},{1... | collective-permute-start | bytes 589832 | tf_op jit(solution)/shard_map/ppermute | solution.py:23
  90.1 20.9 %collective-permute-start.30 = (bf16[16,6144]{1,0:T(8,128)(2,1)S(1)}, bf16[16,6144]{1,0:T(8,128)(2,1)S(1)}, u32[]{:S(2)}, u32[]{:S(2)}) collective-permute-start(bf16[16,6144]{1,0:T(8,128)(2,1)S(1)} %collective-permute-done.26.refs_3_), channel_id=1, source_target_pairs={{0,16},{16,0},{32,48},{48,32},{64,80},{80,64},{96,112},{112,96},{1... | collective-permute-start | bytes 589832 | tf_op jit(solution)/shard_map/ppermute | solution.py:23
  127.5 12.8 %collective-permute-start.31 = (bf16[4,128,768]{2,1,0:T(8,128)(2,1)S(1)}, bf16[4,128,768]{2,1,0:T(8,128)(2,1)S(1)}, u32[]{:S(2)}, u32[]{:S(2)}) collective-permute-start(bf16[4,128,768]{2,1,0:T(8,128)(2,1)S(1)} %down.3), channel_id=1, source_target_pairs={{0,16},{16,0},{32,48},{48,32},{64,80},{80,64},{96,112},{112,96},{1... | collective-permute-start | bytes 2359304 | tf_op jit(solution)/shard_map/ppermute | solution.py:23
  129.1 14.8 %collective-permute-start.20 = (bf16[16,384]{1,0:T(8,128)(2,1)S(1)}, bf16[16,384]{1,0:T(8,128)(2,1)S(1)}, u32[]{:S(2)}, u32[]{:S(2)}) collective-permute-start(bf16[16,384]{1,0:T(8,128)(2,1)S(1)} %get-tuple-element.23), channel_id=1, source_target_pairs={{0,0},{1,1},{2,16},{3,17},{4,32},{5,33},{6,48},{7,49},{8,64},{9,65... | collective-permute-start | bytes 36872 | tf_op jit(solution)/shard_map/ppermute | solution.py:36
  129.7 20.7 %collective-permute-start.21 = (bf16[16,384]{1,0:T(8,128)(2,1)S(1)}, bf16[16,384]{1,0:T(8,128)(2,1)S(1)}, u32[]{:S(2)}, u32[]{:S(2)}) collective-permute-start(bf16[16,384]{1,0:T(8,128)(2,1)S(1)} %get-tuple-element.26), channel_id=1, source_target_pairs={{0,1},{1,0},{2,17},{3,16},{4,33},{5,32},{6,49},{7,48},{8,65},{9,64... | collective-permute-start | bytes 36872 | tf_op jit(solution)/shard_map/ppermute | solution.py:36
  130.4 20.2 %collective-permute-start.22 = (bf16[16,384]{1,0:T(8,128)(2,1)S(1)}, bf16[16,384]{1,0:T(8,128)(2,1)S(1)}, u32[]{:S(2)}, u32[]{:S(2)}) collective-permute-start(bf16[16,384]{1,0:T(8,128)(2,1)S(1)} %get-tuple-element.25), channel_id=1, source_target_pairs={{0,2},{1,3},{2,18},{3,19},{4,34},{5,35},{6,50},{7,51},{8,66},{9,67... | collective-permute-start | bytes 36872 | tf_op jit(solution)/shard_map/ppermute | solution.py:36
  134.6 16.0 %collective-permute-start.23 = (bf16[16,384]{1,0:T(8,128)(2,1)S(1)}, bf16[16,384]{1,0:T(8,128)(2,1)S(1)}, u32[]{:S(2)}, u32[]{:S(2)}) collective-permute-start(bf16[16,384]{1,0:T(8,128)(2,1)S(1)} %get-tuple-element.24), channel_id=1, source_target_pairs={{0,3},{1,2},{2,19},{3,18},{4,35},{5,34},{6,51},{7,50},{8,67},{9,66... | collective-permute-start | bytes 36872 | tf_op jit(solution)/shard_map/ppermute | solution.py:36
  140.5 10.1 %collective-permute-start.32 = (bf16[2,4,16,768]{3,2,1,0:T(8,128)(2,1)S(1)}, bf16[2,4,16,768]{3,2,1,0:T(8,128)(2,1)S(1)}, u32[]{:S(2)}, u32[]{:S(2)}) collective-permute-start(bf16[2,4,16,768]{3,2,1,0:T(8,128)(2,1)S(1)} %get-tuple-element.11), channel_id=1, source_target_pairs={{0,32},{16,48},{32,0},{48,16},{64,96},{80,112},{96,64},{112,80},{1... | collective-permute-start | bytes 589832 | tf_op jit(solution)/shard_map/ppermute | solution.py:23
  143.9 14.3 %collective-permute-start.33 = (bf16[2,4,16,768]{3,2,1,0:T(8,128)(2,1)S(1)}, bf16[2,4,16,768]{3,2,1,0:T(8,128)(2,1)S(1)}, u32[]{:S(2)}, u32[]{:S(2)}) collective-permute-start(bf16[2,4,16,768]{3,2,1,0:T(8,128)(2,1)S(1)} %get-tuple-element.10), channel_id=1, source_target_pairs={{0,64},{16,80},{32,96},{48,112},{64,0},{80,16},{96,32},{112,48},{1... | collective-permute-start | bytes 589832 | tf_op jit(solution)/shard_map/ppermute | solution.py:23
  150.5 11.7 %collective-permute-start.34 = (bf16[2,4,16,768]{3,2,1,0:T(8,128)(2,1)S(1)}, bf16[2,4,16,768]{3,2,1,0:T(8,128)(2,1)S(1)}, u32[]{:S(2)}, u32[]{:S(2)}) collective-permute-start(bf16[2,4,16,768]{3,2,1,0:T(8,128)(2,1)S(1)} %get-tuple-element.9), channel_id=1, source_target_pairs={{0,96},{16,112},{32,64},{48,80},{64,32},{80,48},{96,0},{112,16},{1... | collective-permute-start | bytes 589832 | tf_op jit(solution)/shard_map/ppermute | solution.py:23
  163.5 13.1 %all-to-all-start.1 = ((bf16[16,8,768]{2,1,0:T(8,128)(2,1)}), bf16[16,8,768]{2,1,0:T(8,128)(2,1)S(1)}, u32[]{:S(2)}, u32[]{:S(2)}) async-start(bf16[16,8,768]{2,1,0:T(8,128)(2,1)} %final_sum.1), calls=%async_computation.1 | async-start | bytes 393216 | tf_op jit(solution)/shard_map/all_to_all | solution.py:336
  (21 other events, 274.8 us)

commit v2 on v1

v2 whole, which is shorter than its diff:
```python
import functools

import jax
import jax.numpy as jnp
from jax import lax
from jax.experimental import pallas as pl
from jax.experimental.pallas import tpu as pltpu
from jax.sharding import PartitionSpec as P

STEPS = 4
ROWS = 8
EPS = 1e-06
F32 = jnp.float32
BF16 = jnp.bfloat16
MIB = 1 << 20


def vmem_params(mib):
    return pltpu.CompilerParams(vmem_limit_bytes=mib * MIB)


def over_head(value, bits):
    return lax.ppermute(value, "head", [(i, i ^ bits) for i in range(8)])


def over_exp(value, bits):
    return lax.ppermute(value, "exp", [(i, i ^ bits) for i in range(16)])


def over_all(value, dest):
    pairs = []
    for i in range(128):
        y, c, z, x = i // 32, i // 16 % 2, i // 4 % 4, i % 4
        y, c, z, x = dest(y, c, z, x)
        pairs.append((i, ((y * 2 + c) * 4 + z) * 4 + x))
    return lax.ppermute(value, ("head", "exp"), pairs)


def readout_kernel(decay_ref, qkv_ref, state_ref, gain_ref, out_ref):
    head = pl.program_id(0)
    n, size = STEPS * ROWS, state_ref.shape[2]
    q, k, v = [qkv_ref[:, i].astype(F32).reshape(n, size).astype(BF16) for i in range(3)]
    row = lax.broadcasted_iota(jnp.int32, (n, size), 0)
    row_in = row % ROWS
    q_twice = jnp.concatenate([q, q], axis=1)
    carried = jnp.zeros((n, size), F32)
    for pair in range(ROWS // 2):
        wide = jnp.concatenate([state_ref[2 * pair, 0], state_ref[2 * pair + 1, 0]], axis=1)
        high = wide.astype(BF16)
        low = (wide - high.astype(F32)).astype(BF16)
        both = jnp.dot(
            q_twice, jnp.concatenate([high, low], axis=0), preferred_element_type=F32
        )
        carried = jnp.where(row_in == 2 * pair, both[:, :size], carried)
        carried = jnp.where(row_in == 2 * pair + 1, both[:, size:], carried)
    decay = [decay_ref[t, head] for t in range(STEPS)]
    run = decay[0]
    first = jnp.full((n, size), run, F32)
    for t in range(1, STEPS):
        run = run * decay[t]
        first = jnp.where(row // ROWS == t, run, first)
    row_t = lax.broadcasted_iota(jnp.int32, (n, n), 0)
    row_s = lax.broadcasted_iota(jnp.int32, (n, n), 1)
    mix = jnp.zeros((n, n), F32)
    for t in range(STEPS):
        run = None
        for s in range(t, -1, -1):
            here = row_t - row_s == (t - s) * ROWS
            mix = jnp.where(here & (row_s // ROWS == s), 1.0 if run is None else run, mix)
            run = decay[s] if run is None else run * decay[s]
    scores = lax.dot_general(q, k, (((1,), (1,)), ((), ())), preferred_element_type=F32)
    o = carried * first + jnp.dot(
        scores * mix,
        v.astype(F32),
        precision=lax.Precision.HIGHEST,
        preferred_element_type=F32,
    )
    o = o * lax.rsqrt(jnp.mean(o * o, axis=-1, keepdims=True) + EPS) * gain_ref[...]
    out_ref[...] = o.astype(BF16)


def readouts(step_qkv, decay, state, attn_gain):
    heads, size = state.shape[1], state.shape[2]
    return pl.pallas_call(
        readout_kernel,
        out_shape=jax.ShapeDtypeStruct((STEPS * ROWS, heads * size), BF16),
        grid=(heads,),
        in_specs=[
            pl.BlockSpec(memory_space=pltpu.SMEM),
            pl.BlockSpec((STEPS, 3, ROWS, size), lambda i: (0, 0, 0, i)),
            pl.BlockSpec((ROWS, 1, size, size), lambda i: (0, i, 0, 0)),
            pl.BlockSpec((1, size), lambda i: (0, i)),
        ],
        out_specs=pl.BlockSpec((STEPS * ROWS, size), lambda i: (0, i)),
        compiler_params=vmem_params(56),
        cost_estimate=pl.CostEstimate(
            flops=2 * STEPS * ROWS * ROWS * heads * size * size * 2,
            bytes_accessed=state.size * 4,
            transcendentals=0,
        ),
        name="readout",
    )(decay, step_qkv.transpose(0, 2, 1, 3), state, attn_gain.reshape(1, -1))


def attend_kernel(place_ref, own_ref, got1_ref, got2_ref, got3_ref, *refs):
    hidden_refs, attended_ref, sent_ref = refs[:4], refs[4], refs[5]
    x, z = place_ref[0], place_ref[1]
    rows = []
    for k in range(4):
        total = own_ref[k].astype(F32) + got1_ref[k].astype(F32)
        total += got2_ref[k].astype(F32) + got3_ref[k].astype(F32)
        total += hidden_refs[k][:, : total.shape[1]].astype(F32)
        rows.append(total.astype(BF16))
        attended_ref[k] = rows[k]
    rows = jnp.concatenate(rows, axis=0)
    n = rows.shape[0]
    cols = rows.shape[1]
    names = jnp.concatenate([r[:, cols:].astype(F32) for r in hidden_refs], axis=0)
    across = names.T
    down_i = lax.broadcasted_iota(jnp.int32, (n, n), 0)
    over_i = lax.broadcasted_iota(jnp.int32, (n, n), 1)
    earlier = (down_i // ROWS == over_i // ROWS) & (down_i < over_i)
    slot = lax.broadcasted_iota(jnp.int32, (256, n), 0)
    lane = lax.broadcasted_iota(jnp.int32, (1, n), 1)
    base = lax.bitwise_xor(lane // 16, x) * 4 + lane // ROWS % 2 * 2
    select = jnp.zeros((256, n), F32)
    for j in range(2):
        mine = across[j : j + 1, :]
        rank = jnp.zeros((1, n), F32)
        for other in range(2):
            same = (names[:, other : other + 1] == mine) & earlier
            rank += jnp.sum(same.astype(F32), axis=0, keepdims=True)
        expert = mine.astype(jnp.int32)
        kz = lax.bitwise_xor(expert // 4, z)
        kx = lax.bitwise_xor(expert % 4, x)
        target = (kz * 4 + kx) * 16 + base + rank.astype(jnp.int32)
        select += (slot == target).astype(F32)
    sent = jnp.dot(select.astype(BF16), rows, preferred_element_type=F32).astype(BF16)
    for k in range(16):
        sent_ref[k // 4, k % 4] = sent[16 * k : 16 * k + 16]


def attend(place, own, got, hidden):
    cols = own.shape[-1]
    return pl.pallas_call(
        attend_kernel,
        out_shape=(
            jax.ShapeDtypeStruct((4, 16, cols), BF16),
            jax.ShapeDtypeStruct((4, 4, 16, cols), BF16),
        ),
        in_specs=[pl.BlockSpec(memory_space=pltpu.SMEM)]
        + [pl.BlockSpec(memory_space=pltpu.VMEM)] * 8,
        out_specs=[pl.BlockSpec(memory_space=pltpu.VMEM)] * 2,
        compiler_params=vmem_params(16),
        cost_estimate=pl.CostEstimate(flops=1 << 23, bytes_accessed=1 << 20, transcendentals=0),
        name="attend",
    )(place, own, *got, *hidden)


def norm_kernel(place_ref, gain_ref, *refs):
    got_refs, out_ref = refs[:4], refs[4]
    x, z = place_ref[0], place_ref[1]
    cols = got_refs[0].shape[2]
    total = jnp.zeros((16, cols), F32)
    for ref in got_refs:
        for kz in range(4):
            value = ref[kz].astype(F32)
            total += value * value
    mean = jnp.sum(total, axis=-1, keepdims=True) / (16 * cols)
    scale = lax.rsqrt(mean + EPS)
    for kx, ref in enumerate(got_refs):
        for kz in range(4):
            block = lax.bitwise_xor(z, kz) * 4 + lax.bitwise_xor(x, kx)
            at = pl.ds(pl.multiple_of(block * cols, 128), cols)
            out_ref[:, at] = (ref[kz].astype(F32) * scale * gain_ref[:, at]).astype(BF16)


def norm(place, gain, got):
    cols = got[0].shape[2]
    return pl.pallas_call(
        norm_kernel,
        out_shape=jax.ShapeDtypeStruct((16, 16 * cols), BF16),
        in_specs=[pl.BlockSpec(memory_space=pltpu.SMEM)]
        + [pl.BlockSpec(memory_space=pltpu.VMEM)] * 5,
        out_specs=pl.BlockSpec(memory_space=pltpu.VMEM),
        compiler_params=vmem_params(16),
        cost_estimate=pl.CostEstimate(flops=1 << 20, bytes_accessed=1 << 19, transcendentals=0),
        name="norm",
    )(place, gain.reshape(1, -1), *got)


def gate_up_kernel(*refs):
    x_refs, (gate_ref, up_ref, out_ref, gate_acc, up_acc) = refs[:8], refs[8:]
    step = pl.program_id(0)
    x = jnp.concatenate([r[...] for r in x_refs], axis=0)
    across = (((1,), (1,)), ((), ()))
    gate = lax.dot_general(x, gate_ref[0], across, preferred_element_type=F32)
    up = lax.dot_general(x, up_ref[0], across, preferred_element_type=F32)

    @pl.when(step == 0)
    def _():
        gate_acc[...] = gate
        up_acc[...] = up

    @pl.when(step > 0)
    def _():
        gate_acc[...] += gate
        up_acc[...] += up

    @pl.when(step == pl.num_programs(0) - 1)
    def _():
        g = gate_acc[...]
        out_ref[...] = (g / (1.0 + jnp.exp(-g)) * up_acc[...]).astype(BF16)


def gate_up(pieces, w_gate, w_up):
    slots, width = pieces[0].shape
    hidden = w_gate.shape[2]
    chunk = width // 8
    rows = slots * len(pieces)
    return pl.pallas_call(
        gate_up_kernel,
        out_shape=jax.ShapeDtypeStruct((rows, hidden), BF16),
        grid=(width // chunk,),
        in_specs=[pl.BlockSpec((slots, chunk), lambda i: (0, i))] * len(pieces)
        + [pl.BlockSpec((1, hidden, chunk), lambda i: (0, 0, i))] * 2,
        out_specs=pl.BlockSpec((rows, hidden), lambda i: (0, 0)),
        scratch_shapes=[pltpu.VMEM((rows, hidden), F32)] * 2,
        compiler_params=vmem_params(56),
        cost_estimate=pl.CostEstimate(
            flops=4 * rows * width * hidden,
            bytes_accessed=4 * width * hidden,
            transcendentals=rows * hidden,
        ),
        name="gate_up",
    )(*pieces, w_gate.transpose(0, 2, 1), w_up.transpose(0, 2, 1))


def down_kernel(place_ref, x_ref, w_ref, out_ref):
    out_ref[0] = jnp.dot(x_ref[...], w_ref[0], preferred_element_type=F32).astype(BF16)


def down(place, x, w_down, share):
    rows, hidden = x.shape
    parts = place.shape[0]
    return pl.pallas_call(
        down_kernel,
        out_shape=jax.ShapeDtypeStruct((parts, rows, share), BF16),
        grid_spec=pltpu.PrefetchScalarGridSpec(
            num_scalar_prefetch=1,
            grid=(parts,),
            in_specs=[
                pl.BlockSpec((rows, hidden), lambda i, p: (0, 0)),
                pl.BlockSpec((1, hidden, share), lambda i, p: (0, 0, p[i])),
            ],
            out_specs=pl.BlockSpec((1, rows, share), lambda i, p: (i, 0, 0)),
        ),
        compiler_params=vmem_params(56),
        cost_estimate=pl.CostEstimate(
            flops=2 * rows * hidden * share * parts,
            bytes_accessed=2 * hidden * share * parts,
            transcendentals=0,
        ),
        name="down",
    )(place, x, w_down)


def final_sum_kernel(place_ref, own_ref, got1_ref, got2_ref, got3_ref, out_ref):
    x, z, y, c = [place_ref[i] for i in range(4)]
    for ky in range(4):
        sums = []
        for kc in range(2):
            total = own_ref[0, kc, ky].astype(F32)
            for k, ref in ((1, got1_ref), (2, got2_ref), (3, got3_ref)):
                total += ref[kc, ky ^ k].astype(F32)
            sums.append(total)
        low = jnp.where(c == 0, sums[0], sums[1])
        high = jnp.where(c == 0, sums[1], sums[0])
        for source in range(4):
            at = slice(4 * source, 4 * source + 4)
            block = jnp.concatenate([low[at], high[at]], axis=0)
            kz = lax.bitwise_xor(lax.bitwise_xor(y, ky), z)
            out_ref[kz, lax.bitwise_xor(x, source)] = block.astype(BF16)


def final_sum(place, own, got):
    share = own.shape[-1]
    return pl.pallas_call(
        final_sum_kernel,
        out_shape=jax.ShapeDtypeStruct((4, 4, 8, share), BF16),
        in_specs=[pl.BlockSpec(memory_space=pltpu.SMEM)]
        + [pl.BlockSpec(memory_space=pltpu.VMEM)] * 4,
        out_specs=pl.BlockSpec(memory_space=pltpu.VMEM),
        compiler_params=vmem_params(16),
        cost_estimate=pl.CostEstimate(flops=1 << 20, bytes_accessed=1 << 20, transcendentals=0),
        name="final_sum",
    )(place, own, *got)


def mix_kernel(place_ref, routes_ref, weights_ref, *refs):
    back_refs, out_ref = refs[:4], refs[4]
    x, z = place_ref[0], place_ref[1]
    n = STEPS * ROWS
    names = routes_ref[...]
    weights = weights_ref[...]
    down_i = lax.broadcasted_iota(jnp.int32, (n, n), 0)
    over_i = lax.broadcasted_iota(jnp.int32, (n, n), 1)
    earlier = (down_i // ROWS == over_i // ROWS) & (over_i < down_i)
    across = names.T
    slot = lax.broadcasted_iota(jnp.int32, (n, 128), 1)
    step = lax.broadcasted_iota(jnp.int32, (n, 1), 0) // ROWS
    mix = jnp.zeros((n, 128), F32)
    for j in range(2):
        mine = names[:, j : j + 1]
        rank = jnp.zeros((n, 1), F32)
        for other in range(2):
            same = (across[other : other + 1, :] == mine) & earlier
            rank += jnp.sum(same.astype(F32), axis=1, keepdims=True)
        expert = mine.astype(jnp.int32)
        kz = lax.bitwise_xor(expert // 4, z)
        kx = lax.bitwise_xor(expert % 4, x)
        target = (kx * 4 + kz) * 8 + 2 * step + rank.astype(jnp.int32)
        mix += jnp.where(slot == target, weights[:, j : j + 1], 0.0)
    back = jnp.concatenate(
        [ref[kz].astype(F32) for ref in back_refs for kz in range(4)], axis=0
    )
    out_ref[...] = jnp.dot(
        mix, back, precision=lax.Precision.HIGHEST, preferred_element_type=F32
    ).astype(BF16)


def mixed_rows(place, routes, weights, back):
    share = back[0].shape[-1]
    n = STEPS * ROWS
    routes = jnp.pad(routes.astype(F32).reshape(n, 2), ((0, 0), (0, 126)))
    weights = jnp.pad(weights.reshape(n, 2), ((0, 0), (0, 126)))
    return pl.pallas_call(
        mix_kernel,
        out_shape=jax.ShapeDtypeStruct((n, share), BF16),
        in_specs=[pl.BlockSpec(memory_space=pltpu.SMEM)]
        + [pl.BlockSpec(memory_space=pltpu.VMEM)] * 6,
        out_specs=pl.BlockSpec(memory_space=pltpu.VMEM),
        compiler_params=vmem_params(16),
        cost_estimate=pl.CostEstimate(flops=1 << 24, bytes_accessed=1 << 19, transcendentals=0),
        name="mix",
    )(place, routes, weights, *back)


def shards(
    hidden_in,
    step_qkv,
    decay_rates,
    kv_state,
    attn_gain,
    out_proj,
    ffn_gain,
    routes,
    route_weights,
    w_gate,
    w_up,
    w_down,
):
    width = hidden_in.shape[2]
    cols = width // 16
    share = width // 8
    head, exp = lax.axis_index("head"), lax.axis_index("exp")
    y, c, z, x = head // 2, head % 2, exp // 4, exp % 4
    place = jnp.stack([x, z, y, c]).astype(jnp.int32)

    readout = readouts(step_qkv, decay_rates, kv_state, attn_gain)
    half_a, half_b = readout[: 2 * ROWS], readout[2 * ROWS :]
    by_z = jnp.stack([half_a] + [over_exp(half_a, 4 * k) for k in (1, 2, 3)], 0)
    by_x = jnp.stack([half_b] + [over_exp(half_b, k) for k in (1, 2, 3)], 0)
    all_a = [by_z] + [over_exp(by_z, k) for k in (1, 2, 3)]
    all_b = [by_x] + [over_exp(by_x, 4 * k) for k in (1, 2, 3)]
    depth = readout.shape[1]

    pair_rows = lax.dynamic_slice(hidden_in, (2 * c, 0, y * 4 * cols), (2, ROWS, 4 * cols))
    pair_rows = pair_rows.reshape(2 * ROWS, 4 * cols)
    pair_routes = lax.dynamic_slice(routes, (2 * c, 0, 0), (2, ROWS, 2)).reshape(2 * ROWS, 2)
    pair_routes = jnp.pad(pair_routes.astype(BF16), ((0, 0), (0, 126)))
    blocks = []
    for k in range(4):
        block = lax.dynamic_slice(pair_rows, (0, (x ^ k) * cols), (2 * ROWS, cols))
        blocks.append(jnp.concatenate([block, pair_routes], axis=1))
    blocks, all_b[1] = lax.optimization_barrier((blocks, all_b[1]))
    hidden_rows = [
        over_all(blocks[k], lambda y, c, z, x, k=k: (z, c, y, x ^ k)) for k in range(4)
    ]

    def project(pieces):
        rows = jnp.concatenate([p.reshape(8 * ROWS, depth) for p in pieces], axis=0)
        out = jnp.dot(rows, out_proj, preferred_element_type=F32).astype(BF16)
        return out.reshape(4, 4, 2 * ROWS, cols)

    part_a = project(all_a)
    part_b = project(all_b).transpose(1, 0, 2, 3)
    mine = jnp.where(c == 0, part_a, part_b)
    other = jnp.where(c == 0, part_b, part_a)
    mine = (mine.astype(F32) + over_head(other, 1).astype(F32)).astype(BF16)

    def for_y(k):
        return lax.dynamic_index_in_dim(mine, y ^ k ^ z, 1, keepdims=False)

    got = [over_head(for_y(k), 2 * k) for k in (1, 2, 3)]
    attended, sent = attend(place, for_y(0), got, hidden_rows)

    by_kz = [sent[0]] + [over_exp(sent[k], 4 * k) for k in (1, 2, 3)]
    by_kx = [jnp.stack([by_kz[kz][kx] for kz in range(4)], 0) for kx in range(4)]
    by_kx = by_kx[:1] + [over_exp(by_kx[k], k) for k in (1, 2, 3)]
    normed = norm(place, ffn_gain, by_kx)
    by_y = [normed] + [over_head(normed, 2 * k) for k in (1, 2, 3)]

    attended, by_y[1] = lax.optimization_barrier((attended, by_y[1]))
    by_core = [over_head(piece, 1) for piece in by_y]
    pieces = []
    for k in range(4):
        source = (2 * c + x % 2) ^ k
        block = lax.dynamic_index_in_dim(attended, source ^ x, 0, keepdims=False)
        pieces.append(
            over_all(block, lambda y, c, z, x, k=k: (z, x // 2, y, (2 * c + x % 2) ^ k))
        )
    pieces = jnp.stack(pieces, 0)
    ordered = [lax.dynamic_index_in_dim(pieces, j ^ x, 0, keepdims=False) for j in range(4)]
    attended_out = jnp.concatenate(
        [jnp.concatenate(ordered[:2], axis=1), jnp.concatenate(ordered[2:], axis=1)], axis=0
    ).reshape(STEPS, ROWS, share)

    hidden = gate_up(by_y + by_core, w_gate, w_up)
    ky = jnp.arange(4)
    theirs = down((y ^ ky) * 2 + (1 - c), hidden, w_down, share)
    theirs = over_head(theirs, 1)
    ours = down((y ^ ky) * 2 + c, hidden, w_down, share)
    theirs = theirs.reshape(4, 2, 4, 16, share)
    ours = ours.reshape(4, 2, 4, 16, share)
    both = (ours.astype(F32) + theirs[:, ::-1].astype(F32)).astype(BF16)
    got = [over_head(both[k], 2 * k) for k in (1, 2, 3)]
    results = final_sum(place, both, got)
    by_kz = [results[0]] + [over_exp(results[k], 4 * k) for k in (1, 2, 3)]
    by_kx = [jnp.stack([by_kz[kz][kx] for kz in range(4)], 0) for kx in range(4)]
    by_kx = by_kx[:1] + [over_exp(by_kx[k], k) for k in (1, 2, 3)]
    mixed = mixed_rows(place, routes, route_weights, by_kx)
    return attended_out, mixed.reshape(STEPS, ROWS, share)


def solution(mesh):
    return jax.shard_map(
        shards,
        mesh=mesh,
        in_specs=(
            P(None, "exp", None),
            P(None, "exp", None, "head"),
            P(None, "head"),
            P("exp", "head", None, None),
            P("head"),
            P("head", "exp"),
            P(),
            P(None, "exp", None),
            P(None, "exp", None),
            P("exp", None, "head"),
            P("exp", None, "head"),
            P("exp", "head", None),
        ),
        out_specs=(P(None, "exp", "head"), P(None, "exp", "head")),
        check_vma=False,
    )
```

time: 178 us -> 169 us (0.949)
  local copies, waits for them, and re-layouts: 39.5 us -> 2.74 us
  Pallas kernels: 13.5 us -> 33.1 us
  starting transfers between devices: 67.9 us -> 84.6 us
  blocking collectives: 13.2 us -> 0 us
  waiting for transfers between devices: 35.7 us -> 42.4 us
    unnamed x23 -> x24, local copies, waits for them, and re-layouts: 35.6 us -> 0.68 us
    all_to_all x1 -> x0, blocking collectives: 13.2 us -> none  [shards(): got = lax.all_to_all(sent, 'exp', split_axis=0, concat_axis=0, tiled=True)]
    ppermute x15, starting transfers between devices: 21.2 us -> 34.3 us  [over_head(): return lax.ppermute(value, 'head', [(i, i ^ bits) for i in range(8)])]
    ppermute x12 -> x24, waiting for transfers between devices: 5.63 us -> 18.5 us  [over_exp(): return lax.ppermute(value, 'exp', [(i, i ^ bits) for i in range(16)])]
    all_to_all x1 -> x0, waiting for transfers between devices: 7.69 us -> none  [shards(): lax.all_to_all(results, 'exp', split_axis=0, concat_axis=0, tiled=True)]
    ppermute x12 -> x24, starting transfers between devices: 30.5 us -> 38.1 us  [over_exp(): return lax.ppermute(value, 'exp', [(i, i ^ bits) for i in range(16)])]
    pallas_call x1, Pallas kernels: 4.83 us -> 11.4 us  [gate_up(): pl.pallas_call(gate_up_kernel, out_shape=jax.ShapeDtypeStruct((rows, hidd...]
    pallas_call x2, Pallas kernels: 4.32 us -> 10.4 us  [down(): pl.pallas_call(down_kernel, out_shape=jax.ShapeDtypeStruct((parts, rows,...]
  transfers between devices with their start and end apart: 36 -> 47, of which waited for: 13 -> 22; matrix products, arithmetic and copies ran while one was open for 16% -> 2% of each run, Pallas kernels for 3% -> 3%
where the time goes in v2:
time: 169 us; the launch traced here: 168 us
  starting transfers between devices  84.6 us (50%)
  waiting for transfers between devices  42.4 us (25%)
  Pallas kernels  33.1 us (20%)
  other arithmetic  3.54 us (2%)
  local copies, waits for them, and re-layouts  2.74 us (2%)
    ppermute x24, starting transfers between devices, over_exp(): return lax.ppermute(value, 'exp', [(i, i ^ bits) for i in range(16)])  38.1 us
    ppermute x15, starting transfers between devices, over_head(): return lax.ppermute(value, 'head', [(i, i ^ bits) for i in range(8)])  34.3 us
    ppermute x15, waiting for transfers between devices, over_head(): return lax.ppermute(value, 'head', [(i, i ^ bits) for i in range(8)])  21.5 us
    ppermute x24, waiting for transfers between devices, over_exp(): return lax.ppermute(value, 'exp', [(i, i ^ bits) for i in range(16)])  18.5 us
    ppermute x8, starting transfers between devices, over_all(): return lax.ppermute(value, ('head', 'exp'), pairs)  12.2 us
    pallas_call x1, Pallas kernels, gate_up(): pl.pallas_call(gate_up_kernel, out_shape=jax.ShapeDtypeStruct((rows, hidd...  11.4 us
    pallas_call x2, Pallas kernels, down(): pl.pallas_call(down_kernel, out_shape=jax.ShapeDtypeStruct((parts, rows,...  10.4 us
    pallas_call x1, Pallas kernels, readouts(): pl.pallas_call(readout_kernel, out_shape=jax.ShapeDtypeStruct((STEPS * RO...  7.43 us
  transfers between devices with their start and end apart: 47, of which 22 were waited for; matrix products, arithmetic and copies ran while one was open for 2% of the time, Pallas kernels for 3%

profile of v2, /device:TPU:0, one launch (start us, length us, event | category | flops | bytes accessed | tf_op | source)
XLA Modules:
  0.0 168.3 jit_solution(8826786295478289716)
XLA Ops:
  0.7 7.4 %readout.1 = bf16[32,1024]{1,0:T(8,128)(2,1)} custom-call(f32[4,8]{1,0:T(4,128)} %decay_ref.1, bf16[4,3,8,1024]{3,2,1,0:T(8,128)(2,1)} %bitcast.115, f32[8,8,128,128]{3,2,1,0:T(8,128)} %state_ref.1, f32[1,1024]{1,0:T(1,128)} %bitcast.132), custom_call_target="tpu_custom_call" | custom-call | flops 134217728 | bytes 4194304 | tf_op jit(solution)/shard_map/readout/pallas_call | solution.py:84
  10.5 2.7 %collective-permute-start.7 = (bf16[16,1024]{1,0:T(8,128)(2,1)S(1)}, bf16[16,1024]{1,0:T(8,128)(2,1)S(1)}, u32[]{:S(2)}, u32[]{:S(2)}) collective-permute-start(bf16[16,1024]{1,0:T(8,128)(2,1)S(1)} %get-tuple-element.43), channel_id=1, source_target_pairs={{0,2},{1,3},{2,0},{3,1},{4,6},{5,7},{6,4},{7,5},{8,10},{9,11},{10,... | collective-permute-start | bytes 98312 | tf_op jit(solution)/shard_map/ppermute | solution.py:27
  15.7 3.6 %collective-permute-start.1 = (bf16[16,1024]{1,0:T(8,128)(2,1)S(1)}, bf16[16,1024]{1,0:T(8,128)(2,1)S(1)}, u32[]{:S(2)}, u32[]{:S(2)}) collective-permute-start(bf16[16,1024]{1,0:T(8,128)(2,1)S(1)} %get-tuple-element.44), channel_id=1, source_target_pairs={{0,8},{1,9},{2,10},{3,11},{4,12},{5,13},{6,14},{7,15},{8,0},{9,1},... | collective-permute-start | bytes 98312 | tf_op jit(solution)/shard_map/ppermute | solution.py:27
  20.4 4.6 %collective-permute-start.10 = (bf16[4,16,1024]{2,1,0:T(8,128)(2,1)S(1)}, bf16[4,16,1024]{2,1,0:T(8,128)(2,1)S(1)}, u32[]{:S(2)}, u32[]{:S(2)}) collective-permute-start(bf16[4,16,1024]{2,1,0:T(8,128)(2,1)S(1)} %pad_maximum_fusion.1), channel_id=1, source_target_pairs={{0,8},{1,9},{2,10},{3,11},{4,12},{5,13},{6,14},{7,15},{8,0},{9,1},... | collective-permute-start | bytes 393224 | tf_op jit(solution)/shard_map/ppermute | solution.py:27
  27.2 3.9 %collective-permute-start.4 = (bf16[4,16,1024]{2,1,0:T(8,128)(2,1)S(1)}, bf16[4,16,1024]{2,1,0:T(8,128)(2,1)S(1)}, u32[]{:S(2)}, u32[]{:S(2)}) collective-permute-start(bf16[4,16,1024]{2,1,0:T(8,128)(2,1)S(1)} %pad_maximum_fusion), channel_id=1, source_target_pairs={{0,2},{1,3},{2,0},{3,1},{4,6},{5,7},{6,4},{7,5},{8,10},{9,11},{10,... | collective-permute-start | bytes 393224 | tf_op jit(solution)/shard_map/ppermute | solution.py:27
  32.1 3.4 %collective-permute-done.4 = bf16[4,16,1024]{2,1,0:T(8,128)(2,1)S(1)} collective-permute-done((bf16[4,16,1024]{2,1,0:T(8,128)(2,1)S(1)}, bf16[4,16,1024]{2,1,0:T(8,128)(2,1)S(1)}, u32[]{:S(2)}, u32[]{:S(2)}) %collective-permute-start.4) | collective-permute-done | bytes 131104 | tf_op jit(solution)/shard_map/ppermute | solution.py:27
  40.6 2.8 %collective-permute-start.19 = (bf16[16,512]{1,0:T(8,128)(2,1)S(1)}, bf16[16,512]{1,0:T(8,128)(2,1)S(1)}, u32[]{:S(2)}, u32[]{:S(2)}) collective-permute-start(bf16[16,512]{1,0:T(8,128)(2,1)S(1)} %get-tuple-element.15), channel_id=1, source_target_pairs={{0,3},{1,2},{2,1},{3,0},{4,35},{5,34},{6,33},{7,32},{8,67},{9,66},... | collective-permute-start | bytes 49160 | tf_op jit(solution)/shard_map/ppermute | solution.py:36
  43.5 7.1 %collective-permute-start.13 = (bf16[4,16,384]{2,1,0:T(8,128)(2,1)S(1)}, bf16[4,16,384]{2,1,0:T(8,128)(2,1)S(1)}, u32[]{:S(2)}, u32[]{:S(2)}) collective-permute-start(bf16[4,16,384]{2,1,0:T(8,128)(2,1)S(1)} %get-tuple-element.39), channel_id=1, source_target_pairs={{0,32},{16,48},{32,0},{48,16},{64,96},{80,112},{96,64},{112,80},{1... | collective-permute-start | bytes 147464 | tf_op jit(solution)/shard_map/ppermute | solution.py:23
  50.6 7.7 %collective-permute-start.14 = (bf16[4,16,384]{2,1,0:T(8,128)(2,1)S(1)}, bf16[4,16,384]{2,1,0:T(8,128)(2,1)S(1)}, u32[]{:S(2)}, u32[]{:S(2)}) collective-permute-start(bf16[4,16,384]{2,1,0:T(8,128)(2,1)S(1)} %get-tuple-element.38), channel_id=1, source_target_pairs={{0,64},{16,80},{32,96},{48,112},{64,0},{80,16},{96,32},{112,48},{1... | collective-permute-start | bytes 147464 | tf_op jit(solution)/shard_map/ppermute | solution.py:23
  60.9 2.7 %collective-permute-done.15.got3_ref = bf16[4,16,384]{2,1,0:T(8,128)(2,1)S(1)} collective-permute-done((bf16[4,16,384]{2,1,0:T(8,128)(2,1)S(1)}, bf16[4,16,384]{2,1,0:T(8,128)(2,1)S(1)}, u32[]{:S(2)}, u32[]{:S(2)}) %collective-permute-start.15) | collective-permute-done | bytes 49184 | tf_op jit(solution)/shard_map/ppermute | solution.py:23
  66.4 2.9 %collective-permute-start.22 = (bf16[4,16,384]{2,1,0:T(8,128)(2,1)S(1)}, bf16[4,16,384]{2,1,0:T(8,128)(2,1)S(1)}, u32[]{:S(2)}, u32[]{:S(2)}) collective-permute-start(bf16[4,16,384]{2,1,0:T(8,128)(2,1)S(1)} %get-tuple-element.35), channel_id=1, source_target_pairs={{0,12},{1,13},{2,14},{3,15},{4,8},{5,9},{6,10},{7,11},{8,4},{9,5},... | collective-permute-start | bytes 147464 | tf_op jit(solution)/shard_map/ppermute | solution.py:27
  72.4 3.7 %collective-permute-start.23 = (bf16[4,16,384]{2,1,0:T(8,128)(2,1)S(1)}, bf16[4,16,384]{2,1,0:T(8,128)(2,1)S(1)}, u32[]{:S(2)}, u32[]{:S(2)}) collective-permute-start(bf16[4,16,384]{2,1,0:T(8,128)(2,1)S(1)} %pad_maximum_fusion.3), channel_id=1, source_target_pairs={{0,1},{1,0},{2,3},{3,2},{4,5},{5,4},{6,7},{7,6},{8,9},{9,8},{10,11... | collective-permute-start | bytes 147464 | tf_op jit(solution)/shard_map/ppermute | solution.py:27
  79.6 3.5 %collective-permute-start.31 = (bf16[16,6144]{1,0:T(8,128)(2,1)S(1)}, bf16[16,6144]{1,0:T(8,128)(2,1)S(1)}, u32[]{:S(2)}, u32[]{:S(2)}) collective-permute-start(bf16[16,6144]{1,0:T(8,128)(2,1)S(1)} %norm.1.refs_0_), channel_id=1, source_target_pairs={{0,64},{16,80},{32,96},{48,112},{64,0},{80,16},{96,32},{112,48},{1... | collective-permute-start | bytes 589832 | tf_op jit(solution)/shard_map/ppermute | solution.py:23
  85.1 3.8 %collective-permute-done.31.refs_2_ = bf16[16,6144]{1,0:T(8,128)(2,1)S(1)} collective-permute-done((bf16[16,6144]{1,0:T(8,128)(2,1)S(1)}, bf16[16,6144]{1,0:T(8,128)(2,1)S(1)}, u32[]{:S(2)}, u32[]{:S(2)}) %collective-permute-start.31) | collective-permute-done | bytes 196640 | tf_op jit(solution)/shard_map/ppermute | solution.py:23
  93.0 11.4 %gate_up.1.x_ref = bf16[128,576]{1,0:T(8,128)(2,1)} custom-call(bf16[16,6144]{1,0:T(8,128)(2,1)} %copy-done.1, bf16[16,6144]{1,0:T(8,128)(2,1)} %copy-done.3, bf16[16,6144]{1,0:T(8,128)(2,1)} %copy-done.4, bf16[16,6144]{1,0:T(8,128)(2,1)} %copy-done.5, bf16[16,6144]{1,0:T(8,128)(2,1)} %copy-done.6, bf16[16,6144]{1,0:T(8,128)(2,1)} %copy-done.7, ...), custom_call_target="tpu_custom_call" | custom-call | flops 1811939328 | bytes 14155776 | tf_op jit(solution)/shard_map/gate_up/pallas_call | solution.py:221
  104.4 5.3 %down.3 = bf16[4,128,768]{2,1,0:T(8,128)(2,1)} custom-call(s32[4]{0:T(128)} %fusion.21.place_ref, bf16[128,576]{1,0:T(8,128)(2,1)} %gate_up.1.x_ref, bf16[1,576,6144]{2,1,0:T(8,128)(2,1)} %w_ref.3), custom_call_target="tpu_custom_call" | custom-call | flops 452984832 | bytes 3538944 | tf_op jit(solution)/shard_map/down/pallas_call | solution.py:246
  112.1 4.4 %collective-permute-start.29 = (bf16[16,384]{1,0:T(8,128)(2,1)S(1)}, bf16[16,384]{1,0:T(8,128)(2,1)S(1)}, u32[]{:S(2)}, u32[]{:S(2)}) collective-permute-start(bf16[16,384]{1,0:T(8,128)(2,1)S(1)} %get-tuple-element.63), channel_id=1, source_target_pairs={{0,2},{1,3},{2,18},{3,19},{4,34},{5,35},{6,50},{7,51},{8,66},{9,67... | collective-permute-start | bytes 36872 | tf_op jit(solution)/shard_map/ppermute | solution.py:36
  119.7 5.1 %down.2 = bf16[4,128,768]{2,1,0:T(8,128)(2,1)} custom-call(s32[4]{0:T(128)} %fusion.22.place_ref, bf16[128,576]{1,0:T(8,128)(2,1)} %gate_up.1.x_ref, bf16[1,576,6144]{2,1,0:T(8,128)(2,1)} %w_ref.3), custom_call_target="tpu_custom_call" | custom-call | flops 452984832 | bytes 3538944 | tf_op jit(solution)/shard_map/down/pallas_call | solution.py:246
  126.3 4.0 %collective-permute-start.38 = (bf16[2,4,16,768]{3,2,1,0:T(8,128)(2,1)S(1)}, bf16[2,4,16,768]{3,2,1,0:T(8,128)(2,1)S(1)}, u32[]{:S(2)}, u32[]{:S(2)}) collective-permute-start(bf16[2,4,16,768]{3,2,1,0:T(8,128)(2,1)S(1)} %get-tuple-element.22), channel_id=1, source_target_pairs={{0,32},{16,48},{32,0},{48,16},{64,96},{80,112},{96,64},{112,80},{1... | collective-permute-start | bytes 589832 | tf_op jit(solution)/shard_map/ppermute | solution.py:23
  130.3 9.9 %collective-permute-start.39 = (bf16[2,4,16,768]{3,2,1,0:T(8,128)(2,1)S(1)}, bf16[2,4,16,768]{3,2,1,0:T(8,128)(2,1)S(1)}, u32[]{:S(2)}, u32[]{:S(2)}) collective-permute-start(bf16[2,4,16,768]{3,2,1,0:T(8,128)(2,1)S(1)} %get-tuple-element.21), channel_id=1, source_target_pairs={{0,64},{16,80},{32,96},{48,112},{64,0},{80,16},{96,32},{112,48},{1... | collective-permute-start | bytes 589832 | tf_op jit(solution)/shard_map/ppermute | solution.py:23
  140.8 7.1 %collective-permute-done.39.got2_ref = bf16[2,4,16,768]{3,2,1,0:T(8,128)(2,1)S(1)} collective-permute-done((bf16[2,4,16,768]{3,2,1,0:T(8,128)(2,1)S(1)}, bf16[2,4,16,768]{3,2,1,0:T(8,128)(2,1)S(1)}, u32[]{:S(2)}, u32[]{:S(2)}) %collective-permute-start.39) | collective-permute-done | bytes 196640 | tf_op jit(solution)/shard_map/ppermute | solution.py:23
  152.8 2.8 %collective-permute-start.43 = (bf16[4,8,768]{2,1,0:T(8,128)(2,1)S(1)}, bf16[4,8,768]{2,1,0:T(8,128)(2,1)S(1)}, u32[]{:S(2)}, u32[]{:S(2)}) collective-permute-start(bf16[4,8,768]{2,1,0:T(8,128)(2,1)S(1)} %get-tuple-element.28), channel_id=1, source_target_pairs={{0,12},{1,13},{2,14},{3,15},{4,8},{5,9},{6,10},{7,11},{8,4},{9,5},... | collective-permute-start | bytes 147464 | tf_op jit(solution)/shard_map/ppermute | solution.py:27
  158.2 2.8 %collective-permute-start.46 = (bf16[4,8,768]{2,1,0:T(8,128)(2,1)S(1)}, bf16[4,8,768]{2,1,0:T(8,128)(2,1)S(1)}, u32[]{:S(2)}, u32[]{:S(2)}) collective-permute-start(bf16[4,8,768]{2,1,0:T(8,128)(2,1)S(1)} %pad_maximum_fusion.10), channel_id=1, source_target_pairs={{0,3},{1,2},{2,1},{3,0},{4,7},{5,6},{6,5},{7,4},{8,11},{9,10},{10,... | collective-permute-start | bytes 147464 | tf_op jit(solution)/shard_map/ppermute | solution.py:27
  163.6 3.1 %collective-permute-done.45.refs_2_ = bf16[4,8,768]{2,1,0:T(8,128)(2,1)S(1)} collective-permute-done((bf16[4,8,768]{2,1,0:T(8,128)(2,1)S(1)}, bf16[4,8,768]{2,1,0:T(8,128)(2,1)S(1)}, u32[]{:S(2)}, u32[]{:S(2)}) %collective-permute-start.45) | collective-permute-done | bytes 49184 | tf_op jit(solution)/shard_map/ppermute | solution.py:27
  (147 shorter events, 51.6 us)
Async XLA Ops:
  8.9 11.3 %collective-permute-start.6 = (bf16[16,1024]{1,0:T(8,128)(2,1)S(1)}, bf16[16,1024]{1,0:T(8,128)(2,1)S(1)}, u32[]{:S(2)}, u32[]{:S(2)}) collective-permute-start(bf16[16,1024]{1,0:T(8,128)(2,1)S(1)} %get-tuple-element.43), channel_id=1, source_target_pairs={{0,1},{1,0},{2,3},{3,2},{4,5},{5,4},{6,7},{7,6},{8,9},{9,8},{10,11... | collective-permute-start | bytes 98312 | tf_op jit(solution)/shard_map/ppermute | solution.py:27
  10.5 9.7 %collective-permute-start.7 = (bf16[16,1024]{1,0:T(8,128)(2,1)S(1)}, bf16[16,1024]{1,0:T(8,128)(2,1)S(1)}, u32[]{:S(2)}, u32[]{:S(2)}) collective-permute-start(bf16[16,1024]{1,0:T(8,128)(2,1)S(1)} %get-tuple-element.43), channel_id=1, source_target_pairs={{0,2},{1,3},{2,0},{3,1},{4,6},{5,7},{6,4},{7,5},{8,10},{9,11},{10,... | collective-permute-start | bytes 98312 | tf_op jit(solution)/shard_map/ppermute | solution.py:27
  13.3 7.0 %collective-permute-start.8 = (bf16[16,1024]{1,0:T(8,128)(2,1)S(1)}, bf16[16,1024]{1,0:T(8,128)(2,1)S(1)}, u32[]{:S(2)}, u32[]{:S(2)}) collective-permute-start(bf16[16,1024]{1,0:T(8,128)(2,1)S(1)} %get-tuple-element.43), channel_id=1, source_target_pairs={{0,3},{1,2},{2,1},{3,0},{4,7},{5,6},{6,5},{7,4},{8,11},{9,10},{10,... | collective-permute-start | bytes 98312 | tf_op jit(solution)/shard_map/ppermute | solution.py:27
  13.7 11.3 %collective-permute-start = (bf16[16,1024]{1,0:T(8,128)(2,1)S(1)}, bf16[16,1024]{1,0:T(8,128)(2,1)S(1)}, u32[]{:S(2)}, u32[]{:S(2)}) collective-permute-start(bf16[16,1024]{1,0:T(8,128)(2,1)S(1)} %get-tuple-element.44), channel_id=1, source_target_pairs={{0,4},{1,5},{2,6},{3,7},{4,0},{5,1},{6,2},{7,3},{8,12},{9,13},{10,... | collective-permute-start | bytes 98312 | tf_op jit(solution)/shard_map/ppermute | solution.py:27
  15.7 9.4 %collective-permute-start.1 = (bf16[16,1024]{1,0:T(8,128)(2,1)S(1)}, bf16[16,1024]{1,0:T(8,128)(2,1)S(1)}, u32[]{:S(2)}, u32[]{:S(2)}) collective-permute-start(bf16[16,1024]{1,0:T(8,128)(2,1)S(1)} %get-tuple-element.44), channel_id=1, source_target_pairs={{0,8},{1,9},{2,10},{3,11},{4,12},{5,13},{6,14},{7,15},{8,0},{9,1},... | collective-permute-start | bytes 98312 | tf_op jit(solution)/shard_map/ppermute | solution.py:27
  20.2 6.6 %collective-permute-start.2 = (bf16[16,1024]{1,0:T(8,128)(2,1)S(1)}, bf16[16,1024]{1,0:T(8,128)(2,1)S(1)}, u32[]{:S(2)}, u32[]{:S(2)}) collective-permute-start(bf16[16,1024]{1,0:T(8,128)(2,1)S(1)} %get-tuple-element.44), channel_id=1, source_target_pairs={{0,12},{1,13},{2,14},{3,15},{4,8},{5,9},{6,10},{7,11},{8,4},{9,5},... | collective-permute-start | bytes 98312 | tf_op jit(solution)/shard_map/ppermute | solution.py:27
  20.3 10.9 %collective-permute-start.9 = (bf16[4,16,1024]{2,1,0:T(8,128)(2,1)S(1)}, bf16[4,16,1024]{2,1,0:T(8,128)(2,1)S(1)}, u32[]{:S(2)}, u32[]{:S(2)}) collective-permute-start(bf16[4,16,1024]{2,1,0:T(8,128)(2,1)S(1)} %pad_maximum_fusion.1), channel_id=1, source_target_pairs={{0,4},{1,5},{2,6},{3,7},{4,0},{5,1},{6,2},{7,3},{8,12},{9,13},{10,... | collective-permute-start | bytes 393224 | tf_op jit(solution)/shard_map/ppermute | solution.py:27
  20.4 11.2 %collective-permute-start.10 = (bf16[4,16,1024]{2,1,0:T(8,128)(2,1)S(1)}, bf16[4,16,1024]{2,1,0:T(8,128)(2,1)S(1)}, u32[]{:S(2)}, u32[]{:S(2)}) collective-permute-start(bf16[4,16,1024]{2,1,0:T(8,128)(2,1)S(1)} %pad_maximum_fusion.1), channel_id=1, source_target_pairs={{0,8},{1,9},{2,10},{3,11},{4,12},{5,13},{6,14},{7,15},{8,0},{9,1},... | collective-permute-start | bytes 393224 | tf_op jit(solution)/shard_map/ppermute | solution.py:27
  27.2 8.3 %collective-permute-start.4 = (bf16[4,16,1024]{2,1,0:T(8,128)(2,1)S(1)}, bf16[4,16,1024]{2,1,0:T(8,128)(2,1)S(1)}, u32[]{:S(2)}, u32[]{:S(2)}) collective-permute-start(bf16[4,16,1024]{2,1,0:T(8,128)(2,1)S(1)} %pad_maximum_fusion), channel_id=1, source_target_pairs={{0,2},{1,3},{2,0},{3,1},{4,6},{5,7},{6,4},{7,5},{8,10},{9,11},{10,... | collective-permute-start | bytes 393224 | tf_op jit(solution)/shard_map/ppermute | solution.py:27
  37.9 12.6 %collective-permute-start.16 = (bf16[16,512]{1,0:T(8,128)(2,1)S(1)}, bf16[16,512]{1,0:T(8,128)(2,1)S(1)}, u32[]{:S(2)}, u32[]{:S(2)}) collective-permute-start(bf16[16,512]{1,0:T(8,128)(2,1)S(1)} %get-tuple-element.12), channel_id=1, source_target_pairs={{0,0},{1,1},{2,2},{3,3},{4,32},{5,33},{6,34},{7,35},{8,64},{9,65},... | collective-permute-start | bytes 49160 | tf_op jit(solution)/shard_map/ppermute | solution.py:36
  38.6 19.7 %collective-permute-start.17 = (bf16[16,512]{1,0:T(8,128)(2,1)S(1)}, bf16[16,512]{1,0:T(8,128)(2,1)S(1)}, u32[]{:S(2)}, u32[]{:S(2)}) collective-permute-start(bf16[16,512]{1,0:T(8,128)(2,1)S(1)} %get-tuple-element.13), channel_id=1, source_target_pairs={{0,1},{1,0},{2,3},{3,2},{4,33},{5,32},{6,35},{7,34},{8,65},{9,64},... | collective-permute-start | bytes 49160 | tf_op jit(solution)/shard_map/ppermute | solution.py:36
  38.7 20.2 %collective-permute-start.18 = (bf16[16,512]{1,0:T(8,128)(2,1)S(1)}, bf16[16,512]{1,0:T(8,128)(2,1)S(1)}, u32[]{:S(2)}, u32[]{:S(2)}) collective-permute-start(bf16[16,512]{1,0:T(8,128)(2,1)S(1)} %get-tuple-element.14), channel_id=1, source_target_pairs={{0,2},{1,3},{2,0},{3,1},{4,34},{5,35},{6,32},{7,33},{8,66},{9,67},... | collective-permute-start | bytes 49160 | tf_op jit(solution)/shard_map/ppermute | solution.py:36
  40.6 18.3 %collective-permute-start.19 = (bf16[16,512]{1,0:T(8,128)(2,1)S(1)}, bf16[16,512]{1,0:T(8,128)(2,1)S(1)}, u32[]{:S(2)}, u32[]{:S(2)}) collective-permute-start(bf16[16,512]{1,0:T(8,128)(2,1)S(1)} %get-tuple-element.15), channel_id=1, source_target_pairs={{0,3},{1,2},{2,1},{3,0},{4,35},{5,34},{6,33},{7,32},{8,67},{9,66},... | collective-permute-start | bytes 49160 | tf_op jit(solution)/shard_map/ppermute | solution.py:36
  43.5 15.4 %collective-permute-start.13 = (bf16[4,16,384]{2,1,0:T(8,128)(2,1)S(1)}, bf16[4,16,384]{2,1,0:T(8,128)(2,1)S(1)}, u32[]{:S(2)}, u32[]{:S(2)}) collective-permute-start(bf16[4,16,384]{2,1,0:T(8,128)(2,1)S(1)} %get-tuple-element.39), channel_id=1, source_target_pairs={{0,32},{16,48},{32,0},{48,16},{64,96},{80,112},{96,64},{112,80},{1... | collective-permute-start | bytes 147464 | tf_op jit(solution)/shard_map/ppermute | solution.py:23
  50.6 10.3 %collective-permute-start.14 = (bf16[4,16,384]{2,1,0:T(8,128)(2,1)S(1)}, bf16[4,16,384]{2,1,0:T(8,128)(2,1)S(1)}, u32[]{:S(2)}, u32[]{:S(2)}) collective-permute-start(bf16[4,16,384]{2,1,0:T(8,128)(2,1)S(1)} %get-tuple-element.38), channel_id=1, source_target_pairs={{0,64},{16,80},{32,96},{48,112},{64,0},{80,16},{96,32},{112,48},{1... | collective-permute-start | bytes 147464 | tf_op jit(solution)/shard_map/ppermute | solution.py:23
  79.6 9.3 %collective-permute-start.31 = (bf16[16,6144]{1,0:T(8,128)(2,1)S(1)}, bf16[16,6144]{1,0:T(8,128)(2,1)S(1)}, u32[]{:S(2)}, u32[]{:S(2)}) collective-permute-start(bf16[16,6144]{1,0:T(8,128)(2,1)S(1)} %norm.1.refs_0_), channel_id=1, source_target_pairs={{0,64},{16,80},{32,96},{48,112},{64,0},{80,16},{96,32},{112,48},{1... | collective-permute-start | bytes 589832 | tf_op jit(solution)/shard_map/ppermute | solution.py:23
  83.0 7.9 %collective-permute-start.32 = (bf16[16,6144]{1,0:T(8,128)(2,1)S(1)}, bf16[16,6144]{1,0:T(8,128)(2,1)S(1)}, u32[]{:S(2)}, u32[]{:S(2)}) collective-permute-start(bf16[16,6144]{1,0:T(8,128)(2,1)S(1)} %norm.1.refs_0_), channel_id=1, source_target_pairs={{0,96},{16,112},{32,64},{48,80},{64,32},{80,48},{96,0},{112,16},{1... | collective-permute-start | bytes 589832 | tf_op jit(solution)/shard_map/ppermute | solution.py:23
  84.1 7.4 %collective-permute-start.33 = (bf16[16,6144]{1,0:T(8,128)(2,1)S(1)}, bf16[16,6144]{1,0:T(8,128)(2,1)S(1)}, u32[]{:S(2)}, u32[]{:S(2)}) collective-permute-start(bf16[16,6144]{1,0:T(8,128)(2,1)S(1)} %norm.1.refs_0_), channel_id=1, source_target_pairs={{0,16},{16,0},{32,48},{48,32},{64,80},{80,64},{96,112},{112,96},{1... | collective-permute-start | bytes 589832 | tf_op jit(solution)/shard_map/ppermute | solution.py:23
  109.6 15.2 %collective-permute-start.37 = (bf16[4,128,768]{2,1,0:T(8,128)(2,1)}, bf16[4,128,768]{2,1,0:T(8,128)(2,1)S(1)}, u32[]{:S(2)}, u32[]{:S(2)}) collective-permute-start(bf16[4,128,768]{2,1,0:T(8,128)(2,1)} %down.3), channel_id=1, source_target_pairs={{0,16},{16,0},{32,48},{48,32},{64,80},{80,64},{96,112},{112,96},{1... | collective-permute-start | bytes 2359304 | tf_op jit(solution)/shard_map/ppermute | solution.py:23
  109.8 7.6 %collective-permute-start.27 = (bf16[16,384]{1,0:T(8,128)(2,1)S(1)}, bf16[16,384]{1,0:T(8,128)(2,1)S(1)}, u32[]{:S(2)}, u32[]{:S(2)}) collective-permute-start(bf16[16,384]{1,0:T(8,128)(2,1)S(1)} %get-tuple-element.61), channel_id=1, source_target_pairs={{0,0},{1,1},{2,16},{3,17},{4,32},{5,33},{6,48},{7,49},{8,64},{9,65... | collective-permute-start | bytes 36872 | tf_op jit(solution)/shard_map/ppermute | solution.py:36
  110.4 6.9 %collective-permute-start.28 = (bf16[16,384]{1,0:T(8,128)(2,1)S(1)}, bf16[16,384]{1,0:T(8,128)(2,1)S(1)}, u32[]{:S(2)}, u32[]{:S(2)}) collective-permute-start(bf16[16,384]{1,0:T(8,128)(2,1)S(1)} %get-tuple-element.64), channel_id=1, source_target_pairs={{0,1},{1,0},{2,17},{3,16},{4,33},{5,32},{6,49},{7,48},{8,65},{9,64... | collective-permute-start | bytes 36872 | tf_op jit(solution)/shard_map/ppermute | solution.py:36
  126.3 14.5 %collective-permute-start.38 = (bf16[2,4,16,768]{3,2,1,0:T(8,128)(2,1)S(1)}, bf16[2,4,16,768]{3,2,1,0:T(8,128)(2,1)S(1)}, u32[]{:S(2)}, u32[]{:S(2)}) collective-permute-start(bf16[2,4,16,768]{3,2,1,0:T(8,128)(2,1)S(1)} %get-tuple-element.22), channel_id=1, source_target_pairs={{0,32},{16,48},{32,0},{48,16},{64,96},{80,112},{96,64},{112,80},{1... | collective-permute-start | bytes 589832 | tf_op jit(solution)/shard_map/ppermute | solution.py:23
  130.3 17.7 %collective-permute-start.39 = (bf16[2,4,16,768]{3,2,1,0:T(8,128)(2,1)S(1)}, bf16[2,4,16,768]{3,2,1,0:T(8,128)(2,1)S(1)}, u32[]{:S(2)}, u32[]{:S(2)}) collective-permute-start(bf16[2,4,16,768]{3,2,1,0:T(8,128)(2,1)S(1)} %get-tuple-element.21), channel_id=1, source_target_pairs={{0,64},{16,80},{32,96},{48,112},{64,0},{80,16},{96,32},{112,48},{1... | collective-permute-start | bytes 589832 | tf_op jit(solution)/shard_map/ppermute | solution.py:23
  140.2 9.9 %collective-permute-start.40 = (bf16[2,4,16,768]{3,2,1,0:T(8,128)(2,1)S(1)}, bf16[2,4,16,768]{3,2,1,0:T(8,128)(2,1)S(1)}, u32[]{:S(2)}, u32[]{:S(2)}) collective-permute-start(bf16[2,4,16,768]{3,2,1,0:T(8,128)(2,1)S(1)} %get-tuple-element.20), channel_id=1, source_target_pairs={{0,96},{16,112},{32,64},{48,80},{64,32},{80,48},{96,0},{112,16},{1... | collective-permute-start | bytes 589832 | tf_op jit(solution)/shard_map/ppermute | solution.py:23
  (35 other events, 258.1 us)

commit v3 on v2

--- a/solution.py
+++ b/solution.py
@@ -36,62 +36,75 @@
     return lax.ppermute(value, ("head", "exp"), pairs)
 
 
-def readout_kernel(decay_ref, qkv_ref, state_ref, gain_ref, out_ref):
-    head = pl.program_id(0)
+def bf16_parts(value, count):
+    parts = []
+    for _ in range(count - 1):
+        parts.append(value.astype(BF16))
+        value = value - parts[-1].astype(F32)
+    return parts + [value.astype(BF16)]
+
+
+def readout_kernel(decay_ref, qkv_ref, state_ref, gain_ref, first_out_ref, last_out_ref):
     n, size = STEPS * ROWS, state_ref.shape[2]
-    q, k, v = [qkv_ref[:, i].astype(F32).reshape(n, size).astype(BF16) for i in range(3)]
+    heads = state_ref.shape[1]
     row = lax.broadcasted_iota(jnp.int32, (n, size), 0)
     row_in = row % ROWS
-    q_twice = jnp.concatenate([q, q], axis=1)
-    carried = jnp.zeros((n, size), F32)
-    for pair in range(ROWS // 2):
-        wide = jnp.concatenate([state_ref[2 * pair, 0], state_ref[2 * pair + 1, 0]], axis=1)
-        high = wide.astype(BF16)
-        low = (wide - high.astype(F32)).astype(BF16)
-        both = jnp.dot(
-            q_twice, jnp.concatenate([high, low], axis=0), preferred_element_type=F32
-        )
-        carried = jnp.where(row_in == 2 * pair, both[:, :size], carried)
-        carried = jnp.where(row_in == 2 * pair + 1, both[:, size:], carried)
-    decay = [decay_ref[t, head] for t in range(STEPS)]
-    run = decay[0]
-    first = jnp.full((n, size), run, F32)
-    for t in range(1, STEPS):
-        run = run * decay[t]
-        first = jnp.where(row // ROWS == t, run, first)
     row_t = lax.broadcasted_iota(jnp.int32, (n, n), 0)
     row_s = lax.broadcasted_iota(jnp.int32, (n, n), 1)
-    mix = jnp.zeros((n, n), F32)
-    for t in range(STEPS):
-        run = None
-        for s in range(t, -1, -1):
-            here = row_t - row_s == (t - s) * ROWS
-            mix = jnp.where(here & (row_s // ROWS == s), 1.0 if run is None else run, mix)
-            run = decay[s] if run is None else run * decay[s]
-    scores = lax.dot_general(q, k, (((1,), (1,)), ((), ())), preferred_element_type=F32)
-    o = carried * first + jnp.dot(
-        scores * mix,
-        v.astype(F32),
-        precision=lax.Precision.HIGHEST,
-        preferred_element_type=F32,
-    )
-    o = o * lax.rsqrt(jnp.mean(o * o, axis=-1, keepdims=True) + EPS) * gain_ref[...]
-    out_ref[...] = o.astype(BF16)
+    for h in range(heads):
+        lanes = slice(h * size, (h + 1) * size)
+        q, k, v = [
+            qkv_ref[:, i, :, lanes].astype(F32).reshape(n, size).astype(BF16) for i in range(3)
+        ]
+        q_twice = jnp.concatenate([q, q], axis=1)
+        carried = jnp.zeros((n, size), F32)
+        for pair in range(ROWS // 2):
+            wide = jnp.concatenate([state_ref[2 * pair, h], state_ref[2 * pair + 1, h]], axis=1)
+            both = jnp.dot(
+                q_twice, jnp.concatenate(bf16_parts(wide, 2), axis=0), preferred_element_type=F32
+            )
+            carried = jnp.where(row_in == 2 * pair, both[:, :size], carried)
+            carried = jnp.where(row_in == 2 * pair + 1, both[:, size:], carried)
+        decay = [decay_ref[t, pl.program_id(0) * heads + h] for t in range(STEPS)]
+        run = decay[0]
+        first = jnp.full((n, size), run, F32)
+        for t in range(1, STEPS):
+            run = run * decay[t]
+            first = jnp.where(row // ROWS == t, run, first)
+        mix = jnp.zeros((n, n), F32)
+        for t in range(STEPS):
+            run = None
+            for s in range(t, -1, -1):
+                here = row_t - row_s == (t - s) * ROWS
+                mix = jnp.where(here & (row_s // ROWS == s), 1.0 if run is None else run, mix)
+                run = decay[s] if run is None else run * decay[s]
+        scores = lax.dot_general(q, k, (((1,), (1,)), ((), ())), preferred_element_type=F32)
+        o = carried * first + jnp.dot(
+            jnp.concatenate(bf16_parts(scores * mix, 2), axis=1),
+            jnp.concatenate([v, v], axis=0),
+            preferred_element_type=F32,
+        )
+        o = o * lax.rsqrt(jnp.mean(o * o, axis=-1, keepdims=True) + EPS) * gain_ref[:, lanes]
+        o = o.astype(BF16)
+        first_out_ref[:, lanes] = o[: n // 2]
+        last_out_ref[:, lanes] = o[n // 2 :]
 
 
 def readouts(step_qkv, decay, state, attn_gain):
     heads, size = state.shape[1], state.shape[2]
+    at_once = min(heads, 4)
+    half = STEPS * ROWS // 2
     return pl.pallas_call(
         readout_kernel,
-        out_shape=jax.ShapeDtypeStruct((STEPS * ROWS, heads * size), BF16),
-        grid=(heads,),
+        out_shape=[jax.ShapeDtypeStruct((half, heads * size), BF16)] * 2,
+        grid=(heads // at_once,),
         in_specs=[
             pl.BlockSpec(memory_space=pltpu.SMEM),
-            pl.BlockSpec((STEPS, 3, ROWS, size), lambda i: (0, 0, 0, i)),
-            pl.BlockSpec((ROWS, 1, size, size), lambda i: (0, i, 0, 0)),
-            pl.BlockSpec((1, size), lambda i: (0, i)),
+            pl.BlockSpec((STEPS, 3, ROWS, at_once * size), lambda i: (0, 0, 0, i)),
+            pl.BlockSpec((ROWS, at_once, size, size), lambda i: (0, i, 0, 0)),
+            pl.BlockSpec((1, at_once * size), lambda i: (0, i)),
         ],
-        out_specs=pl.BlockSpec((STEPS * ROWS, size), lambda i: (0, i)),
+        out_specs=[pl.BlockSpec((half, at_once * size), lambda i: (0, i))] * 2,
         compiler_params=vmem_params(56),
         cost_estimate=pl.CostEstimate(
             flops=2 * STEPS * ROWS * ROWS * heads * size * size * 2,
@@ -189,80 +202,93 @@
     )(place, gain.reshape(1, -1), *got)
 
 
-def gate_up_kernel(*refs):
-    x_refs, (gate_ref, up_ref, out_ref, gate_acc, up_acc) = refs[:8], refs[8:]
-    step = pl.program_id(0)
+def fetch_kernel(after_ref, *refs):
+    sems = refs[-1]
+    copies = [
+        pltpu.make_async_copy(refs[i], refs[3 + i], sems.at[i]) for i in range(3)
+    ]
+    for copy in copies:
+        copy.start()
+    for copy in copies:
+        copy.wait()
+
+
+def fetch(after, *weights):
+    return pl.pallas_call(
+        fetch_kernel,
+        out_shape=[pltpu.VMEM(w.shape, w.dtype) for w in weights],
+        in_specs=[pl.BlockSpec(memory_space=pl.ANY)] + [pl.BlockSpec(memory_space=pltpu.HBM)] * 3,
+        out_specs=[pl.BlockSpec(memory_space=pltpu.VMEM)] * 3,
+        scratch_shapes=[pltpu.SemaphoreType.DMA((3,))],
+        compiler_params=vmem_params(30),
+        cost_estimate=pl.CostEstimate(
+            flops=0, bytes_accessed=sum(2 * w.size for w in weights), transcendentals=0
+        ),
+        name="fetch",
+    )(after, *weights)
+
+
+def hidden_kernel(place_ref, *refs):
+    x_refs, (gate_ref, up_ref, down_ref, hidden_ref, theirs_ref) = refs[:8], refs[8:]
+    share = theirs_ref.shape[2]
+    y, c = place_ref[2], place_ref[3]
     x = jnp.concatenate([r[...] for r in x_refs], axis=0)
     across = (((1,), (1,)), ((), ()))
-    gate = lax.dot_general(x, gate_ref[0], across, preferred_element_type=F32)
-    up = lax.dot_general(x, up_ref[0], across, preferred_element_type=F32)
-
-    @pl.when(step == 0)
-    def _():
-        gate_acc[...] = gate
-        up_acc[...] = up
-
-    @pl.when(step > 0)
-    def _():
-        gate_acc[...] += gate
-        up_acc[...] += up
-
-    @pl.when(step == pl.num_programs(0) - 1)
-    def _():
-        g = gate_acc[...]
-        out_ref[...] = (g / (1.0 + jnp.exp(-g)) * up_acc[...]).astype(BF16)
-
-
-def gate_up(pieces, w_gate, w_up):
-    slots, width = pieces[0].shape
-    hidden = w_gate.shape[2]
-    chunk = width // 8
-    rows = slots * len(pieces)
-    return pl.pallas_call(
-        gate_up_kernel,
-        out_shape=jax.ShapeDtypeStruct((rows, hidden), BF16),
-        grid=(width // chunk,),
-        in_specs=[pl.BlockSpec((slots, chunk), lambda i: (0, i))] * len(pieces)
-        + [pl.BlockSpec((1, hidden, chunk), lambda i: (0, 0, i))] * 2,
-        out_specs=pl.BlockSpec((rows, hidden), lambda i: (0, 0)),
-        scratch_shapes=[pltpu.VMEM((rows, hidden), F32)] * 2,
-        compiler_params=vmem_params(56),
+    gate = lax.dot_general(gate_ref[...], x, across, preferred_element_type=F32)
+    up = lax.dot_general(up_ref[...], x, across, preferred_element_type=F32)
+    hidden = (gate / (1.0 + jnp.exp(-gate)) * up).T.astype(BF16)
+    hidden_ref[...] = hidden
+    for k in range(4):
+        block = lax.bitwise_xor(y, k) * 2 + (1 - c)
+        at = pl.ds(pl.multiple_of(block * share, 128), share)
+        theirs_ref[k] = jnp.dot(hidden, down_ref[:, at], preferred_element_type=F32).astype(BF16)
+
+
+def hidden_units(place, pieces, gate, up, down, share):
+    units = gate.shape[0]
+    rows = sum(p.shape[0] for p in pieces)
+    return pl.pallas_call(
+        hidden_kernel,
+        out_shape=(
+            jax.ShapeDtypeStruct((rows, units), BF16),
+            jax.ShapeDtypeStruct((4, rows, share), BF16),
+        ),
+        in_specs=[pl.BlockSpec(memory_space=pltpu.SMEM)]
+        + [pl.BlockSpec(memory_space=pltpu.VMEM)] * (len(pieces) + 3),
+        out_specs=[pl.BlockSpec(memory_space=pltpu.VMEM)] * 2,
+        compiler_params=vmem_params(30),
         cost_estimate=pl.CostEstimate(
-            flops=4 * rows * width * hidden,
-            bytes_accessed=4 * width * hidden,
-            transcendentals=rows * hidden,
-        ),
-        name="gate_up",
-    )(*pieces, w_gate.transpose(0, 2, 1), w_up.transpose(0, 2, 1))
-
-
-def down_kernel(place_ref, x_ref, w_ref, out_ref):
-    out_ref[0] = jnp.dot(x_ref[...], w_ref[0], preferred_element_type=F32).astype(BF16)
-
-
-def down(place, x, w_down, share):
-    rows, hidden = x.shape
-    parts = place.shape[0]
+            flops=5 * rows * gate.size, bytes_accessed=1 << 20, transcendentals=rows * units
+        ),
+        name="hidden_units",
+    )(place, *pieces, gate, up, down)
+
+
+def down_kernel(place_ref, hidden_ref, down_ref, theirs_ref, out_ref):
+    share = out_ref.shape[2]
+    y, c = place_ref[2], place_ref[3]
+    half = hidden_ref.shape[0] // 2
+    for k in range(4):
+        block = lax.bitwise_xor(y, k) * 2 + c
+        at = pl.ds(pl.multiple_of(block * share, 128), share)
+        ours = jnp.dot(hidden_ref[...], down_ref[:, at], preferred_element_type=F32)
+        out_ref[k, :half] = (ours[:half] + theirs_ref[k, half:].astype(F32)).astype(BF16)
+        out_ref[k, half:] = (ours[half:] + theirs_ref[k, :half].astype(F32)).astype(BF16)
+
+
+def down(place, hidden, weight, theirs):
     return pl.pallas_call(
         down_kernel,
-        out_shape=jax.ShapeDtypeStruct((parts, rows, share), BF16),
-        grid_spec=pltpu.PrefetchScalarGridSpec(
-            num_scalar_prefetch=1,
-            grid=(parts,),
-            in_specs=[
-                pl.BlockSpec((rows, hidden), lambda i, p: (0, 0)),
-                pl.BlockSpec((1, hidden, share), lambda i, p: (0, 0, p[i])),
-            ],
-            out_specs=pl.BlockSpec((1, rows, share), lambda i, p: (i, 0, 0)),
-        ),
-        compiler_params=vmem_params(56),
+        out_shape=jax.ShapeDtypeStruct(theirs.shape, BF16),
+        in_specs=[pl.BlockSpec(memory_space=pltpu.SMEM)]
+        + [pl.BlockSpec(memory_space=pltpu.VMEM)] * 3,
+        out_specs=pl.BlockSpec(memory_space=pltpu.VMEM),
+        compiler_params=vmem_params(30),
         cost_estimate=pl.CostEstimate(
-            flops=2 * rows * hidden * share * parts,
-            bytes_accessed=2 * hidden * share * parts,
-            transcendentals=0,
+            flops=hidden.shape[0] * weight.size, bytes_accessed=1 << 20, transcendentals=0
         ),
         name="down",
-    )(place, x, w_down)
+    )(place, hidden, weight, theirs)
 
 
 def final_sum_kernel(place_ref, own_ref, got1_ref, got2_ref, got3_ref, out_ref):
@@ -323,9 +349,11 @@
         mix += jnp.where(slot == target, weights[:, j : j + 1], 0.0)
     back = jnp.concatenate(
         [ref[kz].astype(F32) for ref in back_refs for kz in range(4)], axis=0
-    )
+    ).astype(BF16)
     out_ref[...] = jnp.dot(
-        mix, back, precision=lax.Precision.HIGHEST, preferred_element_type=F32
+        jnp.concatenate(bf16_parts(mix, 3), axis=1),
+        jnp.concatenate([back] * 3, axis=0),
+        preferred_element_type=F32,
     ).astype(BF16)
 
 
@@ -367,13 +395,12 @@
     y, c, z, x = head // 2, head % 2, exp // 4, exp % 4
     place = jnp.stack([x, z, y, c]).astype(jnp.int32)
 
-    readout = readouts(step_qkv, decay_rates, kv_state, attn_gain)
-    half_a, half_b = readout[: 2 * ROWS], readout[2 * ROWS :]
+    half_a, half_b = readouts(step_qkv, decay_rates, kv_state, attn_gain)
     by_z = jnp.stack([half_a] + [over_exp(half_a, 4 * k) for k in (1, 2, 3)], 0)
     by_x = jnp.stack([half_b] + [over_exp(half_b, k) for k in (1, 2, 3)], 0)
     all_a = [by_z] + [over_exp(by_z, k) for k in (1, 2, 3)]
     all_b = [by_x] + [over_exp(by_x, 4 * k) for k in (1, 2, 3)]
-    depth = readout.shape[1]
+    depth = half_a.shape[1]
 
     pair_rows = lax.dynamic_slice(hidden_in, (2 * c, 0, y * 4 * cols), (2, ROWS, 4 * cols))
     pair_rows = pair_rows.reshape(2 * ROWS, 4 * cols)
@@ -393,6 +420,7 @@
         out = jnp.dot(rows, out_proj, preferred_element_type=F32).astype(BF16)
         return out.reshape(4, 4, 2 * ROWS, cols)
 
+    hidden_rows, all_b = lax.optimization_barrier((hidden_rows, all_b))
     part_a = project(all_a)
     part_b = project(all_b).transpose(1, 0, 2, 3)
     mine = jnp.where(c == 0, part_a, part_b)
@@ -411,8 +439,17 @@
     normed = norm(place, ffn_gain, by_kx)
     by_y = [normed] + [over_head(normed, 2 * k) for k in (1, 2, 3)]
 
-    attended, by_y[1] = lax.optimization_barrier((attended, by_y[1]))
     by_core = [over_head(piece, 1) for piece in by_y]
+
+    gate, up, down_weight = fetch(
+        by_y[1], w_gate[0].swapaxes(0, 1), w_up[0].swapaxes(0, 1), w_down[0]
+    )
+    hidden, theirs = hidden_units(place, by_y + by_core, gate, up, down_weight, share)
+    both = down(place, hidden, down_weight, over_head(theirs, 1))
+    both = both.reshape(4, 2, 4, 16, share)
+    got = [over_head(both[k], 2 * k) for k in (1, 2, 3)]
+
+    attended, got[0] = lax.optimization_barrier((attended, got[0]))
     pieces = []
     for k in range(4):
         source = (2 * c + x % 2) ^ k
@@ -420,21 +457,13 @@
         pieces.append(
             over_all(block, lambda y, c, z, x, k=k: (z, x // 2, y, (2 * c + x % 2) ^ k))
         )
+    pieces, got[1] = lax.optimization_barrier((pieces, got[1]))
     pieces = jnp.stack(pieces, 0)
     ordered = [lax.dynamic_index_in_dim(pieces, j ^ x, 0, keepdims=False) for j in range(4)]
     attended_out = jnp.concatenate(
         [jnp.concatenate(ordered[:2], axis=1), jnp.concatenate(ordered[2:], axis=1)], axis=0
     ).reshape(STEPS, ROWS, share)
 
-    hidden = gate_up(by_y + by_core, w_gate, w_up)
-    ky = jnp.arange(4)
-    theirs = down((y ^ ky) * 2 + (1 - c), hidden, w_down, share)
-    theirs = over_head(theirs, 1)
-    ours = down((y ^ ky) * 2 + c, hidden, w_down, share)
-    theirs = theirs.reshape(4, 2, 4, 16, share)
-    ours = ours.reshape(4, 2, 4, 16, share)
-    both = (ours.astype(F32) + theirs[:, ::-1].astype(F32)).astype(BF16)
-    got = [over_head(both[k], 2 * k) for k in (1, 2, 3)]
     results = final_sum(place, both, got)
     by_kz = [results[0]] + [over_exp(results[k], 4 * k) for k in (1, 2, 3)]
     by_kx = [jnp.stack([by_kz[kz][kx] for kz in range(4)], 0) for kx in range(4)]

time: 169 us -> 153 us (0.905)
  Pallas kernels: 33.1 us -> 21.3 us
  waiting for transfers between devices: 42.4 us -> 37.4 us
  starting transfers between devices: 84.6 us -> 86.5 us
    pallas_call x4, Pallas kernels: 29.2 us -> 17.5 us  [the longest x1 7.06 us: fetch(): pl.pallas_call(fetch_kernel, out_shape=[pltpu.VMEM(w.shape, w.dtype) for...]
    ppermute x24, starting transfers between devices: 38.1 us -> 48 us  [over_exp(): return lax.ppermute(value, 'exp', [(i, i ^ bits) for i in range(16)])]
    ppermute x15, starting transfers between devices: 34.3 us -> 25.5 us  [over_head(): return lax.ppermute(value, 'head', [(i, i ^ bits) for i in range(8)])]
    ppermute x15, waiting for transfers between devices: 21.5 us -> 16.7 us  [over_head(): return lax.ppermute(value, 'head', [(i, i ^ bits) for i in range(8)])]
    ppermute x24, waiting for transfers between devices: 18.5 us -> 15.2 us  [over_exp(): return lax.ppermute(value, 'exp', [(i, i ^ bits) for i in range(16)])]
    ppermute x8, waiting for transfers between devices: 2.3 us -> 5.52 us  [over_all(): return lax.ppermute(value, ('head', 'exp'), pairs)]
  transfers between devices with their start and end apart: 47 -> 47, of which waited for: 22 -> 22; matrix products, arithmetic and copies ran while one was open for 2% -> 3% of each run, Pallas kernels for 3% -> 5%
where the time goes in v3:
time: 153 us; the launch traced here: 152 us
  starting transfers between devices  86.5 us (57%)
  waiting for transfers between devices  37.4 us (24%)
  Pallas kernels  21.3 us (14%)
  other arithmetic  3.16 us (2%)
    ppermute x24, starting transfers between devices, over_exp(): return lax.ppermute(value, 'exp', [(i, i ^ bits) for i in range(16)])  48 us
    ppermute x15, starting transfers between devices, over_head(): return lax.ppermute(value, 'head', [(i, i ^ bits) for i in range(8)])  25.5 us
    ppermute x15, waiting for transfers between devices, over_head(): return lax.ppermute(value, 'head', [(i, i ^ bits) for i in range(8)])  16.7 us
    ppermute x24, waiting for transfers between devices, over_exp(): return lax.ppermute(value, 'exp', [(i, i ^ bits) for i in range(16)])  15.2 us
    ppermute x8, starting transfers between devices, over_all(): return lax.ppermute(value, ('head', 'exp'), pairs)  12.9 us
    pallas_call x1, Pallas kernels, fetch(): pl.pallas_call(fetch_kernel, out_shape=[pltpu.VMEM(w.shape, w.dtype) for...  7.06 us
    ppermute x8, waiting for transfers between devices, over_all(): return lax.ppermute(value, ('head', 'exp'), pairs)  5.52 us
    pallas_call x1, Pallas kernels, hidden_units(): pl.pallas_call(hidden_kernel, out_shape=(jax.ShapeDtypeStruct((rows, unit...  5.14 us
  transfers between devices with their start and end apart: 47, of which 22 were waited for; matrix products, arithmetic and copies ran while one was open for 3% of the time, Pallas kernels for 5%

profile of v3, /device:TPU:0, one launch (start us, length us, event | category | flops | bytes accessed | tf_op | source)
XLA Modules:
  0.0 151.6 jit_solution(14965155302519311248)
XLA Ops:
  0.7 3.9 %readout.1 = (bf16[16,1024]{1,0:T(8,128)(2,1)}, bf16[16,1024]{1,0:T(8,128)(2,1)}) custom-call(f32[4,8]{1,0:T(4,128)} %decay_ref.1, bf16[4,3,8,1024]{3,2,1,0:T(8,128)(2,1)} %bitcast.113, f32[8,8,128,128]{3,2,1,0:T(8,128)} %state_ref.1, f32[1,1024]{1,0:T(1,128)} %bitcast.135), custom_call_target="tpu_custom_call" | custom-call | flops 134217728 | bytes 4194304 | tf_op jit(solution)/shard_map/readout/pallas_call | solution.py:97
  4.5 2.8 %collective-permute-start.8 = (bf16[16,1024]{1,0:T(8,128)(2,1)}, bf16[16,1024]{1,0:T(8,128)(2,1)S(1)}, u32[]{:S(2)}, u32[]{:S(2)}) collective-permute-start(bf16[16,1024]{1,0:T(8,128)(2,1)} %get-tuple-element.32), channel_id=1, source_target_pairs={{0,3},{1,2},{2,1},{3,0},{4,7},{5,6},{6,5},{7,4},{8,11},{9,10},{10,... | collective-permute-start | bytes 98312 | tf_op jit(solution)/shard_map/ppermute | solution.py:27
  8.6 4.1 %collective-permute-start.2 = (bf16[16,1024]{1,0:T(8,128)(2,1)}, bf16[16,1024]{1,0:T(8,128)(2,1)S(1)}, u32[]{:S(2)}, u32[]{:S(2)}) collective-permute-start(bf16[16,1024]{1,0:T(8,128)(2,1)} %get-tuple-element.31), channel_id=1, source_target_pairs={{0,12},{1,13},{2,14},{3,15},{4,8},{5,9},{6,10},{7,11},{8,4},{9,5},... | collective-permute-start | bytes 98312 | tf_op jit(solution)/shard_map/ppermute | solution.py:27
  16.5 3.5 %collective-permute-start.14 = (bf16[4,16,1024]{2,1,0:T(8,128)(2,1)S(1)}, bf16[4,16,1024]{2,1,0:T(8,128)(2,1)S(1)}, u32[]{:S(2)}, u32[]{:S(2)}) collective-permute-start(bf16[4,16,1024]{2,1,0:T(8,128)(2,1)S(1)} %pad_maximum_fusion.1), channel_id=1, source_target_pairs={{0,8},{1,9},{2,10},{3,11},{4,12},{5,13},{6,14},{7,15},{8,0},{9,1},... | collective-permute-start | bytes 393224 | tf_op jit(solution)/shard_map/ppermute | solution.py:27
  20.9 2.8 %collective-permute-start.5 = (bf16[4,16,1024]{2,1,0:T(8,128)(2,1)S(1)}, bf16[4,16,1024]{2,1,0:T(8,128)(2,1)S(1)}, u32[]{:S(2)}, u32[]{:S(2)}) collective-permute-start(bf16[4,16,1024]{2,1,0:T(8,128)(2,1)S(1)} %pad_maximum_fusion), channel_id=1, source_target_pairs={{0,3},{1,2},{2,1},{3,0},{4,7},{5,6},{6,5},{7,4},{8,11},{9,10},{10,... | collective-permute-start | bytes 393224 | tf_op jit(solution)/shard_map/ppermute | solution.py:27
  30.4 2.4 %collective-permute-start.12 = (bf16[16,512]{1,0:T(8,128)(2,1)S(1)}, bf16[16,512]{1,0:T(8,128)(2,1)S(1)}, u32[]{:S(2)}, u32[]{:S(2)}) collective-permute-start(bf16[16,512]{1,0:T(8,128)(2,1)S(1)} %get-tuple-element.35), channel_id=1, source_target_pairs={{0,2},{1,3},{2,0},{3,1},{4,34},{5,35},{6,32},{7,33},{8,66},{9,67},... | collective-permute-start | bytes 49160 | tf_op jit(solution)/shard_map/ppermute | solution.py:36
  35.6 2.1 %collective-permute-done.13.refs_3_ = bf16[16,512]{1,0:T(8,128)(2,1)S(1)} collective-permute-done((bf16[16,512]{1,0:T(8,128)(2,1)S(1)}, bf16[16,512]{1,0:T(8,128)(2,1)S(1)}, u32[]{:S(2)}, u32[]{:S(2)}) %collective-permute-start.13) | collective-permute-done | bytes 16416 | tf_op jit(solution)/shard_map/ppermute | solution.py:36
  39.8 6.1 %collective-permute-start.17 = (bf16[4,16,384]{2,1,0:T(8,128)(2,1)S(1)}, bf16[4,16,384]{2,1,0:T(8,128)(2,1)S(1)}, u32[]{:S(2)}, u32[]{:S(2)}) collective-permute-start(bf16[4,16,384]{2,1,0:T(8,128)(2,1)S(1)} %get-tuple-element.79), channel_id=1, source_target_pairs={{0,32},{16,48},{32,0},{48,16},{64,96},{80,112},{96,64},{112,80},{1... | collective-permute-start | bytes 147464 | tf_op jit(solution)/shard_map/ppermute | solution.py:23
  46.0 9.2 %collective-permute-start.18 = (bf16[4,16,384]{2,1,0:T(8,128)(2,1)S(1)}, bf16[4,16,384]{2,1,0:T(8,128)(2,1)S(1)}, u32[]{:S(2)}, u32[]{:S(2)}) collective-permute-start(bf16[4,16,384]{2,1,0:T(8,128)(2,1)S(1)} %get-tuple-element.78), channel_id=1, source_target_pairs={{0,64},{16,80},{32,96},{48,112},{64,0},{80,16},{96,32},{112,48},{1... | collective-permute-start | bytes 147464 | tf_op jit(solution)/shard_map/ppermute | solution.py:23
  55.2 2.7 %collective-permute-done.18.got2_ref = bf16[4,16,384]{2,1,0:T(8,128)(2,1)S(1)} collective-permute-done((bf16[4,16,384]{2,1,0:T(8,128)(2,1)S(1)}, bf16[4,16,384]{2,1,0:T(8,128)(2,1)S(1)}, u32[]{:S(2)}, u32[]{:S(2)}) %collective-permute-start.18) | collective-permute-done | bytes 49184 | tf_op jit(solution)/shard_map/ppermute | solution.py:23
  57.9 2.5 %collective-permute-done.19.got3_ref = bf16[4,16,384]{2,1,0:T(8,128)(2,1)S(1)} collective-permute-done((bf16[4,16,384]{2,1,0:T(8,128)(2,1)S(1)}, bf16[4,16,384]{2,1,0:T(8,128)(2,1)S(1)}, u32[]{:S(2)}, u32[]{:S(2)}) %collective-permute-start.19) | collective-permute-done | bytes 49184 | tf_op jit(solution)/shard_map/ppermute | solution.py:23
  63.3 3.2 %collective-permute-start.21 = (bf16[4,16,384]{2,1,0:T(8,128)(2,1)S(1)}, bf16[4,16,384]{2,1,0:T(8,128)(2,1)S(1)}, u32[]{:S(2)}, u32[]{:S(2)}) collective-permute-start(bf16[4,16,384]{2,1,0:T(8,128)(2,1)S(1)} %get-tuple-element.76), channel_id=1, source_target_pairs={{0,8},{1,9},{2,10},{3,11},{4,12},{5,13},{6,14},{7,15},{8,0},{9,1},... | collective-permute-start | bytes 147464 | tf_op jit(solution)/shard_map/ppermute | solution.py:27
  72.7 2.8 %collective-permute-start.25 = (bf16[4,16,384]{2,1,0:T(8,128)(2,1)S(1)}, bf16[4,16,384]{2,1,0:T(8,128)(2,1)S(1)}, u32[]{:S(2)}, u32[]{:S(2)}) collective-permute-start(bf16[4,16,384]{2,1,0:T(8,128)(2,1)S(1)} %pad_maximum_fusion.5), channel_id=1, source_target_pairs={{0,3},{1,2},{2,1},{3,0},{4,7},{5,6},{6,5},{7,4},{8,11},{9,10},{10,... | collective-permute-start | bytes 147464 | tf_op jit(solution)/shard_map/ppermute | solution.py:27
  78.9 2.0 %collective-permute-start.27 = (bf16[16,6144]{1,0:T(8,128)(2,1)S(1)}, bf16[16,6144]{1,0:T(8,128)(2,1)S(1)}, u32[]{:S(2)}, u32[]{:S(2)}) collective-permute-start(bf16[16,6144]{1,0:T(8,128)(2,1)S(1)} %norm.1.refs_0_), channel_id=1, source_target_pairs={{0,64},{16,80},{32,96},{48,112},{64,0},{80,16},{96,32},{112,48},{1... | collective-permute-start | bytes 589832 | tf_op jit(solution)/shard_map/ppermute | solution.py:23
  80.9 2.7 %collective-permute-start.28 = (bf16[16,6144]{1,0:T(8,128)(2,1)S(1)}, bf16[16,6144]{1,0:T(8,128)(2,1)S(1)}, u32[]{:S(2)}, u32[]{:S(2)}) collective-permute-start(bf16[16,6144]{1,0:T(8,128)(2,1)S(1)} %norm.1.refs_0_), channel_id=1, source_target_pairs={{0,96},{16,112},{32,64},{48,80},{64,32},{80,48},{96,0},{112,16},{1... | collective-permute-start | bytes 589832 | tf_op jit(solution)/shard_map/ppermute | solution.py:23
  84.6 2.2 %collective-permute-done.27.refs_2_ = bf16[16,6144]{1,0:T(8,128)(2,1)S(1)} collective-permute-done((bf16[16,6144]{1,0:T(8,128)(2,1)S(1)}, bf16[16,6144]{1,0:T(8,128)(2,1)S(1)}, u32[]{:S(2)}, u32[]{:S(2)}) %collective-permute-start.27) | collective-permute-done | bytes 196640 | tf_op jit(solution)/shard_map/ppermute | solution.py:23
  88.8 7.1 %fetch.1 = (bf16[576,6144]{1,0:T(8,128)(2,1)S(1)}, bf16[576,6144]{1,0:T(8,128)(2,1)S(1)}, bf16[576,6144]{1,0:T(8,128)(2,1)S(1)}) custom-call(bf16[16,6144]{1,0:T(8,128)(2,1)S(1)} %collective-permute-done.26.after_ref.refs_1_, bf16[576,6144]{1,0:T(8,128)(2,1)} %bitcast.106, bf16[576,6144]{1,0:T(8,128)(2,1)} %bitcast.107, bf16[576,6144]{1,0:T(8,128)(2,1)} %bitcast.108), custom_call_target="tpu_custom_call" | custom-call | bytes 21233664 | tf_op jit(solution)/shard_map/fetch/pallas_call | solution.py:217
  95.9 5.1 %hidden_units.1 = (bf16[128,576]{1,0:T(8,128)(2,1)S(1)}, bf16[4,128,768]{2,1,0:T(8,128)(2,1)S(1)}) custom-call(s32[4]{0:T(128)S(1)} %pad_add_fusion.place_ref, bf16[16,6144]{1,0:T(8,128)(2,1)S(1)} %norm.1.refs_0_, bf16[16,6144]{1,0:T(8,128)(2,1)S(1)} %collective-permute-done.26.after_ref.refs_1_, bf16[16,6144]{1,0:T(8,128)(2,1)S(1)} %collective-permute-done.27.refs_2_, ...), custom_call_target="tpu_custom_call" | custom-call | flops 2264924160 | bytes 1048576 | tf_op jit(solution)/shard_map/hidden_units/pallas_call | solution.py:250
  105.1 4.1 %collective-permute-start.39 = (bf16[2,4,16,768]{3,2,1,0:T(8,128)(2,1)S(1)}, bf16[2,4,16,768]{3,2,1,0:T(8,128)(2,1)S(1)}, u32[]{:S(2)}, u32[]{:S(2)}) collective-permute-start(bf16[2,4,16,768]{3,2,1,0:T(8,128)(2,1)S(1)} %bitcast.115), channel_id=1, source_target_pairs={{0,64},{16,80},{32,96},{48,112},{64,0},{80,16},{96,32},{112,48},{1... | collective-permute-start | bytes 589832 | tf_op jit(solution)/shard_map/ppermute | solution.py:23
  109.8 3.0 %collective-permute-done.34.got1_ref = bf16[2,4,16,768]{3,2,1,0:T(8,128)(2,1)S(1)} collective-permute-done((bf16[2,4,16,768]{3,2,1,0:T(8,128)(2,1)S(1)}, bf16[2,4,16,768]{3,2,1,0:T(8,128)(2,1)S(1)}, u32[]{:S(2)}, u32[]{:S(2)}) %collective-permute-start.34) | collective-permute-done | bytes 196640 | tf_op jit(solution)/shard_map/ppermute | solution.py:23
  113.8 6.4 %collective-permute-start.37 = (bf16[16,384]{1,0:T(8,128)(2,1)S(1)}, bf16[16,384]{1,0:T(8,128)(2,1)S(1)}, u32[]{:S(2)}, u32[]{:S(2)}) collective-permute-start(bf16[16,384]{1,0:T(8,128)(2,1)S(1)} %get-tuple-element.98), channel_id=1, source_target_pairs={{0,2},{1,3},{2,18},{3,19},{4,34},{5,35},{6,50},{7,51},{8,66},{9,67... | collective-permute-start | bytes 36872 | tf_op jit(solution)/shard_map/ppermute | solution.py:36
  124.0 13.3 %collective-permute-start.43 = (bf16[4,8,768]{2,1,0:T(8,128)(2,1)S(1)}, bf16[4,8,768]{2,1,0:T(8,128)(2,1)S(1)}, u32[]{:S(2)}, u32[]{:S(2)}) collective-permute-start(bf16[4,8,768]{2,1,0:T(8,128)(2,1)S(1)} %get-tuple-element.68), channel_id=1, source_target_pairs={{0,12},{1,13},{2,14},{3,15},{4,8},{5,9},{6,10},{7,11},{8,4},{9,5},... | collective-permute-start | bytes 147464 | tf_op jit(solution)/shard_map/ppermute | solution.py:27
  139.4 3.5 %collective-permute-done.42 = bf16[4,8,768]{2,1,0:T(8,128)(2,1)S(1)} collective-permute-done((bf16[4,8,768]{2,1,0:T(8,128)(2,1)S(1)}, bf16[4,8,768]{2,1,0:T(8,128)(2,1)S(1)}, u32[]{:S(2)}, u32[]{:S(2)}) %collective-permute-start.42) | collective-permute-done | bytes 49184 | tf_op jit(solution)/shard_map/ppermute | solution.py:27
  143.7 4.2 %collective-permute-start.46 = (bf16[4,8,768]{2,1,0:T(8,128)(2,1)S(1)}, bf16[4,8,768]{2,1,0:T(8,128)(2,1)S(1)}, u32[]{:S(2)}, u32[]{:S(2)}) collective-permute-start(bf16[4,8,768]{2,1,0:T(8,128)(2,1)S(1)} %pad_maximum_fusion.10), channel_id=1, source_target_pairs={{0,3},{1,2},{2,1},{3,0},{4,7},{5,6},{6,5},{7,4},{8,11},{9,10},{10,... | collective-permute-start | bytes 147464 | tf_op jit(solution)/shard_map/ppermute | solution.py:27
  (127 shorter events, 48.6 us)
Async XLA Ops:
  4.5 9.0 %collective-permute-start.8 = (bf16[16,1024]{1,0:T(8,128)(2,1)}, bf16[16,1024]{1,0:T(8,128)(2,1)S(1)}, u32[]{:S(2)}, u32[]{:S(2)}) collective-permute-start(bf16[16,1024]{1,0:T(8,128)(2,1)} %get-tuple-element.32), channel_id=1, source_target_pairs={{0,3},{1,2},{2,1},{3,0},{4,7},{5,6},{6,5},{7,4},{8,11},{9,10},{10,... | collective-permute-start | bytes 98312 | tf_op jit(solution)/shard_map/ppermute | solution.py:27
  7.4 7.1 %collective-permute-start.7 = (bf16[16,1024]{1,0:T(8,128)(2,1)}, bf16[16,1024]{1,0:T(8,128)(2,1)S(1)}, u32[]{:S(2)}, u32[]{:S(2)}) collective-permute-start(bf16[16,1024]{1,0:T(8,128)(2,1)} %get-tuple-element.32), channel_id=1, source_target_pairs={{0,2},{1,3},{2,0},{3,1},{4,6},{5,7},{6,4},{7,5},{8,10},{9,11},{10,... | collective-permute-start | bytes 98312 | tf_op jit(solution)/shard_map/ppermute | solution.py:27
  8.6 11.4 %collective-permute-start.2 = (bf16[16,1024]{1,0:T(8,128)(2,1)}, bf16[16,1024]{1,0:T(8,128)(2,1)S(1)}, u32[]{:S(2)}, u32[]{:S(2)}) collective-permute-start(bf16[16,1024]{1,0:T(8,128)(2,1)} %get-tuple-element.31), channel_id=1, source_target_pairs={{0,12},{1,13},{2,14},{3,15},{4,8},{5,9},{6,10},{7,11},{8,4},{9,5},... | collective-permute-start | bytes 98312 | tf_op jit(solution)/shard_map/ppermute | solution.py:27
  12.7 7.3 %collective-permute-start.1 = (bf16[16,1024]{1,0:T(8,128)(2,1)}, bf16[16,1024]{1,0:T(8,128)(2,1)S(1)}, u32[]{:S(2)}, u32[]{:S(2)}) collective-permute-start(bf16[16,1024]{1,0:T(8,128)(2,1)} %get-tuple-element.31), channel_id=1, source_target_pairs={{0,8},{1,9},{2,10},{3,11},{4,12},{5,13},{6,14},{7,15},{8,0},{9,1},... | collective-permute-start | bytes 98312 | tf_op jit(solution)/shard_map/ppermute | solution.py:27
  15.3 10.6 %collective-permute-start.9 = (bf16[4,16,1024]{2,1,0:T(8,128)(2,1)S(1)}, bf16[4,16,1024]{2,1,0:T(8,128)(2,1)S(1)}, u32[]{:S(2)}, u32[]{:S(2)}) collective-permute-start(bf16[4,16,1024]{2,1,0:T(8,128)(2,1)S(1)} %pad_maximum_fusion.1), channel_id=1, source_target_pairs={{0,4},{1,5},{2,6},{3,7},{4,0},{5,1},{6,2},{7,3},{8,12},{9,13},{10,... | collective-permute-start | bytes 393224 | tf_op jit(solution)/shard_map/ppermute | solution.py:27
  16.5 9.8 %collective-permute-start.14 = (bf16[4,16,1024]{2,1,0:T(8,128)(2,1)S(1)}, bf16[4,16,1024]{2,1,0:T(8,128)(2,1)S(1)}, u32[]{:S(2)}, u32[]{:S(2)}) collective-permute-start(bf16[4,16,1024]{2,1,0:T(8,128)(2,1)S(1)} %pad_maximum_fusion.1), channel_id=1, source_target_pairs={{0,8},{1,9},{2,10},{3,11},{4,12},{5,13},{6,14},{7,15},{8,0},{9,1},... | collective-permute-start | bytes 393224 | tf_op jit(solution)/shard_map/ppermute | solution.py:27
  24.5 8.3 %collective-permute-start.3 = (bf16[4,16,1024]{2,1,0:T(8,128)(2,1)S(1)}, bf16[4,16,1024]{2,1,0:T(8,128)(2,1)S(1)}, u32[]{:S(2)}, u32[]{:S(2)}) collective-permute-start(bf16[4,16,1024]{2,1,0:T(8,128)(2,1)S(1)} %pad_maximum_fusion), channel_id=1, source_target_pairs={{0,1},{1,0},{2,3},{3,2},{4,5},{5,4},{6,7},{7,6},{8,9},{9,8},{10,11... | collective-permute-start | bytes 393224 | tf_op jit(solution)/shard_map/ppermute | solution.py:27
  25.9 7.9 %collective-permute-start.15 = (bf16[4,16,1024]{2,1,0:T(8,128)(2,1)S(1)}, bf16[4,16,1024]{2,1,0:T(8,128)(2,1)S(1)}, u32[]{:S(2)}, u32[]{:S(2)}) collective-permute-start(bf16[4,16,1024]{2,1,0:T(8,128)(2,1)S(1)} %pad_maximum_fusion.1), channel_id=1, source_target_pairs={{0,12},{1,13},{2,14},{3,15},{4,8},{5,9},{6,10},{7,11},{8,4},{9,5},... | collective-permute-start | bytes 393224 | tf_op jit(solution)/shard_map/ppermute | solution.py:27
  26.4 7.3 %collective-permute-start.10 = (bf16[16,512]{1,0:T(8,128)(2,1)S(1)}, bf16[16,512]{1,0:T(8,128)(2,1)S(1)}, u32[]{:S(2)}, u32[]{:S(2)}) collective-permute-start(bf16[16,512]{1,0:T(8,128)(2,1)S(1)} %get-tuple-element.33), channel_id=1, source_target_pairs={{0,0},{1,1},{2,2},{3,3},{4,32},{5,33},{6,34},{7,35},{8,64},{9,65},... | collective-permute-start | bytes 49160 | tf_op jit(solution)/shard_map/ppermute | solution.py:36
  39.8 15.4 %collective-permute-start.17 = (bf16[4,16,384]{2,1,0:T(8,128)(2,1)S(1)}, bf16[4,16,384]{2,1,0:T(8,128)(2,1)S(1)}, u32[]{:S(2)}, u32[]{:S(2)}) collective-permute-start(bf16[4,16,384]{2,1,0:T(8,128)(2,1)S(1)} %get-tuple-element.79), channel_id=1, source_target_pairs={{0,32},{16,48},{32,0},{48,16},{64,96},{80,112},{96,64},{112,80},{1... | collective-permute-start | bytes 147464 | tf_op jit(solution)/shard_map/ppermute | solution.py:23
  46.0 12.0 %collective-permute-start.18 = (bf16[4,16,384]{2,1,0:T(8,128)(2,1)S(1)}, bf16[4,16,384]{2,1,0:T(8,128)(2,1)S(1)}, u32[]{:S(2)}, u32[]{:S(2)}) collective-permute-start(bf16[4,16,384]{2,1,0:T(8,128)(2,1)S(1)} %get-tuple-element.78), channel_id=1, source_target_pairs={{0,64},{16,80},{32,96},{48,112},{64,0},{80,16},{96,32},{112,48},{1... | collective-permute-start | bytes 147464 | tf_op jit(solution)/shard_map/ppermute | solution.py:23
  78.9 7.9 %collective-permute-start.27 = (bf16[16,6144]{1,0:T(8,128)(2,1)S(1)}, bf16[16,6144]{1,0:T(8,128)(2,1)S(1)}, u32[]{:S(2)}, u32[]{:S(2)}) collective-permute-start(bf16[16,6144]{1,0:T(8,128)(2,1)S(1)} %norm.1.refs_0_), channel_id=1, source_target_pairs={{0,64},{16,80},{32,96},{48,112},{64,0},{80,16},{96,32},{112,48},{1... | collective-permute-start | bytes 589832 | tf_op jit(solution)/shard_map/ppermute | solution.py:23
  80.9 7.9 %collective-permute-start.28 = (bf16[16,6144]{1,0:T(8,128)(2,1)S(1)}, bf16[16,6144]{1,0:T(8,128)(2,1)S(1)}, u32[]{:S(2)}, u32[]{:S(2)}) collective-permute-start(bf16[16,6144]{1,0:T(8,128)(2,1)S(1)} %norm.1.refs_0_), channel_id=1, source_target_pairs={{0,96},{16,112},{32,64},{48,80},{64,32},{80,48},{96,0},{112,16},{1... | collective-permute-start | bytes 589832 | tf_op jit(solution)/shard_map/ppermute | solution.py:23
  83.6 12.3 %collective-permute-start.29 = (bf16[16,6144]{1,0:T(8,128)(2,1)S(1)}, bf16[16,6144]{1,0:T(8,128)(2,1)S(1)}, u32[]{:S(2)}, u32[]{:S(2)}) collective-permute-start(bf16[16,6144]{1,0:T(8,128)(2,1)S(1)} %norm.1.refs_0_), channel_id=1, source_target_pairs={{0,16},{16,0},{32,48},{48,32},{64,80},{80,64},{96,112},{112,96},{1... | collective-permute-start | bytes 589832 | tf_op jit(solution)/shard_map/ppermute | solution.py:23
  84.6 11.3 %collective-permute-start.30 = (bf16[16,6144]{1,0:T(8,128)(2,1)S(1)}, bf16[16,6144]{1,0:T(8,128)(2,1)S(1)}, u32[]{:S(2)}, u32[]{:S(2)}) collective-permute-start(bf16[16,6144]{1,0:T(8,128)(2,1)S(1)} %collective-permute-done.26.after_ref.refs_1_), channel_id=1, source_target_pairs={{0,16},{16,0},{32,48},{48,32},{64,80},{80,64},{96,112},{112,96},{1... | collective-permute-start | bytes 589832 | tf_op jit(solution)/shard_map/ppermute | solution.py:23
  86.8 9.1 %collective-permute-start.31 = (bf16[16,6144]{1,0:T(8,128)(2,1)S(1)}, bf16[16,6144]{1,0:T(8,128)(2,1)S(1)}, u32[]{:S(2)}, u32[]{:S(2)}) collective-permute-start(bf16[16,6144]{1,0:T(8,128)(2,1)S(1)} %collective-permute-done.27.refs_2_), channel_id=1, source_target_pairs={{0,16},{16,0},{32,48},{48,32},{64,80},{80,64},{96,112},{112,96},{1... | collective-permute-start | bytes 589832 | tf_op jit(solution)/shard_map/ppermute | solution.py:23
  88.8 7.1 %collective-permute-start.32 = (bf16[16,6144]{1,0:T(8,128)(2,1)S(1)}, bf16[16,6144]{1,0:T(8,128)(2,1)S(1)}, u32[]{:S(2)}, u32[]{:S(2)}) collective-permute-start(bf16[16,6144]{1,0:T(8,128)(2,1)S(1)} %collective-permute-done.28.refs_3_), channel_id=1, source_target_pairs={{0,16},{16,0},{32,48},{48,32},{64,80},{80,64},{96,112},{112,96},{1... | collective-permute-start | bytes 589832 | tf_op jit(solution)/shard_map/ppermute | solution.py:23
  105.0 7.8 %collective-permute-start.34 = (bf16[2,4,16,768]{3,2,1,0:T(8,128)(2,1)S(1)}, bf16[2,4,16,768]{3,2,1,0:T(8,128)(2,1)S(1)}, u32[]{:S(2)}, u32[]{:S(2)}) collective-permute-start(bf16[2,4,16,768]{3,2,1,0:T(8,128)(2,1)S(1)} %bitcast.116), channel_id=1, source_target_pairs={{0,32},{16,48},{32,0},{48,16},{64,96},{80,112},{96,64},{112,80},{1... | collective-permute-start | bytes 589832 | tf_op jit(solution)/shard_map/ppermute | solution.py:23
  105.1 15.1 %collective-permute-start.39 = (bf16[2,4,16,768]{3,2,1,0:T(8,128)(2,1)S(1)}, bf16[2,4,16,768]{3,2,1,0:T(8,128)(2,1)S(1)}, u32[]{:S(2)}, u32[]{:S(2)}) collective-permute-start(bf16[2,4,16,768]{3,2,1,0:T(8,128)(2,1)S(1)} %bitcast.115), channel_id=1, source_target_pairs={{0,64},{16,80},{32,96},{48,112},{64,0},{80,16},{96,32},{112,48},{1... | collective-permute-start | bytes 589832 | tf_op jit(solution)/shard_map/ppermute | solution.py:23
  109.2 14.1 %collective-permute-start.40 = (bf16[2,4,16,768]{3,2,1,0:T(8,128)(2,1)S(1)}, bf16[2,4,16,768]{3,2,1,0:T(8,128)(2,1)S(1)}, u32[]{:S(2)}, u32[]{:S(2)}) collective-permute-start(bf16[2,4,16,768]{3,2,1,0:T(8,128)(2,1)S(1)} %bitcast.114), channel_id=1, source_target_pairs={{0,96},{16,112},{32,64},{48,80},{64,32},{80,48},{96,0},{112,16},{1... | collective-permute-start | bytes 589832 | tf_op jit(solution)/shard_map/ppermute | solution.py:23
  112.8 9.0 %collective-permute-start.35 = (bf16[16,384]{1,0:T(8,128)(2,1)S(1)}, bf16[16,384]{1,0:T(8,128)(2,1)S(1)}, u32[]{:S(2)}, u32[]{:S(2)}) collective-permute-start(bf16[16,384]{1,0:T(8,128)(2,1)S(1)} %get-tuple-element.100), channel_id=1, source_target_pairs={{0,0},{1,1},{2,16},{3,17},{4,32},{5,33},{6,48},{7,49},{8,64},{9,65... | collective-permute-start | bytes 36872 | tf_op jit(solution)/shard_map/ppermute | solution.py:36
  113.5 8.3 %collective-permute-start.36 = (bf16[16,384]{1,0:T(8,128)(2,1)S(1)}, bf16[16,384]{1,0:T(8,128)(2,1)S(1)}, u32[]{:S(2)}, u32[]{:S(2)}) collective-permute-start(bf16[16,384]{1,0:T(8,128)(2,1)S(1)} %get-tuple-element.99), channel_id=1, source_target_pairs={{0,1},{1,0},{2,17},{3,16},{4,33},{5,32},{6,49},{7,48},{8,65},{9,64... | collective-permute-start | bytes 36872 | tf_op jit(solution)/shard_map/ppermute | solution.py:36
  113.8 8.0 %collective-permute-start.37 = (bf16[16,384]{1,0:T(8,128)(2,1)S(1)}, bf16[16,384]{1,0:T(8,128)(2,1)S(1)}, u32[]{:S(2)}, u32[]{:S(2)}) collective-permute-start(bf16[16,384]{1,0:T(8,128)(2,1)S(1)} %get-tuple-element.98), channel_id=1, source_target_pairs={{0,2},{1,3},{2,18},{3,19},{4,34},{5,35},{6,50},{7,51},{8,66},{9,67... | collective-permute-start | bytes 36872 | tf_op jit(solution)/shard_map/ppermute | solution.py:36
  124.0 15.4 %collective-permute-start.43 = (bf16[4,8,768]{2,1,0:T(8,128)(2,1)S(1)}, bf16[4,8,768]{2,1,0:T(8,128)(2,1)S(1)}, u32[]{:S(2)}, u32[]{:S(2)}) collective-permute-start(bf16[4,8,768]{2,1,0:T(8,128)(2,1)S(1)} %get-tuple-element.68), channel_id=1, source_target_pairs={{0,12},{1,13},{2,14},{3,15},{4,8},{5,9},{6,10},{7,11},{8,4},{9,5},... | collective-permute-start | bytes 147464 | tf_op jit(solution)/shard_map/ppermute | solution.py:27
  (27 other events, 270.3 us)

commit v4 on v3

v4 whole, which is shorter than its diff:
```python
import functools

import jax
import jax.numpy as jnp
from jax import lax
from jax.experimental import pallas as pl
from jax.experimental.pallas import tpu as pltpu
from jax.sharding import PartitionSpec as P

STEPS = 4
ROWS = 8
EPS = 1e-06
F32 = jnp.float32
BF16 = jnp.bfloat16
MIB = 1 << 20


def vmem_params(mib):
    return pltpu.CompilerParams(vmem_limit_bytes=mib * MIB)


def over_head(value, bits):
    return lax.ppermute(value, "head", [(i, i ^ bits) for i in range(8)])


def over_exp(value, bits):
    return lax.ppermute(value, "exp", [(i, i ^ bits) for i in range(16)])


def call(kernel, name, out_shape, place, *arrays, flops=0, limit=30, scratch=()):
    moved = sum(a.size * a.dtype.itemsize for a in arrays)
    result = pl.pallas_call(
        kernel,
        out_shape=out_shape,
        in_specs=[pl.BlockSpec(memory_space=pltpu.SMEM)]
        + [pl.BlockSpec(memory_space=pltpu.VMEM)] * len(arrays),
        out_specs=jax.tree.map(lambda _: pl.BlockSpec(memory_space=pltpu.VMEM), out_shape),
        scratch_shapes=scratch,
        compiler_params=vmem_params(limit),
        cost_estimate=pl.CostEstimate(flops=flops, bytes_accessed=moved, transcendentals=0),
        name=name,
    )(place, *arrays)
    return list(result) if isinstance(out_shape, list) else result


def xor(a, b):
    return lax.bitwise_xor(a, b)


def lanes_from(start, size):
    return pl.ds(pl.multiple_of(start, 128), size)


def columns_of(table):
    rows = lax.broadcasted_iota(jnp.int32, (ROWS, ROWS), 0)
    lanes = lax.broadcasted_iota(jnp.int32, (ROWS, ROWS), 1)
    return lax.dot_general(
        (rows == lanes).astype(F32),
        table,
        (((1,), (1,)), ((), ())),
        precision=lax.Precision.HIGHEST,
        preferred_element_type=F32,
    )


def widened(pair):
    lane = lax.broadcasted_iota(jnp.int32, (pair.shape[0], 128), 1)
    return jnp.where(lane == 0, pair[:, :1], jnp.where(lane == 1, pair[:, 1:2], 0.0))


def bf16_parts(value, count):
    parts = []
    for _ in range(count - 1):
        parts.append(value.astype(BF16))
        value = value - parts[-1].astype(F32)
    return parts + [value.astype(BF16)]


def readout_kernel(
    place_ref, decay_ref, routes_ref, hidden_ref, qkv_ref, state_ref, gain_ref, *out_refs
):
    first_refs, last_ref = out_refs[:4], out_refs[4]
    z, c = place_ref[1], place_ref[3]
    depth = last_ref.shape[1]
    quarter = hidden_ref.shape[2] // 4

    @pl.when(pl.program_id(0) == 0)
    def _():
        names = [columns_of(routes_ref[2 * c + t].astype(F32)) for t in range(2)]
        names = widened(jnp.concatenate(names, axis=0)).astype(BF16)
        for k, ref in enumerate(first_refs):
            at = lanes_from(xor(z, k) * quarter, quarter)
            rows = [hidden_ref[2 * c + t, :, at].astype(F32) for t in range(2)]
            ref[:, depth : depth + quarter] = jnp.concatenate(rows, axis=0).astype(BF16)
            ref[:, depth + quarter :] = names

    n, size = STEPS * ROWS, state_ref.shape[2]
    heads = state_ref.shape[1]
    row = lax.broadcasted_iota(jnp.int32, (n, size), 0)
    row_in = row % ROWS
    row_t = lax.broadcasted_iota(jnp.int32, (n, n), 0)
    row_s = lax.broadcasted_iota(jnp.int32, (n, n), 1)
    for h in range(heads):
        lanes = slice(h * size, (h + 1) * size)
        q, k, v = [
            qkv_ref[:, i, :, lanes].astype(F32).reshape(n, size).astype(BF16) for i in range(3)
        ]
        q_twice = jnp.concatenate([q, q], axis=1)
        carried = jnp.zeros((n, size), F32)
        for pair in range(ROWS // 2):
            wide = jnp.concatenate([state_ref[2 * pair, h], state_ref[2 * pair + 1, h]], axis=1)
            both = jnp.dot(
                q_twice, jnp.concatenate(bf16_parts(wide, 2), axis=0), preferred_element_type=F32
            )
            carried = jnp.where(row_in == 2 * pair, both[:, :size], carried)
            carried = jnp.where(row_in == 2 * pair + 1, both[:, size:], carried)
        decay = [decay_ref[t, pl.program_id(0) * heads + h] for t in range(STEPS)]
        run = decay[0]
        first = jnp.full((n, size), run, F32)
        for t in range(1, STEPS):
            run = run * decay[t]
            first = jnp.where(row // ROWS == t, run, first)
        mix = jnp.zeros((n, n), F32)
        for t in range(STEPS):
            run = None
            for s in range(t, -1, -1):
                here = row_t - row_s == (t - s) * ROWS
                mix = jnp.where(here & (row_s // ROWS == s), 1.0 if run is None else run, mix)
                run = decay[s] if run is None else run * decay[s]
        scores = lax.dot_general(q, k, (((1,), (1,)), ((), ())), preferred_element_type=F32)
        o = carried * first + jnp.dot(
            jnp.concatenate(bf16_parts(scores * mix, 2), axis=1),
            jnp.concatenate([v, v], axis=0),
            preferred_element_type=F32,
        )
        o = o * lax.rsqrt(jnp.mean(o * o, axis=-1, keepdims=True) + EPS) * gain_ref[:, lanes]
        o = o.astype(BF16)
        at = lanes_from((pl.program_id(0) * heads + h) * size, size)
        for ref in first_refs:
            ref[:, at] = o[: n // 2]
        last_ref[:, at] = o[n // 2 :]


def readouts(place, step_qkv, decay, state, attn_gain, hidden_in, routes):
    heads, size = state.shape[1], state.shape[2]
    at_once = min(heads, 4)
    half = STEPS * ROWS // 2
    depth = heads * size
    packed = depth + hidden_in.shape[2] // 4 + 128
    whole = lambda i: (0, 0)
    return pl.pallas_call(
        readout_kernel,
        out_shape=[jax.ShapeDtypeStruct((half, packed), BF16)] * 4
        + [jax.ShapeDtypeStruct((half, depth), BF16)],
        grid=(heads // at_once,),
        in_specs=[
            pl.BlockSpec(memory_space=pltpu.SMEM),
            pl.BlockSpec(memory_space=pltpu.SMEM),
            pl.BlockSpec((STEPS, 2, ROWS), lambda i: (0, 0, 0)),
            pl.BlockSpec(hidden_in.shape, lambda i: (0, 0, 0)),
            pl.BlockSpec((STEPS, 3, ROWS, at_once * size), lambda i: (0, 0, 0, i)),
            pl.BlockSpec((ROWS, at_once, size, size), lambda i: (0, i, 0, 0)),
            pl.BlockSpec((1, at_once * size), lambda i: (0, i)),
        ],
        out_specs=[pl.BlockSpec((half, packed), whole)] * 4 + [pl.BlockSpec((half, depth), whole)],
        compiler_params=vmem_params(56),
        cost_estimate=pl.CostEstimate(
            flops=2 * STEPS * ROWS * ROWS * heads * size * size * 2,
            bytes_accessed=state.size * 4,
            transcendentals=0,
        ),
        name="readout",
    )(
        place,
        decay,
        routes.transpose(0, 2, 1),
        hidden_in,
        step_qkv.transpose(0, 2, 1, 3),
        state,
        attn_gain.reshape(1, -1),
    )


def spread_kernel(place_ref, *refs):
    in_refs, out_refs, held_ref = refs[:4], refs[4:8], refs[8]
    x, z, y = place_ref[0], place_ref[1], place_ref[2]
    wide = out_refs[0].shape[2]
    depth = wide - 128
    held = in_refs[0][:, depth:]
    for k in (1, 2, 3):
        held = jnp.where(xor(z, y) == k, in_refs[k][:, depth:], held)
    held_ref[...] = held
    cols = (held.shape[1] - 128) // 4
    for kx, ref in enumerate(out_refs):
        for kz in range(4):
            ref[kz, :, :depth] = in_refs[kz][:, :depth]
            if kz * 128 < cols:
                at = lanes_from(xor(x, kx) * cols + kz * 128, 128)
                ref[kz, :, depth:] = held_ref[:, at]
            else:
                ref[kz, :, depth:] = held[:, 4 * cols :]


def spread(place, pieces, depth):
    out = [jax.ShapeDtypeStruct((4, 16, depth + 128), BF16)] * 4
    scratch = [pltpu.VMEM((16, pieces[0].shape[1] - depth), BF16)]
    return call(spread_kernel, "spread", out, place, *pieces, scratch=scratch)


def project_kernel(place_ref, *refs):
    a_refs, b_refs, (weight_ref, mine_ref, other_ref) = refs[:4], refs[4:8], refs[8:]
    c = place_ref[3]
    depth = weight_ref.shape[0]

    def product(ref):
        rows = ref[:, :, :depth].reshape(64, depth)
        return jnp.dot(rows, weight_ref[...], preferred_element_type=F32).astype(BF16)

    for k in range(4):
        a, b = product(a_refs[k]), product(b_refs[k])
        for j in range(4):
            at = slice(16 * j, 16 * j + 16)

            @pl.when(c == 0)
            def _():
                mine_ref[k, j] = a[at]
                other_ref[j, k] = b[at]

            @pl.when(c == 1)
            def _():
                other_ref[k, j] = a[at]
                mine_ref[j, k] = b[at]


def project(place, all_a, all_b, weight):
    out = [jax.ShapeDtypeStruct((4, 4, 16, weight.shape[1]), BF16)] * 2
    flops = 2 * 512 * weight.size
    return call(project_kernel, "project", out, place, *all_a, *all_b, weight, flops=flops)


def by_y_kernel(place_ref, mine_ref, got_ref, *out_refs):
    z, y = place_ref[1], place_ref[2]
    for k, ref in enumerate(out_refs):
        kz = xor(xor(y, z), k)
        for kx in range(4):
            total = mine_ref[kx, kz].astype(F32) + got_ref[kx, kz].astype(F32)
            ref[kx] = total.astype(BF16)


def sums_by_y(place, mine, got):
    out = [jax.ShapeDtypeStruct((4, 16, mine.shape[3]), BF16)] * 4
    return call(by_y_kernel, "sums_by_y", out, place, mine, got)


def attend_kernel(place_ref, *refs):
    sum_refs, hidden_refs, out_refs = refs[:4], refs[4:8], refs[8:12]
    x, z = place_ref[0], place_ref[1]
    cols = out_refs[0].shape[2]
    depth = hidden_refs[0].shape[2] - 128
    rows, names = [], []
    for k in range(4):
        parts = [hidden_refs[k][j, :, depth:].astype(F32) for j in range(4)]
        names.append(parts[3])
        total = jnp.concatenate(parts[: cols // 128], axis=1)
        for ref in sum_refs:
            total += ref[k].astype(F32)
        rows.append(total.astype(BF16))
        for ref in out_refs:
            ref[4 + k] = rows[k]
    rows = jnp.concatenate(rows, axis=0)
    n = rows.shape[0]
    names = jnp.concatenate(names, axis=0)
    across = names.T
    down_i = lax.broadcasted_iota(jnp.int32, (n, n), 0)
    over_i = lax.broadcasted_iota(jnp.int32, (n, n), 1)
    earlier = (down_i // ROWS == over_i // ROWS) & (down_i < over_i)
    slot = lax.broadcasted_iota(jnp.int32, (256, n), 0)
    lane = lax.broadcasted_iota(jnp.int32, (1, n), 1)
    base = lax.bitwise_xor(lane // 16, x) * 4 + lane // ROWS % 2 * 2
    select = jnp.zeros((256, n), F32)
    for j in range(2):
        mine = across[j : j + 1, :]
        rank = jnp.zeros((1, n), F32)
        for other in range(2):
            same = (names[:, other : other + 1] == mine) & earlier
            rank += jnp.sum(same.astype(F32), axis=0, keepdims=True)
        expert = mine.astype(jnp.int32)
        kz = lax.bitwise_xor(expert // 4, z)
        kx = lax.bitwise_xor(expert % 4, x)
        target = (kz * 4 + kx) * 16 + base + rank.astype(jnp.int32)
        select += (slot == target).astype(F32)
    sent = jnp.dot(select.astype(BF16), rows, preferred_element_type=F32).astype(BF16)
    for k in range(16):
        out_refs[k // 4][k % 4] = sent[16 * k : 16 * k + 16]


def attend(place, sums, hidden):
    out = [jax.ShapeDtypeStruct((8,) + sums[0].shape[1:], BF16)] * 4
    return call(attend_kernel, "attend", out, place, *sums, *hidden, flops=1 << 23)


def turn_kernel(place_ref, *refs):
    in_refs, out_refs = refs[:4], refs[4:8]
    for kx, ref in enumerate(out_refs):
        for kz in range(4):
            ref[kz] = in_refs[kz][kx]
            ref[4 + kz] = in_refs[kz][4 + kx]


def turn(place, pieces):
    out = [jax.ShapeDtypeStruct(pieces[0].shape, BF16)] * 4
    return call(turn_kernel, "turn", out, place, *pieces)


def norm_kernel(place_ref, gain_ref, *refs):
    got_refs, out_refs = refs[:4], refs[4:8]
    x, z, y = place_ref[0], place_ref[1], place_ref[2]
    cols = got_refs[0].shape[2]
    total = jnp.zeros((16, cols), F32)
    for ref in got_refs:
        for kz in range(4):
            value = ref[kz].astype(F32)
            total += value * value
    mean = jnp.sum(total, axis=-1, keepdims=True) / (16 * cols)
    scale = lax.rsqrt(mean + EPS)
    for kx, ref in enumerate(got_refs):
        for kz in range(4):
            at = lanes_from((xor(z, kz) * 4 + xor(x, kx)) * cols, cols)
            value = (ref[kz].astype(F32) * scale * gain_ref[:, at]).astype(BF16)
            for out_ref in out_refs:
                out_ref[:, at] = value
        for k, out_ref in enumerate(out_refs):
            at = lanes_from((16 + xor(x, kx)) * cols, cols)
            out_ref[:, at] = ref[4 + xor(xor(z, y), k)]


def norm(place, gain, got):
    out = [jax.ShapeDtypeStruct((16, 20 * got[0].shape[2]), BF16)] * 4
    return call(norm_kernel, "norm", out, place, gain.reshape(1, -1), *got)


def owned_kernel(place_ref, *refs):
    own_refs, other_refs, out_ref = refs[:4], refs[4:8], refs[8]
    z, y, c = place_ref[1], place_ref[2], place_ref[3]
    share = out_ref.shape[1]
    start = own_refs[0].shape[1] - 2 * share
    at = lanes_from(start + c * share, share)
    for k in range(4):

        @pl.when(xor(z, y) == k)
        def _():
            out_ref[pl.ds(pl.multiple_of(16 * c, 16), 16), :] = own_refs[k][:, at]
            out_ref[pl.ds(pl.multiple_of(16 - 16 * c, 16), 16), :] = other_refs[k][:, at]


def owned(place, by_y, by_core, share):
    out = jax.ShapeDtypeStruct((STEPS * ROWS, share), BF16)
    return call(owned_kernel, "owned", out, place, *by_y, *by_core)


def fetch_kernel(after_ref, in_ref, out_ref, sem):
    copy = pltpu.make_async_copy(in_ref, out_ref, sem)
    copy.start()
    copy.wait()


def fetch(after, weight):
    return pl.pallas_call(
        fetch_kernel,
        out_shape=pltpu.VMEM(weight.shape, weight.dtype),
        in_specs=[pl.BlockSpec(memory_space=pl.ANY), pl.BlockSpec(memory_space=pltpu.HBM)],
        out_specs=pl.BlockSpec(memory_space=pltpu.VMEM),
        scratch_shapes=[pltpu.SemaphoreType.DMA],
        compiler_params=vmem_params(12),
        cost_estimate=pl.CostEstimate(
            flops=0, bytes_accessed=2 * weight.size, transcendentals=0
        ),
        name="fetch",
    )(after, weight)


def hidden_kernel(place_ref, *refs):
    x_refs, (gate_ref, up_ref, down_ref, hidden_ref, theirs_ref) = refs[:8], refs[8:]
    share = theirs_ref.shape[2]
    y, c = place_ref[2], place_ref[3]
    x = jnp.concatenate([r[:, : gate_ref.shape[1]] for r in x_refs], axis=0)
    across = (((1,), (1,)), ((), ()))
    gate = lax.dot_general(gate_ref[...], x, across, preferred_element_type=F32)
    up = lax.dot_general(up_ref[...], x, across, preferred_element_type=F32)
    hidden = (gate / (1.0 + jnp.exp(-gate)) * up).T.astype(BF16)
    hidden_ref[...] = hidden
    for k in range(4):
        block = lax.bitwise_xor(y, k) * 2 + (1 - c)
        at = pl.ds(pl.multiple_of(block * share, 128), share)
        theirs_ref[k] = jnp.dot(hidden, down_ref[:, at], preferred_element_type=F32).astype(BF16)


def hidden_units(place, pieces, gate, up, down_weight, share):
    units = gate.shape[0]
    rows = sum(p.shape[0] for p in pieces)
    out = [
        jax.ShapeDtypeStruct((rows, units), BF16),
        jax.ShapeDtypeStruct((4, rows, share), BF16),
    ]
    flops = 5 * rows * gate.size
    return call(
        hidden_kernel, "hidden_units", out, place, *pieces, gate, up, down_weight, flops=flops
    )


def down_kernel(place_ref, hidden_ref, down_ref, theirs_ref, *out_refs):
    share = out_refs[0].shape[1]
    y, c = place_ref[2], place_ref[3]
    half = hidden_ref.shape[0] // 2
    for k in range(4):
        block = lax.bitwise_xor(y, k) * 2 + c
        at = pl.ds(pl.multiple_of(block * share, 128), share)
        ours = jnp.dot(hidden_ref[...], down_ref[:, at], preferred_element_type=F32)
        out_refs[k][:half] = (ours[:half] + theirs_ref[k, half:].astype(F32)).astype(BF16)
        out_refs[k][half:] = (ours[half:] + theirs_ref[k, :half].astype(F32)).astype(BF16)


def down(place, hidden, weight, theirs):
    out = [jax.ShapeDtypeStruct(theirs.shape[1:], BF16)] * 4
    flops = hidden.shape[0] * weight.size
    return call(down_kernel, "down", out, place, hidden, weight, theirs, flops=flops)


def final_sum_kernel(place_ref, own_ref, got1_ref, got2_ref, got3_ref, out_ref):
    x, z, y, c = [place_ref[i] for i in range(4)]
    for ky in range(4):
        sums = []
        for kc in range(2):
            at = slice((kc * 4 + ky) * 16, (kc * 4 + ky) * 16 + 16)
            total = own_ref[at].astype(F32)
            for k, ref in ((1, got1_ref), (2, got2_ref), (3, got3_ref)):
                at = slice((kc * 4 + (ky ^ k)) * 16, (kc * 4 + (ky ^ k)) * 16 + 16)
                total += ref[at].astype(F32)
            sums.append(total)
        low = jnp.where(c == 0, sums[0], sums[1])
        high = jnp.where(c == 0, sums[1], sums[0])
        for source in range(4):
            at = slice(4 * source, 4 * source + 4)
            block = jnp.concatenate([low[at], high[at]], axis=0)
            kz = lax.bitwise_xor(lax.bitwise_xor(y, ky), z)
            out_ref[kz, lax.bitwise_xor(x, source)] = block.astype(BF16)


def final_sum(place, sums):
    out = jax.ShapeDtypeStruct((4, 4, 8, sums[0].shape[1]), BF16)
    return call(final_sum_kernel, "final_sum", out, place, *sums)


def mix_kernel(place_ref, routes_ref, weights_ref, *refs):
    back_refs, out_ref = refs[:4], refs[4]
    x, z = place_ref[0], place_ref[1]
    n = STEPS * ROWS
    names = [columns_of(routes_ref[t].astype(F32)) for t in range(STEPS)]
    names = widened(jnp.concatenate(names, axis=0))
    weights = [columns_of(weights_ref[t]) for t in range(STEPS)]
    weights = jnp.concatenate(weights, axis=0)
    down_i = lax.broadcasted_iota(jnp.int32, (n, n), 0)
    over_i = lax.broadcasted_iota(jnp.int32, (n, n), 1)
    earlier = (down_i // ROWS == over_i // ROWS) & (over_i < down_i)
    across = names.T
    slot = lax.broadcasted_iota(jnp.int32, (n, 128), 1)
    step = lax.broadcasted_iota(jnp.int32, (n, 1), 0) // ROWS
    mix = jnp.zeros((n, 128), F32)
    for j in range(2):
        mine = names[:, j : j + 1]
        rank = jnp.zeros((n, 1), F32)
        for other in range(2):
            same = (across[other : other + 1, :] == mine) & earlier
            rank += jnp.sum(same.astype(F32), axis=1, keepdims=True)
        expert = mine.astype(jnp.int32)
        kz = lax.bitwise_xor(expert // 4, z)
        kx = lax.bitwise_xor(expert % 4, x)
        target = (kx * 4 + kz) * 8 + 2 * step + rank.astype(jnp.int32)
        mix += jnp.where(slot == target, weights[:, j : j + 1], 0.0)
    back = jnp.concatenate(
        [ref[kz].astype(F32) for ref in back_refs for kz in range(4)], axis=0
    ).astype(BF16)
    out_ref[...] = jnp.dot(
        jnp.concatenate(bf16_parts(mix, 3), axis=1),
        jnp.concatenate([back] * 3, axis=0),
        preferred_element_type=F32,
    ).astype(BF16)


def mixed_rows(place, routes, weights, back):
    out = jax.ShapeDtypeStruct((STEPS * ROWS, back[0].shape[-1]), BF16)
    arrays = (routes.transpose(0, 2, 1), weights.transpose(0, 2, 1), *back)
    return call(mix_kernel, "mix", out, place, *arrays, flops=1 << 24)


def shards(
    hidden_in,
    step_qkv,
    decay_rates,
    kv_state,
    attn_gain,
    out_proj,
    ffn_gain,
    routes,
    route_weights,
    w_gate,
    w_up,
    w_down,
):
    share = hidden_in.shape[2] // 8
    head, exp = lax.axis_index("head"), lax.axis_index("exp")
    y, c, z, x = head // 2, head % 2, exp // 4, exp % 4
    place = jnp.stack([x, z, y, c]).astype(jnp.int32)

    *half_a, half_b = readouts(
        place, step_qkv, decay_rates, kv_state, attn_gain, hidden_in, routes
    )
    by_z = half_a[:1] + [over_exp(half_a[k], 4 * k) for k in (1, 2, 3)]
    by_x = jnp.stack([half_b] + [over_exp(half_b, k) for k in (1, 2, 3)], 0)
    by_z = spread(place, by_z, half_b.shape[1])
    all_a = by_z[:1] + [over_exp(by_z[k], k) for k in (1, 2, 3)]
    all_b = [by_x] + [over_exp(by_x, 4 * k) for k in (1, 2, 3)]

    mine, other = project(place, all_a, all_b, out_proj)
    sums = sums_by_y(place, mine, over_head(other, 1))
    sums = sums[:1] + [over_head(sums[k], 2 * k) for k in (1, 2, 3)]

    pieces = attend(place, sums, all_a)
    pieces = turn(place, pieces[:1] + [over_exp(pieces[k], 4 * k) for k in (1, 2, 3)])
    pieces = norm(place, ffn_gain, pieces[:1] + [over_exp(pieces[k], k) for k in (1, 2, 3)])
    by_y = pieces[:1] + [over_head(pieces[k], 2 * k) for k in (1, 2, 3)]
    by_core = [over_head(piece, 1) for piece in by_y]
    attended = owned(place, by_y, by_core, share)

    gate = fetch(by_x, w_gate[0].swapaxes(0, 1))
    up = fetch(by_x, w_up[0].swapaxes(0, 1))
    down_weight = fetch(by_x, w_down[0])
    hidden, theirs = hidden_units(place, by_y + by_core, gate, up, down_weight, share)
    sums = down(place, hidden, down_weight, over_head(theirs, 1))
    results = final_sum(place, sums[:1] + [over_head(sums[k], 2 * k) for k in (1, 2, 3)])

    by_kz = [results[0]] + [over_exp(results[k], 4 * k) for k in (1, 2, 3)]
    by_kx = [jnp.stack([by_kz[kz][kx] for kz in range(4)], 0) for kx in range(4)]
    by_kx = by_kx[:1] + [over_exp(by_kx[k], k) for k in (1, 2, 3)]
    mixed = mixed_rows(place, routes, route_weights, by_kx)
    return attended.reshape(STEPS, ROWS, share), mixed.reshape(STEPS, ROWS, share)


def solution(mesh):
    return jax.shard_map(
        shards,
        mesh=mesh,
        in_specs=(
            P(None, "exp", None),
            P(None, "exp", None, "head"),
            P(None, "head"),
            P("exp", "head", None, None),
            P("head"),
            P("head", "exp"),
            P(),
            P(None, "exp", None),
            P(None, "exp", None),
            P("exp", None, "head"),
            P("exp", None, "head"),
            P("exp", "head", None),
        ),
        out_specs=(P(None, "exp", "head"), P(None, "exp", "head")),
        check_vma=False,
    )
```

time: 153 us -> 138 us (0.902)
  starting transfers between devices: 86.5 us -> 53.9 us
  waiting for transfers between devices: 37.4 us -> 53.8 us
  local copies, waits for them, and re-layouts: 1.32 us -> 5.84 us
  other arithmetic: 3.16 us -> 1.46 us
    ppermute x8 -> x0, starting transfers between devices: 12.9 us -> none  [over_all(): return lax.ppermute(value, ('head', 'exp'), pairs)]
    ppermute x24, waiting for transfers between devices: 15.2 us -> 27.7 us  [over_exp(): return lax.ppermute(value, 'exp', [(i, i ^ bits) for i in range(16)])]
    ppermute x15, starting transfers between devices: 25.5 us -> 15 us  [over_head(): return lax.ppermute(value, 'head', [(i, i ^ bits) for i in range(8)])]
    ppermute x15, waiting for transfers between devices: 16.7 us -> 26.1 us  [over_head(): return lax.ppermute(value, 'head', [(i, i ^ bits) for i in range(8)])]
    ppermute x24, starting transfers between devices: 48 us -> 38.8 us  [over_exp(): return lax.ppermute(value, 'exp', [(i, i ^ bits) for i in range(16)])]
    unnamed x8 -> x22, local copies, waits for them, and re-layouts: 0.03 us -> 5.81 us
    ppermute x8 -> x0, waiting for transfers between devices: 5.52 us -> none  [over_all(): return lax.ppermute(value, ('head', 'exp'), pairs)]
    pallas_call x8 -> x15, Pallas kernels: 21.3 us -> 21.7 us  [the longest x11 15.7 us: call(): pl.pallas_call(kernel, out_shape=out_shape, in_specs=[pl.BlockSpec(memory...]
  transfers between devices with their start and end apart: 47 -> 39, of which waited for: 22 -> 25; matrix products, arithmetic and copies ran while one was open for 3% -> 0% of each run, Pallas kernels for 5% -> 2%
where the time goes in v4:
time: 138 us
  starting transfers between devices  53.9 us (39%)
  waiting for transfers between devices  53.8 us (39%)
  Pallas kernels  21.7 us (16%)
  local copies, waits for them, and re-layouts  5.84 us (4%)
  other arithmetic  1.46 us (1%)
    ppermute x24, starting transfers between devices, over_exp(): return lax.ppermute(value, 'exp', [(i, i ^ bits) for i in range(16)])  38.8 us
    ppermute x24, waiting for transfers between devices, over_exp(): return lax.ppermute(value, 'exp', [(i, i ^ bits) for i in range(16)])  27.7 us
    ppermute x15, waiting for transfers between devices, over_head(): return lax.ppermute(value, 'head', [(i, i ^ bits) for i in range(8)])  26.1 us
    pallas_call x11, Pallas kernels, call(): pl.pallas_call(kernel, out_shape=out_shape, in_specs=[pl.BlockSpec(memory...  15.7 us
    ppermute x15, starting transfers between devices, over_head(): return lax.ppermute(value, 'head', [(i, i ^ bits) for i in range(8)])  15 us
    unnamed x22, local copies, waits for them, and re-layouts  5.81 us
    pallas_call x1, Pallas kernels, readouts(): pl.pallas_call(readout_kernel, out_shape=[jax.ShapeDtypeStruct((half, pac...  4.49 us
  transfers between devices with their start and end apart: 39, of which 25 were waited for; matrix products, arithmetic and copies ran while one was open for 0% of the time, Pallas kernels for 2%

profile of v4, /device:TPU:0, one launch (start us, length us, event | category | flops | bytes accessed | tf_op | source)
XLA Modules:
  0.0 137.7 jit_solution(9459986334233033605)
XLA Ops:
  1.3 4.5 %readout.1 = (bf16[16,2688]{1,0:T(8,128)(2,1)}, bf16[16,2688]{1,0:T(8,128)(2,1)}, bf16[16,2688]{1,0:T(8,128)(2,1)}, bf16[16,2688]{1,0:T(8,128)(2,1)}, bf16[16,1024]{1,0:T(8,128)(2,1)}) custom-call(s32[4]{0:T(128)} %pad_add_fusion.place_ref, f32[4,8]{1,0:T(4,128)} %decay_ref.1, s32[4,2,8]{2,1,0:T(2,128)} %bitcast.44, bf16[4,8,6144]{2,1,0:T(8,128)(2,1)} %hidden_ref.1, ...), custom_call_target="tpu_custom_call" | custom-call | flops 134217728 | bytes 4194304 | tf_op jit(solution)/shard_map/readout/pallas_call | solution.py:151
  5.8 3.2 %collective-permute-start.7 = (bf16[16,1024]{1,0:T(8,128)(2,1)}, bf16[16,1024]{1,0:T(8,128)(2,1)S(1)}, u32[]{:S(2)}, u32[]{:S(2)}) collective-permute-start(bf16[16,1024]{1,0:T(8,128)(2,1)} %get-tuple-element.43), channel_id=1, source_target_pairs={{0,2},{1,3},{2,0},{3,1},{4,6},{5,7},{6,4},{7,5},{8,10},{9,11},{10,... | collective-permute-start | bytes 98312 | tf_op jit(solution)/shard_map/ppermute | solution.py:27
  11.5 2.8 %collective-permute-done.8 = bf16[16,1024]{1,0:T(8,128)(2,1)S(1)} collective-permute-done((bf16[16,1024]{1,0:T(8,128)(2,1)}, bf16[16,1024]{1,0:T(8,128)(2,1)S(1)}, u32[]{:S(2)}, u32[]{:S(2)}) %collective-permute-start.8) | collective-permute-done | bytes 32800 | tf_op jit(solution)/shard_map/ppermute | solution.py:27
  15.1 4.0 %collective-permute-start.10 = (bf16[4,16,1024]{2,1,0:T(8,128)(2,1)S(1)}, bf16[4,16,1024]{2,1,0:T(8,128)(2,1)S(1)}, u32[]{:S(2)}, u32[]{:S(2)}) collective-permute-start(bf16[4,16,1024]{2,1,0:T(8,128)(2,1)S(1)} %pad_maximum_fusion.refs_4_.after_ref), channel_id=1, source_target_pairs={{0,8},{1,9},{2,10},{3,11},{4,12},{5,13},{6,14},{7,15},{8,0},{9,1},... | collective-permute-start | bytes 393224 | tf_op jit(solution)/shard_map/ppermute | solution.py:27
  21.3 2.5 %collective-permute-start.2 = (bf16[16,2688]{1,0:T(8,128)(2,1)}, bf16[16,2688]{1,0:T(8,128)(2,1)S(1)}, u32[]{:S(2)}, u32[]{:S(2)}) collective-permute-start(bf16[16,2688]{1,0:T(8,128)(2,1)} %get-tuple-element.38), channel_id=1, source_target_pairs={{0,12},{1,13},{2,14},{3,15},{4,8},{5,9},{6,10},{7,11},{8,4},{9,5},... | collective-permute-start | bytes 258056 | tf_op jit(solution)/shard_map/ppermute | solution.py:27
  29.5 3.5 %collective-permute-start.4 = (bf16[4,16,1152]{2,1,0:T(8,128)(2,1)S(1)}, bf16[4,16,1152]{2,1,0:T(8,128)(2,1)S(1)}, u32[]{:S(2)}, u32[]{:S(2)}) collective-permute-start(bf16[4,16,1152]{2,1,0:T(8,128)(2,1)S(1)} %get-tuple-element.41), channel_id=1, source_target_pairs={{0,2},{1,3},{2,0},{3,1},{4,6},{5,7},{6,4},{7,5},{8,10},{9,11},{10,... | collective-permute-start | bytes 442376 | tf_op jit(solution)/shard_map/ppermute | solution.py:27
  34.2 2.5 %collective-permute-start.11 = (bf16[4,16,1024]{2,1,0:T(8,128)(2,1)S(1)}, bf16[4,16,1024]{2,1,0:T(8,128)(2,1)S(1)}, u32[]{:S(2)}, u32[]{:S(2)}) collective-permute-start(bf16[4,16,1024]{2,1,0:T(8,128)(2,1)S(1)} %pad_maximum_fusion.refs_4_.after_ref), channel_id=1, source_target_pairs={{0,12},{1,13},{2,14},{3,15},{4,8},{5,9},{6,10},{7,11},{8,4},{9,5},... | collective-permute-start | bytes 393224 | tf_op jit(solution)/shard_map/ppermute | solution.py:27
  36.6 3.7 %collective-permute-done.11.refs_7_ = bf16[4,16,1024]{2,1,0:T(8,128)(2,1)S(1)} collective-permute-done((bf16[4,16,1024]{2,1,0:T(8,128)(2,1)S(1)}, bf16[4,16,1024]{2,1,0:T(8,128)(2,1)S(1)}, u32[]{:S(2)}, u32[]{:S(2)}) %collective-permute-start.11) | collective-permute-done | bytes 131104 | tf_op jit(solution)/shard_map/ppermute | solution.py:27
  48.7 2.9 %collective-permute-start.14 = (bf16[4,16,384]{2,1,0:T(8,128)(2,1)S(1)}, bf16[4,16,384]{2,1,0:T(8,128)(2,1)S(1)}, u32[]{:S(2)}, u32[]{:S(2)}) collective-permute-start(bf16[4,16,384]{2,1,0:T(8,128)(2,1)S(1)} %get-tuple-element.48), channel_id=1, source_target_pairs={{0,64},{16,80},{32,96},{48,112},{64,0},{80,16},{96,32},{112,48},{1... | collective-permute-start | bytes 147464 | tf_op jit(solution)/shard_map/ppermute | solution.py:23
  51.8 2.6 %collective-permute-done.14.refs_2_ = bf16[4,16,384]{2,1,0:T(8,128)(2,1)S(1)} collective-permute-done((bf16[4,16,384]{2,1,0:T(8,128)(2,1)S(1)}, bf16[4,16,384]{2,1,0:T(8,128)(2,1)S(1)}, u32[]{:S(2)}, u32[]{:S(2)}) %collective-permute-start.14) | collective-permute-done | bytes 49184 | tf_op jit(solution)/shard_map/ppermute | solution.py:23
  54.4 2.5 %collective-permute-done.15.refs_3_ = bf16[4,16,384]{2,1,0:T(8,128)(2,1)S(1)} collective-permute-done((bf16[4,16,384]{2,1,0:T(8,128)(2,1)S(1)}, bf16[4,16,384]{2,1,0:T(8,128)(2,1)S(1)}, u32[]{:S(2)}, u32[]{:S(2)}) %collective-permute-start.15) | collective-permute-done | bytes 49184 | tf_op jit(solution)/shard_map/ppermute | solution.py:23
  57.8 2.7 %collective-permute-start.17 = (bf16[8,16,384]{2,1,0:T(8,128)(2,1)S(1)}, bf16[8,16,384]{2,1,0:T(8,128)(2,1)S(1)}, u32[]{:S(2)}, u32[]{:S(2)}) collective-permute-start(bf16[8,16,384]{2,1,0:T(8,128)(2,1)S(1)} %get-tuple-element.52), channel_id=1, source_target_pairs={{0,8},{1,9},{2,10},{3,11},{4,12},{5,13},{6,14},{7,15},{8,0},{9,1},... | collective-permute-start | bytes 294920 | tf_op jit(solution)/shard_map/ppermute | solution.py:27
  67.0 3.5 %collective-permute-start.20 = (bf16[8,16,384]{2,1,0:T(8,128)(2,1)S(1)}, bf16[8,16,384]{2,1,0:T(8,128)(2,1)S(1)}, u32[]{:S(2)}, u32[]{:S(2)}) collective-permute-start(bf16[8,16,384]{2,1,0:T(8,128)(2,1)S(1)} %get-tuple-element.56), channel_id=1, source_target_pairs={{0,2},{1,3},{2,0},{3,1},{4,6},{5,7},{6,4},{7,5},{8,10},{9,11},{10,... | collective-permute-start | bytes 294920 | tf_op jit(solution)/shard_map/ppermute | solution.py:27
  71.7 2.4 %collective-permute-done.20.refs_2_ = bf16[8,16,384]{2,1,0:T(8,128)(2,1)S(1)} collective-permute-done((bf16[8,16,384]{2,1,0:T(8,128)(2,1)S(1)}, bf16[8,16,384]{2,1,0:T(8,128)(2,1)S(1)}, u32[]{:S(2)}, u32[]{:S(2)}) %collective-permute-start.20) | collective-permute-done | bytes 98336 | tf_op jit(solution)/shard_map/ppermute | solution.py:27
  78.8 3.0 %collective-permute-start.24 = (bf16[16,7680]{1,0:T(8,128)(2,1)S(1)}, bf16[16,7680]{1,0:T(8,128)(2,1)S(1)}, u32[]{:S(2)}, u32[]{:S(2)}) collective-permute-start(bf16[16,7680]{1,0:T(8,128)(2,1)S(1)} %get-tuple-element.61), channel_id=1, source_target_pairs={{0,96},{16,112},{32,64},{48,80},{64,32},{80,48},{96,0},{112,16},{1... | collective-permute-start | bytes 737288 | tf_op jit(solution)/shard_map/ppermute | solution.py:23
  84.0 2.4 %collective-permute-done.23.refs_2_ = bf16[16,7680]{1,0:T(8,128)(2,1)S(1)} collective-permute-done((bf16[16,7680]{1,0:T(8,128)(2,1)S(1)}, bf16[16,7680]{1,0:T(8,128)(2,1)S(1)}, u32[]{:S(2)}, u32[]{:S(2)}) %collective-permute-start.23) | collective-permute-done | bytes 245792 | tf_op jit(solution)/shard_map/ppermute | solution.py:23
  86.4 2.5 %collective-permute-done.24.refs_3_ = bf16[16,7680]{1,0:T(8,128)(2,1)S(1)} collective-permute-done((bf16[16,7680]{1,0:T(8,128)(2,1)S(1)}, bf16[16,7680]{1,0:T(8,128)(2,1)S(1)}, u32[]{:S(2)}, u32[]{:S(2)}) %collective-permute-start.24) | collective-permute-done | bytes 245792 | tf_op jit(solution)/shard_map/ppermute | solution.py:23
  93.5 5.1 %hidden_units.1 = (bf16[128,576]{1,0:T(8,128)(2,1)S(1)}, bf16[4,128,768]{2,1,0:T(8,128)(2,1)S(1)}) custom-call(s32[4]{0:T(128)S(1)} %copy-done.2, bf16[16,7680]{1,0:T(8,128)(2,1)S(1)} %get-tuple-element.58.refs_0_, bf16[16,7680]{1,0:T(8,128)(2,1)S(1)} %collective-permute-done.22.refs_1_, bf16[16,7680]{1,0:T(8,128)(2,1)S(1)} %collective-permute-done.23.refs_2_, ...), custom_call_target="tpu_custom_call" | custom-call | flops 2264924160 | bytes 23199744 | tf_op jit(solution)/shard_map/hidden_units/pallas_call | solution.py:32
  102.7 4.5 %collective-permute-start.31 = (bf16[128,768]{1,0:T(8,128)(2,1)S(1)}, bf16[128,768]{1,0:T(8,128)(2,1)S(1)}, u32[]{:S(2)}, u32[]{:S(2)}) collective-permute-start(bf16[128,768]{1,0:T(8,128)(2,1)S(1)} %get-tuple-element.66), channel_id=1, source_target_pairs={{0,64},{16,80},{32,96},{48,112},{64,0},{80,16},{96,32},{112,48},{1... | collective-permute-start | bytes 589832 | tf_op jit(solution)/shard_map/ppermute | solution.py:23
  110.4 6.3 %collective-permute-done.31.got2_ref = bf16[128,768]{1,0:T(8,128)(2,1)S(1)} collective-permute-done((bf16[128,768]{1,0:T(8,128)(2,1)S(1)}, bf16[128,768]{1,0:T(8,128)(2,1)S(1)}, u32[]{:S(2)}, u32[]{:S(2)}) %collective-permute-start.31) | collective-permute-done | bytes 196640 | tf_op jit(solution)/shard_map/ppermute | solution.py:23
  116.7 2.6 %collective-permute-done.32.got3_ref = bf16[128,768]{1,0:T(8,128)(2,1)S(1)} collective-permute-done((bf16[128,768]{1,0:T(8,128)(2,1)S(1)}, bf16[128,768]{1,0:T(8,128)(2,1)S(1)}, u32[]{:S(2)}, u32[]{:S(2)}) %collective-permute-start.32) | collective-permute-done | bytes 196640 | tf_op jit(solution)/shard_map/ppermute | solution.py:23
  120.1 3.5 %collective-permute-start.34 = (bf16[4,8,768]{2,1,0:T(8,128)(2,1)S(1)}, bf16[4,8,768]{2,1,0:T(8,128)(2,1)S(1)}, u32[]{:S(2)}, u32[]{:S(2)}) collective-permute-start(bf16[4,8,768]{2,1,0:T(8,128)(2,1)S(1)} %get-tuple-element.74), channel_id=1, source_target_pairs={{0,8},{1,9},{2,10},{3,11},{4,12},{5,13},{6,14},{7,15},{8,0},{9,1},... | collective-permute-start | bytes 147464 | tf_op jit(solution)/shard_map/ppermute | solution.py:27
  126.1 2.7 %collective-permute-done.35 = bf16[4,8,768]{2,1,0:T(8,128)(2,1)S(1)} collective-permute-done((bf16[4,8,768]{2,1,0:T(8,128)(2,1)S(1)}, bf16[4,8,768]{2,1,0:T(8,128)(2,1)S(1)}, u32[]{:S(2)}, u32[]{:S(2)}) %collective-permute-start.35) | collective-permute-done | bytes 49184 | tf_op jit(solution)/shard_map/ppermute | solution.py:27
  130.9 2.3 %collective-permute-start.36 = (bf16[4,8,768]{2,1,0:T(8,128)(2,1)S(1)}, bf16[4,8,768]{2,1,0:T(8,128)(2,1)S(1)}, u32[]{:S(2)}, u32[]{:S(2)}) collective-permute-start(bf16[4,8,768]{2,1,0:T(8,128)(2,1)S(1)} %pad_maximum_fusion.2), channel_id=1, source_target_pairs={{0,1},{1,0},{2,3},{3,2},{4,5},{5,4},{6,7},{7,6},{8,9},{9,8},{10,11... | collective-permute-start | bytes 147464 | tf_op jit(solution)/shard_map/ppermute | solution.py:27
  (104 shorter events, 58.8 us)
Async XLA Ops:
  5.8 5.7 %collective-permute-start.7 = (bf16[16,1024]{1,0:T(8,128)(2,1)}, bf16[16,1024]{1,0:T(8,128)(2,1)S(1)}, u32[]{:S(2)}, u32[]{:S(2)}) collective-permute-start(bf16[16,1024]{1,0:T(8,128)(2,1)} %get-tuple-element.43), channel_id=1, source_target_pairs={{0,2},{1,3},{2,0},{3,1},{4,6},{5,7},{6,4},{7,5},{8,10},{9,11},{10,... | collective-permute-start | bytes 98312 | tf_op jit(solution)/shard_map/ppermute | solution.py:27
  15.1 21.5 %collective-permute-start.10 = (bf16[4,16,1024]{2,1,0:T(8,128)(2,1)S(1)}, bf16[4,16,1024]{2,1,0:T(8,128)(2,1)S(1)}, u32[]{:S(2)}, u32[]{:S(2)}) collective-permute-start(bf16[4,16,1024]{2,1,0:T(8,128)(2,1)S(1)} %pad_maximum_fusion.refs_4_.after_ref), channel_id=1, source_target_pairs={{0,8},{1,9},{2,10},{3,11},{4,12},{5,13},{6,14},{7,15},{8,0},{9,1},... | collective-permute-start | bytes 393224 | tf_op jit(solution)/shard_map/ppermute | solution.py:27
  20.1 6.2 %collective-permute-start.1 = (bf16[16,2688]{1,0:T(8,128)(2,1)}, bf16[16,2688]{1,0:T(8,128)(2,1)S(1)}, u32[]{:S(2)}, u32[]{:S(2)}) collective-permute-start(bf16[16,2688]{1,0:T(8,128)(2,1)} %get-tuple-element.37), channel_id=1, source_target_pairs={{0,8},{1,9},{2,10},{3,11},{4,12},{5,13},{6,14},{7,15},{8,0},{9,1},... | collective-permute-start | bytes 258056 | tf_op jit(solution)/shard_map/ppermute | solution.py:27
  21.3 6.0 %collective-permute-start.2 = (bf16[16,2688]{1,0:T(8,128)(2,1)}, bf16[16,2688]{1,0:T(8,128)(2,1)S(1)}, u32[]{:S(2)}, u32[]{:S(2)}) collective-permute-start(bf16[16,2688]{1,0:T(8,128)(2,1)} %get-tuple-element.38), channel_id=1, source_target_pairs={{0,12},{1,13},{2,14},{3,15},{4,8},{5,9},{6,10},{7,11},{8,4},{9,5},... | collective-permute-start | bytes 258056 | tf_op jit(solution)/shard_map/ppermute | solution.py:27
  29.4 12.2 %collective-permute-start.3 = (bf16[4,16,1152]{2,1,0:T(8,128)(2,1)S(1)}, bf16[4,16,1152]{2,1,0:T(8,128)(2,1)S(1)}, u32[]{:S(2)}, u32[]{:S(2)}) collective-permute-start(bf16[4,16,1152]{2,1,0:T(8,128)(2,1)S(1)} %get-tuple-element.40), channel_id=1, source_target_pairs={{0,1},{1,0},{2,3},{3,2},{4,5},{5,4},{6,7},{7,6},{8,9},{9,8},{10,11... | collective-permute-start | bytes 442376 | tf_op jit(solution)/shard_map/ppermute | solution.py:27
  29.5 12.1 %collective-permute-start.4 = (bf16[4,16,1152]{2,1,0:T(8,128)(2,1)S(1)}, bf16[4,16,1152]{2,1,0:T(8,128)(2,1)S(1)}, u32[]{:S(2)}, u32[]{:S(2)}) collective-permute-start(bf16[4,16,1152]{2,1,0:T(8,128)(2,1)S(1)} %get-tuple-element.41), channel_id=1, source_target_pairs={{0,2},{1,3},{2,0},{3,1},{4,6},{5,7},{6,4},{7,5},{8,10},{9,11},{10,... | collective-permute-start | bytes 442376 | tf_op jit(solution)/shard_map/ppermute | solution.py:27
  33.0 8.7 %collective-permute-start.5 = (bf16[4,16,1152]{2,1,0:T(8,128)(2,1)S(1)}, bf16[4,16,1152]{2,1,0:T(8,128)(2,1)S(1)}, u32[]{:S(2)}, u32[]{:S(2)}) collective-permute-start(bf16[4,16,1152]{2,1,0:T(8,128)(2,1)S(1)} %get-tuple-element.42), channel_id=1, source_target_pairs={{0,3},{1,2},{2,1},{3,0},{4,7},{5,6},{6,5},{7,4},{8,11},{9,10},{10,... | collective-permute-start | bytes 442376 | tf_op jit(solution)/shard_map/ppermute | solution.py:27
  34.2 6.2 %collective-permute-start.11 = (bf16[4,16,1024]{2,1,0:T(8,128)(2,1)S(1)}, bf16[4,16,1024]{2,1,0:T(8,128)(2,1)S(1)}, u32[]{:S(2)}, u32[]{:S(2)}) collective-permute-start(bf16[4,16,1024]{2,1,0:T(8,128)(2,1)S(1)} %pad_maximum_fusion.refs_4_.after_ref), channel_id=1, source_target_pairs={{0,12},{1,13},{2,14},{3,15},{4,8},{5,9},{6,10},{7,11},{8,4},{9,5},... | collective-permute-start | bytes 393224 | tf_op jit(solution)/shard_map/ppermute | solution.py:27
  48.7 5.7 %collective-permute-start.14 = (bf16[4,16,384]{2,1,0:T(8,128)(2,1)S(1)}, bf16[4,16,384]{2,1,0:T(8,128)(2,1)S(1)}, u32[]{:S(2)}, u32[]{:S(2)}) collective-permute-start(bf16[4,16,384]{2,1,0:T(8,128)(2,1)S(1)} %get-tuple-element.48), channel_id=1, source_target_pairs={{0,64},{16,80},{32,96},{48,112},{64,0},{80,16},{96,32},{112,48},{1... | collective-permute-start | bytes 147464 | tf_op jit(solution)/shard_map/ppermute | solution.py:23
  57.8 6.4 %collective-permute-start.17 = (bf16[8,16,384]{2,1,0:T(8,128)(2,1)S(1)}, bf16[8,16,384]{2,1,0:T(8,128)(2,1)S(1)}, u32[]{:S(2)}, u32[]{:S(2)}) collective-permute-start(bf16[8,16,384]{2,1,0:T(8,128)(2,1)S(1)} %get-tuple-element.52), channel_id=1, source_target_pairs={{0,8},{1,9},{2,10},{3,11},{4,12},{5,13},{6,14},{7,15},{8,0},{9,1},... | collective-permute-start | bytes 294920 | tf_op jit(solution)/shard_map/ppermute | solution.py:27
  60.5 5.8 %collective-permute-start.18 = (bf16[8,16,384]{2,1,0:T(8,128)(2,1)S(1)}, bf16[8,16,384]{2,1,0:T(8,128)(2,1)S(1)}, u32[]{:S(2)}, u32[]{:S(2)}) collective-permute-start(bf16[8,16,384]{2,1,0:T(8,128)(2,1)S(1)} %get-tuple-element.53), channel_id=1, source_target_pairs={{0,12},{1,13},{2,14},{3,15},{4,8},{5,9},{6,10},{7,11},{8,4},{9,5},... | collective-permute-start | bytes 294920 | tf_op jit(solution)/shard_map/ppermute | solution.py:27
  67.0 7.1 %collective-permute-start.20 = (bf16[8,16,384]{2,1,0:T(8,128)(2,1)S(1)}, bf16[8,16,384]{2,1,0:T(8,128)(2,1)S(1)}, u32[]{:S(2)}, u32[]{:S(2)}) collective-permute-start(bf16[8,16,384]{2,1,0:T(8,128)(2,1)S(1)} %get-tuple-element.56), channel_id=1, source_target_pairs={{0,2},{1,3},{2,0},{3,1},{4,6},{5,7},{6,4},{7,5},{8,10},{9,11},{10,... | collective-permute-start | bytes 294920 | tf_op jit(solution)/shard_map/ppermute | solution.py:27
  70.5 5.8 %collective-permute-start.21 = (bf16[8,16,384]{2,1,0:T(8,128)(2,1)S(1)}, bf16[8,16,384]{2,1,0:T(8,128)(2,1)S(1)}, u32[]{:S(2)}, u32[]{:S(2)}) collective-permute-start(bf16[8,16,384]{2,1,0:T(8,128)(2,1)S(1)} %get-tuple-element.57), channel_id=1, source_target_pairs={{0,3},{1,2},{2,1},{3,0},{4,7},{5,6},{6,5},{7,4},{8,11},{9,10},{10,... | collective-permute-start | bytes 294920 | tf_op jit(solution)/shard_map/ppermute | solution.py:27
  77.1 6.9 %collective-permute-start.22 = (bf16[16,7680]{1,0:T(8,128)(2,1)S(1)}, bf16[16,7680]{1,0:T(8,128)(2,1)S(1)}, u32[]{:S(2)}, u32[]{:S(2)}) collective-permute-start(bf16[16,7680]{1,0:T(8,128)(2,1)S(1)} %get-tuple-element.59), channel_id=1, source_target_pairs={{0,32},{16,48},{32,0},{48,16},{64,96},{80,112},{96,64},{112,80},{1... | collective-permute-start | bytes 737288 | tf_op jit(solution)/shard_map/ppermute | solution.py:23
  77.2 9.2 %collective-permute-start.23 = (bf16[16,7680]{1,0:T(8,128)(2,1)S(1)}, bf16[16,7680]{1,0:T(8,128)(2,1)S(1)}, u32[]{:S(2)}, u32[]{:S(2)}) collective-permute-start(bf16[16,7680]{1,0:T(8,128)(2,1)S(1)} %get-tuple-element.60), channel_id=1, source_target_pairs={{0,64},{16,80},{32,96},{48,112},{64,0},{80,16},{96,32},{112,48},{1... | collective-permute-start | bytes 737288 | tf_op jit(solution)/shard_map/ppermute | solution.py:23
  78.8 10.0 %collective-permute-start.24 = (bf16[16,7680]{1,0:T(8,128)(2,1)S(1)}, bf16[16,7680]{1,0:T(8,128)(2,1)S(1)}, u32[]{:S(2)}, u32[]{:S(2)}) collective-permute-start(bf16[16,7680]{1,0:T(8,128)(2,1)S(1)} %get-tuple-element.61), channel_id=1, source_target_pairs={{0,96},{16,112},{32,64},{48,80},{64,32},{80,48},{96,0},{112,16},{1... | collective-permute-start | bytes 737288 | tf_op jit(solution)/shard_map/ppermute | solution.py:23
  81.9 11.6 %collective-permute-start.25 = (bf16[16,7680]{1,0:T(8,128)(2,1)S(1)}, bf16[16,7680]{1,0:T(8,128)(2,1)S(1)}, u32[]{:S(2)}, u32[]{:S(2)}) collective-permute-start(bf16[16,7680]{1,0:T(8,128)(2,1)S(1)} %get-tuple-element.58.refs_0_), channel_id=1, source_target_pairs={{0,16},{16,0},{32,48},{48,32},{64,80},{80,64},{96,112},{112,96},{1... | collective-permute-start | bytes 737288 | tf_op jit(solution)/shard_map/ppermute | solution.py:23
  84.0 9.5 %collective-permute-start.26 = (bf16[16,7680]{1,0:T(8,128)(2,1)S(1)}, bf16[16,7680]{1,0:T(8,128)(2,1)S(1)}, u32[]{:S(2)}, u32[]{:S(2)}) collective-permute-start(bf16[16,7680]{1,0:T(8,128)(2,1)S(1)} %collective-permute-done.22.refs_1_), channel_id=1, source_target_pairs={{0,16},{16,0},{32,48},{48,32},{64,80},{80,64},{96,112},{112,96},{1... | collective-permute-start | bytes 737288 | tf_op jit(solution)/shard_map/ppermute | solution.py:23
  86.4 7.2 %collective-permute-start.27 = (bf16[16,7680]{1,0:T(8,128)(2,1)S(1)}, bf16[16,7680]{1,0:T(8,128)(2,1)S(1)}, u32[]{:S(2)}, u32[]{:S(2)}) collective-permute-start(bf16[16,7680]{1,0:T(8,128)(2,1)S(1)} %collective-permute-done.23.refs_2_), channel_id=1, source_target_pairs={{0,16},{16,0},{32,48},{48,32},{64,80},{80,64},{96,112},{112,96},{1... | collective-permute-start | bytes 737288 | tf_op jit(solution)/shard_map/ppermute | solution.py:23
  102.6 7.8 %collective-permute-start.30 = (bf16[128,768]{1,0:T(8,128)(2,1)S(1)}, bf16[128,768]{1,0:T(8,128)(2,1)S(1)}, u32[]{:S(2)}, u32[]{:S(2)}) collective-permute-start(bf16[128,768]{1,0:T(8,128)(2,1)S(1)} %get-tuple-element.65), channel_id=1, source_target_pairs={{0,32},{16,48},{32,0},{48,16},{64,96},{80,112},{96,64},{112,80},{1... | collective-permute-start | bytes 589832 | tf_op jit(solution)/shard_map/ppermute | solution.py:23
  102.7 14.0 %collective-permute-start.31 = (bf16[128,768]{1,0:T(8,128)(2,1)S(1)}, bf16[128,768]{1,0:T(8,128)(2,1)S(1)}, u32[]{:S(2)}, u32[]{:S(2)}) collective-permute-start(bf16[128,768]{1,0:T(8,128)(2,1)S(1)} %get-tuple-element.66), channel_id=1, source_target_pairs={{0,64},{16,80},{32,96},{48,112},{64,0},{80,16},{96,32},{112,48},{1... | collective-permute-start | bytes 589832 | tf_op jit(solution)/shard_map/ppermute | solution.py:23
  107.1 12.1 %collective-permute-start.32 = (bf16[128,768]{1,0:T(8,128)(2,1)S(1)}, bf16[128,768]{1,0:T(8,128)(2,1)S(1)}, u32[]{:S(2)}, u32[]{:S(2)}) collective-permute-start(bf16[128,768]{1,0:T(8,128)(2,1)S(1)} %get-tuple-element.67), channel_id=1, source_target_pairs={{0,96},{16,112},{32,64},{48,80},{64,32},{80,48},{96,0},{112,16},{1... | collective-permute-start | bytes 589832 | tf_op jit(solution)/shard_map/ppermute | solution.py:23
  120.1 6.1 %collective-permute-start.34 = (bf16[4,8,768]{2,1,0:T(8,128)(2,1)S(1)}, bf16[4,8,768]{2,1,0:T(8,128)(2,1)S(1)}, u32[]{:S(2)}, u32[]{:S(2)}) collective-permute-start(bf16[4,8,768]{2,1,0:T(8,128)(2,1)S(1)} %get-tuple-element.74), channel_id=1, source_target_pairs={{0,8},{1,9},{2,10},{3,11},{4,12},{5,13},{6,14},{7,15},{8,0},{9,1},... | collective-permute-start | bytes 147464 | tf_op jit(solution)/shard_map/ppermute | solution.py:27
  130.1 5.7 %collective-permute-start.37 = (bf16[4,8,768]{2,1,0:T(8,128)(2,1)S(1)}, bf16[4,8,768]{2,1,0:T(8,128)(2,1)S(1)}, u32[]{:S(2)}, u32[]{:S(2)}) collective-permute-start(bf16[4,8,768]{2,1,0:T(8,128)(2,1)S(1)} %pad_maximum_fusion.3), channel_id=1, source_target_pairs={{0,2},{1,3},{2,0},{3,1},{4,6},{5,7},{6,4},{7,5},{8,10},{9,11},{10,... | collective-permute-start | bytes 147464 | tf_op jit(solution)/shard_map/ppermute | solution.py:27
  (26 other events, 329.9 us)

commit v5 on v4

v5 whole, which is shorter than its diff:
```python
import functools

import jax
import jax.numpy as jnp
from jax import lax
from jax.experimental import pallas as pl
from jax.experimental.pallas import tpu as pltpu
from jax.sharding import PartitionSpec as P

STEPS = 4
ROWS = 8
EPS = 1e-06
F32 = jnp.float32
BF16 = jnp.bfloat16
MIB = 1 << 20


def vmem_params(mib):
    return pltpu.CompilerParams(vmem_limit_bytes=mib * MIB)


def over(axis, value, bits):
    return lax.ppermute(value, axis, [(i, i ^ bits) for i in range(lax.axis_size(axis))])


def exchange(value, axes):
    return lax.all_to_all(value, axes, split_axis=0, concat_axis=0, tiled=True)


def call(kernel, name, out_shape, place, *arrays, flops=0, limit=16, scratch=()):
    moved = sum(a.size * a.dtype.itemsize for a in arrays)
    result = pl.pallas_call(
        kernel,
        out_shape=out_shape,
        in_specs=[pl.BlockSpec(memory_space=pltpu.SMEM)]
        + [pl.BlockSpec(memory_space=pltpu.VMEM)] * len(arrays),
        out_specs=jax.tree.map(lambda _: pl.BlockSpec(memory_space=pltpu.VMEM), out_shape),
        scratch_shapes=scratch,
        compiler_params=vmem_params(limit),
        cost_estimate=pl.CostEstimate(flops=flops, bytes_accessed=moved, transcendentals=0),
        name=name,
    )(place, *arrays)
    return list(result) if isinstance(out_shape, list) else result


def xor(a, b):
    return lax.bitwise_xor(a, b)


def lanes_from(start, size):
    return pl.ds(pl.multiple_of(start, 128), size)


def columns_of(table):
    rows = lax.broadcasted_iota(jnp.int32, (ROWS, ROWS), 0)
    lanes = lax.broadcasted_iota(jnp.int32, (ROWS, ROWS), 1)
    return lax.dot_general(
        (rows == lanes).astype(F32),
        table,
        (((1,), (1,)), ((), ())),
        precision=lax.Precision.HIGHEST,
        preferred_element_type=F32,
    )


def widened(pair):
    lane = lax.broadcasted_iota(jnp.int32, (pair.shape[0], 128), 1)
    return jnp.where(lane == 0, pair[:, :1], jnp.where(lane == 1, pair[:, 1:2], 0.0))


def bf16_parts(value, count):
    parts = []
    for _ in range(count - 1):
        parts.append(value.astype(BF16))
        value = value - parts[-1].astype(F32)
    return parts + [value.astype(BF16)]


def readout_kernel(
    place_ref, decay_ref, routes_ref, hidden_ref, qkv_ref, state_ref, gain_ref, out_ref
):
    c = place_ref[2]
    cols = hidden_ref.shape[2] // 16
    depth = out_ref.shape[2] - 256

    @pl.when(pl.program_id(0) == 0)
    def _():
        names = [columns_of(routes_ref[2 * c + t].astype(F32)) for t in range(2)]
        names = widened(jnp.concatenate(names, axis=0)).astype(BF16)
        for i in range(16):
            at = slice(i * cols, (i + 1) * cols)
            rows = [hidden_ref[2 * c + t, :, at].astype(F32) for t in range(2)]
            rows = jnp.concatenate(rows, axis=0).astype(BF16)
            out_ref[i, :16, depth:] = rows[:, :256]
            out_ref[i, 16:, depth : depth + 128] = rows[:, 256:]
            out_ref[i, 16:, depth + 128 :] = names

    n, size = STEPS * ROWS, state_ref.shape[2]
    heads = state_ref.shape[1]
    row = lax.broadcasted_iota(jnp.int32, (n, size), 0)
    row_in = row % ROWS
    row_t = lax.broadcasted_iota(jnp.int32, (n, n), 0)
    row_s = lax.broadcasted_iota(jnp.int32, (n, n), 1)
    for h in range(heads):
        lanes = slice(h * size, (h + 1) * size)
        q, k, v = [
            qkv_ref[:, i, :, lanes].astype(F32).reshape(n, size).astype(BF16) for i in range(3)
        ]
        q_twice = jnp.concatenate([q, q], axis=1)
        carried = jnp.zeros((n, size), F32)
        for pair in range(ROWS // 2):
            wide = jnp.concatenate([state_ref[2 * pair, h], state_ref[2 * pair + 1, h]], axis=1)
            both = jnp.dot(
                q_twice, jnp.concatenate(bf16_parts(wide, 2), axis=0), preferred_element_type=F32
            )
            carried = jnp.where(row_in == 2 * pair, both[:, :size], carried)
            carried = jnp.where(row_in == 2 * pair + 1, both[:, size:], carried)
        decay = [decay_ref[t, pl.program_id(0) * heads + h] for t in range(STEPS)]
        run = decay[0]
        first = jnp.full((n, size), run, F32)
        for t in range(1, STEPS):
            run = run * decay[t]
            first = jnp.where(row // ROWS == t, run, first)
        mix = jnp.zeros((n, n), F32)
        for t in range(STEPS):
            run = None
            for s in range(t, -1, -1):
                here = row_t - row_s == (t - s) * ROWS
                mix = jnp.where(here & (row_s // ROWS == s), 1.0 if run is None else run, mix)
                run = decay[s] if run is None else run * decay[s]
        scores = lax.dot_general(q, k, (((1,), (1,)), ((), ())), preferred_element_type=F32)
        o = carried * first + jnp.dot(
            jnp.concatenate(bf16_parts(scores * mix, 2), axis=1),
            jnp.concatenate([v, v], axis=0),
            preferred_element_type=F32,
        )
        o = o * lax.rsqrt(jnp.mean(o * o, axis=-1, keepdims=True) + EPS) * gain_ref[:, lanes]
        o = o.astype(BF16)
        at = lanes_from((pl.program_id(0) * heads + h) * size, size)
        for i in range(16):
            out_ref[i, :, at] = o


def readouts(place, step_qkv, decay, state, attn_gain, hidden_in, routes):
    heads, size = state.shape[1], state.shape[2]
    at_once = min(heads, 4)
    n = STEPS * ROWS
    packed = heads * size + 256
    return pl.pallas_call(
        readout_kernel,
        out_shape=jax.ShapeDtypeStruct((16, n, packed), BF16),
        grid=(heads // at_once,),
        in_specs=[
            pl.BlockSpec(memory_space=pltpu.SMEM),
            pl.BlockSpec(memory_space=pltpu.SMEM),
            pl.BlockSpec((STEPS, 2, ROWS), lambda i: (0, 0, 0)),
            pl.BlockSpec(hidden_in.shape, lambda i: (0, 0, 0)),
            pl.BlockSpec((STEPS, 3, ROWS, at_once * size), lambda i: (0, 0, 0, i)),
            pl.BlockSpec((ROWS, at_once, size, size), lambda i: (0, i, 0, 0)),
            pl.BlockSpec((1, at_once * size), lambda i: (0, i)),
        ],
        out_specs=pl.BlockSpec((16, n, packed), lambda i: (0, 0, 0)),
        compiler_params=vmem_params(56),
        cost_estimate=pl.CostEstimate(
            flops=2 * STEPS * ROWS * ROWS * heads * size * size * 2,
            bytes_accessed=state.size * 4,
            transcendentals=0,
        ),
        name="readout",
    )(
        place,
        decay,
        routes.transpose(0, 2, 1),
        hidden_in,
        step_qkv.transpose(0, 2, 1, 3),
        state,
        attn_gain.reshape(1, -1),
    )


def project_kernel(place_ref, got_ref, weight_ref, mine_ref, other_ref):
    c = place_ref[2]
    depth = weight_ref.shape[0]
    for part in range(2):
        rows = got_ref[8 * part : 8 * part + 8, :, :depth].reshape(256, depth)
        out = jnp.dot(rows, weight_ref[...], preferred_element_type=F32).astype(BF16)
        for i in range(8):
            a = out[32 * i : 32 * i + 16]
            b = out[32 * i + 16 : 32 * i + 32]
            mine_ref[8 * part + i] = jnp.where(c == 0, a, b)
            other_ref[8 * part + i] = jnp.where(c == 0, b, a)


def project(place, got, weight):
    out = [jax.ShapeDtypeStruct((16, 16, weight.shape[1]), BF16)] * 2
    return call(project_kernel, "project", out, place, got, weight, flops=1024 * weight.size)


def by_y_kernel(place_ref, mine_ref, got_ref, *out_refs):
    y = place_ref[1]
    for k, ref in enumerate(out_refs):
        for x in range(4):
            i = xor(y, k) * 4 + x
            ref[x] = (mine_ref[i].astype(F32) + got_ref[i].astype(F32)).astype(BF16)


def sums_by_y(place, mine, got):
    out = [jax.ShapeDtypeStruct((4,) + mine.shape[1:], BF16)] * 4
    return call(by_y_kernel, "sums_by_y", out, place, mine, got)


def attend_kernel(place_ref, got_ref, *refs):
    sum_refs, out_ref = refs[:4], refs[4]
    y = place_ref[1]
    cols = out_ref.shape[2]
    depth = got_ref.shape[2] - 256
    rows, names = [], []
    for x in range(4):
        i = y * 4 + x
        tail = got_ref[i, 16:, depth:].astype(F32)
        names.append(tail[:, 128:])
        total = jnp.concatenate([got_ref[i, :16, depth:].astype(F32), tail[:, :128]], axis=1)
        for ref in sum_refs:
            total += ref[x].astype(F32)
        rows.append(total.astype(BF16))
        for z in range(4):
            out_ref[4 * z + x, 16:] = rows[x]
    rows = jnp.concatenate(rows, axis=0)
    n = rows.shape[0]
    names = jnp.concatenate(names, axis=0)
    across = names.T
    down_i = lax.broadcasted_iota(jnp.int32, (n, n), 0)
    over_i = lax.broadcasted_iota(jnp.int32, (n, n), 1)
    earlier = (down_i // ROWS == over_i // ROWS) & (down_i < over_i)
    slot = lax.broadcasted_iota(jnp.int32, (256, n), 0)
    lane = lax.broadcasted_iota(jnp.int32, (1, n), 1)
    base = lane // 16 * 4 + lane // ROWS % 2 * 2
    select = jnp.zeros((256, n), F32)
    for j in range(2):
        mine = across[j : j + 1, :]
        rank = jnp.zeros((1, n), F32)
        for other in range(2):
            same = (names[:, other : other + 1] == mine) & earlier
            rank += jnp.sum(same.astype(F32), axis=0, keepdims=True)
        target = mine.astype(jnp.int32) * 16 + base + rank.astype(jnp.int32)
        select += (slot == target).astype(F32)
    sent = jnp.dot(select.astype(BF16), rows, preferred_element_type=F32).astype(BF16)
    for i in range(16):
        out_ref[i, :16] = sent[16 * i : 16 * i + 16]


def attend(place, got, sums):
    out = jax.ShapeDtypeStruct((16, 32, sums[0].shape[2]), BF16)
    return call(attend_kernel, "attend", out, place, got, *sums, flops=1 << 23)


def norm_kernel(place_ref, gain_ref, got_ref, *out_refs):
    y = place_ref[1]
    cols = got_ref.shape[2]
    total = jnp.zeros((16, cols), F32)
    for i in range(16):
        value = got_ref[i, :16].astype(F32)
        total += value * value
    mean = jnp.sum(total, axis=-1, keepdims=True) / (16 * cols)
    scale = lax.rsqrt(mean + EPS)
    for i in range(16):
        at = slice(i * cols, (i + 1) * cols)
        value = (got_ref[i, :16].astype(F32) * scale * gain_ref[:, at]).astype(BF16)
        for out_ref in out_refs:
            out_ref[:, at] = value
    for k, out_ref in enumerate(out_refs):
        for x in range(4):
            at = slice((16 + x) * cols, (17 + x) * cols)
            out_ref[:, at] = got_ref[xor(y, k) * 4 + x, 16:]


def norm(place, gain, got):
    out = [jax.ShapeDtypeStruct((16, 20 * got.shape[2]), BF16)] * 4
    return call(norm_kernel, "norm", out, place, gain.reshape(1, -1), got)


def owned_kernel(place_ref, *refs):
    own_refs, other_refs, out_ref = refs[:4], refs[4:8], refs[8]
    z, y, c = place_ref[0], place_ref[1], place_ref[2]
    share = out_ref.shape[1]
    start = own_refs[0].shape[1] - 2 * share
    at = lanes_from(start + c * share, share)
    for k in range(4):

        @pl.when(xor(z, y) == k)
        def _():
            out_ref[pl.ds(pl.multiple_of(16 * c, 16), 16), :] = own_refs[k][:, at]
            out_ref[pl.ds(pl.multiple_of(16 - 16 * c, 16), 16), :] = other_refs[k][:, at]


def owned(place, by_y, by_core, share):
    out = jax.ShapeDtypeStruct((STEPS * ROWS, share), BF16)
    return call(owned_kernel, "owned", out, place, *by_y, *by_core)


def fetch_kernel(after_ref, *refs):
    in_refs, out_refs, done_ref, sems = refs[:3], refs[3:6], refs[6], refs[7]
    copies = [pltpu.make_async_copy(a, b, sems.at[i]) for i, (a, b) in enumerate(zip(in_refs, out_refs))]
    for copy in copies:
        copy.start()
    done_ref[...] = jnp.zeros_like(done_ref)
    for copy in copies:
        copy.wait()


def fetch(after, *weights):
    return pl.pallas_call(
        fetch_kernel,
        out_shape=[pltpu.VMEM(w.shape, w.dtype) for w in weights]
        + [jax.ShapeDtypeStruct((8, 128), F32)],
        in_specs=[pl.BlockSpec(memory_space=pl.ANY)]
        + [pl.BlockSpec(memory_space=pltpu.HBM)] * len(weights),
        out_specs=[pl.BlockSpec(memory_space=pltpu.VMEM)] * (len(weights) + 1),
        scratch_shapes=[pltpu.SemaphoreType.DMA((len(weights),))],
        compiler_params=vmem_params(36),
        cost_estimate=pl.CostEstimate(
            flops=0, bytes_accessed=sum(2 * w.size for w in weights), transcendentals=0
        ),
        name="fetch",
    )(after, *weights)


def hidden_kernel(place_ref, *refs):
    x_refs, (gate_ref, up_ref, down_ref, _, hidden_ref, theirs_ref) = refs[:8], refs[8:]
    share = theirs_ref.shape[2]
    y, c = place_ref[1], place_ref[2]
    x = jnp.concatenate([r[:, : gate_ref.shape[1]] for r in x_refs], axis=0)
    across = (((1,), (1,)), ((), ()))
    gate = lax.dot_general(gate_ref[...], x, across, preferred_element_type=F32)
    up = lax.dot_general(up_ref[...], x, across, preferred_element_type=F32)
    hidden = (gate / (1.0 + jnp.exp(-gate)) * up).T.astype(BF16)
    hidden_ref[...] = hidden
    for k in range(4):
        block = lax.bitwise_xor(y, k) * 2 + (1 - c)
        at = pl.ds(pl.multiple_of(block * share, 128), share)
        theirs_ref[k] = jnp.dot(hidden, down_ref[:, at], preferred_element_type=F32).astype(BF16)


def hidden_units(place, pieces, gate, up, down_weight, done, share):
    units = gate.shape[0]
    rows = sum(p.shape[0] for p in pieces)
    out = [
        jax.ShapeDtypeStruct((rows, units), BF16),
        jax.ShapeDtypeStruct((4, rows, share), BF16),
    ]
    flops = 5 * rows * gate.size
    arrays = (*pieces, gate, up, down_weight, done)
    return call(hidden_kernel, "hidden_units", out, place, *arrays, flops=flops)


def down_kernel(place_ref, hidden_ref, down_ref, theirs_ref, out_ref):
    share = out_ref.shape[2]
    y, c = place_ref[1], place_ref[2]
    half = hidden_ref.shape[0] // 2
    for k in range(4):
        column = xor(y, k)
        at = lanes_from((column * 2 + c) * share, share)
        ours = jnp.dot(hidden_ref[...], down_ref[:, at], preferred_element_type=F32)
        same = ours[:half] + theirs_ref[k, half:].astype(F32)
        flip = ours[half:] + theirs_ref[k, :half].astype(F32)
        low = jnp.where(c == 0, same, flip)
        high = jnp.where(c == 0, flip, same)
        for ky in range(4):
            for x in range(4):
                rows = slice(16 * ky + 4 * x, 16 * ky + 4 * x + 4)
                block = jnp.concatenate([low[rows], high[rows]], axis=0)
                out_ref[column * 16 + xor(y, ky) * 4 + x] = block.astype(BF16)


def down(place, hidden, weight, theirs):
    out = jax.ShapeDtypeStruct((64, 8, theirs.shape[2]), BF16)
    flops = hidden.shape[0] * weight.size
    return call(down_kernel, "down", out, place, hidden, weight, theirs, flops=flops)


def mix_kernel(place_ref, routes_ref, weights_ref, back_ref, out_ref):
    n = STEPS * ROWS
    names = [columns_of(routes_ref[t].astype(F32)) for t in range(STEPS)]
    names = widened(jnp.concatenate(names, axis=0))
    weights = [columns_of(weights_ref[t]) for t in range(STEPS)]
    weights = jnp.concatenate(weights, axis=0)
    down_i = lax.broadcasted_iota(jnp.int32, (n, n), 0)
    over_i = lax.broadcasted_iota(jnp.int32, (n, n), 1)
    earlier = (down_i // ROWS == over_i // ROWS) & (over_i < down_i)
    across = names.T
    slot = lax.broadcasted_iota(jnp.int32, (n, 128), 1)
    step = lax.broadcasted_iota(jnp.int32, (n, 1), 0) // ROWS
    mix = jnp.zeros((n, 128), F32)
    for j in range(2):
        mine = names[:, j : j + 1]
        rank = jnp.zeros((n, 1), F32)
        for other in range(2):
            same = (across[other : other + 1, :] == mine) & earlier
            rank += jnp.sum(same.astype(F32), axis=1, keepdims=True)
        target = mine.astype(jnp.int32) * 8 + 2 * step + rank.astype(jnp.int32)
        mix += jnp.where(slot == target, weights[:, j : j + 1], 0.0)
    back = back_ref[...].astype(F32)
    back = (back[:16] + back[16:32]) + (back[32:48] + back[48:])
    back = back.reshape(128, back.shape[2]).astype(BF16)
    out_ref[...] = jnp.dot(
        jnp.concatenate(bf16_parts(mix, 3), axis=1),
        jnp.concatenate([back] * 3, axis=0),
        preferred_element_type=F32,
    ).astype(BF16)


def mixed_rows(place, routes, weights, back):
    out = jax.ShapeDtypeStruct((STEPS * ROWS, back.shape[2]), BF16)
    arrays = (routes.transpose(0, 2, 1), weights.transpose(0, 2, 1), back)
    return call(mix_kernel, "mix", out, place, *arrays, flops=1 << 24)


def shards(
    hidden_in,
    step_qkv,
    decay_rates,
    kv_state,
    attn_gain,
    out_proj,
    ffn_gain,
    routes,
    route_weights,
    w_gate,
    w_up,
    w_down,
):
    share = hidden_in.shape[2] // 8
    place = jnp.stack([lax.axis_index(axis) for axis in ("z", "y", "c")]).astype(jnp.int32)

    sent = readouts(place, step_qkv, decay_rates, kv_state, attn_gain, hidden_in, routes)
    got = exchange(sent, ("z", "x"))

    mine, other = project(place, got, out_proj)
    sums = sums_by_y(place, mine, over("c", other, 1))
    sums = sums[:1] + [over("y", sums[k], k) for k in (1, 2, 3)]

    pieces = norm(place, ffn_gain, exchange(attend(place, got, sums), ("z", "x")))
    by_y = pieces[:1] + [over("y", pieces[k], k) for k in (1, 2, 3)]
    gate, up, down_weight, done = fetch(
        pieces[1], w_gate[0].swapaxes(0, 1), w_up[0].swapaxes(0, 1), w_down[0]
    )
    by_y, done = lax.optimization_barrier((by_y, done))
    by_core = [over("c", piece, 1) for piece in by_y]
    attended = owned(place, by_y, by_core, share)

    hidden, theirs = hidden_units(place, by_y + by_core, gate, up, down_weight, done, share)
    sums = down(place, hidden, down_weight, over("c", theirs, 1))

    mixed = mixed_rows(place, routes, route_weights, exchange(sums, ("y", "z", "x")))
    return attended.reshape(STEPS, ROWS, share), mixed.reshape(STEPS, ROWS, share)


def solution(mesh):
    exp, head = ("z", "x"), ("y", "c")
    return jax.shard_map(
        shards,
        mesh=jax.sharding.Mesh(mesh.devices.reshape(4, 2, 4, 4), head + exp),
        in_specs=(
            P(None, exp, None),
            P(None, exp, None, head),
            P(None, head),
            P(exp, head, None, None),
            P(head),
            P(head, exp),
            P(),
            P(None, exp, None),
            P(None, exp, None),
            P(exp, None, head),
            P(exp, None, head),
            P(exp, head, None),
        ),
        out_specs=(P(None, exp, head), P(None, exp, head)),
        check_vma=False,
    )
```

time: 138 us -> 110 us (0.80)
  blocking collectives: 0 us -> 40.2 us
  starting transfers between devices: 53.9 us -> 14.3 us
  waiting for transfers between devices: 53.8 us -> 26.2 us
  local copies, waits for them, and re-layouts: 5.84 us -> 0.76 us
  Pallas kernels: 21.7 us -> 26.3 us
    ppermute x39 -> x12, starting transfers between devices: 53.9 us -> 9.7 us  [over(): lax.ppermute(value, axis, [(i, i ^ bits) for i in range(lax.axis_size(axi...]
    ppermute x39 -> x12, waiting for transfers between devices: 53.8 us -> 10.6 us  [over(): lax.ppermute(value, axis, [(i, i ^ bits) for i in range(lax.axis_size(axi...]
    all_to_all x0 -> x2, blocking collectives: none -> 40.2 us  [exchange(): return lax.all_to_all(value, axes, split_axis=0, concat_axis=0, tiled=True)]
    all_to_all x0 -> x1, waiting for transfers between devices: none -> 15.5 us  [exchange(): return lax.all_to_all(value, axes, split_axis=0, concat_axis=0, tiled=True)]
    pallas_call x4 -> x2, Pallas kernels: 5.94 us -> 12.3 us  [the longest x1 7.65 us: fetch(): pl.pallas_call(fetch_kernel, out_shape=[pltpu.VMEM(w.shape, w.dtype) for...]
    unnamed x22 -> x34, local copies, waits for them, and re-layouts: 5.81 us -> 0.76 us
    all_to_all x0 -> x1, starting transfers between devices: none -> 4.64 us  [exchange(): return lax.all_to_all(value, axes, split_axis=0, concat_axis=0, tiled=True)]
    pallas_call x11 -> x8, Pallas kernels: 15.7 us -> 14 us  [call(): pl.pallas_call(kernel, out_shape=out_shape, in_specs=[pl.BlockSpec(memory...]
  transfers between devices with their start and end apart: 39 -> 13, of which waited for: 25 -> 10; matrix products, arithmetic and copies ran while one was open for 0% -> 0% of each run, Pallas kernels for 2% -> 8%
where the time goes in v5:
time: 110 us; the launch traced here: 109 us
  blocking collectives  40.2 us (37%)
  Pallas kernels  26.3 us (24%)
  waiting for transfers between devices  26.2 us (24%)
  starting transfers between devices  14.3 us (13%)
    all_to_all x2, blocking collectives, exchange(): return lax.all_to_all(value, axes, split_axis=0, concat_axis=0, tiled=True)  40.2 us
    all_to_all x1, waiting for transfers between devices, exchange(): return lax.all_to_all(value, axes, split_axis=0, concat_axis=0, tiled=True)  15.5 us
    pallas_call x8, Pallas kernels, call(): pl.pallas_call(kernel, out_shape=out_shape, in_specs=[pl.BlockSpec(memory...  14 us
    ppermute x12, waiting for transfers between devices, over(): lax.ppermute(value, axis, [(i, i ^ bits) for i in range(lax.axis_size(axi...  10.6 us
    ppermute x12, starting transfers between devices, over(): lax.ppermute(value, axis, [(i, i ^ bits) for i in range(lax.axis_size(axi...  9.7 us
    pallas_call x1, Pallas kernels, fetch(): pl.pallas_call(fetch_kernel, out_shape=[pltpu.VMEM(w.shape, w.dtype) for...  7.65 us
    all_to_all x1, starting transfers between devices, exchange(): return lax.all_to_all(value, axes, split_axis=0, concat_axis=0, tiled=True)  4.64 us
    pallas_call x1, Pallas kernels, readouts(): pl.pallas_call(readout_kernel, out_shape=jax.ShapeDtypeStruct((16, n, pac...  4.61 us
  transfers between devices with their start and end apart: 13, of which 10 were waited for; matrix products, arithmetic and copies ran while one was open for 0% of the time, Pallas kernels for 8%

profile of v5, /device:TPU:0, one launch (start us, length us, event | category | flops | bytes accessed | tf_op | source)
XLA Modules:
  0.0 109.2 jit_solution(11765059936663555526)
XLA Ops:
  0.7 0.6 pad_add_fusion.place_ref
  1.2 4.6 %readout.1 = bf16[16,32,1280]{2,1,0:T(8,128)(2,1)} custom-call(s32[3]{0:T(128)} %pad_add_fusion.place_ref, f32[4,8]{1,0:T(4,128)} %decay_ref.1, s32[4,2,8]{2,1,0:T(2,128)} %bitcast.18, bf16[4,8,6144]{2,1,0:T(8,128)(2,1)} %hidden_ref.1, bf16[4,3,8,1024]{3,2,1,0:T(8,128)(2,1)} %bitcast.24, f32[8,8,128,128]{3,2,1,0:T(8,128)} %state_ref.1, f32[1,1024]{1,0:T(1,128)} %bitcast.27), custom_call_target="tpu_custom_call" | custom-call | flops 134217728 | bytes 4194304 | tf_op jit(solution)/shard_map/readout/pallas_call | solution.py:149
  5.8 27.9 %all_to_all.15.got_ref = bf16[16,32,1280]{2,1,0:T(8,128)(2,1)S(1)} all-to-all(bf16[16,32,1280]{2,1,0:T(8,128)(2,1)} %readout.1), channel_id=1, replica_groups=mesh['y'=4,'c'=2,'z'=4,'x'=4] {'z','x'}, dimensions={0} | all-to-all | bytes 2621440 | tf_op jit(solution)/shard_map/all_to_all | solution.py:27
  33.8 1.3 %project.1 = (bf16[16,16,384]{2,1,0:T(8,128)(2,1)S(1)}, bf16[16,16,384]{2,1,0:T(8,128)(2,1)S(1)}) custom-call(s32[3]{0:T(128)S(1)} %copy-done.10, bf16[16,32,1280]{2,1,0:T(8,128)(2,1)S(1)} %all_to_all.15.got_ref, bf16[1024,384]{1,0:T(8,128)(2,1)S(1)} %copy-done.8), custom_call_target="tpu_custom_call" | custom-call | flops 402653184 | bytes 2097152 | tf_op jit(solution)/shard_map/project/pallas_call | solution.py:32
  35.1 1.4 %collective-permute-done.got_ref = bf16[16,16,384]{2,1,0:T(8,128)(2,1)S(1)} collective-permute-done((bf16[16,16,384]{2,1,0:T(8,128)(2,1)S(1)}, bf16[16,16,384]{2,1,0:T(8,128)(2,1)S(1)}, u32[]{:S(2)}, u32[]{:S(2)}) %collective-permute-start) | collective-permute-done | bytes 196640 | tf_op jit(solution)/shard_map/ppermute | solution.py:23
  36.6 0.6 sums_by_y.1
  37.2 1.7 %collective-permute-start.1 = (bf16[4,16,384]{2,1,0:T(8,128)(2,1)S(1)}, bf16[4,16,384]{2,1,0:T(8,128)(2,1)S(1)}, u32[]{:S(2)}, u32[]{:S(2)}) collective-permute-start(bf16[4,16,384]{2,1,0:T(8,128)(2,1)S(1)} %get-tuple-element.26), channel_id=1, source_target_pairs={{0,32},{32,0},{64,96},{96,64},{1,33},{33,1},{65,97},{97,65},{2,34}... | collective-permute-start | bytes 147464 | tf_op jit(solution)/shard_map/ppermute | solution.py:23
  38.8 2.9 %collective-permute-start.2 = (bf16[4,16,384]{2,1,0:T(8,128)(2,1)S(1)}, bf16[4,16,384]{2,1,0:T(8,128)(2,1)S(1)}, u32[]{:S(2)}, u32[]{:S(2)}) collective-permute-start(bf16[4,16,384]{2,1,0:T(8,128)(2,1)S(1)} %get-tuple-element.27), channel_id=1, source_target_pairs={{0,64},{32,96},{64,0},{96,32},{1,65},{33,97},{65,1},{97,33},{2,66}... | collective-permute-start | bytes 147464 | tf_op jit(solution)/shard_map/ppermute | solution.py:23
  41.9 2.6 %collective-permute-done.2.refs_2_ = bf16[4,16,384]{2,1,0:T(8,128)(2,1)S(1)} collective-permute-done((bf16[4,16,384]{2,1,0:T(8,128)(2,1)S(1)}, bf16[4,16,384]{2,1,0:T(8,128)(2,1)S(1)}, u32[]{:S(2)}, u32[]{:S(2)}) %collective-permute-start.2) | collective-permute-done | bytes 49184 | tf_op jit(solution)/shard_map/ppermute | solution.py:23
  44.5 2.5 %collective-permute-done.3.refs_3_ = bf16[4,16,384]{2,1,0:T(8,128)(2,1)S(1)} collective-permute-done((bf16[4,16,384]{2,1,0:T(8,128)(2,1)S(1)}, bf16[4,16,384]{2,1,0:T(8,128)(2,1)S(1)}, u32[]{:S(2)}, u32[]{:S(2)}) %collective-permute-start.3) | collective-permute-done | bytes 49184 | tf_op jit(solution)/shard_map/ppermute | solution.py:23
  47.0 0.9 attend.1
  47.9 12.3 %all_to_all.16.got_ref = bf16[16,32,384]{2,1,0:T(8,128)(2,1)S(1)} all-to-all(bf16[16,32,384]{2,1,0:T(8,128)(2,1)S(1)} %attend.1), channel_id=1, replica_groups=mesh['y'=4,'c'=2,'z'=4,'x'=4] {'z','x'}, dimensions={0} | all-to-all | bytes 786432 | tf_op jit(solution)/shard_map/all_to_all | solution.py:27
  60.2 0.7 norm.1
  61.3 1.3 %collective-permute-start.6 = (bf16[16,7680]{1,0:T(8,128)(2,1)S(1)}, bf16[16,7680]{1,0:T(8,128)(2,1)S(1)}, u32[]{:S(2)}, u32[]{:S(2)}) collective-permute-start(bf16[16,7680]{1,0:T(8,128)(2,1)S(1)} %get-tuple-element.32), channel_id=1, source_target_pairs={{0,96},{32,64},{64,32},{96,0},{1,97},{33,65},{65,33},{97,1},{2,98}... | collective-permute-start | bytes 737288 | tf_op jit(solution)/shard_map/ppermute | solution.py:23
  62.6 1.9 %collective-permute-start.4 = (bf16[16,7680]{1,0:T(8,128)(2,1)S(1)}, bf16[16,7680]{1,0:T(8,128)(2,1)S(1)}, u32[]{:S(2)}, u32[]{:S(2)}) collective-permute-start(bf16[16,7680]{1,0:T(8,128)(2,1)S(1)} %get-tuple-element.30.after_ref), channel_id=1, source_target_pairs={{0,32},{32,0},{64,96},{96,64},{1,33},{33,1},{65,97},{97,65},{2,34}... | collective-permute-start | bytes 737288 | tf_op jit(solution)/shard_map/ppermute | solution.py:23
  64.5 7.7 %fetch.1 = (bf16[576,6144]{1,0:T(8,128)(2,1)S(1)}, bf16[576,6144]{1,0:T(8,128)(2,1)S(1)}, bf16[576,6144]{1,0:T(8,128)(2,1)S(1)}, f32[8,128]{1,0:T(8,128)}) custom-call(bf16[16,7680]{1,0:T(8,128)(2,1)} %copy-done.9, bf16[576,6144]{1,0:T(8,128)(2,1)} %bitcast.21, bf16[576,6144]{1,0:T(8,128)(2,1)} %bitcast.22, bf16[576,6144]{1,0:T(8,128)(2,1)} %bitcast.23), custom_call_target="tpu_custom_call" | custom-call | bytes 21233664 | tf_op jit(solution)/shard_map/fetch/pallas_call | solution.py:312
  75.2 0.7 copy-done.16
  75.9 5.1 %hidden_units.1 = (bf16[128,576]{1,0:T(8,128)(2,1)S(1)}, bf16[4,128,768]{2,1,0:T(8,128)(2,1)S(1)}) custom-call(s32[3]{0:T(128)S(1)} %copy-done.11, bf16[16,7680]{1,0:T(8,128)(2,1)S(1)} %get-tuple-element.34.refs_0_, bf16[16,7680]{1,0:T(8,128)(2,1)S(1)} %collective-permute-done.4.refs_1_, bf16[16,7680]{1,0:T(8,128)(2,1)S(1)} %collective-permute-done.5.refs_2_, ...), custom_call_target="tpu_custom_call" | custom-call | flops 2264924160 | bytes 23203840 | tf_op jit(solution)/shard_map/hidden_units/pallas_call | solution.py:32
  81.4 2.1 %collective-permute-done.11.theirs_ref = bf16[4,128,768]{2,1,0:T(8,128)(2,1)S(1)} collective-permute-done((bf16[4,128,768]{2,1,0:T(8,128)(2,1)S(1)}, bf16[4,128,768]{2,1,0:T(8,128)(2,1)S(1)}, u32[]{:S(2)}, u32[]{:S(2)}) %collective-permute-start.11) | collective-permute-done | bytes 786464 | tf_op jit(solution)/shard_map/ppermute | solution.py:23
  83.5 2.5 %down.1 = bf16[64,8,768]{2,1,0:T(8,128)(2,1)} custom-call(s32[3]{0:T(128)S(1)} %copy-done.11, bf16[128,576]{1,0:T(8,128)(2,1)S(1)} %get-tuple-element.42.hidden_ref, bf16[576,6144]{1,0:T(8,128)(2,1)S(1)} %get-tuple-element.40.refs_10_.down_ref, bf16[4,128,768]{2,1,0:T(8,128)(2,1)S(1)} %collective-permute-done.11.theirs_ref), custom_call_target="tpu_custom_call" | custom-call | flops 452984832 | bytes 8011776 | tf_op jit(solution)/shard_map/down/pallas_call | solution.py:32
  86.0 4.6 %all-to-all-start.2 = ((bf16[64,8,768]{2,1,0:T(8,128)(2,1)}), bf16[64,8,768]{2,1,0:T(8,128)(2,1)S(1)}, u32[]{:S(2)}, u32[]{:S(2)}) async-start(bf16[64,8,768]{2,1,0:T(8,128)(2,1)} %down.1), calls=%async_computation.2 | async-start | bytes 1572864 | tf_op jit(solution)/shard_map/all_to_all | solution.py:27
  90.7 1.2 %owned.1 = bf16[32,768]{1,0:T(8,128)(2,1)} custom-call(s32[3]{0:T(128)S(1)} %copy-done.12, bf16[16,7680]{1,0:T(8,128)(2,1)S(1)} %get-tuple-element.34.refs_0_, bf16[16,7680]{1,0:T(8,128)(2,1)S(1)} %collective-permute-done.4.refs_1_, bf16[16,7680]{1,0:T(8,128)(2,1)S(1)} %collective-permute-done.5.refs_2_, ...), custom_call_target="tpu_custom_call" | custom-call | bytes 1966080 | tf_op jit(solution)/shard_map/owned/pallas_call | solution.py:32
  91.9 15.5 %all-to-all-done.2.back_ref = bf16[64,8,768]{2,1,0:T(8,128)(2,1)S(1)} async-done(((bf16[64,8,768]{2,1,0:T(8,128)(2,1)}), bf16[64,8,768]{2,1,0:T(8,128)(2,1)S(1)}, u32[]{:S(2)}, u32[]{:S(2)}) %all-to-all-start.2) | async-done | bytes 786464 | tf_op jit(solution)/shard_map/all_to_all | solution.py:27
  107.4 1.8 %mix.1 = bf16[32,768]{1,0:T(8,128)(2,1)} custom-call(s32[3]{0:T(128)S(1)} %copy-done.12, s32[4,2,8]{2,1,0:T(2,128)S(1)} %bitcast.19, f32[4,2,8]{2,1,0:T(2,128)S(1)} %bitcast.20, bf16[64,8,768]{2,1,0:T(8,128)(2,1)S(1)} %all-to-all-done.2.back_ref), custom_call_target="tpu_custom_call" | custom-call | flops 16777216 | bytes 786944 | tf_op jit(solution)/shard_map/mix/pallas_call | solution.py:32
  (49 shorter events, 4.0 us)
Async XLA Ops:
  0.6 33.1 %copy-start.8 = (bf16[1024,384]{1,0:T(8,128)(2,1)S(1)}, bf16[1024,384]{1,0:T(8,128)(2,1)}, u32[]{:S(2)}) copy-start(bf16[1024,384]{1,0:T(8,128)(2,1)} %weight_ref.1) | copy-start | bytes 2359300
  0.6 59.5 %copy-start.13 = (f32[6144]{0:T(1024)S(1)}, f32[6144]{0:T(1024)}, u32[]{:S(2)}) copy-start(f32[6144]{0:T(1024)} %param.18) | copy-start | bytes 73732
  1.2 32.5 %copy-start.10 = (s32[3]{0:T(128)S(1)}, s32[3]{0:T(128)}, u32[]{:S(2)}) copy-start(s32[3]{0:T(128)} %pad_add_fusion.place_ref) | copy-start | bytes 40
  35.0 1.5 %collective-permute-start = (bf16[16,16,384]{2,1,0:T(8,128)(2,1)S(1)}, bf16[16,16,384]{2,1,0:T(8,128)(2,1)S(1)}, u32[]{:S(2)}, u32[]{:S(2)}) collective-permute-start(bf16[16,16,384]{2,1,0:T(8,128)(2,1)S(1)} %get-tuple-element.24), channel_id=1, source_target_pairs={{0,16},{16,0},{1,17},{17,1},{2,18},{18,2},{3,19},{19,3},{4,20},{20... | collective-permute-start | bytes 589832 | tf_op jit(solution)/shard_map/ppermute | solution.py:23
  37.2 4.8 %collective-permute-start.1 = (bf16[4,16,384]{2,1,0:T(8,128)(2,1)S(1)}, bf16[4,16,384]{2,1,0:T(8,128)(2,1)S(1)}, u32[]{:S(2)}, u32[]{:S(2)}) collective-permute-start(bf16[4,16,384]{2,1,0:T(8,128)(2,1)S(1)} %get-tuple-element.26), channel_id=1, source_target_pairs={{0,32},{32,0},{64,96},{96,64},{1,33},{33,1},{65,97},{97,65},{2,34}... | collective-permute-start | bytes 147464 | tf_op jit(solution)/shard_map/ppermute | solution.py:23
  38.8 5.7 %collective-permute-start.2 = (bf16[4,16,384]{2,1,0:T(8,128)(2,1)S(1)}, bf16[4,16,384]{2,1,0:T(8,128)(2,1)S(1)}, u32[]{:S(2)}, u32[]{:S(2)}) collective-permute-start(bf16[4,16,384]{2,1,0:T(8,128)(2,1)S(1)} %get-tuple-element.27), channel_id=1, source_target_pairs={{0,64},{32,96},{64,0},{96,32},{1,65},{33,97},{65,1},{97,33},{2,66}... | collective-permute-start | bytes 147464 | tf_op jit(solution)/shard_map/ppermute | solution.py:23
  41.7 5.3 %collective-permute-start.3 = (bf16[4,16,384]{2,1,0:T(8,128)(2,1)S(1)}, bf16[4,16,384]{2,1,0:T(8,128)(2,1)S(1)}, u32[]{:S(2)}, u32[]{:S(2)}) collective-permute-start(bf16[4,16,384]{2,1,0:T(8,128)(2,1)S(1)} %get-tuple-element.28), channel_id=1, source_target_pairs={{0,96},{32,64},{64,32},{96,0},{1,97},{33,65},{65,33},{97,1},{2,98}... | collective-permute-start | bytes 147464 | tf_op jit(solution)/shard_map/ppermute | solution.py:23
  60.9 11.2 %collective-permute-start.5 = (bf16[16,7680]{1,0:T(8,128)(2,1)S(1)}, bf16[16,7680]{1,0:T(8,128)(2,1)S(1)}, u32[]{:S(2)}, u32[]{:S(2)}) collective-permute-start(bf16[16,7680]{1,0:T(8,128)(2,1)S(1)} %get-tuple-element.31), channel_id=1, source_target_pairs={{0,64},{32,96},{64,0},{96,32},{1,65},{33,97},{65,1},{97,33},{2,66}... | collective-permute-start | bytes 737288 | tf_op jit(solution)/shard_map/ppermute | solution.py:23
  61.3 11.3 %collective-permute-start.6 = (bf16[16,7680]{1,0:T(8,128)(2,1)S(1)}, bf16[16,7680]{1,0:T(8,128)(2,1)S(1)}, u32[]{:S(2)}, u32[]{:S(2)}) collective-permute-start(bf16[16,7680]{1,0:T(8,128)(2,1)S(1)} %get-tuple-element.32), channel_id=1, source_target_pairs={{0,96},{32,64},{64,32},{96,0},{1,97},{33,65},{65,33},{97,1},{2,98}... | collective-permute-start | bytes 737288 | tf_op jit(solution)/shard_map/ppermute | solution.py:23
  62.6 10.0 %collective-permute-start.4 = (bf16[16,7680]{1,0:T(8,128)(2,1)S(1)}, bf16[16,7680]{1,0:T(8,128)(2,1)S(1)}, u32[]{:S(2)}, u32[]{:S(2)}) collective-permute-start(bf16[16,7680]{1,0:T(8,128)(2,1)S(1)} %get-tuple-element.30.after_ref), channel_id=1, source_target_pairs={{0,32},{32,0},{64,96},{96,64},{1,33},{33,1},{65,97},{97,65},{2,34}... | collective-permute-start | bytes 737288 | tf_op jit(solution)/shard_map/ppermute | solution.py:23
  64.5 10.7 %copy-start.11 = (s32[3]{0:T(128)S(1)}, s32[3]{0:T(128)}, u32[]{:S(2)}) copy-start(s32[3]{0:T(128)} %pad_add_fusion.place_ref) | copy-start | bytes 40
  72.6 1.5 %collective-permute-start.7 = (bf16[16,7680]{1,0:T(8,128)(2,1)S(1)}, bf16[16,7680]{1,0:T(8,128)(2,1)S(1)}, u32[]{:S(2)}, u32[]{:S(2)}) collective-permute-start(bf16[16,7680]{1,0:T(8,128)(2,1)S(1)} %get-tuple-element.34.refs_0_), channel_id=1, source_target_pairs={{0,16},{16,0},{1,17},{17,1},{2,18},{18,2},{3,19},{19,3},{4,20},{20... | collective-permute-start | bytes 737288 | tf_op jit(solution)/shard_map/ppermute | solution.py:23
  72.6 1.9 %collective-permute-start.8 = (bf16[16,7680]{1,0:T(8,128)(2,1)S(1)}, bf16[16,7680]{1,0:T(8,128)(2,1)S(1)}, u32[]{:S(2)}, u32[]{:S(2)}) collective-permute-start(bf16[16,7680]{1,0:T(8,128)(2,1)S(1)} %collective-permute-done.4.refs_1_), channel_id=1, source_target_pairs={{0,16},{16,0},{1,17},{17,1},{2,18},{18,2},{3,19},{19,3},{4,20},{20... | collective-permute-start | bytes 737288 | tf_op jit(solution)/shard_map/ppermute | solution.py:23
  73.1 1.7 %collective-permute-start.9 = (bf16[16,7680]{1,0:T(8,128)(2,1)S(1)}, bf16[16,7680]{1,0:T(8,128)(2,1)S(1)}, u32[]{:S(2)}, u32[]{:S(2)}) collective-permute-start(bf16[16,7680]{1,0:T(8,128)(2,1)S(1)} %collective-permute-done.5.refs_2_), channel_id=1, source_target_pairs={{0,16},{16,0},{1,17},{17,1},{2,18},{18,2},{3,19},{19,3},{4,20},{20... | collective-permute-start | bytes 737288 | tf_op jit(solution)/shard_map/ppermute | solution.py:23
  73.1 2.1 %collective-permute-start.10 = (bf16[16,7680]{1,0:T(8,128)(2,1)S(1)}, bf16[16,7680]{1,0:T(8,128)(2,1)S(1)}, u32[]{:S(2)}, u32[]{:S(2)}) collective-permute-start(bf16[16,7680]{1,0:T(8,128)(2,1)S(1)} %collective-permute-done.6.refs_3_), channel_id=1, source_target_pairs={{0,16},{16,0},{1,17},{17,1},{2,18},{18,2},{3,19},{19,3},{4,20},{20... | collective-permute-start | bytes 737288 | tf_op jit(solution)/shard_map/ppermute | solution.py:23
  81.1 9.5 %copy-start.12 = (s32[3]{0:T(128)S(1)}, s32[3]{0:T(128)}, u32[]{:S(2)}) copy-start(s32[3]{0:T(128)} %pad_add_fusion.place_ref) | copy-start | bytes 40
  81.1 26.3 %copy-start.14 = (s32[4,8,2]{1,2,0:T(2,128)S(1)}, s32[4,8,2]{1,2,0:T(2,128)}, u32[]{:S(2)}) copy-start(s32[4,8,2]{1,2,0:T(2,128)} %param.19) | copy-start | bytes 772
  81.1 26.3 %copy-start.15 = (f32[4,8,2]{1,2,0:T(2,128)S(1)}, f32[4,8,2]{1,2,0:T(2,128)}, u32[]{:S(2)}) copy-start(f32[4,8,2]{1,2,0:T(2,128)} %param.20) | copy-start | bytes 772
  81.1 9.5 %copy-start.1 = (bf16[16,7680]{1,0:T(8,128)(2,1)S(1)}, bf16[16,7680]{1,0:T(8,128)(2,1)}, u32[]{:S(2)}) copy-start(bf16[16,7680]{1,0:T(8,128)(2,1)} %copy-done) | copy-start | bytes 737284
  81.1 9.5 %copy-start.3 = (bf16[16,7680]{1,0:T(8,128)(2,1)S(1)}, bf16[16,7680]{1,0:T(8,128)(2,1)}, u32[]{:S(2)}) copy-start(bf16[16,7680]{1,0:T(8,128)(2,1)} %copy-done.2) | copy-start | bytes 737284
  81.1 9.5 %copy-start.5 = (bf16[16,7680]{1,0:T(8,128)(2,1)S(1)}, bf16[16,7680]{1,0:T(8,128)(2,1)}, u32[]{:S(2)}) copy-start(bf16[16,7680]{1,0:T(8,128)(2,1)} %copy-done.4) | copy-start | bytes 737284
  81.1 9.5 %copy-start.7 = (bf16[16,7680]{1,0:T(8,128)(2,1)S(1)}, bf16[16,7680]{1,0:T(8,128)(2,1)}, u32[]{:S(2)}) copy-start(bf16[16,7680]{1,0:T(8,128)(2,1)} %copy-done.6) | copy-start | bytes 737284
  81.1 2.4 %collective-permute-start.11 = (bf16[4,128,768]{2,1,0:T(8,128)(2,1)S(1)}, bf16[4,128,768]{2,1,0:T(8,128)(2,1)S(1)}, u32[]{:S(2)}, u32[]{:S(2)}) collective-permute-start(bf16[4,128,768]{2,1,0:T(8,128)(2,1)S(1)} %get-tuple-element.43), channel_id=1, source_target_pairs={{0,16},{16,0},{1,17},{17,1},{2,18},{18,2},{3,19},{19,3},{4,20},{20... | collective-permute-start | bytes 2359304 | tf_op jit(solution)/shard_map/ppermute | solution.py:23
  86.0 21.4 %all-to-all-start.2 = ((bf16[64,8,768]{2,1,0:T(8,128)(2,1)}), bf16[64,8,768]{2,1,0:T(8,128)(2,1)S(1)}, u32[]{:S(2)}, u32[]{:S(2)}) async-start(bf16[64,8,768]{2,1,0:T(8,128)(2,1)} %down.1), calls=%async_computation.2 | async-start | bytes 1572864 | tf_op jit(solution)/shard_map/all_to_all | solution.py:27
  (6 other events, 29.8 us)

commit v6 on v5

--- a/solution.py
+++ b/solution.py
@@ -19,32 +19,36 @@
     return pltpu.CompilerParams(vmem_limit_bytes=mib * MIB)
 
 
-def over(axis, value, bits):
-    return lax.ppermute(value, axis, [(i, i ^ bits) for i in range(lax.axis_size(axis))])
+def over(axis, value, shift):
+    size = lax.axis_size(axis)
+    return lax.ppermute(value, axis, [(i, (i + shift) % size) for i in range(size)])
 
 
 def exchange(value, axes):
     return lax.all_to_all(value, axes, split_axis=0, concat_axis=0, tiled=True)
 
 
-def call(kernel, name, out_shape, place, *arrays, flops=0, limit=16, scratch=()):
+def call(kernel, name, out_shape, *arrays, flops=0, limit=10, scratch=()):
     moved = sum(a.size * a.dtype.itemsize for a in arrays)
     result = pl.pallas_call(
-        kernel,
+        lambda *refs: kernel(device_place(), *refs),
         out_shape=out_shape,
-        in_specs=[pl.BlockSpec(memory_space=pltpu.SMEM)]
-        + [pl.BlockSpec(memory_space=pltpu.VMEM)] * len(arrays),
+        in_specs=[pl.BlockSpec(memory_space=pltpu.VMEM)] * len(arrays),
         out_specs=jax.tree.map(lambda _: pl.BlockSpec(memory_space=pltpu.VMEM), out_shape),
         scratch_shapes=scratch,
         compiler_params=vmem_params(limit),
         cost_estimate=pl.CostEstimate(flops=flops, bytes_accessed=moved, transcendentals=0),
         name=name,
-    )(place, *arrays)
+    )(*arrays)
     return list(result) if isinstance(out_shape, list) else result
 
 
-def xor(a, b):
-    return lax.bitwise_xor(a, b)
+def device_place():
+    return [lax.axis_index(axis) for axis in ("z", "y", "c")]
+
+
+def turned(a, b):
+    return lax.bitwise_and(a + b, 3)
 
 
 def lanes_from(start, size):
@@ -77,9 +81,9 @@
 
 
 def readout_kernel(
-    place_ref, decay_ref, routes_ref, hidden_ref, qkv_ref, state_ref, gain_ref, out_ref
+    decay_ref, routes_ref, hidden_ref, qkv_ref, state_ref, gain_ref, out_ref
 ):
-    c = place_ref[2]
+    c = lax.axis_index("c")
     cols = hidden_ref.shape[2] // 16
     depth = out_ref.shape[2] - 256
 
@@ -141,7 +145,7 @@
             out_ref[i, :, at] = o
 
 
-def readouts(place, step_qkv, decay, state, attn_gain, hidden_in, routes):
+def readouts(step_qkv, decay, state, attn_gain, hidden_in, routes):
     heads, size = state.shape[1], state.shape[2]
     at_once = min(heads, 4)
     n = STEPS * ROWS
@@ -151,7 +155,6 @@
         out_shape=jax.ShapeDtypeStruct((16, n, packed), BF16),
         grid=(heads // at_once,),
         in_specs=[
-            pl.BlockSpec(memory_space=pltpu.SMEM),
             pl.BlockSpec(memory_space=pltpu.SMEM),
             pl.BlockSpec((STEPS, 2, ROWS), lambda i: (0, 0, 0)),
             pl.BlockSpec(hidden_in.shape, lambda i: (0, 0, 0)),
@@ -168,7 +171,6 @@
         ),
         name="readout",
     )(
-        place,
         decay,
         routes.transpose(0, 2, 1),
         hidden_in,
@@ -178,7 +180,7 @@
     )
 
 
-def project_kernel(place_ref, got_ref, weight_ref, mine_ref, other_ref):
+def project_kernel(place_ref, got_ref, weight_ref, done_ref, mine_ref, other_ref):
     c = place_ref[2]
     depth = weight_ref.shape[0]
     for part in range(2):
@@ -191,43 +193,36 @@
             other_ref[8 * part + i] = jnp.where(c == 0, b, a)
 
 
-def project(place, got, weight):
+def project(got, weight, done):
     out = [jax.ShapeDtypeStruct((16, 16, weight.shape[1]), BF16)] * 2
-    return call(project_kernel, "project", out, place, got, weight, flops=1024 * weight.size)
+    flops = 1024 * weight.size
+    return call(project_kernel, "project", out, got, weight, done, flops=flops)
 
 
 def by_y_kernel(place_ref, mine_ref, got_ref, *out_refs):
     y = place_ref[1]
     for k, ref in enumerate(out_refs):
         for x in range(4):
-            i = xor(y, k) * 4 + x
+            i = turned(y, k) * 4 + x
             ref[x] = (mine_ref[i].astype(F32) + got_ref[i].astype(F32)).astype(BF16)
 
 
-def sums_by_y(place, mine, got):
+def sums_by_y(mine, got):
     out = [jax.ShapeDtypeStruct((4,) + mine.shape[1:], BF16)] * 4
-    return call(by_y_kernel, "sums_by_y", out, place, mine, got)
-
-
-def attend_kernel(place_ref, got_ref, *refs):
-    sum_refs, out_ref = refs[:4], refs[4]
+    return call(by_y_kernel, "sums_by_y", out, mine, got)
+
+
+def slots_kernel(place_ref, got_ref, select_ref, hidden_ref):
     y = place_ref[1]
-    cols = out_ref.shape[2]
     depth = got_ref.shape[2] - 256
-    rows, names = [], []
+    names = []
     for x in range(4):
         i = y * 4 + x
-        tail = got_ref[i, 16:, depth:].astype(F32)
-        names.append(tail[:, 128:])
-        total = jnp.concatenate([got_ref[i, :16, depth:].astype(F32), tail[:, :128]], axis=1)
-        for ref in sum_refs:
-            total += ref[x].astype(F32)
-        rows.append(total.astype(BF16))
-        for z in range(4):
-            out_ref[4 * z + x, 16:] = rows[x]
-    rows = jnp.concatenate(rows, axis=0)
-    n = rows.shape[0]
+        tail = got_ref[i, 16:, depth:]
+        names.append(tail[:, 128:].astype(F32))
+        hidden_ref[x] = jnp.concatenate([got_ref[i, :16, depth:], tail[:, :128]], axis=1)
     names = jnp.concatenate(names, axis=0)
+    n = names.shape[0]
     across = names.T
     down_i = lax.broadcasted_iota(jnp.int32, (n, n), 0)
     over_i = lax.broadcasted_iota(jnp.int32, (n, n), 1)
@@ -244,14 +239,33 @@
             rank += jnp.sum(same.astype(F32), axis=0, keepdims=True)
         target = mine.astype(jnp.int32) * 16 + base + rank.astype(jnp.int32)
         select += (slot == target).astype(F32)
-    sent = jnp.dot(select.astype(BF16), rows, preferred_element_type=F32).astype(BF16)
+    select_ref[...] = select.astype(BF16)
+
+
+def slots(got, cols):
+    out = [jax.ShapeDtypeStruct((256, 64), BF16), jax.ShapeDtypeStruct((4, 16, cols), BF16)]
+    return call(slots_kernel, "slots", out, got, flops=1 << 20)
+
+
+def attend_kernel(place_ref, select_ref, hidden_ref, *refs):
+    sum_refs, out_ref = refs[:4], refs[4]
+    rows = []
+    for x in range(4):
+        total = hidden_ref[x].astype(F32)
+        for ref in sum_refs:
+            total += ref[x].astype(F32)
+        rows.append(total.astype(BF16))
+        for z in range(4):
+            out_ref[4 * z + x, 16:] = rows[x]
+    rows = jnp.concatenate(rows, axis=0)
+    sent = jnp.dot(select_ref[...], rows, preferred_element_type=F32).astype(BF16)
     for i in range(16):
         out_ref[i, :16] = sent[16 * i : 16 * i + 16]
 
 
-def attend(place, got, sums):
-    out = jax.ShapeDtypeStruct((16, 32, sums[0].shape[2]), BF16)
-    return call(attend_kernel, "attend", out, place, got, *sums, flops=1 << 23)
+def attend(select, hidden, sums):
+    out = jax.ShapeDtypeStruct((16, 32, hidden.shape[2]), BF16)
+    return call(attend_kernel, "attend", out, select, hidden, *sums, flops=1 << 23)
 
 
 def norm_kernel(place_ref, gain_ref, got_ref, *out_refs):
@@ -271,12 +285,12 @@
     for k, out_ref in enumerate(out_refs):
         for x in range(4):
             at = slice((16 + x) * cols, (17 + x) * cols)
-            out_ref[:, at] = got_ref[xor(y, k) * 4 + x, 16:]
-
-
-def norm(place, gain, got):
+            out_ref[:, at] = got_ref[turned(y, 4 - k) * 4 + x, 16:]
+
+
+def norm(gain, got):
     out = [jax.ShapeDtypeStruct((16, 20 * got.shape[2]), BF16)] * 4
-    return call(norm_kernel, "norm", out, place, gain.reshape(1, -1), got)
+    return call(norm_kernel, "norm", out, gain.reshape(1, -1), got)
 
 
 def owned_kernel(place_ref, *refs):
@@ -287,15 +301,15 @@
     at = lanes_from(start + c * share, share)
     for k in range(4):
 
-        @pl.when(xor(z, y) == k)
+        @pl.when(turned(z, 4 - y) == k)
         def _():
             out_ref[pl.ds(pl.multiple_of(16 * c, 16), 16), :] = own_refs[k][:, at]
             out_ref[pl.ds(pl.multiple_of(16 - 16 * c, 16), 16), :] = other_refs[k][:, at]
 
 
-def owned(place, by_y, by_core, share):
+def owned(by_y, by_core, share):
     out = jax.ShapeDtypeStruct((STEPS * ROWS, share), BF16)
-    return call(owned_kernel, "owned", out, place, *by_y, *by_core)
+    return call(owned_kernel, "owned", out, *by_y, *by_core)
 
 
 def fetch_kernel(after_ref, *refs):
@@ -326,7 +340,7 @@
 
 
 def hidden_kernel(place_ref, *refs):
-    x_refs, (gate_ref, up_ref, down_ref, _, hidden_ref, theirs_ref) = refs[:8], refs[8:]
+    x_refs, (gate_ref, up_ref, down_ref, hidden_ref, theirs_ref) = refs[:8], refs[8:]
     share = theirs_ref.shape[2]
     y, c = place_ref[1], place_ref[2]
     x = jnp.concatenate([r[:, : gate_ref.shape[1]] for r in x_refs], axis=0)
@@ -336,12 +350,12 @@
     hidden = (gate / (1.0 + jnp.exp(-gate)) * up).T.astype(BF16)
     hidden_ref[...] = hidden
     for k in range(4):
-        block = lax.bitwise_xor(y, k) * 2 + (1 - c)
+        block = turned(y, k) * 2 + (1 - c)
         at = pl.ds(pl.multiple_of(block * share, 128), share)
         theirs_ref[k] = jnp.dot(hidden, down_ref[:, at], preferred_element_type=F32).astype(BF16)
 
 
-def hidden_units(place, pieces, gate, up, down_weight, done, share):
+def hidden_units(pieces, gate, up, down_weight, share):
     units = gate.shape[0]
     rows = sum(p.shape[0] for p in pieces)
     out = [
@@ -349,36 +363,45 @@
         jax.ShapeDtypeStruct((4, rows, share), BF16),
     ]
     flops = 5 * rows * gate.size
-    arrays = (*pieces, gate, up, down_weight, done)
-    return call(hidden_kernel, "hidden_units", out, place, *arrays, flops=flops)
-
-
-def down_kernel(place_ref, hidden_ref, down_ref, theirs_ref, out_ref):
+    arrays = (*pieces, gate, up, down_weight)
+    return call(hidden_kernel, "hidden_units", out, *arrays, flops=flops)
+
+
+def down_kernel(place_ref, hidden_ref, down_ref, out_ref):
     share = out_ref.shape[2]
     y, c = place_ref[1], place_ref[2]
-    half = hidden_ref.shape[0] // 2
     for k in range(4):
-        column = xor(y, k)
-        at = lanes_from((column * 2 + c) * share, share)
-        ours = jnp.dot(hidden_ref[...], down_ref[:, at], preferred_element_type=F32)
-        same = ours[:half] + theirs_ref[k, half:].astype(F32)
-        flip = ours[half:] + theirs_ref[k, :half].astype(F32)
+        at = lanes_from((turned(y, k) * 2 + c) * share, share)
+        out_ref[k] = jnp.dot(hidden_ref[...], down_ref[:, at], preferred_element_type=F32)
+
+
+def down(hidden, weight, share):
+    out = jax.ShapeDtypeStruct((4, hidden.shape[0], share), F32)
+    flops = hidden.shape[0] * weight.size
+    return call(down_kernel, "down", out, hidden, weight, flops=flops)
+
+
+def cores_kernel(place_ref, ours_ref, theirs_ref, out_ref):
+    y, c = place_ref[1], place_ref[2]
+    half = ours_ref.shape[1] // 2
+    for k in range(4):
+        same = ours_ref[k, :half] + theirs_ref[k, half:].astype(F32)
+        flip = ours_ref[k, half:] + theirs_ref[k, :half].astype(F32)
         low = jnp.where(c == 0, same, flip)
         high = jnp.where(c == 0, flip, same)
         for ky in range(4):
             for x in range(4):
                 rows = slice(16 * ky + 4 * x, 16 * ky + 4 * x + 4)
                 block = jnp.concatenate([low[rows], high[rows]], axis=0)
-                out_ref[column * 16 + xor(y, ky) * 4 + x] = block.astype(BF16)
-
-
-def down(place, hidden, weight, theirs):
+                out_ref[turned(y, k) * 16 + turned(y, ky) * 4 + x] = block.astype(BF16)
+
+
+def cores_sum(ours, theirs):
     out = jax.ShapeDtypeStruct((64, 8, theirs.shape[2]), BF16)
-    flops = hidden.shape[0] * weight.size
-    return call(down_kernel, "down", out, place, hidden, weight, theirs, flops=flops)
-
-
-def mix_kernel(place_ref, routes_ref, weights_ref, back_ref, out_ref):
+    return call(cores_kernel, "cores_sum", out, ours, theirs)
+
+
+def weights_kernel(place_ref, routes_ref, weights_ref, out_ref):
     n = STEPS * ROWS
     names = [columns_of(routes_ref[t].astype(F32)) for t in range(STEPS)]
     names = widened(jnp.concatenate(names, axis=0))
@@ -399,20 +422,27 @@
             rank += jnp.sum(same.astype(F32), axis=1, keepdims=True)
         target = mine.astype(jnp.int32) * 8 + 2 * step + rank.astype(jnp.int32)
         mix += jnp.where(slot == target, weights[:, j : j + 1], 0.0)
+    out_ref[...] = jnp.concatenate(bf16_parts(mix, 3), axis=1)
+
+
+def mix_weights(routes, weights):
+    out = jax.ShapeDtypeStruct((STEPS * ROWS, 384), BF16)
+    arrays = (routes.transpose(0, 2, 1), weights.transpose(0, 2, 1))
+    return call(weights_kernel, "mix_weights", out, *arrays, flops=1 << 20)
+
+
+def mix_kernel(place_ref, mix_ref, back_ref, out_ref):
     back = back_ref[...].astype(F32)
     back = (back[:16] + back[16:32]) + (back[32:48] + back[48:])
     back = back.reshape(128, back.shape[2]).astype(BF16)
     out_ref[...] = jnp.dot(
-        jnp.concatenate(bf16_parts(mix, 3), axis=1),
-        jnp.concatenate([back] * 3, axis=0),
-        preferred_element_type=F32,
+        mix_ref[...], jnp.concatenate([back] * 3, axis=0), preferred_element_type=F32
     ).astype(BF16)
 
 
-def mixed_rows(place, routes, weights, back):
+def mixed_rows(mix, back):
     out = jax.ShapeDtypeStruct((STEPS * ROWS, back.shape[2]), BF16)
-    arrays = (routes.transpose(0, 2, 1), weights.transpose(0, 2, 1), back)
-    return call(mix_kernel, "mix", out, place, *arrays, flops=1 << 24)
+    return call(mix_kernel, "mix", out, mix, back, flops=1 << 24)
 
 
 def shards(
@@ -430,28 +460,30 @@
     w_down,
 ):
     share = hidden_in.shape[2] // 8
-    place = jnp.stack([lax.axis_index(axis) for axis in ("z", "y", "c")]).astype(jnp.int32)
-
-    sent = readouts(place, step_qkv, decay_rates, kv_state, attn_gain, hidden_in, routes)
+
+    sent = readouts(step_qkv, decay_rates, kv_state, attn_gain, hidden_in, routes)
+    gate, up, down_weight, done = fetch(
+        sent, w_gate[0].swapaxes(0, 1), w_up[0].swapaxes(0, 1), w_down[0]
+    )
     got = exchange(sent, ("z", "x"))
 
-    mine, other = project(place, got, out_proj)
-    sums = sums_by_y(place, mine, over("c", other, 1))
+    mine, other = project(got, out_proj, done)
+    sums = sums_by_y(mine, over("c", other, 1))
+    select, hidden = slots(got, out_proj.shape[1])
     sums = sums[:1] + [over("y", sums[k], k) for k in (1, 2, 3)]
 
-    pieces = norm(place, ffn_gain, exchange(attend(place, got, sums), ("z", "x")))
-    by_y = pieces[:1] + [over("y", pieces[k], k) for k in (1, 2, 3)]
-    gate, up, down_weight, done = fetch(
-        pieces[1], w_gate[0].swapaxes(0, 1), w_up[0].swapaxes(0, 1), w_down[0]
-    )
-    by_y, done = lax.optimization_barrier((by_y, done))
+    pieces = exchange(attend(select, hidden, sums), ("z", "x"))
+    pieces = norm(ffn_gain, pieces)
+    by_y = pieces[:1] + [over("y", pieces[k], -k) for k in (1, 2, 3)]
     by_core = [over("c", piece, 1) for piece in by_y]
-    attended = owned(place, by_y, by_core, share)
-
-    hidden, theirs = hidden_units(place, by_y + by_core, gate, up, down_weight, done, share)
-    sums = down(place, hidden, down_weight, over("c", theirs, 1))
-
-    mixed = mixed_rows(place, routes, route_weights, exchange(sums, ("y", "z", "x")))
+
+    hidden, theirs = hidden_units(by_y + by_core, gate, up, down_weight, share)
+    theirs = over("c", theirs, 1)
+    sums = cores_sum(down(hidden, down_weight, share), theirs)
+
+    attended = owned(by_y, by_core, share)
+    mix = mix_weights(routes, route_weights)
+    mixed = mixed_rows(mix, exchange(sums, ("y", "z", "x")))
     return attended.reshape(STEPS, ROWS, share), mixed.reshape(STEPS, ROWS, share)
 
 

time: 110 us -> 114 us (1.036)
  blocking collectives: 40.2 us -> 12.4 us
  local copies, waits for them, and re-layouts: 0.76 us -> 18.4 us
  starting transfers between devices: 14.3 us -> 24.6 us
  waiting for transfers between devices: 26.2 us -> 34.7 us
  Pallas kernels: 26.3 us -> 22.3 us
    all_to_all x2 -> x1, blocking collectives: 40.2 us -> 12.4 us  [exchange(): return lax.all_to_all(value, axes, split_axis=0, concat_axis=0, tiled=True)]
    unnamed x34 -> x22, local copies, waits for them, and re-layouts: 0.76 us -> 18.4 us
    all_to_all x1 -> x2, starting transfers between devices: 4.64 us -> 14.3 us  [exchange(): return lax.all_to_all(value, axes, split_axis=0, concat_axis=0, tiled=True)]
    ppermute x12, waiting for transfers between devices: 10.6 us -> 15 us  [over(): lax.ppermute(value, axis, [(i, (i + shift) % size) for i in range(size)])]
    all_to_all x1 -> x2, waiting for transfers between devices: 15.5 us -> 19.8 us  [exchange(): return lax.all_to_all(value, axes, split_axis=0, concat_axis=0, tiled=True)]
    pallas_call x8 -> x11, Pallas kernels: 14 us -> 9.96 us  [call(): pl.pallas_call(lambda *refs: kernel(device_place(), *refs), out_shape=out...]
  transfers between devices with their start and end apart: 13 -> 14, of which waited for: 10 -> 11; matrix products, arithmetic and copies ran while one was open for 0% -> 0% of each run, Pallas kernels for 8% -> 9%
where the time goes in v6:
time: 114 us; the launch traced here: 113 us
  waiting for transfers between devices  34.7 us (30%)
  starting transfers between devices  24.6 us (22%)
  Pallas kernels  22.3 us (20%)
  local copies, waits for them, and re-layouts  18.4 us (16%)
  blocking collectives  12.4 us (11%)
    all_to_all x2, waiting for transfers between devices, exchange(): return lax.all_to_all(value, axes, split_axis=0, concat_axis=0, tiled=True)  19.8 us
    unnamed x22, local copies, waits for them, and re-layouts  18.4 us
    ppermute x12, waiting for transfers between devices, over(): lax.ppermute(value, axis, [(i, (i + shift) % size) for i in range(size)])  15 us
    all_to_all x2, starting transfers between devices, exchange(): return lax.all_to_all(value, axes, split_axis=0, concat_axis=0, tiled=True)  14.3 us
    all_to_all x1, blocking collectives, exchange(): return lax.all_to_all(value, axes, split_axis=0, concat_axis=0, tiled=True)  12.4 us
    ppermute x12, starting transfers between devices, over(): lax.ppermute(value, axis, [(i, (i + shift) % size) for i in range(size)])  10.3 us
    pallas_call x11, Pallas kernels, call(): pl.pallas_call(lambda *refs: kernel(device_place(), *refs), out_shape=out...  9.96 us
    pallas_call x1, Pallas kernels, fetch(): pl.pallas_call(fetch_kernel, out_shape=[pltpu.VMEM(w.shape, w.dtype) for...  7.73 us
  transfers between devices with their start and end apart: 14, of which 11 were waited for; matrix products, arithmetic and copies ran while one was open for 0% of the time, Pallas kernels for 9%

profile of v6, /device:TPU:0, one launch (start us, length us, event | category | flops | bytes accessed | tf_op | source)
XLA Modules:
  0.0 113.2 jit_solution(9459094561888945158)
XLA Ops:
  0.6 4.6 %readout.1.after_ref = bf16[16,32,1280]{2,1,0:T(8,128)(2,1)} custom-call(f32[4,8]{1,0:T(4,128)} %decay_ref.1, s32[4,2,8]{2,1,0:T(2,128)} %bitcast.15, bf16[4,8,6144]{2,1,0:T(8,128)(2,1)} %hidden_ref.1, bf16[4,3,8,1024]{3,2,1,0:T(8,128)(2,1)} %bitcast.21, f32[8,8,128,128]{3,2,1,0:T(8,128)} %state_ref.1, f32[1,1024]{1,0:T(1,128)} %bitcast.24), custom_call_target="tpu_custom_call" | custom-call | flops 134217728 | bytes 4194304 | tf_op jit(solution)/shard_map/readout/pallas_call | solution.py:153
  5.3 8.0 %all-to-all-start = ((bf16[16,32,1280]{2,1,0:T(8,128)(2,1)}), bf16[16,32,1280]{2,1,0:T(8,128)(2,1)S(1)}, u32[]{:S(2)}, u32[]{:S(2)}) async-start(bf16[16,32,1280]{2,1,0:T(8,128)(2,1)} %readout.1.after_ref), calls=%async_computation | async-start | bytes 2621440 | tf_op jit(solution)/shard_map/all_to_all | solution.py:28
  13.3 7.7 %fetch.1 = (bf16[576,6144]{1,0:T(8,128)(2,1)S(1)}, bf16[576,6144]{1,0:T(8,128)(2,1)S(1)}, bf16[576,6144]{1,0:T(8,128)(2,1)S(1)}, f32[8,128]{1,0:T(8,128)}) custom-call(bf16[16,32,1280]{2,1,0:T(8,128)(2,1)} %readout.1.after_ref, bf16[576,6144]{1,0:T(8,128)(2,1)} %bitcast.18, bf16[576,6144]{1,0:T(8,128)(2,1)} %bitcast.19, bf16[576,6144]{1,0:T(8,128)(2,1)} %bitcast.20), custom_call_target="tpu_custom_call" | custom-call | bytes 21233664 | tf_op jit(solution)/shard_map/fetch/pallas_call | solution.py:326
  21.0 2.8 %copy-done = bf16[576,6144]{1,0:T(8,128)(2,1)} copy-done((bf16[576,6144]{1,0:T(8,128)(2,1)}, bf16[576,6144]{1,0:T(8,128)(2,1)S(1)}, u32[]{:S(2)}) %copy-start) | copy-done | bytes 7077912
  23.8 2.9 %copy-done.2 = bf16[576,6144]{1,0:T(8,128)(2,1)} copy-done((bf16[576,6144]{1,0:T(8,128)(2,1)}, bf16[576,6144]{1,0:T(8,128)(2,1)S(1)}, u32[]{:S(2)}) %copy-start.2) | copy-done | bytes 7077912
  26.7 2.9 %copy-done.4 = bf16[576,6144]{1,0:T(8,128)(2,1)} copy-done((bf16[576,6144]{1,0:T(8,128)(2,1)}, bf16[576,6144]{1,0:T(8,128)(2,1)S(1)}, u32[]{:S(2)}) %copy-start.4) | copy-done | bytes 7077912
  29.6 4.4 %all-to-all-done.refs_0_ = bf16[16,32,1280]{2,1,0:T(8,128)(2,1)S(1)} async-done(((bf16[16,32,1280]{2,1,0:T(8,128)(2,1)}), bf16[16,32,1280]{2,1,0:T(8,128)(2,1)S(1)}, u32[]{:S(2)}, u32[]{:S(2)}) %all-to-all-start) | async-done | bytes 1310752 | tf_op jit(solution)/shard_map/all_to_all | solution.py:28
  35.6 1.4 %collective-permute-done.refs_1_ = bf16[16,16,384]{2,1,0:T(8,128)(2,1)S(1)} collective-permute-done((bf16[16,16,384]{2,1,0:T(8,128)(2,1)S(1)}, bf16[16,16,384]{2,1,0:T(8,128)(2,1)S(1)}, u32[]{:S(2)}, u32[]{:S(2)}) %collective-permute-start) | collective-permute-done | bytes 196640 | tf_op jit(solution)/shard_map/ppermute | solution.py:24
  37.0 1.6 %collective-permute-start.1 = (bf16[4,16,384]{2,1,0:T(8,128)(2,1)S(1)}, bf16[4,16,384]{2,1,0:T(8,128)(2,1)S(1)}, u32[]{:S(2)}, u32[]{:S(2)}) collective-permute-start(bf16[4,16,384]{2,1,0:T(8,128)(2,1)S(1)} %get-tuple-element.26), channel_id=1, source_target_pairs={{0,32},{32,64},{64,96},{96,0},{1,33},{33,65},{65,97},{97,1},{2,34}... | collective-permute-start | bytes 147464 | tf_op jit(solution)/shard_map/ppermute | solution.py:24
  38.7 2.9 %collective-permute-start.2 = (bf16[4,16,384]{2,1,0:T(8,128)(2,1)S(1)}, bf16[4,16,384]{2,1,0:T(8,128)(2,1)S(1)}, u32[]{:S(2)}, u32[]{:S(2)}) collective-permute-start(bf16[4,16,384]{2,1,0:T(8,128)(2,1)S(1)} %get-tuple-element.27), channel_id=1, source_target_pairs={{0,64},{32,96},{64,0},{96,32},{1,65},{33,97},{65,1},{97,33},{2,66}... | collective-permute-start | bytes 147464 | tf_op jit(solution)/shard_map/ppermute | solution.py:24
  41.6 1.3 %collective-permute-start.3 = (bf16[4,16,384]{2,1,0:T(8,128)(2,1)S(1)}, bf16[4,16,384]{2,1,0:T(8,128)(2,1)S(1)}, u32[]{:S(2)}, u32[]{:S(2)}) collective-permute-start(bf16[4,16,384]{2,1,0:T(8,128)(2,1)S(1)} %get-tuple-element.28), channel_id=1, source_target_pairs={{0,96},{32,0},{64,32},{96,64},{1,97},{33,1},{65,33},{97,65},{2,98}... | collective-permute-start | bytes 147464 | tf_op jit(solution)/shard_map/ppermute | solution.py:24
  43.1 1.3 %collective-permute-done.2.refs_4_ = bf16[4,16,384]{2,1,0:T(8,128)(2,1)S(1)} collective-permute-done((bf16[4,16,384]{2,1,0:T(8,128)(2,1)S(1)}, bf16[4,16,384]{2,1,0:T(8,128)(2,1)S(1)}, u32[]{:S(2)}, u32[]{:S(2)}) %collective-permute-start.2) | collective-permute-done | bytes 49184 | tf_op jit(solution)/shard_map/ppermute | solution.py:24
  44.4 1.3 %collective-permute-done.3.refs_5_ = bf16[4,16,384]{2,1,0:T(8,128)(2,1)S(1)} collective-permute-done((bf16[4,16,384]{2,1,0:T(8,128)(2,1)S(1)}, bf16[4,16,384]{2,1,0:T(8,128)(2,1)S(1)}, u32[]{:S(2)}, u32[]{:S(2)}) %collective-permute-start.3) | collective-permute-done | bytes 49184 | tf_op jit(solution)/shard_map/ppermute | solution.py:24
  45.9 12.4 %all_to_all.15.refs_1_ = bf16[16,32,384]{2,1,0:T(8,128)(2,1)S(1)} all-to-all(bf16[16,32,384]{2,1,0:T(8,128)(2,1)S(1)} %attend.1), channel_id=1, replica_groups=mesh['y'=4,'c'=2,'z'=4,'x'=4] {'z','x'}, dimensions={0} | all-to-all | bytes 786432 | tf_op jit(solution)/shard_map/all_to_all | solution.py:28
  58.8 3.0 %collective-permute-start.4 = (bf16[16,7680]{1,0:T(8,128)(2,1)S(1)}, bf16[16,7680]{1,0:T(8,128)(2,1)S(1)}, u32[]{:S(2)}, u32[]{:S(2)}) collective-permute-start(bf16[16,7680]{1,0:T(8,128)(2,1)S(1)} %get-tuple-element.30), channel_id=1, source_target_pairs={{0,96},{32,0},{64,32},{96,64},{1,97},{33,1},{65,33},{97,65},{2,98}... | collective-permute-start | bytes 737288 | tf_op jit(solution)/shard_map/ppermute | solution.py:24
  62.6 5.5 %collective-permute-done.6.refs_3_ = bf16[16,7680]{1,0:T(8,128)(2,1)S(1)} collective-permute-done((bf16[16,7680]{1,0:T(8,128)(2,1)S(1)}, bf16[16,7680]{1,0:T(8,128)(2,1)S(1)}, u32[]{:S(2)}, u32[]{:S(2)}) %collective-permute-start.6) | collective-permute-done | bytes 245792 | tf_op jit(solution)/shard_map/ppermute | solution.py:24
  68.1 1.6 %collective-permute-done.4.refs_1_ = bf16[16,7680]{1,0:T(8,128)(2,1)S(1)} collective-permute-done((bf16[16,7680]{1,0:T(8,128)(2,1)S(1)}, bf16[16,7680]{1,0:T(8,128)(2,1)S(1)}, u32[]{:S(2)}, u32[]{:S(2)}) %collective-permute-start.4) | collective-permute-done | bytes 245792 | tf_op jit(solution)/shard_map/ppermute | solution.py:24
  72.3 3.0 %copy-done.1 = bf16[576,6144]{1,0:T(8,128)(2,1)S(1)} copy-done((bf16[576,6144]{1,0:T(8,128)(2,1)S(1)}, bf16[576,6144]{1,0:T(8,128)(2,1)}, u32[]{:S(2)}) %copy-start.1) | copy-done | bytes 7077912
  75.3 3.0 %copy-done.3 = bf16[576,6144]{1,0:T(8,128)(2,1)S(1)} copy-done((bf16[576,6144]{1,0:T(8,128)(2,1)S(1)}, bf16[576,6144]{1,0:T(8,128)(2,1)}, u32[]{:S(2)}) %copy-start.3) | copy-done | bytes 7077912
  78.3 3.0 %copy-done.5 = bf16[576,6144]{1,0:T(8,128)(2,1)S(1)} copy-done((bf16[576,6144]{1,0:T(8,128)(2,1)S(1)}, bf16[576,6144]{1,0:T(8,128)(2,1)}, u32[]{:S(2)}) %copy-start.5) | copy-done | bytes 7077912
  81.3 4.6 %hidden_units.1 = (bf16[128,576]{1,0:T(8,128)(2,1)S(1)}, bf16[4,128,768]{2,1,0:T(8,128)(2,1)S(1)}) custom-call(bf16[16,7680]{1,0:T(8,128)(2,1)S(1)} %get-tuple-element.29.refs_0_, bf16[16,7680]{1,0:T(8,128)(2,1)S(1)} %collective-permute-done.4.refs_1_, bf16[16,7680]{1,0:T(8,128)(2,1)S(1)} %collective-permute-done.5.refs_2_, ...), custom_call_target="tpu_custom_call" | custom-call | flops 2264924160 | bytes 23199744 | tf_op jit(solution)/shard_map/hidden_units/pallas_call | solution.py:33
  87.0 1.3 %collective-permute-done.11.refs_1_ = bf16[4,128,768]{2,1,0:T(8,128)(2,1)S(1)} collective-permute-done((bf16[4,128,768]{2,1,0:T(8,128)(2,1)S(1)}, bf16[4,128,768]{2,1,0:T(8,128)(2,1)S(1)}, u32[]{:S(2)}, u32[]{:S(2)}) %collective-permute-start.11) | collective-permute-done | bytes 786464 | tf_op jit(solution)/shard_map/ppermute | solution.py:24
  89.5 6.3 %all-to-all-start.2 = ((bf16[64,8,768]{2,1,0:T(8,128)(2,1)}), bf16[64,8,768]{2,1,0:T(8,128)(2,1)S(1)}, u32[]{:S(2)}, u32[]{:S(2)}) async-start(bf16[64,8,768]{2,1,0:T(8,128)(2,1)} %cores_sum.1), calls=%async_computation.2 | async-start | bytes 1572864 | tf_op jit(solution)/shard_map/all_to_all | solution.py:28
  97.0 15.3 %all-to-all-done.2.refs_1_ = bf16[64,8,768]{2,1,0:T(8,128)(2,1)S(1)} async-done(((bf16[64,8,768]{2,1,0:T(8,128)(2,1)}), bf16[64,8,768]{2,1,0:T(8,128)(2,1)S(1)}, u32[]{:S(2)}, u32[]{:S(2)}) %all-to-all-start.2) | async-done | bytes 786464 | tf_op jit(solution)/shard_map/all_to_all | solution.py:28
  (40 shorter events, 10.0 us)
Async XLA Ops:
  5.3 28.8 %all-to-all-start = ((bf16[16,32,1280]{2,1,0:T(8,128)(2,1)}), bf16[16,32,1280]{2,1,0:T(8,128)(2,1)S(1)}, u32[]{:S(2)}, u32[]{:S(2)}) async-start(bf16[16,32,1280]{2,1,0:T(8,128)(2,1)} %readout.1.after_ref), calls=%async_computation | async-start | bytes 2621440 | tf_op jit(solution)/shard_map/all_to_all | solution.py:28
  13.2 20.8 %copy-start.6 = (bf16[1024,384]{1,0:T(8,128)(2,1)S(1)}, bf16[1024,384]{1,0:T(8,128)(2,1)}, u32[]{:S(2)}) copy-start(bf16[1024,384]{1,0:T(8,128)(2,1)} %refs_1_.1) | copy-start | bytes 2359300
  13.2 45.1 %copy-start.7 = (f32[6144]{0:T(1024)S(1)}, f32[6144]{0:T(1024)}, u32[]{:S(2)}) copy-start(f32[6144]{0:T(1024)} %param.18) | copy-start | bytes 73732
  21.0 2.8 %copy-start = (bf16[576,6144]{1,0:T(8,128)(2,1)}, bf16[576,6144]{1,0:T(8,128)(2,1)S(1)}, u32[]{:S(2)}) copy-start(bf16[576,6144]{1,0:T(8,128)(2,1)S(1)} %get-tuple-element.35.refs_10_.refs_1_) | copy-start | bytes 21233668
  23.8 2.9 %copy-start.2 = (bf16[576,6144]{1,0:T(8,128)(2,1)}, bf16[576,6144]{1,0:T(8,128)(2,1)S(1)}, u32[]{:S(2)}) copy-start(bf16[576,6144]{1,0:T(8,128)(2,1)S(1)} %get-tuple-element.33.refs_8_) | copy-start | bytes 21233668
  26.7 2.9 %copy-start.4 = (bf16[576,6144]{1,0:T(8,128)(2,1)}, bf16[576,6144]{1,0:T(8,128)(2,1)S(1)}, u32[]{:S(2)}) copy-start(bf16[576,6144]{1,0:T(8,128)(2,1)S(1)} %get-tuple-element.34.refs_9_) | copy-start | bytes 21233668
  35.5 1.5 %collective-permute-start = (bf16[16,16,384]{2,1,0:T(8,128)(2,1)S(1)}, bf16[16,16,384]{2,1,0:T(8,128)(2,1)S(1)}, u32[]{:S(2)}, u32[]{:S(2)}) collective-permute-start(bf16[16,16,384]{2,1,0:T(8,128)(2,1)S(1)} %get-tuple-element.24), channel_id=1, source_target_pairs={{0,16},{16,0},{1,17},{17,1},{2,18},{18,2},{3,19},{19,3},{4,20},{20... | collective-permute-start | bytes 589832 | tf_op jit(solution)/shard_map/ppermute | solution.py:24
  37.0 6.1 %collective-permute-start.1 = (bf16[4,16,384]{2,1,0:T(8,128)(2,1)S(1)}, bf16[4,16,384]{2,1,0:T(8,128)(2,1)S(1)}, u32[]{:S(2)}, u32[]{:S(2)}) collective-permute-start(bf16[4,16,384]{2,1,0:T(8,128)(2,1)S(1)} %get-tuple-element.26), channel_id=1, source_target_pairs={{0,32},{32,64},{64,96},{96,0},{1,33},{33,65},{65,97},{97,1},{2,34}... | collective-permute-start | bytes 147464 | tf_op jit(solution)/shard_map/ppermute | solution.py:24
  38.7 5.7 %collective-permute-start.2 = (bf16[4,16,384]{2,1,0:T(8,128)(2,1)S(1)}, bf16[4,16,384]{2,1,0:T(8,128)(2,1)S(1)}, u32[]{:S(2)}, u32[]{:S(2)}) collective-permute-start(bf16[4,16,384]{2,1,0:T(8,128)(2,1)S(1)} %get-tuple-element.27), channel_id=1, source_target_pairs={{0,64},{32,96},{64,0},{96,32},{1,65},{33,97},{65,1},{97,33},{2,66}... | collective-permute-start | bytes 147464 | tf_op jit(solution)/shard_map/ppermute | solution.py:24
  41.6 4.1 %collective-permute-start.3 = (bf16[4,16,384]{2,1,0:T(8,128)(2,1)S(1)}, bf16[4,16,384]{2,1,0:T(8,128)(2,1)S(1)}, u32[]{:S(2)}, u32[]{:S(2)}) collective-permute-start(bf16[4,16,384]{2,1,0:T(8,128)(2,1)S(1)} %get-tuple-element.28), channel_id=1, source_target_pairs={{0,96},{32,0},{64,32},{96,64},{1,97},{33,1},{65,33},{97,65},{2,98}... | collective-permute-start | bytes 147464 | tf_op jit(solution)/shard_map/ppermute | solution.py:24
  58.5 9.6 %collective-permute-start.6 = (bf16[16,7680]{1,0:T(8,128)(2,1)S(1)}, bf16[16,7680]{1,0:T(8,128)(2,1)S(1)}, u32[]{:S(2)}, u32[]{:S(2)}) collective-permute-start(bf16[16,7680]{1,0:T(8,128)(2,1)S(1)} %get-tuple-element.32), channel_id=1, source_target_pairs={{0,32},{32,64},{64,96},{96,0},{1,33},{33,65},{65,97},{97,1},{2,34}... | collective-permute-start | bytes 737288 | tf_op jit(solution)/shard_map/ppermute | solution.py:24
  58.8 10.9 %collective-permute-start.4 = (bf16[16,7680]{1,0:T(8,128)(2,1)S(1)}, bf16[16,7680]{1,0:T(8,128)(2,1)S(1)}, u32[]{:S(2)}, u32[]{:S(2)}) collective-permute-start(bf16[16,7680]{1,0:T(8,128)(2,1)S(1)} %get-tuple-element.30), channel_id=1, source_target_pairs={{0,96},{32,0},{64,32},{96,64},{1,97},{33,1},{65,33},{97,65},{2,98}... | collective-permute-start | bytes 737288 | tf_op jit(solution)/shard_map/ppermute | solution.py:24
  61.8 9.0 %collective-permute-start.5 = (bf16[16,7680]{1,0:T(8,128)(2,1)S(1)}, bf16[16,7680]{1,0:T(8,128)(2,1)S(1)}, u32[]{:S(2)}, u32[]{:S(2)}) collective-permute-start(bf16[16,7680]{1,0:T(8,128)(2,1)S(1)} %get-tuple-element.31), channel_id=1, source_target_pairs={{0,64},{32,96},{64,0},{96,32},{1,65},{33,97},{65,1},{97,33},{2,66}... | collective-permute-start | bytes 737288 | tf_op jit(solution)/shard_map/ppermute | solution.py:24
  62.6 8.2 %collective-permute-start.7 = (bf16[16,7680]{1,0:T(8,128)(2,1)S(1)}, bf16[16,7680]{1,0:T(8,128)(2,1)S(1)}, u32[]{:S(2)}, u32[]{:S(2)}) collective-permute-start(bf16[16,7680]{1,0:T(8,128)(2,1)S(1)} %get-tuple-element.29.refs_0_), channel_id=1, source_target_pairs={{0,16},{16,0},{1,17},{17,1},{2,18},{18,2},{3,19},{19,3},{4,20},{20... | collective-permute-start | bytes 737288 | tf_op jit(solution)/shard_map/ppermute | solution.py:24
  68.1 2.6 %collective-permute-start.10 = (bf16[16,7680]{1,0:T(8,128)(2,1)S(1)}, bf16[16,7680]{1,0:T(8,128)(2,1)S(1)}, u32[]{:S(2)}, u32[]{:S(2)}) collective-permute-start(bf16[16,7680]{1,0:T(8,128)(2,1)S(1)} %collective-permute-done.6.refs_3_), channel_id=1, source_target_pairs={{0,16},{16,0},{1,17},{17,1},{2,18},{18,2},{3,19},{19,3},{4,20},{20... | collective-permute-start | bytes 737288 | tf_op jit(solution)/shard_map/ppermute | solution.py:24
  69.7 1.5 %collective-permute-start.8 = (bf16[16,7680]{1,0:T(8,128)(2,1)S(1)}, bf16[16,7680]{1,0:T(8,128)(2,1)S(1)}, u32[]{:S(2)}, u32[]{:S(2)}) collective-permute-start(bf16[16,7680]{1,0:T(8,128)(2,1)S(1)} %collective-permute-done.4.refs_1_), channel_id=1, source_target_pairs={{0,16},{16,0},{1,17},{17,1},{2,18},{18,2},{3,19},{19,3},{4,20},{20... | collective-permute-start | bytes 737288 | tf_op jit(solution)/shard_map/ppermute | solution.py:24
  70.8 1.5 %collective-permute-start.9 = (bf16[16,7680]{1,0:T(8,128)(2,1)S(1)}, bf16[16,7680]{1,0:T(8,128)(2,1)S(1)}, u32[]{:S(2)}, u32[]{:S(2)}) collective-permute-start(bf16[16,7680]{1,0:T(8,128)(2,1)S(1)} %collective-permute-done.5.refs_2_), channel_id=1, source_target_pairs={{0,16},{16,0},{1,17},{17,1},{2,18},{18,2},{3,19},{19,3},{4,20},{20... | collective-permute-start | bytes 737288 | tf_op jit(solution)/shard_map/ppermute | solution.py:24
  72.3 3.0 %copy-start.1 = (bf16[576,6144]{1,0:T(8,128)(2,1)S(1)}, bf16[576,6144]{1,0:T(8,128)(2,1)}, u32[]{:S(2)}) copy-start(bf16[576,6144]{1,0:T(8,128)(2,1)} %copy-done) | copy-start | bytes 21233668
  75.3 3.0 %copy-start.3 = (bf16[576,6144]{1,0:T(8,128)(2,1)S(1)}, bf16[576,6144]{1,0:T(8,128)(2,1)}, u32[]{:S(2)}) copy-start(bf16[576,6144]{1,0:T(8,128)(2,1)} %copy-done.2) | copy-start | bytes 21233668
  78.3 3.0 %copy-start.5 = (bf16[576,6144]{1,0:T(8,128)(2,1)S(1)}, bf16[576,6144]{1,0:T(8,128)(2,1)}, u32[]{:S(2)}) copy-start(bf16[576,6144]{1,0:T(8,128)(2,1)} %copy-done.4) | copy-start | bytes 21233668
  85.9 9.9 %copy-start.8 = (s32[4,8,2]{1,2,0:T(2,128)S(1)}, s32[4,8,2]{1,2,0:T(2,128)}, u32[]{:S(2)}) copy-start(s32[4,8,2]{1,2,0:T(2,128)} %param.19) | copy-start | bytes 772
  85.9 9.9 %copy-start.10 = (f32[4,8,2]{1,2,0:T(2,128)S(1)}, f32[4,8,2]{1,2,0:T(2,128)}, u32[]{:S(2)}) copy-start(f32[4,8,2]{1,2,0:T(2,128)} %param.20) | copy-start | bytes 772
  85.9 2.4 %collective-permute-start.11 = (bf16[4,128,768]{2,1,0:T(8,128)(2,1)S(1)}, bf16[4,128,768]{2,1,0:T(8,128)(2,1)S(1)}, u32[]{:S(2)}, u32[]{:S(2)}) collective-permute-start(bf16[4,128,768]{2,1,0:T(8,128)(2,1)S(1)} %get-tuple-element.37), channel_id=1, source_target_pairs={{0,16},{16,0},{1,17},{17,1},{2,18},{18,2},{3,19},{19,3},{4,20},{20... | collective-permute-start | bytes 2359304 | tf_op jit(solution)/shard_map/ppermute | solution.py:24
  89.5 22.8 %all-to-all-start.2 = ((bf16[64,8,768]{2,1,0:T(8,128)(2,1)}), bf16[64,8,768]{2,1,0:T(8,128)(2,1)S(1)}, u32[]{:S(2)}, u32[]{:S(2)}) async-start(bf16[64,8,768]{2,1,0:T(8,128)(2,1)} %cores_sum.1), calls=%async_computation.2 | async-start | bytes 1572864 | tf_op jit(solution)/shard_map/all_to_all | solution.py:28
  (1 other events, 0.7 us)

commit v7 on v6

--- a/solution.py
+++ b/solution.py
@@ -119,9 +119,11 @@
             )
             carried = jnp.where(row_in == 2 * pair, both[:, :size], carried)
             carried = jnp.where(row_in == 2 * pair + 1, both[:, size:], carried)
-        decay = [decay_ref[t, pl.program_id(0) * heads + h] for t in range(STEPS)]
+        here = lax.broadcasted_iota(jnp.int32, decay_ref.shape, 1) == pl.program_id(0) * heads + h
+        decay = jnp.sum(jnp.where(here, decay_ref[...], 0.0), axis=1, keepdims=True)
+        decay = [decay[t : t + 1] for t in range(STEPS)]
         run = decay[0]
-        first = jnp.full((n, size), run, F32)
+        first = jnp.broadcast_to(run, (n, size))
         for t in range(1, STEPS):
             run = run * decay[t]
             first = jnp.where(row // ROWS == t, run, first)
@@ -155,7 +157,7 @@
         out_shape=jax.ShapeDtypeStruct((16, n, packed), BF16),
         grid=(heads // at_once,),
         in_specs=[
-            pl.BlockSpec(memory_space=pltpu.SMEM),
+            pl.BlockSpec(decay.shape, lambda i: (0, 0)),
             pl.BlockSpec((STEPS, 2, ROWS), lambda i: (0, 0, 0)),
             pl.BlockSpec(hidden_in.shape, lambda i: (0, 0, 0)),
             pl.BlockSpec((STEPS, 3, ROWS, at_once * size), lambda i: (0, 0, 0, i)),
@@ -180,7 +182,7 @@
     )
 
 
-def project_kernel(place_ref, got_ref, weight_ref, done_ref, mine_ref, other_ref):
+def project_kernel(place_ref, got_ref, weight_ref, mine_ref, other_ref):
     c = place_ref[2]
     depth = weight_ref.shape[0]
     for part in range(2):
@@ -193,10 +195,10 @@
             other_ref[8 * part + i] = jnp.where(c == 0, b, a)
 
 
-def project(got, weight, done):
+def project(got, weight):
     out = [jax.ShapeDtypeStruct((16, 16, weight.shape[1]), BF16)] * 2
     flops = 1024 * weight.size
-    return call(project_kernel, "project", out, got, weight, done, flops=flops)
+    return call(project_kernel, "project", out, got, weight, flops=flops)
 
 
 def by_y_kernel(place_ref, mine_ref, got_ref, *out_refs):
@@ -326,7 +328,7 @@
     return pl.pallas_call(
         fetch_kernel,
         out_shape=[pltpu.VMEM(w.shape, w.dtype) for w in weights]
-        + [jax.ShapeDtypeStruct((8, 128), F32)],
+        + [pltpu.VMEM((8, 128), F32)],
         in_specs=[pl.BlockSpec(memory_space=pl.ANY)]
         + [pl.BlockSpec(memory_space=pltpu.HBM)] * len(weights),
         out_specs=[pl.BlockSpec(memory_space=pltpu.VMEM)] * (len(weights) + 1),
@@ -340,7 +342,7 @@
 
 
 def hidden_kernel(place_ref, *refs):
-    x_refs, (gate_ref, up_ref, down_ref, hidden_ref, theirs_ref) = refs[:8], refs[8:]
+    x_refs, (gate_ref, up_ref, down_ref, _, hidden_ref, theirs_ref) = refs[:8], refs[8:]
     share = theirs_ref.shape[2]
     y, c = place_ref[1], place_ref[2]
     x = jnp.concatenate([r[:, : gate_ref.shape[1]] for r in x_refs], axis=0)
@@ -355,7 +357,7 @@
         theirs_ref[k] = jnp.dot(hidden, down_ref[:, at], preferred_element_type=F32).astype(BF16)
 
 
-def hidden_units(pieces, gate, up, down_weight, share):
+def hidden_units(pieces, gate, up, down_weight, done, share):
     units = gate.shape[0]
     rows = sum(p.shape[0] for p in pieces)
     out = [
@@ -363,7 +365,7 @@
         jax.ShapeDtypeStruct((4, rows, share), BF16),
     ]
     flops = 5 * rows * gate.size
-    arrays = (*pieces, gate, up, down_weight)
+    arrays = (*pieces, gate, up, down_weight, done)
     return call(hidden_kernel, "hidden_units", out, *arrays, flops=flops)
 
 
@@ -462,12 +464,9 @@
     share = hidden_in.shape[2] // 8
 
     sent = readouts(step_qkv, decay_rates, kv_state, attn_gain, hidden_in, routes)
-    gate, up, down_weight, done = fetch(
-        sent, w_gate[0].swapaxes(0, 1), w_up[0].swapaxes(0, 1), w_down[0]
-    )
     got = exchange(sent, ("z", "x"))
 
-    mine, other = project(got, out_proj, done)
+    mine, other = project(got, out_proj)
     sums = sums_by_y(mine, over("c", other, 1))
     select, hidden = slots(got, out_proj.shape[1])
     sums = sums[:1] + [over("y", sums[k], k) for k in (1, 2, 3)]
@@ -475,9 +474,13 @@
     pieces = exchange(attend(select, hidden, sums), ("z", "x"))
     pieces = norm(ffn_gain, pieces)
     by_y = pieces[:1] + [over("y", pieces[k], -k) for k in (1, 2, 3)]
+    gate, up, down_weight, done = fetch(
+        pieces[1], w_gate[0].swapaxes(0, 1), w_up[0].swapaxes(0, 1), w_down[0]
+    )
+    by_y, done = lax.optimization_barrier((by_y, done))
     by_core = [over("c", piece, 1) for piece in by_y]
 
-    hidden, theirs = hidden_units(by_y + by_core, gate, up, down_weight, share)
+    hidden, theirs = hidden_units(by_y + by_core, gate, up, down_weight, done, share)
     theirs = over("c", theirs, 1)
     sums = cores_sum(down(hidden, down_weight, share), theirs)
 

time: 114 us -> 104 us (0.912)
  blocking collectives: 12.4 us -> 40.2 us
  local copies, waits for them, and re-layouts: 18.4 us -> 0.03 us
  waiting for transfers between devices: 34.7 us -> 25.4 us
  starting transfers between devices: 24.6 us -> 15.5 us
    all_to_all x1 -> x2, blocking collectives: 12.4 us -> 40.2 us  [exchange(): return lax.all_to_all(value, axes, split_axis=0, concat_axis=0, tiled=True)]
    unnamed x22 -> x10, local copies, waits for them, and re-layouts: 18.4 us -> 0.03 us
    all_to_all x2 -> x1, starting transfers between devices: 14.3 us -> 4.64 us  [exchange(): return lax.all_to_all(value, axes, split_axis=0, concat_axis=0, tiled=True)]
    ppermute x12, waiting for transfers between devices: 15 us -> 9.81 us  [over(): lax.ppermute(value, axis, [(i, (i + shift) % size) for i in range(size)])]
    all_to_all x2 -> x1, waiting for transfers between devices: 19.8 us -> 15.6 us  [exchange(): return lax.all_to_all(value, axes, split_axis=0, concat_axis=0, tiled=True)]
  transfers between devices with their start and end apart: 14 -> 13, of which waited for: 11 -> 11; matrix products, arithmetic and copies ran while one was open for 0% -> 0% of each run, Pallas kernels for 9% -> 9%
where the time goes in v7:
time: 104 us
  blocking collectives  40.2 us (39%)
  waiting for transfers between devices  25.4 us (24%)
  Pallas kernels  21.8 us (21%)
  starting transfers between devices  15.5 us (15%)
    all_to_all x2, blocking collectives, exchange(): return lax.all_to_all(value, axes, split_axis=0, concat_axis=0, tiled=True)  40.2 us
    all_to_all x1, waiting for transfers between devices, exchange(): return lax.all_to_all(value, axes, split_axis=0, concat_axis=0, tiled=True)  15.6 us
    ppermute x12, starting transfers between devices, over(): lax.ppermute(value, axis, [(i, (i + shift) % size) for i in range(size)])  10.8 us
    pallas_call x11, Pallas kernels, call(): pl.pallas_call(lambda *refs: kernel(device_place(), *refs), out_shape=out...  9.98 us
    ppermute x12, waiting for transfers between devices, over(): lax.ppermute(value, axis, [(i, (i + shift) % size) for i in range(size)])  9.81 us
    pallas_call x1, Pallas kernels, fetch(): pl.pallas_call(fetch_kernel, out_shape=[pltpu.VMEM(w.shape, w.dtype) for...  7.06 us
    pallas_call x1, Pallas kernels, readouts(): pl.pallas_call(readout_kernel, out_shape=jax.ShapeDtypeStruct((16, n, pac...  4.74 us
    all_to_all x1, starting transfers between devices, exchange(): return lax.all_to_all(value, axes, split_axis=0, concat_axis=0, tiled=True)  4.64 us
  transfers between devices with their start and end apart: 13, of which 11 were waited for; matrix products, arithmetic and copies ran while one was open for 0% of the time, Pallas kernels for 9%

profile of v7, /device:TPU:0, one launch (start us, length us, event | category | flops | bytes accessed | tf_op | source)
XLA Modules:
  0.0 103.7 jit_solution(7885094068410634721)
XLA Ops:
  0.7 4.7 %readout.1 = bf16[16,32,1280]{2,1,0:T(8,128)(2,1)} custom-call(f32[4,8]{1,0:T(4,128)} %decay_ref.1, s32[4,2,8]{2,1,0:T(2,128)} %bitcast.15, bf16[4,8,6144]{2,1,0:T(8,128)(2,1)} %hidden_ref.1, bf16[4,3,8,1024]{3,2,1,0:T(8,128)(2,1)} %bitcast.21, f32[8,8,128,128]{3,2,1,0:T(8,128)} %state_ref.1, f32[1,1024]{1,0:T(1,128)} %bitcast.24), custom_call_target="tpu_custom_call" | custom-call | flops 134217728 | bytes 4194304 | tf_op jit(solution)/shard_map/readout/pallas_call | solution.py:155
  5.4 27.9 %all_to_all.15.refs_0_ = bf16[16,32,1280]{2,1,0:T(8,128)(2,1)S(1)} all-to-all(bf16[16,32,1280]{2,1,0:T(8,128)(2,1)} %readout.1), channel_id=1, replica_groups=mesh['y'=4,'c'=2,'z'=4,'x'=4] {'z','x'}, dimensions={0} | all-to-all | bytes 2621440 | tf_op jit(solution)/shard_map/all_to_all | solution.py:28
  33.3 0.7 project.1
  34.1 1.4 %collective-permute-done.refs_1_ = bf16[16,16,384]{2,1,0:T(8,128)(2,1)S(1)} collective-permute-done((bf16[16,16,384]{2,1,0:T(8,128)(2,1)S(1)}, bf16[16,16,384]{2,1,0:T(8,128)(2,1)S(1)}, u32[]{:S(2)}, u32[]{:S(2)}) %collective-permute-start) | collective-permute-done | bytes 196640 | tf_op jit(solution)/shard_map/ppermute | solution.py:24
  35.6 1.6 %collective-permute-start.1 = (bf16[4,16,384]{2,1,0:T(8,128)(2,1)S(1)}, bf16[4,16,384]{2,1,0:T(8,128)(2,1)S(1)}, u32[]{:S(2)}, u32[]{:S(2)}) collective-permute-start(bf16[4,16,384]{2,1,0:T(8,128)(2,1)S(1)} %get-tuple-element.30), channel_id=1, source_target_pairs={{0,32},{32,64},{64,96},{96,0},{1,33},{33,65},{65,97},{97,1},{2,34}... | collective-permute-start | bytes 147464 | tf_op jit(solution)/shard_map/ppermute | solution.py:24
  37.3 2.9 %collective-permute-start.2 = (bf16[4,16,384]{2,1,0:T(8,128)(2,1)S(1)}, bf16[4,16,384]{2,1,0:T(8,128)(2,1)S(1)}, u32[]{:S(2)}, u32[]{:S(2)}) collective-permute-start(bf16[4,16,384]{2,1,0:T(8,128)(2,1)S(1)} %get-tuple-element.31), channel_id=1, source_target_pairs={{0,64},{32,96},{64,0},{96,32},{1,65},{33,97},{65,1},{97,33},{2,66}... | collective-permute-start | bytes 147464 | tf_op jit(solution)/shard_map/ppermute | solution.py:24
  40.2 1.3 %collective-permute-start.3 = (bf16[4,16,384]{2,1,0:T(8,128)(2,1)S(1)}, bf16[4,16,384]{2,1,0:T(8,128)(2,1)S(1)}, u32[]{:S(2)}, u32[]{:S(2)}) collective-permute-start(bf16[4,16,384]{2,1,0:T(8,128)(2,1)S(1)} %get-tuple-element.32), channel_id=1, source_target_pairs={{0,96},{32,0},{64,32},{96,64},{1,97},{33,1},{65,33},{97,65},{2,98}... | collective-permute-start | bytes 147464 | tf_op jit(solution)/shard_map/ppermute | solution.py:24
  41.7 1.3 %collective-permute-done.2.refs_4_ = bf16[4,16,384]{2,1,0:T(8,128)(2,1)S(1)} collective-permute-done((bf16[4,16,384]{2,1,0:T(8,128)(2,1)S(1)}, bf16[4,16,384]{2,1,0:T(8,128)(2,1)S(1)}, u32[]{:S(2)}, u32[]{:S(2)}) %collective-permute-start.2) | collective-permute-done | bytes 49184 | tf_op jit(solution)/shard_map/ppermute | solution.py:24
  43.0 1.3 %collective-permute-done.3.refs_5_ = bf16[4,16,384]{2,1,0:T(8,128)(2,1)S(1)} collective-permute-done((bf16[4,16,384]{2,1,0:T(8,128)(2,1)S(1)}, bf16[4,16,384]{2,1,0:T(8,128)(2,1)S(1)}, u32[]{:S(2)}, u32[]{:S(2)}) %collective-permute-start.3) | collective-permute-done | bytes 49184 | tf_op jit(solution)/shard_map/ppermute | solution.py:24
  44.5 12.3 %all_to_all.16.refs_1_ = bf16[16,32,384]{2,1,0:T(8,128)(2,1)S(1)} all-to-all(bf16[16,32,384]{2,1,0:T(8,128)(2,1)S(1)} %attend.1), channel_id=1, replica_groups=mesh['y'=4,'c'=2,'z'=4,'x'=4] {'z','x'}, dimensions={0} | all-to-all | bytes 786432 | tf_op jit(solution)/shard_map/all_to_all | solution.py:28
  57.0 2.6 %collective-permute-start.4 = (bf16[16,7680]{1,0:T(8,128)(2,1)S(1)}, bf16[16,7680]{1,0:T(8,128)(2,1)S(1)}, u32[]{:S(2)}, u32[]{:S(2)}) collective-permute-start(bf16[16,7680]{1,0:T(8,128)(2,1)S(1)} %get-tuple-element.34.after_ref), channel_id=1, source_target_pairs={{0,96},{32,0},{64,32},{96,64},{1,97},{33,1},{65,33},{97,65},{2,98}... | collective-permute-start | bytes 737288 | tf_op jit(solution)/shard_map/ppermute | solution.py:24
  59.6 0.9 collective-permute-start.6
  60.5 7.1 %fetch.1 = (bf16[576,6144]{1,0:T(8,128)(2,1)S(1)}, bf16[576,6144]{1,0:T(8,128)(2,1)S(1)}, bf16[576,6144]{1,0:T(8,128)(2,1)S(1)}, f32[8,128]{1,0:T(8,128)S(1)}) custom-call(bf16[16,7680]{1,0:T(8,128)(2,1)} %copy-done.1, bf16[576,6144]{1,0:T(8,128)(2,1)} %bitcast.18, bf16[576,6144]{1,0:T(8,128)(2,1)} %bitcast.19, bf16[576,6144]{1,0:T(8,128)(2,1)} %bitcast.20), custom_call_target="tpu_custom_call" | custom-call | bytes 21233664 | tf_op jit(solution)/shard_map/fetch/pallas_call | solution.py:328
  67.6 0.8 collective-permute-done.5.refs_2_
  68.4 2.2 %collective-permute-done.6.refs_3_ = bf16[16,7680]{1,0:T(8,128)(2,1)S(1)} collective-permute-done((bf16[16,7680]{1,0:T(8,128)(2,1)S(1)}, bf16[16,7680]{1,0:T(8,128)(2,1)S(1)}, u32[]{:S(2)}, u32[]{:S(2)}) %collective-permute-start.6) | collective-permute-done | bytes 245792 | tf_op jit(solution)/shard_map/ppermute | solution.py:24
  73.2 4.6 %hidden_units.1 = (bf16[128,576]{1,0:T(8,128)(2,1)S(1)}, bf16[4,128,768]{2,1,0:T(8,128)(2,1)S(1)}) custom-call(bf16[16,7680]{1,0:T(8,128)(2,1)S(1)} %get-tuple-element.38.refs_0_, bf16[16,7680]{1,0:T(8,128)(2,1)S(1)} %collective-permute-done.4.refs_1_, bf16[16,7680]{1,0:T(8,128)(2,1)S(1)} %collective-permute-done.5.refs_2_, ...), custom_call_target="tpu_custom_call" | custom-call | flops 2264924160 | bytes 23203840 | tf_op jit(solution)/shard_map/hidden_units/pallas_call | solution.py:33
  78.1 0.9 down.1.refs_0_
  78.9 1.3 %collective-permute-done.11.refs_1_ = bf16[4,128,768]{2,1,0:T(8,128)(2,1)S(1)} collective-permute-done((bf16[4,128,768]{2,1,0:T(8,128)(2,1)S(1)}, bf16[4,128,768]{2,1,0:T(8,128)(2,1)S(1)}, u32[]{:S(2)}, u32[]{:S(2)}) %collective-permute-start.11) | collective-permute-done | bytes 786464 | tf_op jit(solution)/shard_map/ppermute | solution.py:24
  80.2 1.2 %cores_sum.1 = bf16[64,8,768]{2,1,0:T(8,128)(2,1)} custom-call(f32[4,128,768]{2,1,0:T(8,128)S(1)} %down.1.refs_0_, bf16[4,128,768]{2,1,0:T(8,128)(2,1)S(1)} %collective-permute-done.11.refs_1_), custom_call_target="tpu_custom_call" | custom-call | bytes 2359296 | tf_op jit(solution)/shard_map/cores_sum/pallas_call | solution.py:33
  81.4 4.6 %all-to-all-start.2 = ((bf16[64,8,768]{2,1,0:T(8,128)(2,1)}), bf16[64,8,768]{2,1,0:T(8,128)(2,1)S(1)}, u32[]{:S(2)}, u32[]{:S(2)}) async-start(bf16[64,8,768]{2,1,0:T(8,128)(2,1)} %cores_sum.1), calls=%async_computation.2 | async-start | bytes 1572864 | tf_op jit(solution)/shard_map/all_to_all | solution.py:28
  86.0 0.5 mix_weights.1.refs_0_
  86.5 0.7 owned.1
  87.2 15.6 %all-to-all-done.2.refs_1_ = bf16[64,8,768]{2,1,0:T(8,128)(2,1)S(1)} async-done(((bf16[64,8,768]{2,1,0:T(8,128)(2,1)}), bf16[64,8,768]{2,1,0:T(8,128)(2,1)S(1)}, u32[]{:S(2)}, u32[]{:S(2)}) %all-to-all-start.2) | async-done | bytes 786464 | tf_op jit(solution)/shard_map/all_to_all | solution.py:28
  102.8 0.9 mix.1
  (27 shorter events, 3.5 us)
Async XLA Ops:
  0.6 32.7 %copy-start = (bf16[1024,384]{1,0:T(8,128)(2,1)S(1)}, bf16[1024,384]{1,0:T(8,128)(2,1)}, u32[]{:S(2)}) copy-start(bf16[1024,384]{1,0:T(8,128)(2,1)} %refs_1_.1) | copy-start | bytes 2359300
  0.6 56.1 %copy-start.2 = (f32[6144]{0:T(1024)S(1)}, f32[6144]{0:T(1024)}, u32[]{:S(2)}) copy-start(f32[6144]{0:T(1024)} %param.18) | copy-start | bytes 73732
  34.0 1.5 %collective-permute-start = (bf16[16,16,384]{2,1,0:T(8,128)(2,1)S(1)}, bf16[16,16,384]{2,1,0:T(8,128)(2,1)S(1)}, u32[]{:S(2)}, u32[]{:S(2)}) collective-permute-start(bf16[16,16,384]{2,1,0:T(8,128)(2,1)S(1)} %get-tuple-element.28), channel_id=1, source_target_pairs={{0,16},{16,0},{1,17},{17,1},{2,18},{18,2},{3,19},{19,3},{4,20},{20... | collective-permute-start | bytes 589832 | tf_op jit(solution)/shard_map/ppermute | solution.py:24
  35.6 6.1 %collective-permute-start.1 = (bf16[4,16,384]{2,1,0:T(8,128)(2,1)S(1)}, bf16[4,16,384]{2,1,0:T(8,128)(2,1)S(1)}, u32[]{:S(2)}, u32[]{:S(2)}) collective-permute-start(bf16[4,16,384]{2,1,0:T(8,128)(2,1)S(1)} %get-tuple-element.30), channel_id=1, source_target_pairs={{0,32},{32,64},{64,96},{96,0},{1,33},{33,65},{65,97},{97,1},{2,34}... | collective-permute-start | bytes 147464 | tf_op jit(solution)/shard_map/ppermute | solution.py:24
  37.3 5.7 %collective-permute-start.2 = (bf16[4,16,384]{2,1,0:T(8,128)(2,1)S(1)}, bf16[4,16,384]{2,1,0:T(8,128)(2,1)S(1)}, u32[]{:S(2)}, u32[]{:S(2)}) collective-permute-start(bf16[4,16,384]{2,1,0:T(8,128)(2,1)S(1)} %get-tuple-element.31), channel_id=1, source_target_pairs={{0,64},{32,96},{64,0},{96,32},{1,65},{33,97},{65,1},{97,33},{2,66}... | collective-permute-start | bytes 147464 | tf_op jit(solution)/shard_map/ppermute | solution.py:24
  40.2 4.1 %collective-permute-start.3 = (bf16[4,16,384]{2,1,0:T(8,128)(2,1)S(1)}, bf16[4,16,384]{2,1,0:T(8,128)(2,1)S(1)}, u32[]{:S(2)}, u32[]{:S(2)}) collective-permute-start(bf16[4,16,384]{2,1,0:T(8,128)(2,1)S(1)} %get-tuple-element.32), channel_id=1, source_target_pairs={{0,96},{32,0},{64,32},{96,64},{1,97},{33,1},{65,33},{97,65},{2,98}... | collective-permute-start | bytes 147464 | tf_op jit(solution)/shard_map/ppermute | solution.py:24
  56.9 3.6 %copy-start.1 = (bf16[16,7680]{1,0:T(8,128)(2,1)}, bf16[16,7680]{1,0:T(8,128)(2,1)S(1)}, u32[]{:S(2)}) copy-start(bf16[16,7680]{1,0:T(8,128)(2,1)S(1)} %get-tuple-element.34.after_ref) | copy-start | bytes 737284
  57.0 10.7 %collective-permute-start.4 = (bf16[16,7680]{1,0:T(8,128)(2,1)S(1)}, bf16[16,7680]{1,0:T(8,128)(2,1)S(1)}, u32[]{:S(2)}, u32[]{:S(2)}) collective-permute-start(bf16[16,7680]{1,0:T(8,128)(2,1)S(1)} %get-tuple-element.34.after_ref), channel_id=1, source_target_pairs={{0,96},{32,0},{64,32},{96,64},{1,97},{33,1},{65,33},{97,65},{2,98}... | collective-permute-start | bytes 737288 | tf_op jit(solution)/shard_map/ppermute | solution.py:24
  59.6 8.9 %collective-permute-start.5 = (bf16[16,7680]{1,0:T(8,128)(2,1)S(1)}, bf16[16,7680]{1,0:T(8,128)(2,1)S(1)}, u32[]{:S(2)}, u32[]{:S(2)}) collective-permute-start(bf16[16,7680]{1,0:T(8,128)(2,1)S(1)} %get-tuple-element.35), channel_id=1, source_target_pairs={{0,64},{32,96},{64,0},{96,32},{1,65},{33,97},{65,1},{97,33},{2,66}... | collective-permute-start | bytes 737288 | tf_op jit(solution)/shard_map/ppermute | solution.py:24
  59.6 11.1 %collective-permute-start.6 = (bf16[16,7680]{1,0:T(8,128)(2,1)S(1)}, bf16[16,7680]{1,0:T(8,128)(2,1)S(1)}, u32[]{:S(2)}, u32[]{:S(2)}) collective-permute-start(bf16[16,7680]{1,0:T(8,128)(2,1)S(1)} %get-tuple-element.36), channel_id=1, source_target_pairs={{0,32},{32,64},{64,96},{96,0},{1,33},{33,65},{65,97},{97,1},{2,34}... | collective-permute-start | bytes 737288 | tf_op jit(solution)/shard_map/ppermute | solution.py:24
  70.6 1.5 %collective-permute-start.10 = (bf16[16,7680]{1,0:T(8,128)(2,1)S(1)}, bf16[16,7680]{1,0:T(8,128)(2,1)S(1)}, u32[]{:S(2)}, u32[]{:S(2)}) collective-permute-start(bf16[16,7680]{1,0:T(8,128)(2,1)S(1)} %collective-permute-done.6.refs_3_), channel_id=1, source_target_pairs={{0,16},{16,0},{1,17},{17,1},{2,18},{18,2},{3,19},{19,3},{4,20},{20... | collective-permute-start | bytes 737288 | tf_op jit(solution)/shard_map/ppermute | solution.py:24
  70.6 1.9 %collective-permute-start.7 = (bf16[16,7680]{1,0:T(8,128)(2,1)S(1)}, bf16[16,7680]{1,0:T(8,128)(2,1)S(1)}, u32[]{:S(2)}, u32[]{:S(2)}) collective-permute-start(bf16[16,7680]{1,0:T(8,128)(2,1)S(1)} %get-tuple-element.38.refs_0_), channel_id=1, source_target_pairs={{0,16},{16,0},{1,17},{17,1},{2,18},{18,2},{3,19},{19,3},{4,20},{20... | collective-permute-start | bytes 737288 | tf_op jit(solution)/shard_map/ppermute | solution.py:24
  71.2 1.7 %collective-permute-start.8 = (bf16[16,7680]{1,0:T(8,128)(2,1)S(1)}, bf16[16,7680]{1,0:T(8,128)(2,1)S(1)}, u32[]{:S(2)}, u32[]{:S(2)}) collective-permute-start(bf16[16,7680]{1,0:T(8,128)(2,1)S(1)} %collective-permute-done.4.refs_1_), channel_id=1, source_target_pairs={{0,16},{16,0},{1,17},{17,1},{2,18},{18,2},{3,19},{19,3},{4,20},{20... | collective-permute-start | bytes 737288 | tf_op jit(solution)/shard_map/ppermute | solution.py:24
  71.2 2.1 %collective-permute-start.9 = (bf16[16,7680]{1,0:T(8,128)(2,1)S(1)}, bf16[16,7680]{1,0:T(8,128)(2,1)S(1)}, u32[]{:S(2)}, u32[]{:S(2)}) collective-permute-start(bf16[16,7680]{1,0:T(8,128)(2,1)S(1)} %collective-permute-done.5.refs_2_), channel_id=1, source_target_pairs={{0,16},{16,0},{1,17},{17,1},{2,18},{18,2},{3,19},{19,3},{4,20},{20... | collective-permute-start | bytes 737288 | tf_op jit(solution)/shard_map/ppermute | solution.py:24
  77.8 8.2 %copy-start.3 = (s32[4,8,2]{1,2,0:T(2,128)S(1)}, s32[4,8,2]{1,2,0:T(2,128)}, u32[]{:S(2)}) copy-start(s32[4,8,2]{1,2,0:T(2,128)} %param.19) | copy-start | bytes 772
  77.8 8.2 %copy-start.4 = (f32[4,8,2]{1,2,0:T(2,128)S(1)}, f32[4,8,2]{1,2,0:T(2,128)}, u32[]{:S(2)}) copy-start(f32[4,8,2]{1,2,0:T(2,128)} %param.20) | copy-start | bytes 772
  77.8 2.4 %collective-permute-start.11 = (bf16[4,128,768]{2,1,0:T(8,128)(2,1)S(1)}, bf16[4,128,768]{2,1,0:T(8,128)(2,1)S(1)}, u32[]{:S(2)}, u32[]{:S(2)}) collective-permute-start(bf16[4,128,768]{2,1,0:T(8,128)(2,1)S(1)} %get-tuple-element.47), channel_id=1, source_target_pairs={{0,16},{16,0},{1,17},{17,1},{2,18},{18,2},{3,19},{19,3},{4,20},{20... | collective-permute-start | bytes 2359304 | tf_op jit(solution)/shard_map/ppermute | solution.py:24
  81.4 21.4 %all-to-all-start.2 = ((bf16[64,8,768]{2,1,0:T(8,128)(2,1)}), bf16[64,8,768]{2,1,0:T(8,128)(2,1)S(1)}, u32[]{:S(2)}, u32[]{:S(2)}) async-start(bf16[64,8,768]{2,1,0:T(8,128)(2,1)} %cores_sum.1), calls=%async_computation.2 | async-start | bytes 1572864 | tf_op jit(solution)/shard_map/all_to_all | solution.py:28

commit v8 on v7

--- a/solution.py
+++ b/solution.py
@@ -83,21 +83,19 @@
 def readout_kernel(
     decay_ref, routes_ref, hidden_ref, qkv_ref, state_ref, gain_ref, out_ref
 ):
-    c = lax.axis_index("c")
+    y = lax.axis_index("y")
     cols = hidden_ref.shape[2] // 16
-    depth = out_ref.shape[2] - 256
+    depth = out_ref.shape[2] - 128
 
     @pl.when(pl.program_id(0) == 0)
     def _():
-        names = [columns_of(routes_ref[2 * c + t].astype(F32)) for t in range(2)]
-        names = widened(jnp.concatenate(names, axis=0)).astype(BF16)
+        names = widened(columns_of(routes_ref[y].astype(F32)))
         for i in range(16):
-            at = slice(i * cols, (i + 1) * cols)
-            rows = [hidden_ref[2 * c + t, :, at].astype(F32) for t in range(2)]
-            rows = jnp.concatenate(rows, axis=0).astype(BF16)
-            out_ref[i, :16, depth:] = rows[:, :256]
-            out_ref[i, 16:, depth : depth + 128] = rows[:, 256:]
-            out_ref[i, 16:, depth + 128 :] = names
+            rows = hidden_ref[y, :, i * cols : (i + 1) * cols].astype(F32)
+            first = jnp.concatenate([rows[:, :128], rows[:, 128:256]], axis=0)
+            last = jnp.concatenate([rows[:, 256:], names], axis=0)
+            out_ref[i, :16, depth:] = first.astype(BF16)
+            out_ref[i, 16:, depth:] = last.astype(BF16)
 
     n, size = STEPS * ROWS, state_ref.shape[2]
     heads = state_ref.shape[1]
@@ -151,7 +149,7 @@
     heads, size = state.shape[1], state.shape[2]
     at_once = min(heads, 4)
     n = STEPS * ROWS
-    packed = heads * size + 256
+    packed = heads * size + 128
     return pl.pallas_call(
         readout_kernel,
         out_shape=jax.ShapeDtypeStruct((16, n, packed), BF16),
@@ -185,44 +183,42 @@
 def project_kernel(place_ref, got_ref, weight_ref, mine_ref, other_ref):
     c = place_ref[2]
     depth = weight_ref.shape[0]
+    halves = []
     for part in range(2):
         rows = got_ref[8 * part : 8 * part + 8, :, :depth].reshape(256, depth)
-        out = jnp.dot(rows, weight_ref[...], preferred_element_type=F32).astype(BF16)
-        for i in range(8):
-            a = out[32 * i : 32 * i + 16]
-            b = out[32 * i + 16 : 32 * i + 32]
-            mine_ref[8 * part + i] = jnp.where(c == 0, a, b)
-            other_ref[8 * part + i] = jnp.where(c == 0, b, a)
+        halves.append(jnp.dot(rows, weight_ref[...], preferred_element_type=F32))
+    mine = jnp.where(c == 0, halves[0], halves[1]).astype(BF16)
+    other = jnp.where(c == 0, halves[1], halves[0]).astype(BF16)
+    mine_ref[...] = mine.reshape(mine_ref.shape)
+    other_ref[...] = other.reshape(other_ref.shape)
 
 
 def project(got, weight):
-    out = [jax.ShapeDtypeStruct((16, 16, weight.shape[1]), BF16)] * 2
-    flops = 1024 * weight.size
-    return call(project_kernel, "project", out, got, weight, flops=flops)
+    out = [jax.ShapeDtypeStruct((8, STEPS, ROWS, weight.shape[1]), BF16)] * 2
+    return call(project_kernel, "project", out, got, weight, flops=1024 * weight.size)
 
 
 def by_y_kernel(place_ref, mine_ref, got_ref, *out_refs):
     y = place_ref[1]
     for k, ref in enumerate(out_refs):
-        for x in range(4):
-            i = turned(y, k) * 4 + x
-            ref[x] = (mine_ref[i].astype(F32) + got_ref[i].astype(F32)).astype(BF16)
+        t = turned(y, k)
+        for i in range(8):
+            ref[i] = (mine_ref[i, t].astype(F32) + got_ref[i, t].astype(F32)).astype(BF16)
 
 
 def sums_by_y(mine, got):
-    out = [jax.ShapeDtypeStruct((4,) + mine.shape[1:], BF16)] * 4
+    out = [jax.ShapeDtypeStruct((8,) + mine.shape[2:], BF16)] * 4
     return call(by_y_kernel, "sums_by_y", out, mine, got)
 
 
 def slots_kernel(place_ref, got_ref, select_ref, hidden_ref):
-    y = place_ref[1]
-    depth = got_ref.shape[2] - 256
+    c = place_ref[2]
+    depth = got_ref.shape[2] - 128
     names = []
-    for x in range(4):
-        i = y * 4 + x
-        tail = got_ref[i, 16:, depth:]
-        names.append(tail[:, 128:].astype(F32))
-        hidden_ref[x] = jnp.concatenate([got_ref[i, :16, depth:], tail[:, :128]], axis=1)
+    for i in range(8):
+        tail = got_ref[8 * c + i, :, depth:].astype(F32)
+        hidden_ref[i] = jnp.concatenate([tail[:8], tail[8:16], tail[16:24]], axis=1)
+        names.append(tail[24:])
     names = jnp.concatenate(names, axis=0)
     n = names.shape[0]
     across = names.T
@@ -230,8 +226,7 @@
     over_i = lax.broadcasted_iota(jnp.int32, (n, n), 1)
     earlier = (down_i // ROWS == over_i // ROWS) & (down_i < over_i)
     slot = lax.broadcasted_iota(jnp.int32, (256, n), 0)
-    lane = lax.broadcasted_iota(jnp.int32, (1, n), 1)
-    base = lane // 16 * 4 + lane // ROWS % 2 * 2
+    base = lax.broadcasted_iota(jnp.int32, (1, n), 1) // ROWS * 2
     select = jnp.zeros((256, n), F32)
     for j in range(2):
         mine = across[j : j + 1, :]
@@ -245,72 +240,74 @@
 
 
 def slots(got, cols):
-    out = [jax.ShapeDtypeStruct((256, 64), BF16), jax.ShapeDtypeStruct((4, 16, cols), BF16)]
+    out = [jax.ShapeDtypeStruct((256, 64), BF16), jax.ShapeDtypeStruct((8, ROWS, cols), F32)]
     return call(slots_kernel, "slots", out, got, flops=1 << 20)
 
 
 def attend_kernel(place_ref, select_ref, hidden_ref, *refs):
     sum_refs, out_ref = refs[:4], refs[4]
     rows = []
-    for x in range(4):
-        total = hidden_ref[x].astype(F32)
+    for i in range(8):
+        total = hidden_ref[i]
         for ref in sum_refs:
-            total += ref[x].astype(F32)
-        rows.append(total.astype(BF16))
-        for z in range(4):
-            out_ref[4 * z + x, 16:] = rows[x]
-    rows = jnp.concatenate(rows, axis=0)
-    sent = jnp.dot(select_ref[...], rows, preferred_element_type=F32).astype(BF16)
+            total += ref[i].astype(F32)
+        rows.append(total)
+        total = total.astype(BF16)
+        for j in range(2):
+            out_ref[8 * j + i, 2] = total
+    rows = jnp.concatenate(rows, axis=0).astype(BF16)
+    sent = jnp.dot(select_ref[...], rows, preferred_element_type=F32)
     for i in range(16):
-        out_ref[i, :16] = sent[16 * i : 16 * i + 16]
+        for j in range(2):
+            out_ref[i, j] = sent[16 * i + 8 * j : 16 * i + 8 * j + 8].astype(BF16)
 
 
 def attend(select, hidden, sums):
-    out = jax.ShapeDtypeStruct((16, 32, hidden.shape[2]), BF16)
+    out = jax.ShapeDtypeStruct((16, 3) + hidden.shape[1:], BF16)
     return call(attend_kernel, "attend", out, select, hidden, *sums, flops=1 << 23)
 
 
 def norm_kernel(place_ref, gain_ref, got_ref, *out_refs):
     y = place_ref[1]
-    cols = got_ref.shape[2]
+    cols = got_ref.shape[3]
     total = jnp.zeros((16, cols), F32)
+    slots = []
     for i in range(16):
-        value = got_ref[i, :16].astype(F32)
+        value = jnp.concatenate([got_ref[i, j].astype(F32) for j in range(2)], axis=0)
+        slots.append(value)
         total += value * value
     mean = jnp.sum(total, axis=-1, keepdims=True) / (16 * cols)
     scale = lax.rsqrt(mean + EPS)
     for i in range(16):
         at = slice(i * cols, (i + 1) * cols)
-        value = (got_ref[i, :16].astype(F32) * scale * gain_ref[:, at]).astype(BF16)
+        value = (slots[i] * scale * gain_ref[:, at]).astype(BF16)
         for out_ref in out_refs:
             out_ref[:, at] = value
     for k, out_ref in enumerate(out_refs):
-        for x in range(4):
-            at = slice((16 + x) * cols, (17 + x) * cols)
-            out_ref[:, at] = got_ref[turned(y, 4 - k) * 4 + x, 16:]
+        for i in range(2):
+            at = slice((16 + i) * cols, (17 + i) * cols)
+            rows = [got_ref[turned(y, 4 - k) * 4 + 2 * core + i, 2] for core in range(2)]
+            rows = jnp.concatenate([r.astype(F32) for r in rows], axis=0)
+            out_ref[:, at] = rows.astype(BF16)
 
 
 def norm(gain, got):
-    out = [jax.ShapeDtypeStruct((16, 20 * got.shape[2]), BF16)] * 4
+    out = [jax.ShapeDtypeStruct((16, 18 * got.shape[3]), BF16)] * 4
     return call(norm_kernel, "norm", out, gain.reshape(1, -1), got)
 
 
 def owned_kernel(place_ref, *refs):
     own_refs, other_refs, out_ref = refs[:4], refs[4:8], refs[8]
-    z, y, c = place_ref[0], place_ref[1], place_ref[2]
-    share = out_ref.shape[1]
-    start = own_refs[0].shape[1] - 2 * share
-    at = lanes_from(start + c * share, share)
+    z, y, c = place_ref
+    start = own_refs[0].shape[1] - out_ref.shape[2]
     for k in range(4):
-
-        @pl.when(turned(z, 4 - y) == k)
-        def _():
-            out_ref[pl.ds(pl.multiple_of(16 * c, 16), 16), :] = own_refs[k][:, at]
-            out_ref[pl.ds(pl.multiple_of(16 - 16 * c, 16), 16), :] = other_refs[k][:, at]
+        rows = jnp.where(z // 2 == c, own_refs[k][:, start:], other_refs[k][:, start:])
+        rows = rows.astype(F32)
+        out_ref[turned(y, k)] = jnp.where(c == 0, rows[:ROWS], rows[ROWS:]).astype(BF16)
 
 
 def owned(by_y, by_core, share):
-    out = jax.ShapeDtypeStruct((STEPS * ROWS, share), BF16)
+    out = jax.ShapeDtypeStruct((STEPS, ROWS, share), BF16)
     return call(owned_kernel, "owned", out, *by_y, *by_core)
 
 
@@ -350,6 +347,13 @@
     gate = lax.dot_general(gate_ref[...], x, across, preferred_element_type=F32)
     up = lax.dot_general(up_ref[...], x, across, preferred_element_type=F32)
     hidden = (gate / (1.0 + jnp.exp(-gate)) * up).T.astype(BF16)
+    n = hidden.shape[0]
+    row = lax.broadcasted_iota(jnp.int32, (n, n), 0)
+    lane = lax.broadcasted_iota(jnp.int32, (n, n), 1)
+    source = lax.bitwise_xor(row // 64, c) * 64 + turned(row // 2, 4 - y) * 16
+    source += row // 8 % 8 * 2 + row % 2
+    moved = (lane == source).astype(F32).astype(BF16)
+    hidden = jnp.dot(moved, hidden, preferred_element_type=F32).astype(BF16)
     hidden_ref[...] = hidden
     for k in range(4):
         block = turned(y, k) * 2 + (1 - c)
@@ -384,23 +388,15 @@
 
 
 def cores_kernel(place_ref, ours_ref, theirs_ref, out_ref):
-    y, c = place_ref[1], place_ref[2]
-    half = ours_ref.shape[1] // 2
     for k in range(4):
-        same = ours_ref[k, :half] + theirs_ref[k, half:].astype(F32)
-        flip = ours_ref[k, half:] + theirs_ref[k, :half].astype(F32)
-        low = jnp.where(c == 0, same, flip)
-        high = jnp.where(c == 0, flip, same)
-        for ky in range(4):
-            for x in range(4):
-                rows = slice(16 * ky + 4 * x, 16 * ky + 4 * x + 4)
-                block = jnp.concatenate([low[rows], high[rows]], axis=0)
-                out_ref[turned(y, k) * 16 + turned(y, ky) * 4 + x] = block.astype(BF16)
+        total = ours_ref[k] + theirs_ref[k].astype(F32)
+        out_ref[turned(place_ref[1], k)] = total.astype(BF16)
 
 
 def cores_sum(ours, theirs):
-    out = jax.ShapeDtypeStruct((64, 8, theirs.shape[2]), BF16)
-    return call(cores_kernel, "cores_sum", out, ours, theirs)
+    out = jax.ShapeDtypeStruct(theirs.shape, BF16)
+    out = call(cores_kernel, "cores_sum", out, ours, theirs)
+    return out.reshape(64, 8, theirs.shape[2])
 
 
 def weights_kernel(place_ref, routes_ref, weights_ref, out_ref):
@@ -471,8 +467,7 @@
     select, hidden = slots(got, out_proj.shape[1])
     sums = sums[:1] + [over("y", sums[k], k) for k in (1, 2, 3)]
 
-    pieces = exchange(attend(select, hidden, sums), ("z", "x"))
-    pieces = norm(ffn_gain, pieces)
+    pieces = norm(ffn_gain, exchange(attend(select, hidden, sums), ("z", "x")))
     by_y = pieces[:1] + [over("y", pieces[k], -k) for k in (1, 2, 3)]
     gate, up, down_weight, done = fetch(
         pieces[1], w_gate[0].swapaxes(0, 1), w_up[0].swapaxes(0, 1), w_down[0]
@@ -487,7 +482,7 @@
     attended = owned(by_y, by_core, share)
     mix = mix_weights(routes, route_weights)
     mixed = mixed_rows(mix, exchange(sums, ("y", "z", "x")))
-    return attended.reshape(STEPS, ROWS, share), mixed.reshape(STEPS, ROWS, share)
+    return attended, mixed.reshape(STEPS, ROWS, share)
 
 
 def solution(mesh):

time: 104 us -> 101 us (0.971)
  blocking collectives: 40.2 us -> 38.5 us
  waiting for transfers between devices: 25.4 us -> 24.2 us
    all_to_all x2, blocking collectives: 40.2 us -> 38.5 us  [exchange(): return lax.all_to_all(value, axes, split_axis=0, concat_axis=0, tiled=True)]
    ppermute x12, waiting for transfers between devices: 9.81 us -> 8.59 us  [over(): lax.ppermute(value, axis, [(i, (i + shift) % size) for i in range(size)])]
  transfers between devices with their start and end apart: 13 -> 13, of which waited for: 11 -> 10; matrix products, arithmetic and copies ran while one was open for 0% -> 0% of each run, Pallas kernels for 9% -> 9%
where the time goes in v8:
time: 101 us
  blocking collectives  38.5 us (38%)
  waiting for transfers between devices  24.2 us (24%)
  Pallas kernels  21.7 us (21%)
  starting transfers between devices  15.5 us (15%)
    all_to_all x2, blocking collectives, exchange(): return lax.all_to_all(value, axes, split_axis=0, concat_axis=0, tiled=True)  38.5 us
    all_to_all x1, waiting for transfers between devices, exchange(): return lax.all_to_all(value, axes, split_axis=0, concat_axis=0, tiled=True)  15.6 us
    ppermute x12, starting transfers between devices, over(): lax.ppermute(value, axis, [(i, (i + shift) % size) for i in range(size)])  10.8 us
    pallas_call x11, Pallas kernels, call(): pl.pallas_call(lambda *refs: kernel(device_place(), *refs), out_shape=out...  9.96 us
    ppermute x12, waiting for transfers between devices, over(): lax.ppermute(value, axis, [(i, (i + shift) % size) for i in range(size)])  8.59 us
    pallas_call x1, Pallas kernels, fetch(): pl.pallas_call(fetch_kernel, out_shape=[pltpu.VMEM(w.shape, w.dtype) for...  7.06 us
    pallas_call x1, Pallas kernels, readouts(): pl.pallas_call(readout_kernel, out_shape=jax.ShapeDtypeStruct((16, n, pac...  4.66 us
    all_to_all x1, starting transfers between devices, exchange(): return lax.all_to_all(value, axes, split_axis=0, concat_axis=0, tiled=True)  4.64 us
  transfers between devices with their start and end apart: 13, of which 10 were waited for; matrix products, arithmetic and copies ran while one was open for 0% of the time, Pallas kernels for 9%

profile of v8, /device:TPU:0, one launch (start us, length us, event | category | flops | bytes accessed | tf_op | source)
XLA Modules:
  0.0 100.7 jit_solution(16777004634234302920)
XLA Ops:
  0.7 4.7 %readout.1 = bf16[16,32,1152]{2,1,0:T(8,128)(2,1)} custom-call(f32[4,8]{1,0:T(4,128)} %decay_ref.1, s32[4,2,8]{2,1,0:T(2,128)} %bitcast.15, bf16[4,8,6144]{2,1,0:T(8,128)(2,1)} %hidden_ref.1, bf16[4,3,8,1024]{3,2,1,0:T(8,128)(2,1)} %bitcast.21, f32[8,8,128,128]{3,2,1,0:T(8,128)} %state_ref.1, f32[1,1024]{1,0:T(1,128)} %bitcast.23), custom_call_target="tpu_custom_call" | custom-call | flops 134217728 | bytes 4194304 | tf_op jit(solution)/shard_map/readout/pallas_call | solution.py:153
  5.3 26.5 %all_to_all.15.refs_0_ = bf16[16,32,1152]{2,1,0:T(8,128)(2,1)S(1)} all-to-all(bf16[16,32,1152]{2,1,0:T(8,128)(2,1)} %readout.1), channel_id=1, replica_groups=mesh['y'=4,'c'=2,'z'=4,'x'=4] {'z','x'}, dimensions={0} | all-to-all | bytes 2359296 | tf_op jit(solution)/shard_map/all_to_all | solution.py:28
  31.8 0.7 project.1
  32.6 1.4 %collective-permute-done.refs_1_ = bf16[8,4,8,384]{3,2,1,0:T(8,128)(2,1)S(1)} collective-permute-done((bf16[8,4,8,384]{3,2,1,0:T(8,128)(2,1)S(1)}, bf16[8,4,8,384]{3,2,1,0:T(8,128)(2,1)S(1)}, u32[]{:S(2)}, u32[]{:S(2)}) %collective-permute-start) | collective-permute-done | bytes 196640 | tf_op jit(solution)/shard_map/ppermute | solution.py:24
  34.1 1.6 %collective-permute-start.1 = (bf16[8,8,384]{2,1,0:T(8,128)(2,1)S(1)}, bf16[8,8,384]{2,1,0:T(8,128)(2,1)S(1)}, u32[]{:S(2)}, u32[]{:S(2)}) collective-permute-start(bf16[8,8,384]{2,1,0:T(8,128)(2,1)S(1)} %get-tuple-element.30), channel_id=1, source_target_pairs={{0,32},{32,64},{64,96},{96,0},{1,33},{33,65},{65,97},{97,1},{2,34}... | collective-permute-start | bytes 147464 | tf_op jit(solution)/shard_map/ppermute | solution.py:24
  35.8 2.9 %collective-permute-start.2 = (bf16[8,8,384]{2,1,0:T(8,128)(2,1)S(1)}, bf16[8,8,384]{2,1,0:T(8,128)(2,1)S(1)}, u32[]{:S(2)}, u32[]{:S(2)}) collective-permute-start(bf16[8,8,384]{2,1,0:T(8,128)(2,1)S(1)} %get-tuple-element.31), channel_id=1, source_target_pairs={{0,64},{32,96},{64,0},{96,32},{1,65},{33,97},{65,1},{97,33},{2,66}... | collective-permute-start | bytes 147464 | tf_op jit(solution)/shard_map/ppermute | solution.py:24
  38.7 1.3 %collective-permute-start.3 = (bf16[8,8,384]{2,1,0:T(8,128)(2,1)S(1)}, bf16[8,8,384]{2,1,0:T(8,128)(2,1)S(1)}, u32[]{:S(2)}, u32[]{:S(2)}) collective-permute-start(bf16[8,8,384]{2,1,0:T(8,128)(2,1)S(1)} %get-tuple-element.32), channel_id=1, source_target_pairs={{0,96},{32,0},{64,32},{96,64},{1,97},{33,1},{65,33},{97,65},{2,98}... | collective-permute-start | bytes 147464 | tf_op jit(solution)/shard_map/ppermute | solution.py:24
  40.2 1.3 %collective-permute-done.2.refs_4_ = bf16[8,8,384]{2,1,0:T(8,128)(2,1)S(1)} collective-permute-done((bf16[8,8,384]{2,1,0:T(8,128)(2,1)S(1)}, bf16[8,8,384]{2,1,0:T(8,128)(2,1)S(1)}, u32[]{:S(2)}, u32[]{:S(2)}) %collective-permute-start.2) | collective-permute-done | bytes 49184 | tf_op jit(solution)/shard_map/ppermute | solution.py:24
  41.5 1.3 %collective-permute-done.3.refs_5_ = bf16[8,8,384]{2,1,0:T(8,128)(2,1)S(1)} collective-permute-done((bf16[8,8,384]{2,1,0:T(8,128)(2,1)S(1)}, bf16[8,8,384]{2,1,0:T(8,128)(2,1)S(1)}, u32[]{:S(2)}, u32[]{:S(2)}) %collective-permute-start.3) | collective-permute-done | bytes 49184 | tf_op jit(solution)/shard_map/ppermute | solution.py:24
  43.0 11.9 %all_to_all.16.refs_1_ = bf16[16,3,8,384]{3,2,1,0:T(8,128)(2,1)S(1)} all-to-all(bf16[16,3,8,384]{3,2,1,0:T(8,128)(2,1)S(1)} %attend.1), channel_id=1, replica_groups=mesh['y'=4,'c'=2,'z'=4,'x'=4] {'z','x'}, dimensions={0} | all-to-all | bytes 589824 | tf_op jit(solution)/shard_map/all_to_all | solution.py:28
  55.1 2.6 %collective-permute-start.4 = (bf16[16,6912]{1,0:T(8,128)(2,1)S(1)}, bf16[16,6912]{1,0:T(8,128)(2,1)S(1)}, u32[]{:S(2)}, u32[]{:S(2)}) collective-permute-start(bf16[16,6912]{1,0:T(8,128)(2,1)S(1)} %get-tuple-element.34.after_ref), channel_id=1, source_target_pairs={{0,96},{32,0},{64,32},{96,64},{1,97},{33,1},{65,33},{97,65},{2,98}... | collective-permute-start | bytes 663560 | tf_op jit(solution)/shard_map/ppermute | solution.py:24
  57.7 0.9 collective-permute-start.6
  58.7 7.1 %fetch.1 = (bf16[576,6144]{1,0:T(8,128)(2,1)S(1)}, bf16[576,6144]{1,0:T(8,128)(2,1)S(1)}, bf16[576,6144]{1,0:T(8,128)(2,1)S(1)}, f32[8,128]{1,0:T(8,128)S(1)}) custom-call(bf16[16,6912]{1,0:T(8,128)(2,1)} %copy-done.1, bf16[576,6144]{1,0:T(8,128)(2,1)} %bitcast.18, bf16[576,6144]{1,0:T(8,128)(2,1)} %bitcast.19, bf16[576,6144]{1,0:T(8,128)(2,1)} %bitcast.20), custom_call_target="tpu_custom_call" | custom-call | bytes 21233664 | tf_op jit(solution)/shard_map/fetch/pallas_call | solution.py:325
  65.8 1.9 %collective-permute-done.6.refs_3_ = bf16[16,6912]{1,0:T(8,128)(2,1)S(1)} collective-permute-done((bf16[16,6912]{1,0:T(8,128)(2,1)S(1)}, bf16[16,6912]{1,0:T(8,128)(2,1)S(1)}, u32[]{:S(2)}, u32[]{:S(2)}) %collective-permute-start.6) | collective-permute-done | bytes 221216 | tf_op jit(solution)/shard_map/ppermute | solution.py:24
  67.7 0.5 collective-permute-start.7
  70.2 4.7 %hidden_units.1 = (bf16[128,576]{1,0:T(8,128)(2,1)S(1)}, bf16[4,128,768]{2,1,0:T(8,128)(2,1)S(1)}) custom-call(bf16[16,6912]{1,0:T(8,128)(2,1)S(1)} %get-tuple-element.38.refs_0_, bf16[16,6912]{1,0:T(8,128)(2,1)S(1)} %collective-permute-done.4.refs_1_, bf16[16,6912]{1,0:T(8,128)(2,1)S(1)} %collective-permute-done.5.refs_2_, ...), custom_call_target="tpu_custom_call" | custom-call | flops 2264924160 | bytes 23007232 | tf_op jit(solution)/shard_map/hidden_units/pallas_call | solution.py:33
  75.2 0.9 down.1.refs_0_
  76.1 1.2 %collective-permute-done.11.refs_1_ = bf16[4,128,768]{2,1,0:T(8,128)(2,1)S(1)} collective-permute-done((bf16[4,128,768]{2,1,0:T(8,128)(2,1)S(1)}, bf16[4,128,768]{2,1,0:T(8,128)(2,1)S(1)}, u32[]{:S(2)}, u32[]{:S(2)}) %collective-permute-start.11) | collective-permute-done | bytes 786464 | tf_op jit(solution)/shard_map/ppermute | solution.py:24
  77.3 1.0 %cores_sum.1 = bf16[4,128,768]{2,1,0:T(8,128)(2,1)} custom-call(f32[4,128,768]{2,1,0:T(8,128)S(1)} %down.1.refs_0_, bf16[4,128,768]{2,1,0:T(8,128)(2,1)S(1)} %collective-permute-done.11.refs_1_), custom_call_target="tpu_custom_call" | custom-call | bytes 2359296 | tf_op jit(solution)/shard_map/cores_sum/pallas_call | solution.py:33
  78.3 4.6 %all-to-all-start.2 = ((bf16[64,8,768]{2,1,0:T(8,128)(2,1)}), bf16[64,8,768]{2,1,0:T(8,128)(2,1)S(1)}, u32[]{:S(2)}, u32[]{:S(2)}) async-start(bf16[64,8,768]{2,1,0:T(8,128)(2,1)} %bitcast.10), calls=%async_computation.2 | async-start | bytes 1572864 | tf_op jit(solution)/shard_map/all_to_all | solution.py:28
  83.0 0.5 mix_weights.1.refs_0_
  83.5 0.7 owned.1
  84.2 15.6 %all-to-all-done.2.refs_1_ = bf16[64,8,768]{2,1,0:T(8,128)(2,1)S(1)} async-done(((bf16[64,8,768]{2,1,0:T(8,128)(2,1)}), bf16[64,8,768]{2,1,0:T(8,128)(2,1)S(1)}, u32[]{:S(2)}, u32[]{:S(2)}) %all-to-all-start.2) | async-done | bytes 786464 | tf_op jit(solution)/shard_map/all_to_all | solution.py:28
  99.8 0.9 mix.1
  (27 shorter events, 3.0 us)
Async XLA Ops:
  0.6 31.2 %copy-start = (bf16[1024,384]{1,0:T(8,128)(2,1)S(1)}, bf16[1024,384]{1,0:T(8,128)(2,1)}, u32[]{:S(2)}) copy-start(bf16[1024,384]{1,0:T(8,128)(2,1)} %refs_1_.1) | copy-start | bytes 2359300
  0.6 54.3 %copy-start.2 = (f32[6144]{0:T(1024)S(1)}, f32[6144]{0:T(1024)}, u32[]{:S(2)}) copy-start(f32[6144]{0:T(1024)} %param.18) | copy-start | bytes 73732
  32.5 1.5 %collective-permute-start = (bf16[8,4,8,384]{3,2,1,0:T(8,128)(2,1)S(1)}, bf16[8,4,8,384]{3,2,1,0:T(8,128)(2,1)S(1)}, u32[]{:S(2)}, u32[]{:S(2)}) collective-permute-start(bf16[8,4,8,384]{3,2,1,0:T(8,128)(2,1)S(1)} %get-tuple-element.28), channel_id=1, source_target_pairs={{0,16},{16,0},{1,17},{17,1},{2,18},{18,2},{3,19},{19,3},{4,20},{20... | collective-permute-start | bytes 589832 | tf_op jit(solution)/shard_map/ppermute | solution.py:24
  34.1 6.1 %collective-permute-start.1 = (bf16[8,8,384]{2,1,0:T(8,128)(2,1)S(1)}, bf16[8,8,384]{2,1,0:T(8,128)(2,1)S(1)}, u32[]{:S(2)}, u32[]{:S(2)}) collective-permute-start(bf16[8,8,384]{2,1,0:T(8,128)(2,1)S(1)} %get-tuple-element.30), channel_id=1, source_target_pairs={{0,32},{32,64},{64,96},{96,0},{1,33},{33,65},{65,97},{97,1},{2,34}... | collective-permute-start | bytes 147464 | tf_op jit(solution)/shard_map/ppermute | solution.py:24
  35.8 5.7 %collective-permute-start.2 = (bf16[8,8,384]{2,1,0:T(8,128)(2,1)S(1)}, bf16[8,8,384]{2,1,0:T(8,128)(2,1)S(1)}, u32[]{:S(2)}, u32[]{:S(2)}) collective-permute-start(bf16[8,8,384]{2,1,0:T(8,128)(2,1)S(1)} %get-tuple-element.31), channel_id=1, source_target_pairs={{0,64},{32,96},{64,0},{96,32},{1,65},{33,97},{65,1},{97,33},{2,66}... | collective-permute-start | bytes 147464 | tf_op jit(solution)/shard_map/ppermute | solution.py:24
  38.7 4.1 %collective-permute-start.3 = (bf16[8,8,384]{2,1,0:T(8,128)(2,1)S(1)}, bf16[8,8,384]{2,1,0:T(8,128)(2,1)S(1)}, u32[]{:S(2)}, u32[]{:S(2)}) collective-permute-start(bf16[8,8,384]{2,1,0:T(8,128)(2,1)S(1)} %get-tuple-element.32), channel_id=1, source_target_pairs={{0,96},{32,0},{64,32},{96,64},{1,97},{33,1},{65,33},{97,65},{2,98}... | collective-permute-start | bytes 147464 | tf_op jit(solution)/shard_map/ppermute | solution.py:24
  55.1 3.6 %copy-start.1 = (bf16[16,6912]{1,0:T(8,128)(2,1)}, bf16[16,6912]{1,0:T(8,128)(2,1)S(1)}, u32[]{:S(2)}) copy-start(bf16[16,6912]{1,0:T(8,128)(2,1)S(1)} %get-tuple-element.34.after_ref) | copy-start | bytes 663556
  55.1 10.7 %collective-permute-start.4 = (bf16[16,6912]{1,0:T(8,128)(2,1)S(1)}, bf16[16,6912]{1,0:T(8,128)(2,1)S(1)}, u32[]{:S(2)}, u32[]{:S(2)}) collective-permute-start(bf16[16,6912]{1,0:T(8,128)(2,1)S(1)} %get-tuple-element.34.after_ref), channel_id=1, source_target_pairs={{0,96},{32,0},{64,32},{96,64},{1,97},{33,1},{65,33},{97,65},{2,98}... | collective-permute-start | bytes 663560 | tf_op jit(solution)/shard_map/ppermute | solution.py:24
  57.7 8.1 %collective-permute-start.5 = (bf16[16,6912]{1,0:T(8,128)(2,1)S(1)}, bf16[16,6912]{1,0:T(8,128)(2,1)S(1)}, u32[]{:S(2)}, u32[]{:S(2)}) collective-permute-start(bf16[16,6912]{1,0:T(8,128)(2,1)S(1)} %get-tuple-element.35), channel_id=1, source_target_pairs={{0,64},{32,96},{64,0},{96,32},{1,65},{33,97},{65,1},{97,33},{2,66}... | collective-permute-start | bytes 663560 | tf_op jit(solution)/shard_map/ppermute | solution.py:24
  57.7 10.0 %collective-permute-start.6 = (bf16[16,6912]{1,0:T(8,128)(2,1)S(1)}, bf16[16,6912]{1,0:T(8,128)(2,1)S(1)}, u32[]{:S(2)}, u32[]{:S(2)}) collective-permute-start(bf16[16,6912]{1,0:T(8,128)(2,1)S(1)} %get-tuple-element.36), channel_id=1, source_target_pairs={{0,32},{32,64},{64,96},{96,0},{1,33},{33,65},{65,97},{97,1},{2,34}... | collective-permute-start | bytes 663560 | tf_op jit(solution)/shard_map/ppermute | solution.py:24
  67.7 1.5 %collective-permute-start.10 = (bf16[16,6912]{1,0:T(8,128)(2,1)S(1)}, bf16[16,6912]{1,0:T(8,128)(2,1)S(1)}, u32[]{:S(2)}, u32[]{:S(2)}) collective-permute-start(bf16[16,6912]{1,0:T(8,128)(2,1)S(1)} %collective-permute-done.6.refs_3_), channel_id=1, source_target_pairs={{0,16},{16,0},{1,17},{17,1},{2,18},{18,2},{3,19},{19,3},{4,20},{20... | collective-permute-start | bytes 663560 | tf_op jit(solution)/shard_map/ppermute | solution.py:24
  67.7 1.8 %collective-permute-start.7 = (bf16[16,6912]{1,0:T(8,128)(2,1)S(1)}, bf16[16,6912]{1,0:T(8,128)(2,1)S(1)}, u32[]{:S(2)}, u32[]{:S(2)}) collective-permute-start(bf16[16,6912]{1,0:T(8,128)(2,1)S(1)} %get-tuple-element.38.refs_0_), channel_id=1, source_target_pairs={{0,16},{16,0},{1,17},{17,1},{2,18},{18,2},{3,19},{19,3},{4,20},{20... | collective-permute-start | bytes 663560 | tf_op jit(solution)/shard_map/ppermute | solution.py:24
  68.3 1.6 %collective-permute-start.8 = (bf16[16,6912]{1,0:T(8,128)(2,1)S(1)}, bf16[16,6912]{1,0:T(8,128)(2,1)S(1)}, u32[]{:S(2)}, u32[]{:S(2)}) collective-permute-start(bf16[16,6912]{1,0:T(8,128)(2,1)S(1)} %collective-permute-done.4.refs_1_), channel_id=1, source_target_pairs={{0,16},{16,0},{1,17},{17,1},{2,18},{18,2},{3,19},{19,3},{4,20},{20... | collective-permute-start | bytes 663560 | tf_op jit(solution)/shard_map/ppermute | solution.py:24
  68.3 1.9 %collective-permute-start.9 = (bf16[16,6912]{1,0:T(8,128)(2,1)S(1)}, bf16[16,6912]{1,0:T(8,128)(2,1)S(1)}, u32[]{:S(2)}, u32[]{:S(2)}) collective-permute-start(bf16[16,6912]{1,0:T(8,128)(2,1)S(1)} %collective-permute-done.5.refs_2_), channel_id=1, source_target_pairs={{0,16},{16,0},{1,17},{17,1},{2,18},{18,2},{3,19},{19,3},{4,20},{20... | collective-permute-start | bytes 663560 | tf_op jit(solution)/shard_map/ppermute | solution.py:24
  74.9 8.1 %copy-start.3 = (s32[4,8,2]{1,2,0:T(2,128)S(1)}, s32[4,8,2]{1,2,0:T(2,128)}, u32[]{:S(2)}) copy-start(s32[4,8,2]{1,2,0:T(2,128)} %param.19) | copy-start | bytes 772
  74.9 8.1 %copy-start.4 = (f32[4,8,2]{1,2,0:T(2,128)S(1)}, f32[4,8,2]{1,2,0:T(2,128)}, u32[]{:S(2)}) copy-start(f32[4,8,2]{1,2,0:T(2,128)} %param.20) | copy-start | bytes 772
  74.9 2.4 %collective-permute-start.11 = (bf16[4,128,768]{2,1,0:T(8,128)(2,1)S(1)}, bf16[4,128,768]{2,1,0:T(8,128)(2,1)S(1)}, u32[]{:S(2)}, u32[]{:S(2)}) collective-permute-start(bf16[4,128,768]{2,1,0:T(8,128)(2,1)S(1)} %get-tuple-element.47), channel_id=1, source_target_pairs={{0,16},{16,0},{1,17},{17,1},{2,18},{18,2},{3,19},{19,3},{4,20},{20... | collective-permute-start | bytes 2359304 | tf_op jit(solution)/shard_map/ppermute | solution.py:24
  78.3 21.5 %all-to-all-start.2 = ((bf16[64,8,768]{2,1,0:T(8,128)(2,1)}), bf16[64,8,768]{2,1,0:T(8,128)(2,1)S(1)}, u32[]{:S(2)}, u32[]{:S(2)}) async-start(bf16[64,8,768]{2,1,0:T(8,128)(2,1)} %bitcast.10), calls=%async_computation.2 | async-start | bytes 1572864 | tf_op jit(solution)/shard_map/all_to_all | solution.py:28

commit v9 on v8

--- a/solution.py
+++ b/solution.py
@@ -152,7 +152,7 @@
     packed = heads * size + 128
     return pl.pallas_call(
         readout_kernel,
-        out_shape=jax.ShapeDtypeStruct((16, n, packed), BF16),
+        out_shape=pltpu.VMEM((16, n, packed), BF16),
         grid=(heads // at_once,),
         in_specs=[
             pl.BlockSpec(decay.shape, lambda i: (0, 0)),
@@ -163,7 +163,7 @@
             pl.BlockSpec((1, at_once * size), lambda i: (0, i)),
         ],
         out_specs=pl.BlockSpec((16, n, packed), lambda i: (0, 0, 0)),
-        compiler_params=vmem_params(56),
+        compiler_params=vmem_params(58),
         cost_estimate=pl.CostEstimate(
             flops=2 * STEPS * ROWS * ROWS * heads * size * size * 2,
             bytes_accessed=state.size * 4,
@@ -472,7 +472,7 @@
     gate, up, down_weight, done = fetch(
         pieces[1], w_gate[0].swapaxes(0, 1), w_up[0].swapaxes(0, 1), w_down[0]
     )
-    by_y, done = lax.optimization_barrier((by_y, done))
+    by_y[2], done = lax.optimization_barrier((by_y[2], done))
     by_core = [over("c", piece, 1) for piece in by_y]
 
     hidden, theirs = hidden_units(by_y + by_core, gate, up, down_weight, done, share)

time: 101 us -> 98.9 us (0.979)
  waiting for transfers between devices: 24.2 us -> 21.9 us
  starting transfers between devices: 15.5 us -> 17 us
    ppermute x12, waiting for transfers between devices: 8.59 us -> 6.38 us  [over(): lax.ppermute(value, axis, [(i, (i + shift) % size) for i in range(size)])]
    all_to_all x1, starting transfers between devices: 4.64 us -> 5.95 us  [exchange(): return lax.all_to_all(value, axes, split_axis=0, concat_axis=0, tiled=True)]
  transfers between devices with their start and end apart: 13 -> 13, of which waited for: 10 -> 8; matrix products, arithmetic and copies ran while one was open for 0% -> 0% of each run, Pallas kernels for 9% -> 9%
where the time goes in v9:
time: 98.9 us; the launch traced here: 98.6 us
  blocking collectives  38.3 us (39%)
  waiting for transfers between devices  21.9 us (22%)
  Pallas kernels  20.7 us (21%)
  starting transfers between devices  17 us (17%)
    all_to_all x2, blocking collectives, exchange(): return lax.all_to_all(value, axes, split_axis=0, concat_axis=0, tiled=True)  38.3 us
    all_to_all x1, waiting for transfers between devices, exchange(): return lax.all_to_all(value, axes, split_axis=0, concat_axis=0, tiled=True)  15.5 us
    ppermute x12, starting transfers between devices, over(): lax.ppermute(value, axis, [(i, (i + shift) % size) for i in range(size)])  11.1 us
    pallas_call x11, Pallas kernels, call(): pl.pallas_call(lambda *refs: kernel(device_place(), *refs), out_shape=out...  9.95 us
    pallas_call x1, Pallas kernels, fetch(): pl.pallas_call(fetch_kernel, out_shape=[pltpu.VMEM(w.shape, w.dtype) for...  7.06 us
    ppermute x12, waiting for transfers between devices, over(): lax.ppermute(value, axis, [(i, (i + shift) % size) for i in range(size)])  6.38 us
    all_to_all x1, starting transfers between devices, exchange(): return lax.all_to_all(value, axes, split_axis=0, concat_axis=0, tiled=True)  5.95 us
    pallas_call x1, Pallas kernels, readouts(): pl.pallas_call(readout_kernel, out_shape=pltpu.VMEM((16, n, packed), BF16...  3.65 us
  transfers between devices with their start and end apart: 13, of which 8 were waited for; matrix products, arithmetic and copies ran while one was open for 0% of the time, Pallas kernels for 9%

profile of v9, /device:TPU:0, one launch (start us, length us, event | category | flops | bytes accessed | tf_op | source)
XLA Modules:
  0.0 98.6 jit_solution(5749506508381011222)
XLA Ops:
  0.7 3.7 %readout.1 = bf16[16,32,1152]{2,1,0:T(8,128)(2,1)S(1)} custom-call(f32[4,8]{1,0:T(4,128)} %decay_ref.1, s32[4,2,8]{2,1,0:T(2,128)} %bitcast.15, bf16[4,8,6144]{2,1,0:T(8,128)(2,1)} %hidden_ref.1, bf16[4,3,8,1024]{3,2,1,0:T(8,128)(2,1)} %bitcast.21, f32[8,8,128,128]{3,2,1,0:T(8,128)} %state_ref.1, f32[1,1024]{1,0:T(1,128)} %bitcast.23), custom_call_target="tpu_custom_call" | custom-call | flops 134217728 | bytes 4194304 | tf_op jit(solution)/shard_map/readout/pallas_call | solution.py:153
  4.3 26.3 %all_to_all.15.refs_0_ = bf16[16,32,1152]{2,1,0:T(8,128)(2,1)S(1)} all-to-all(bf16[16,32,1152]{2,1,0:T(8,128)(2,1)S(1)} %readout.1), channel_id=1, replica_groups=mesh['y'=4,'c'=2,'z'=4,'x'=4] {'z','x'}, dimensions={0} | all-to-all | bytes 2359296 | tf_op jit(solution)/shard_map/all_to_all | solution.py:28
  30.6 0.7 project.1
  31.4 1.4 %collective-permute-done.refs_1_ = bf16[8,4,8,384]{3,2,1,0:T(8,128)(2,1)S(1)} collective-permute-done((bf16[8,4,8,384]{3,2,1,0:T(8,128)(2,1)S(1)}, bf16[8,4,8,384]{3,2,1,0:T(8,128)(2,1)S(1)}, u32[]{:S(2)}, u32[]{:S(2)}) %collective-permute-start) | collective-permute-done | bytes 196640 | tf_op jit(solution)/shard_map/ppermute | solution.py:24
  32.9 1.6 %collective-permute-start.1 = (bf16[8,8,384]{2,1,0:T(8,128)(2,1)S(1)}, bf16[8,8,384]{2,1,0:T(8,128)(2,1)S(1)}, u32[]{:S(2)}, u32[]{:S(2)}) collective-permute-start(bf16[8,8,384]{2,1,0:T(8,128)(2,1)S(1)} %get-tuple-element.27), channel_id=1, source_target_pairs={{0,32},{32,64},{64,96},{96,0},{1,33},{33,65},{65,97},{97,1},{2,34}... | collective-permute-start | bytes 147464 | tf_op jit(solution)/shard_map/ppermute | solution.py:24
  34.6 2.9 %collective-permute-start.2 = (bf16[8,8,384]{2,1,0:T(8,128)(2,1)S(1)}, bf16[8,8,384]{2,1,0:T(8,128)(2,1)S(1)}, u32[]{:S(2)}, u32[]{:S(2)}) collective-permute-start(bf16[8,8,384]{2,1,0:T(8,128)(2,1)S(1)} %get-tuple-element.28), channel_id=1, source_target_pairs={{0,64},{32,96},{64,0},{96,32},{1,65},{33,97},{65,1},{97,33},{2,66}... | collective-permute-start | bytes 147464 | tf_op jit(solution)/shard_map/ppermute | solution.py:24
  37.5 1.3 %collective-permute-start.3 = (bf16[8,8,384]{2,1,0:T(8,128)(2,1)S(1)}, bf16[8,8,384]{2,1,0:T(8,128)(2,1)S(1)}, u32[]{:S(2)}, u32[]{:S(2)}) collective-permute-start(bf16[8,8,384]{2,1,0:T(8,128)(2,1)S(1)} %get-tuple-element.29), channel_id=1, source_target_pairs={{0,96},{32,0},{64,32},{96,64},{1,97},{33,1},{65,33},{97,65},{2,98}... | collective-permute-start | bytes 147464 | tf_op jit(solution)/shard_map/ppermute | solution.py:24
  39.0 1.3 %collective-permute-done.2.refs_4_ = bf16[8,8,384]{2,1,0:T(8,128)(2,1)S(1)} collective-permute-done((bf16[8,8,384]{2,1,0:T(8,128)(2,1)S(1)}, bf16[8,8,384]{2,1,0:T(8,128)(2,1)S(1)}, u32[]{:S(2)}, u32[]{:S(2)}) %collective-permute-start.2) | collective-permute-done | bytes 49184 | tf_op jit(solution)/shard_map/ppermute | solution.py:24
  40.3 1.3 %collective-permute-done.3.refs_5_ = bf16[8,8,384]{2,1,0:T(8,128)(2,1)S(1)} collective-permute-done((bf16[8,8,384]{2,1,0:T(8,128)(2,1)S(1)}, bf16[8,8,384]{2,1,0:T(8,128)(2,1)S(1)}, u32[]{:S(2)}, u32[]{:S(2)}) %collective-permute-start.3) | collective-permute-done | bytes 49184 | tf_op jit(solution)/shard_map/ppermute | solution.py:24
  41.8 11.9 %all_to_all.16.refs_1_ = bf16[16,3,8,384]{3,2,1,0:T(8,128)(2,1)S(1)} all-to-all(bf16[16,3,8,384]{3,2,1,0:T(8,128)(2,1)S(1)} %attend.1), channel_id=1, replica_groups=mesh['y'=4,'c'=2,'z'=4,'x'=4] {'z','x'}, dimensions={0} | all-to-all | bytes 589824 | tf_op jit(solution)/shard_map/all_to_all | solution.py:28
  53.9 1.6 %collective-permute-start.5 = (bf16[16,6912]{1,0:T(8,128)(2,1)S(1)}, bf16[16,6912]{1,0:T(8,128)(2,1)S(1)}, u32[]{:S(2)}, u32[]{:S(2)}) collective-permute-start(bf16[16,6912]{1,0:T(8,128)(2,1)S(1)} %get-tuple-element.32), channel_id=1, source_target_pairs={{0,64},{32,96},{64,0},{96,32},{1,65},{33,97},{65,1},{97,33},{2,66}... | collective-permute-start | bytes 663560 | tf_op jit(solution)/shard_map/ppermute | solution.py:24
  55.5 1.3 %collective-permute-start.4 = (bf16[16,6912]{1,0:T(8,128)(2,1)S(1)}, bf16[16,6912]{1,0:T(8,128)(2,1)S(1)}, u32[]{:S(2)}, u32[]{:S(2)}) collective-permute-start(bf16[16,6912]{1,0:T(8,128)(2,1)S(1)} %get-tuple-element.31.after_ref), channel_id=1, source_target_pairs={{0,96},{32,0},{64,32},{96,64},{1,97},{33,1},{65,33},{97,65},{2,98}... | collective-permute-start | bytes 663560 | tf_op jit(solution)/shard_map/ppermute | solution.py:24
  56.8 0.7 collective-permute-start.6
  57.5 7.1 %fetch.1 = (bf16[576,6144]{1,0:T(8,128)(2,1)S(1)}, bf16[576,6144]{1,0:T(8,128)(2,1)S(1)}, bf16[576,6144]{1,0:T(8,128)(2,1)S(1)}, f32[8,128]{1,0:T(8,128)S(1)}) custom-call(bf16[16,6912]{1,0:T(8,128)(2,1)} %copy-done.1, bf16[576,6144]{1,0:T(8,128)(2,1)} %bitcast.18, bf16[576,6144]{1,0:T(8,128)(2,1)} %bitcast.19, bf16[576,6144]{1,0:T(8,128)(2,1)} %bitcast.20), custom_call_target="tpu_custom_call" | custom-call | bytes 21233664 | tf_op jit(solution)/shard_map/fetch/pallas_call | solution.py:325
  64.6 0.6 collective-permute-start.9
  65.7 0.6 collective-permute-done.9.refs_6_
  67.0 4.7 %hidden_units.1 = (bf16[128,576]{1,0:T(8,128)(2,1)S(1)}, bf16[4,128,768]{2,1,0:T(8,128)(2,1)S(1)}) custom-call(bf16[16,6912]{1,0:T(8,128)(2,1)S(1)} %get-tuple-element.30.refs_0_, bf16[16,6912]{1,0:T(8,128)(2,1)S(1)} %collective-permute-done.4.refs_1_, bf16[16,6912]{1,0:T(8,128)(2,1)S(1)} %collective-permute-done.5.refs_2_, ...), custom_call_target="tpu_custom_call" | custom-call | flops 2264924160 | bytes 23007232 | tf_op jit(solution)/shard_map/hidden_units/pallas_call | solution.py:33
  72.2 0.9 down.1.refs_0_
  73.0 1.1 %collective-permute-done.11.refs_1_ = bf16[4,128,768]{2,1,0:T(8,128)(2,1)S(1)} collective-permute-done((bf16[4,128,768]{2,1,0:T(8,128)(2,1)S(1)}, bf16[4,128,768]{2,1,0:T(8,128)(2,1)S(1)}, u32[]{:S(2)}, u32[]{:S(2)}) %collective-permute-start.11) | collective-permute-done | bytes 786464 | tf_op jit(solution)/shard_map/ppermute | solution.py:24
  74.1 1.0 %cores_sum.1 = bf16[4,128,768]{2,1,0:T(8,128)(2,1)} custom-call(f32[4,128,768]{2,1,0:T(8,128)S(1)} %down.1.refs_0_, bf16[4,128,768]{2,1,0:T(8,128)(2,1)S(1)} %collective-permute-done.11.refs_1_), custom_call_target="tpu_custom_call" | custom-call | bytes 2359296 | tf_op jit(solution)/shard_map/cores_sum/pallas_call | solution.py:33
  75.1 6.0 %all-to-all-start.2 = ((bf16[64,8,768]{2,1,0:T(8,128)(2,1)}), bf16[64,8,768]{2,1,0:T(8,128)(2,1)S(1)}, u32[]{:S(2)}, u32[]{:S(2)}) async-start(bf16[64,8,768]{2,1,0:T(8,128)(2,1)} %bitcast.10), calls=%async_computation.2 | async-start | bytes 1572864 | tf_op jit(solution)/shard_map/all_to_all | solution.py:28
  81.6 0.7 owned.1
  82.3 15.5 %all-to-all-done.2.refs_1_ = bf16[64,8,768]{2,1,0:T(8,128)(2,1)S(1)} async-done(((bf16[64,8,768]{2,1,0:T(8,128)(2,1)}), bf16[64,8,768]{2,1,0:T(8,128)(2,1)S(1)}, u32[]{:S(2)}, u32[]{:S(2)}) %all-to-all-start.2) | async-done | bytes 786464 | tf_op jit(solution)/shard_map/all_to_all | solution.py:28
  97.8 0.9 mix.1
  (27 shorter events, 2.8 us)
Async XLA Ops:
  0.6 30.0 %copy-start = (bf16[1024,384]{1,0:T(8,128)(2,1)S(1)}, bf16[1024,384]{1,0:T(8,128)(2,1)}, u32[]{:S(2)}) copy-start(bf16[1024,384]{1,0:T(8,128)(2,1)} %refs_1_.1) | copy-start | bytes 2359300
  0.6 53.1 %copy-start.2 = (f32[6144]{0:T(1024)S(1)}, f32[6144]{0:T(1024)}, u32[]{:S(2)}) copy-start(f32[6144]{0:T(1024)} %param.18) | copy-start | bytes 73732
  31.3 1.5 %collective-permute-start = (bf16[8,4,8,384]{3,2,1,0:T(8,128)(2,1)S(1)}, bf16[8,4,8,384]{3,2,1,0:T(8,128)(2,1)S(1)}, u32[]{:S(2)}, u32[]{:S(2)}) collective-permute-start(bf16[8,4,8,384]{3,2,1,0:T(8,128)(2,1)S(1)} %get-tuple-element.25), channel_id=1, source_target_pairs={{0,16},{16,0},{1,17},{17,1},{2,18},{18,2},{3,19},{19,3},{4,20},{20... | collective-permute-start | bytes 589832 | tf_op jit(solution)/shard_map/ppermute | solution.py:24
  32.9 6.1 %collective-permute-start.1 = (bf16[8,8,384]{2,1,0:T(8,128)(2,1)S(1)}, bf16[8,8,384]{2,1,0:T(8,128)(2,1)S(1)}, u32[]{:S(2)}, u32[]{:S(2)}) collective-permute-start(bf16[8,8,384]{2,1,0:T(8,128)(2,1)S(1)} %get-tuple-element.27), channel_id=1, source_target_pairs={{0,32},{32,64},{64,96},{96,0},{1,33},{33,65},{65,97},{97,1},{2,34}... | collective-permute-start | bytes 147464 | tf_op jit(solution)/shard_map/ppermute | solution.py:24
  34.6 5.7 %collective-permute-start.2 = (bf16[8,8,384]{2,1,0:T(8,128)(2,1)S(1)}, bf16[8,8,384]{2,1,0:T(8,128)(2,1)S(1)}, u32[]{:S(2)}, u32[]{:S(2)}) collective-permute-start(bf16[8,8,384]{2,1,0:T(8,128)(2,1)S(1)} %get-tuple-element.28), channel_id=1, source_target_pairs={{0,64},{32,96},{64,0},{96,32},{1,65},{33,97},{65,1},{97,33},{2,66}... | collective-permute-start | bytes 147464 | tf_op jit(solution)/shard_map/ppermute | solution.py:24
  37.5 4.1 %collective-permute-start.3 = (bf16[8,8,384]{2,1,0:T(8,128)(2,1)S(1)}, bf16[8,8,384]{2,1,0:T(8,128)(2,1)S(1)}, u32[]{:S(2)}, u32[]{:S(2)}) collective-permute-start(bf16[8,8,384]{2,1,0:T(8,128)(2,1)S(1)} %get-tuple-element.29), channel_id=1, source_target_pairs={{0,96},{32,0},{64,32},{96,64},{1,97},{33,1},{65,33},{97,65},{2,98}... | collective-permute-start | bytes 147464 | tf_op jit(solution)/shard_map/ppermute | solution.py:24
  53.9 3.6 %copy-start.1 = (bf16[16,6912]{1,0:T(8,128)(2,1)}, bf16[16,6912]{1,0:T(8,128)(2,1)S(1)}, u32[]{:S(2)}) copy-start(bf16[16,6912]{1,0:T(8,128)(2,1)S(1)} %get-tuple-element.31.after_ref) | copy-start | bytes 663556
  53.9 10.7 %collective-permute-start.5 = (bf16[16,6912]{1,0:T(8,128)(2,1)S(1)}, bf16[16,6912]{1,0:T(8,128)(2,1)S(1)}, u32[]{:S(2)}, u32[]{:S(2)}) collective-permute-start(bf16[16,6912]{1,0:T(8,128)(2,1)S(1)} %get-tuple-element.32), channel_id=1, source_target_pairs={{0,64},{32,96},{64,0},{96,32},{1,65},{33,97},{65,1},{97,33},{2,66}... | collective-permute-start | bytes 663560 | tf_op jit(solution)/shard_map/ppermute | solution.py:24
  55.5 9.7 %collective-permute-start.4 = (bf16[16,6912]{1,0:T(8,128)(2,1)S(1)}, bf16[16,6912]{1,0:T(8,128)(2,1)S(1)}, u32[]{:S(2)}, u32[]{:S(2)}) collective-permute-start(bf16[16,6912]{1,0:T(8,128)(2,1)S(1)} %get-tuple-element.31.after_ref), channel_id=1, source_target_pairs={{0,96},{32,0},{64,32},{96,64},{1,97},{33,1},{65,33},{97,65},{2,98}... | collective-permute-start | bytes 663560 | tf_op jit(solution)/shard_map/ppermute | solution.py:24
  56.8 8.5 %collective-permute-start.6 = (bf16[16,6912]{1,0:T(8,128)(2,1)S(1)}, bf16[16,6912]{1,0:T(8,128)(2,1)S(1)}, u32[]{:S(2)}, u32[]{:S(2)}) collective-permute-start(bf16[16,6912]{1,0:T(8,128)(2,1)S(1)} %get-tuple-element.35), channel_id=1, source_target_pairs={{0,32},{32,64},{64,96},{96,0},{1,33},{33,65},{65,97},{97,1},{2,34}... | collective-permute-start | bytes 663560 | tf_op jit(solution)/shard_map/ppermute | solution.py:24
  57.5 8.2 %collective-permute-start.7 = (bf16[16,6912]{1,0:T(8,128)(2,1)S(1)}, bf16[16,6912]{1,0:T(8,128)(2,1)S(1)}, u32[]{:S(2)}, u32[]{:S(2)}) collective-permute-start(bf16[16,6912]{1,0:T(8,128)(2,1)S(1)} %get-tuple-element.30.refs_0_), channel_id=1, source_target_pairs={{0,16},{16,0},{1,17},{17,1},{2,18},{18,2},{3,19},{19,3},{4,20},{20... | collective-permute-start | bytes 663560 | tf_op jit(solution)/shard_map/ppermute | solution.py:24
  64.6 1.7 %collective-permute-start.9 = (bf16[16,6912]{1,0:T(8,128)(2,1)S(1)}, bf16[16,6912]{1,0:T(8,128)(2,1)S(1)}, u32[]{:S(2)}, u32[]{:S(2)}) collective-permute-start(bf16[16,6912]{1,0:T(8,128)(2,1)S(1)} %collective-permute-done.5.refs_2_), channel_id=1, source_target_pairs={{0,16},{16,0},{1,17},{17,1},{2,18},{18,2},{3,19},{19,3},{4,20},{20... | collective-permute-start | bytes 663560 | tf_op jit(solution)/shard_map/ppermute | solution.py:24
  65.2 1.5 %collective-permute-start.8 = (bf16[16,6912]{1,0:T(8,128)(2,1)S(1)}, bf16[16,6912]{1,0:T(8,128)(2,1)S(1)}, u32[]{:S(2)}, u32[]{:S(2)}) collective-permute-start(bf16[16,6912]{1,0:T(8,128)(2,1)S(1)} %collective-permute-done.4.refs_1_), channel_id=1, source_target_pairs={{0,16},{16,0},{1,17},{17,1},{2,18},{18,2},{3,19},{19,3},{4,20},{20... | collective-permute-start | bytes 663560 | tf_op jit(solution)/shard_map/ppermute | solution.py:24
  65.3 1.7 %collective-permute-start.10 = (bf16[16,6912]{1,0:T(8,128)(2,1)S(1)}, bf16[16,6912]{1,0:T(8,128)(2,1)S(1)}, u32[]{:S(2)}, u32[]{:S(2)}) collective-permute-start(bf16[16,6912]{1,0:T(8,128)(2,1)S(1)} %collective-permute-done.6.refs_3_), channel_id=1, source_target_pairs={{0,16},{16,0},{1,17},{17,1},{2,18},{18,2},{3,19},{19,3},{4,20},{20... | collective-permute-start | bytes 663560 | tf_op jit(solution)/shard_map/ppermute | solution.py:24
  71.7 9.4 %copy-start.3 = (s32[4,8,2]{1,2,0:T(2,128)S(1)}, s32[4,8,2]{1,2,0:T(2,128)}, u32[]{:S(2)}) copy-start(s32[4,8,2]{1,2,0:T(2,128)} %param.19) | copy-start | bytes 772
  71.8 9.4 %copy-start.4 = (f32[4,8,2]{1,2,0:T(2,128)S(1)}, f32[4,8,2]{1,2,0:T(2,128)}, u32[]{:S(2)}) copy-start(f32[4,8,2]{1,2,0:T(2,128)} %param.20) | copy-start | bytes 772
  71.8 2.4 %collective-permute-start.11 = (bf16[4,128,768]{2,1,0:T(8,128)(2,1)S(1)}, bf16[4,128,768]{2,1,0:T(8,128)(2,1)S(1)}, u32[]{:S(2)}, u32[]{:S(2)}) collective-permute-start(bf16[4,128,768]{2,1,0:T(8,128)(2,1)S(1)} %get-tuple-element.41), channel_id=1, source_target_pairs={{0,16},{16,0},{1,17},{17,1},{2,18},{18,2},{3,19},{19,3},{4,20},{20... | collective-permute-start | bytes 2359304 | tf_op jit(solution)/shard_map/ppermute | solution.py:24
  75.1 22.6 %all-to-all-start.2 = ((bf16[64,8,768]{2,1,0:T(8,128)(2,1)}), bf16[64,8,768]{2,1,0:T(8,128)(2,1)S(1)}, u32[]{:S(2)}, u32[]{:S(2)}) async-start(bf16[64,8,768]{2,1,0:T(8,128)(2,1)} %bitcast.10), calls=%async_computation.2 | async-start | bytes 1572864 | tf_op jit(solution)/shard_map/all_to_all | solution.py:28

commit v10 on v9

--- a/solution.py
+++ b/solution.py
@@ -91,7 +91,7 @@
     def _():
         names = widened(columns_of(routes_ref[y].astype(F32)))
         for i in range(16):
-            rows = hidden_ref[y, :, i * cols : (i + 1) * cols].astype(F32)
+            rows = hidden_ref[0, :, i * cols : (i + 1) * cols].astype(F32)
             first = jnp.concatenate([rows[:, :128], rows[:, 128:256]], axis=0)
             last = jnp.concatenate([rows[:, 256:], names], axis=0)
             out_ref[i, :16, depth:] = first.astype(BF16)
@@ -157,7 +157,7 @@
         in_specs=[
             pl.BlockSpec(decay.shape, lambda i: (0, 0)),
             pl.BlockSpec((STEPS, 2, ROWS), lambda i: (0, 0, 0)),
-            pl.BlockSpec(hidden_in.shape, lambda i: (0, 0, 0)),
+            pl.BlockSpec((1,) + hidden_in.shape[1:], lambda i: (lax.axis_index("y"), 0, 0)),
             pl.BlockSpec((STEPS, 3, ROWS, at_once * size), lambda i: (0, 0, 0, i)),
             pl.BlockSpec((ROWS, at_once, size, size), lambda i: (0, i, 0, 0)),
             pl.BlockSpec((1, at_once * size), lambda i: (0, i)),
@@ -465,7 +465,7 @@
     mine, other = project(got, out_proj)
     sums = sums_by_y(mine, over("c", other, 1))
     select, hidden = slots(got, out_proj.shape[1])
-    sums = sums[:1] + [over("y", sums[k], k) for k in (1, 2, 3)]
+    sums = sums[:1] + [over("y", sums[k], k) for k in (2, 1, 3)]
 
     pieces = norm(ffn_gain, exchange(attend(select, hidden, sums), ("z", "x")))
     by_y = pieces[:1] + [over("y", pieces[k], -k) for k in (1, 2, 3)]

time: 98.9 us -> 99.3 us (level)
  starting transfers between devices: 17 us -> 18.1 us
    ppermute x12, starting transfers between devices: 11.1 us -> 12.3 us  [over(): lax.ppermute(value, axis, [(i, (i + shift) % size) for i in range(size)])]
  transfers between devices with their start and end apart: 13 -> 13, of which waited for: 8 -> 7; matrix products, arithmetic and copies ran while one was open for 0% -> 0% of each run, Pallas kernels for 9% -> 9%
where the time goes in v10:
time: 99.3 us; the launch traced here: 99 us
  blocking collectives  38.3 us (39%)
  waiting for transfers between devices  21.2 us (21%)
  Pallas kernels  20.6 us (21%)
  starting transfers between devices  18.1 us (18%)
    all_to_all x2, blocking collectives, exchange(): return lax.all_to_all(value, axes, split_axis=0, concat_axis=0, tiled=True)  38.3 us
    all_to_all x1, waiting for transfers between devices, exchange(): return lax.all_to_all(value, axes, split_axis=0, concat_axis=0, tiled=True)  15.5 us
    ppermute x12, starting transfers between devices, over(): lax.ppermute(value, axis, [(i, (i + shift) % size) for i in range(size)])  12.3 us
    pallas_call x11, Pallas kernels, call(): pl.pallas_call(lambda *refs: kernel(device_place(), *refs), out_shape=out...  9.95 us
    pallas_call x1, Pallas kernels, fetch(): pl.pallas_call(fetch_kernel, out_shape=[pltpu.VMEM(w.shape, w.dtype) for...  7.06 us
    all_to_all x1, starting transfers between devices, exchange(): return lax.all_to_all(value, axes, split_axis=0, concat_axis=0, tiled=True)  5.86 us
    ppermute x12, waiting for transfers between devices, over(): lax.ppermute(value, axis, [(i, (i + shift) % size) for i in range(size)])  5.7 us
    pallas_call x1, Pallas kernels, readouts(): pl.pallas_call(readout_kernel, out_shape=pltpu.VMEM((16, n, packed), BF16...  3.61 us
  transfers between devices with their start and end apart: 13, of which 7 were waited for; matrix products, arithmetic and copies ran while one was open for 0% of the time, Pallas kernels for 9%

profile of v10, /device:TPU:0, one launch (start us, length us, event | category | flops | bytes accessed | tf_op | source)
XLA Modules:
  0.0 99.0 jit_solution(4353820444642936067)
XLA Ops:
  0.7 3.6 %readout.1 = bf16[16,32,1152]{2,1,0:T(8,128)(2,1)S(1)} custom-call(f32[4,8]{1,0:T(4,128)} %decay_ref.1, s32[4,2,8]{2,1,0:T(2,128)} %bitcast.15, bf16[4,8,6144]{2,1,0:T(8,128)(2,1)} %hidden_ref.1, bf16[4,3,8,1024]{3,2,1,0:T(8,128)(2,1)} %bitcast.21, f32[8,8,128,128]{3,2,1,0:T(8,128)} %state_ref.1, f32[1,1024]{1,0:T(1,128)} %bitcast.23), custom_call_target="tpu_custom_call" | custom-call | flops 134217728 | bytes 4194304 | tf_op jit(solution)/shard_map/readout/pallas_call | solution.py:153
  4.3 26.3 %all_to_all.15.refs_0_ = bf16[16,32,1152]{2,1,0:T(8,128)(2,1)S(1)} all-to-all(bf16[16,32,1152]{2,1,0:T(8,128)(2,1)S(1)} %readout.1), channel_id=1, replica_groups=mesh['y'=4,'c'=2,'z'=4,'x'=4] {'z','x'}, dimensions={0} | all-to-all | bytes 2359296 | tf_op jit(solution)/shard_map/all_to_all | solution.py:28
  30.6 0.7 project.1
  31.4 1.4 %collective-permute-done.refs_1_ = bf16[8,4,8,384]{3,2,1,0:T(8,128)(2,1)S(1)} collective-permute-done((bf16[8,4,8,384]{3,2,1,0:T(8,128)(2,1)S(1)}, bf16[8,4,8,384]{3,2,1,0:T(8,128)(2,1)S(1)}, u32[]{:S(2)}, u32[]{:S(2)}) %collective-permute-start) | collective-permute-done | bytes 196640 | tf_op jit(solution)/shard_map/ppermute | solution.py:24
  32.9 3.3 %collective-permute-start.1 = (bf16[8,8,384]{2,1,0:T(8,128)(2,1)S(1)}, bf16[8,8,384]{2,1,0:T(8,128)(2,1)S(1)}, u32[]{:S(2)}, u32[]{:S(2)}) collective-permute-start(bf16[8,8,384]{2,1,0:T(8,128)(2,1)S(1)} %get-tuple-element.27), channel_id=1, source_target_pairs={{0,64},{32,96},{64,0},{96,32},{1,65},{33,97},{65,1},{97,33},{2,66}... | collective-permute-start | bytes 147464 | tf_op jit(solution)/shard_map/ppermute | solution.py:24
  36.2 0.7 collective-permute-start.2
  36.8 2.6 %collective-permute-start.3 = (bf16[8,8,384]{2,1,0:T(8,128)(2,1)S(1)}, bf16[8,8,384]{2,1,0:T(8,128)(2,1)S(1)}, u32[]{:S(2)}, u32[]{:S(2)}) collective-permute-start(bf16[8,8,384]{2,1,0:T(8,128)(2,1)S(1)} %get-tuple-element.29), channel_id=1, source_target_pairs={{0,96},{32,0},{64,32},{96,64},{1,97},{33,1},{65,33},{97,65},{2,98}... | collective-permute-start | bytes 147464 | tf_op jit(solution)/shard_map/ppermute | solution.py:24
  39.6 1.9 %collective-permute-done.2.refs_4_ = bf16[8,8,384]{2,1,0:T(8,128)(2,1)S(1)} collective-permute-done((bf16[8,8,384]{2,1,0:T(8,128)(2,1)S(1)}, bf16[8,8,384]{2,1,0:T(8,128)(2,1)S(1)}, u32[]{:S(2)}, u32[]{:S(2)}) %collective-permute-start.2) | collective-permute-done | bytes 49184 | tf_op jit(solution)/shard_map/ppermute | solution.py:24
  41.7 11.9 %all_to_all.16.refs_1_ = bf16[16,3,8,384]{3,2,1,0:T(8,128)(2,1)S(1)} all-to-all(bf16[16,3,8,384]{3,2,1,0:T(8,128)(2,1)S(1)} %attend.1), channel_id=1, replica_groups=mesh['y'=4,'c'=2,'z'=4,'x'=4] {'z','x'}, dimensions={0} | all-to-all | bytes 589824 | tf_op jit(solution)/shard_map/all_to_all | solution.py:28
  53.8 1.5 %collective-permute-start.5 = (bf16[16,6912]{1,0:T(8,128)(2,1)S(1)}, bf16[16,6912]{1,0:T(8,128)(2,1)S(1)}, u32[]{:S(2)}, u32[]{:S(2)}) collective-permute-start(bf16[16,6912]{1,0:T(8,128)(2,1)S(1)} %get-tuple-element.32), channel_id=1, source_target_pairs={{0,64},{32,96},{64,0},{96,32},{1,65},{33,97},{65,1},{97,33},{2,66}... | collective-permute-start | bytes 663560 | tf_op jit(solution)/shard_map/ppermute | solution.py:24
  55.4 1.8 %collective-permute-start.4 = (bf16[16,6912]{1,0:T(8,128)(2,1)S(1)}, bf16[16,6912]{1,0:T(8,128)(2,1)S(1)}, u32[]{:S(2)}, u32[]{:S(2)}) collective-permute-start(bf16[16,6912]{1,0:T(8,128)(2,1)S(1)} %get-tuple-element.31.after_ref), channel_id=1, source_target_pairs={{0,96},{32,0},{64,32},{96,64},{1,97},{33,1},{65,33},{97,65},{2,98}... | collective-permute-start | bytes 663560 | tf_op jit(solution)/shard_map/ppermute | solution.py:24
  57.2 0.8 collective-permute-start.6
  58.0 7.1 %fetch.1 = (bf16[576,6144]{1,0:T(8,128)(2,1)S(1)}, bf16[576,6144]{1,0:T(8,128)(2,1)S(1)}, bf16[576,6144]{1,0:T(8,128)(2,1)S(1)}, f32[8,128]{1,0:T(8,128)S(1)}) custom-call(bf16[16,6912]{1,0:T(8,128)(2,1)} %copy-done.1, bf16[576,6144]{1,0:T(8,128)(2,1)} %bitcast.18, bf16[576,6144]{1,0:T(8,128)(2,1)} %bitcast.19, bf16[576,6144]{1,0:T(8,128)(2,1)} %bitcast.20), custom_call_target="tpu_custom_call" | custom-call | bytes 21233664 | tf_op jit(solution)/shard_map/fetch/pallas_call | solution.py:325
  65.1 0.6 collective-permute-start.9
  66.2 0.6 collective-permute-done.9.refs_6_
  67.5 4.7 %hidden_units.1 = (bf16[128,576]{1,0:T(8,128)(2,1)S(1)}, bf16[4,128,768]{2,1,0:T(8,128)(2,1)S(1)}) custom-call(bf16[16,6912]{1,0:T(8,128)(2,1)S(1)} %get-tuple-element.30.refs_0_, bf16[16,6912]{1,0:T(8,128)(2,1)S(1)} %collective-permute-done.4.refs_1_, bf16[16,6912]{1,0:T(8,128)(2,1)S(1)} %collective-permute-done.5.refs_2_, ...), custom_call_target="tpu_custom_call" | custom-call | flops 2264924160 | bytes 23007232 | tf_op jit(solution)/shard_map/hidden_units/pallas_call | solution.py:33
  72.6 0.9 down.1.refs_0_
  73.5 1.1 %collective-permute-done.11.refs_1_ = bf16[4,128,768]{2,1,0:T(8,128)(2,1)S(1)} collective-permute-done((bf16[4,128,768]{2,1,0:T(8,128)(2,1)S(1)}, bf16[4,128,768]{2,1,0:T(8,128)(2,1)S(1)}, u32[]{:S(2)}, u32[]{:S(2)}) %collective-permute-start.11) | collective-permute-done | bytes 786464 | tf_op jit(solution)/shard_map/ppermute | solution.py:24
  74.6 1.0 %cores_sum.1 = bf16[4,128,768]{2,1,0:T(8,128)(2,1)} custom-call(f32[4,128,768]{2,1,0:T(8,128)S(1)} %down.1.refs_0_, bf16[4,128,768]{2,1,0:T(8,128)(2,1)S(1)} %collective-permute-done.11.refs_1_), custom_call_target="tpu_custom_call" | custom-call | bytes 2359296 | tf_op jit(solution)/shard_map/cores_sum/pallas_call | solution.py:33
  75.6 5.9 %all-to-all-start.2 = ((bf16[64,8,768]{2,1,0:T(8,128)(2,1)}), bf16[64,8,768]{2,1,0:T(8,128)(2,1)S(1)}, u32[]{:S(2)}, u32[]{:S(2)}) async-start(bf16[64,8,768]{2,1,0:T(8,128)(2,1)} %bitcast.10), calls=%async_computation.2 | async-start | bytes 1572864 | tf_op jit(solution)/shard_map/all_to_all | solution.py:28
  81.5 0.5 mix_weights.1.refs_0_
  82.0 0.7 owned.1
  82.7 15.5 %all-to-all-done.2.refs_1_ = bf16[64,8,768]{2,1,0:T(8,128)(2,1)S(1)} async-done(((bf16[64,8,768]{2,1,0:T(8,128)(2,1)}), bf16[64,8,768]{2,1,0:T(8,128)(2,1)S(1)}, u32[]{:S(2)}, u32[]{:S(2)}) %all-to-all-start.2) | async-done | bytes 786464 | tf_op jit(solution)/shard_map/all_to_all | solution.py:28
  98.1 0.9 mix.1
  (27 shorter events, 2.3 us)
Async XLA Ops:
  0.6 30.0 %copy-start = (bf16[1024,384]{1,0:T(8,128)(2,1)S(1)}, bf16[1024,384]{1,0:T(8,128)(2,1)}, u32[]{:S(2)}) copy-start(bf16[1024,384]{1,0:T(8,128)(2,1)} %refs_1_.1) | copy-start | bytes 2359300
  0.6 53.0 %copy-start.2 = (f32[6144]{0:T(1024)S(1)}, f32[6144]{0:T(1024)}, u32[]{:S(2)}) copy-start(f32[6144]{0:T(1024)} %param.18) | copy-start | bytes 73732
  31.3 1.5 %collective-permute-start = (bf16[8,4,8,384]{3,2,1,0:T(8,128)(2,1)S(1)}, bf16[8,4,8,384]{3,2,1,0:T(8,128)(2,1)S(1)}, u32[]{:S(2)}, u32[]{:S(2)}) collective-permute-start(bf16[8,4,8,384]{3,2,1,0:T(8,128)(2,1)S(1)} %get-tuple-element.25), channel_id=1, source_target_pairs={{0,16},{16,0},{1,17},{17,1},{2,18},{18,2},{3,19},{19,3},{4,20},{20... | collective-permute-start | bytes 589832 | tf_op jit(solution)/shard_map/ppermute | solution.py:24
  32.9 6.7 %collective-permute-start.1 = (bf16[8,8,384]{2,1,0:T(8,128)(2,1)S(1)}, bf16[8,8,384]{2,1,0:T(8,128)(2,1)S(1)}, u32[]{:S(2)}, u32[]{:S(2)}) collective-permute-start(bf16[8,8,384]{2,1,0:T(8,128)(2,1)S(1)} %get-tuple-element.27), channel_id=1, source_target_pairs={{0,64},{32,96},{64,0},{96,32},{1,65},{33,97},{65,1},{97,33},{2,66}... | collective-permute-start | bytes 147464 | tf_op jit(solution)/shard_map/ppermute | solution.py:24
  36.2 5.3 %collective-permute-start.2 = (bf16[8,8,384]{2,1,0:T(8,128)(2,1)S(1)}, bf16[8,8,384]{2,1,0:T(8,128)(2,1)S(1)}, u32[]{:S(2)}, u32[]{:S(2)}) collective-permute-start(bf16[8,8,384]{2,1,0:T(8,128)(2,1)S(1)} %get-tuple-element.28), channel_id=1, source_target_pairs={{0,32},{32,64},{64,96},{96,0},{1,33},{33,65},{65,97},{97,1},{2,34}... | collective-permute-start | bytes 147464 | tf_op jit(solution)/shard_map/ppermute | solution.py:24
  36.8 4.6 %collective-permute-start.3 = (bf16[8,8,384]{2,1,0:T(8,128)(2,1)S(1)}, bf16[8,8,384]{2,1,0:T(8,128)(2,1)S(1)}, u32[]{:S(2)}, u32[]{:S(2)}) collective-permute-start(bf16[8,8,384]{2,1,0:T(8,128)(2,1)S(1)} %get-tuple-element.29), channel_id=1, source_target_pairs={{0,96},{32,0},{64,32},{96,64},{1,97},{33,1},{65,33},{97,65},{2,98}... | collective-permute-start | bytes 147464 | tf_op jit(solution)/shard_map/ppermute | solution.py:24
  53.8 4.2 %copy-start.1 = (bf16[16,6912]{1,0:T(8,128)(2,1)}, bf16[16,6912]{1,0:T(8,128)(2,1)S(1)}, u32[]{:S(2)}) copy-start(bf16[16,6912]{1,0:T(8,128)(2,1)S(1)} %get-tuple-element.31.after_ref) | copy-start | bytes 663556
  53.8 11.2 %collective-permute-start.5 = (bf16[16,6912]{1,0:T(8,128)(2,1)S(1)}, bf16[16,6912]{1,0:T(8,128)(2,1)S(1)}, u32[]{:S(2)}, u32[]{:S(2)}) collective-permute-start(bf16[16,6912]{1,0:T(8,128)(2,1)S(1)} %get-tuple-element.32), channel_id=1, source_target_pairs={{0,64},{32,96},{64,0},{96,32},{1,65},{33,97},{65,1},{97,33},{2,66}... | collective-permute-start | bytes 663560 | tf_op jit(solution)/shard_map/ppermute | solution.py:24
  55.4 10.3 %collective-permute-start.4 = (bf16[16,6912]{1,0:T(8,128)(2,1)S(1)}, bf16[16,6912]{1,0:T(8,128)(2,1)S(1)}, u32[]{:S(2)}, u32[]{:S(2)}) collective-permute-start(bf16[16,6912]{1,0:T(8,128)(2,1)S(1)} %get-tuple-element.31.after_ref), channel_id=1, source_target_pairs={{0,96},{32,0},{64,32},{96,64},{1,97},{33,1},{65,33},{97,65},{2,98}... | collective-permute-start | bytes 663560 | tf_op jit(solution)/shard_map/ppermute | solution.py:24
  57.2 8.6 %collective-permute-start.6 = (bf16[16,6912]{1,0:T(8,128)(2,1)S(1)}, bf16[16,6912]{1,0:T(8,128)(2,1)S(1)}, u32[]{:S(2)}, u32[]{:S(2)}) collective-permute-start(bf16[16,6912]{1,0:T(8,128)(2,1)S(1)} %get-tuple-element.35), channel_id=1, source_target_pairs={{0,32},{32,64},{64,96},{96,0},{1,33},{33,65},{65,97},{97,1},{2,34}... | collective-permute-start | bytes 663560 | tf_op jit(solution)/shard_map/ppermute | solution.py:24
  58.0 8.2 %collective-permute-start.7 = (bf16[16,6912]{1,0:T(8,128)(2,1)S(1)}, bf16[16,6912]{1,0:T(8,128)(2,1)S(1)}, u32[]{:S(2)}, u32[]{:S(2)}) collective-permute-start(bf16[16,6912]{1,0:T(8,128)(2,1)S(1)} %get-tuple-element.30.refs_0_), channel_id=1, source_target_pairs={{0,16},{16,0},{1,17},{17,1},{2,18},{18,2},{3,19},{19,3},{4,20},{20... | collective-permute-start | bytes 663560 | tf_op jit(solution)/shard_map/ppermute | solution.py:24
  65.1 1.7 %collective-permute-start.9 = (bf16[16,6912]{1,0:T(8,128)(2,1)S(1)}, bf16[16,6912]{1,0:T(8,128)(2,1)S(1)}, u32[]{:S(2)}, u32[]{:S(2)}) collective-permute-start(bf16[16,6912]{1,0:T(8,128)(2,1)S(1)} %collective-permute-done.5.refs_2_), channel_id=1, source_target_pairs={{0,16},{16,0},{1,17},{17,1},{2,18},{18,2},{3,19},{19,3},{4,20},{20... | collective-permute-start | bytes 663560 | tf_op jit(solution)/shard_map/ppermute | solution.py:24
  65.7 1.5 %collective-permute-start.8 = (bf16[16,6912]{1,0:T(8,128)(2,1)S(1)}, bf16[16,6912]{1,0:T(8,128)(2,1)S(1)}, u32[]{:S(2)}, u32[]{:S(2)}) collective-permute-start(bf16[16,6912]{1,0:T(8,128)(2,1)S(1)} %collective-permute-done.4.refs_1_), channel_id=1, source_target_pairs={{0,16},{16,0},{1,17},{17,1},{2,18},{18,2},{3,19},{19,3},{4,20},{20... | collective-permute-start | bytes 663560 | tf_op jit(solution)/shard_map/ppermute | solution.py:24
  65.8 1.7 %collective-permute-start.10 = (bf16[16,6912]{1,0:T(8,128)(2,1)S(1)}, bf16[16,6912]{1,0:T(8,128)(2,1)S(1)}, u32[]{:S(2)}, u32[]{:S(2)}) collective-permute-start(bf16[16,6912]{1,0:T(8,128)(2,1)S(1)} %collective-permute-done.6.refs_3_), channel_id=1, source_target_pairs={{0,16},{16,0},{1,17},{17,1},{2,18},{18,2},{3,19},{19,3},{4,20},{20... | collective-permute-start | bytes 663560 | tf_op jit(solution)/shard_map/ppermute | solution.py:24
  72.2 9.3 %copy-start.3 = (s32[4,8,2]{1,2,0:T(2,128)S(1)}, s32[4,8,2]{1,2,0:T(2,128)}, u32[]{:S(2)}) copy-start(s32[4,8,2]{1,2,0:T(2,128)} %param.19) | copy-start | bytes 772
  72.2 9.3 %copy-start.4 = (f32[4,8,2]{1,2,0:T(2,128)S(1)}, f32[4,8,2]{1,2,0:T(2,128)}, u32[]{:S(2)}) copy-start(f32[4,8,2]{1,2,0:T(2,128)} %param.20) | copy-start | bytes 772
  72.2 2.4 %collective-permute-start.11 = (bf16[4,128,768]{2,1,0:T(8,128)(2,1)S(1)}, bf16[4,128,768]{2,1,0:T(8,128)(2,1)S(1)}, u32[]{:S(2)}, u32[]{:S(2)}) collective-permute-start(bf16[4,128,768]{2,1,0:T(8,128)(2,1)S(1)} %get-tuple-element.41), channel_id=1, source_target_pairs={{0,16},{16,0},{1,17},{17,1},{2,18},{18,2},{3,19},{19,3},{4,20},{20... | collective-permute-start | bytes 2359304 | tf_op jit(solution)/shard_map/ppermute | solution.py:24
  75.6 22.5 %all-to-all-start.2 = ((bf16[64,8,768]{2,1,0:T(8,128)(2,1)}), bf16[64,8,768]{2,1,0:T(8,128)(2,1)S(1)}, u32[]{:S(2)}, u32[]{:S(2)}) async-start(bf16[64,8,768]{2,1,0:T(8,128)(2,1)} %bitcast.10), calls=%async_computation.2 | async-start | bytes 1572864 | tf_op jit(solution)/shard_map/all_to_all | solution.py:28
